TPU v7x, 32 devices: a whole 2x2x4 slice. The times are simulated.
32 devices in a mesh: section: 2 (over z_hi), dp: 8 (over y, x, core), shard: 2 (over z_lo).
Axes of the slice: x: 2, y: 2, z: 4 (z_hi: 2, z_lo: 2; z = z_hi * 2 + z_lo), core: 2. Of those that a mesh axis runs over, the one named last changes fastest.
Arguments:
- tokens: bfloat16 [2, 2048, 1536], P(None, 'dp'), may hold values from -6 to 6
- lengths: int32 [2, 8, 4], P(None, 'dp'), may hold values from 1 to 128, 256 in all within a row
- routes: int32 [2, 2, 2048, 4], P('section', None, 'dp'), may hold values from 0 to 7, all different within a row; in each aligned block of 256 rows (0 to 255, 256 to 511, ..., all dimensions but the last counted through in order) at most 256 rows name the same one
- gates: float32 [2, 2, 2048, 4], P('section', None, 'dp'), may hold values from 0.15 to 0.4
- attn_gain: float32 [2, 1536], P('section'), may hold values from 0.5 to 1.5
- q_weight: bfloat16 [2, 1536, 1536], P('section', None, 'shard'), may hold values from -0.15625 to 0.15625
- key_projection: bfloat16 [2, 1536, 256], P('section', None, 'shard'), may hold values from -0.15625 to 0.15625
- value_projection: bfloat16 [2, 1536, 256], P('section', None, 'shard'), may hold values from -0.15625 to 0.15625
- o_weight: bfloat16 [2, 1536, 1536], P('section', None, 'shard'), may hold values from -0.3125 to 0.3125
- mlp_gain: float32 [2, 1536], P('section'), may hold values from 0.5 to 1.5
- expert_gate: bfloat16 [2, 8, 1536, 768], P('section', 'dp', None, 'shard'), may hold values from -0.15625 to 0.15625
- expert_up: bfloat16 [2, 8, 1536, 768], P('section', 'dp', None, 'shard'), may hold values from -0.15625 to 0.15625
- expert_down: bfloat16 [2, 8, 768, 1536], P('section', 'dp', 'shard'), may hold values from -0.4375 to 0.4375
- cotangent: bfloat16 [2, 2048, 1536], P(None, 'dp'), may hold values from -6 to 6
Outputs:
- section_out: bfloat16 [2, 2, 2048, 1536], P('section', None, 'dp', 'shard')
- input_grad: float32 [2, 2, 2048, 1536], P('section', None, 'dp', 'shard')
- attn_gain_grad: float32 [2, 1536], P('section', 'dp')
- q_weight_grad: float32 [2, 1536, 1536], P('section', 'dp', 'shard')
- k_weight_grad: float32 [2, 1536, 256], P('section', 'dp', 'shard')
- v_weight_grad: float32 [2, 1536, 256], P('section', 'dp', 'shard')
- o_weight_grad: float32 [2, 1536, 1536], P('section', 'dp', 'shard')
- mlp_gain_grad: float32 [2, 1536], P('section', 'dp')
- expert_gate_grad: float32 [2, 8, 1536, 768], P('section', 'dp', None, 'shard')
- expert_up_grad: float32 [2, 8, 1536, 768], P('section', 'dp', None, 'shard')
- expert_down_grad: float32 [2, 8, 768, 1536], P('section', 'dp', 'shard')
Inputs may be any that keep to these rules, and one draw needn't show every extreme that they name: `routes`: in each aligned block of 256 rows (one section, micro-batch and index of dp), no expert is named by more than 256 rows, a bound that some block reaches. The 4 lengths of a block sum to 256; the longest is exactly 128.
All inputs are finite; a program needn't handle non-finite values.
Results may differ from a plain program's by a relative error of at most 0.03.
Values may be sent and summed in bfloat16 or wider, within the bound.
No kernel may reach another device: no remote copies, remote signals or barrier semaphores. Data moves between devices by JAX's collectives and lax.ppermute only.
A program may use at most 256 MiB of HBM per device.

v0:
```python
import functools

import jax
import jax.numpy as jnp
import numpy as np
from jax import lax
from jax.experimental import pallas as pl
from jax.experimental.pallas import tpu as pltpu
from jax.sharding import PartitionSpec as P

HEAD_SIZE = 128
epsilon = 1e-06
masked_value = -1e30
bf16 = jnp.bfloat16
f32 = jnp.float32


def wide(a):
    return a.astype(f32)


def dot_nn(a, b):
    return lax.dot_general(a, b, (((1,), (0,)), ((), ())), preferred_element_type=f32)


def dot_nt(a, b):
    return lax.dot_general(a, b, (((1,), (1,)), ((), ())), preferred_element_type=f32)


def dot_tn(a, b):
    return lax.dot_general(a, b, (((0,), (0,)), ((), ())), preferred_element_type=f32)


class Cube:
    def __init__(self):
        peers = lax.axis_size("dp")
        bits = [1 << i for i in range(peers.bit_length() - 1)]
        rest = bits[1:]
        self.core = ("dp", bits[0])
        self.x = ("dp", rest[0])
        self.y = ("dp", rest[len(rest) // 2])
        self.z = ("shard", 1)
        self.extra = [("dp", b) for b in rest if b not in (self.x[1], self.y[1])]
        inner = [0]
        for _, bit in self.extra:
            inner = inner + [m | bit for m in inner]
        self.inner = np.array(inner)
        x, y = self.x[1], self.y[1]
        stages = [[(0, 0)], [(x, 0), (y, 0), (0, 1)], [(x | y, 0), (y, 1), (x, 1)], [(x | y, 1)]]
        self.stages = [(g, [(m | self.core[1], s) for m, s in g]) for g in stages]


def swap(value, direction):
    axis, bit = direction
    return lax.ppermute(value, axis, [(i, i ^ bit) for i in range(lax.axis_size(axis))])


def thirds(rows):
    step = -(-rows // 48) * 16
    return [(0, step), (step, 2 * step), (2 * step, rows)]


together = lax.optimization_barrier


def after(payload, thunks, step):
    if step >= len(thunks) or thunks[step] is None:
        return payload, lambda: ()
    inputs, work = thunks[step]
    payload, inputs = together((payload, inputs()))
    return payload, lambda: work(*inputs)


def gather_rows(cube, own, work, side=()):
    core = cube.core
    own, beside = after(own, side, 0)
    near = [swap(own, d) for d in (cube.x, cube.y, cube.z)]
    mine0, other0 = work(0, [own, swap(own, core)])
    near, mine0, other0, _ = together((near, mine0, other0, beside()))

    near, beside = after(near, side, 1)
    middle = [swap(block, d) for block, d in zip(near, (cube.y, cube.z, cube.x))]
    in0 = swap(other0, core)
    mine1, other1 = work(1, [*near, *[swap(block, core) for block in near]])
    middle, in0, mine1, other1, _ = together((middle, in0, mine1, other1, beside()))

    middle, beside = after(middle, side, 2)
    cuts = thirds(own.shape[0])
    last = [
        swap(block[lo:hi], d) for block, d, (lo, hi) in zip(middle, (cube.z, cube.x, cube.y), cuts)
    ]
    in1 = swap(other1, core)
    mine2, other2 = work(2, [*middle, *[swap(block, core) for block in middle]])
    last, in1, mine2, other2, _ = together((last, in1, mine2, other2, beside()))

    in2 = swap(other2, core)
    mine3, other3 = work(3, [*last, *[swap(block, core) for block in last]])
    return [(mine0, in0), (mine1, in1), (mine2, in2), (mine3, swap(other3, core))]


def low_sum(*terms):
    return sum(wide(t) for t in terms).astype(bf16)


def reduce_rows(cube, pairs, side=()):
    own, near, middle, last = pairs
    rows = last[0].shape[0]

    def block(i, pair):
        return [g[i * rows : (i + 1) * rows] for g in pair]

    cuts = thirds(rows)
    sent, beside = after(low_sum(*last), side, 0)
    arrived = [swap(sent[lo:hi], d) for d, (lo, hi) in zip((cube.z, cube.x, cube.y), cuts)]
    arrived, middle, _ = together((arrived, middle, beside()))
    sent = [
        low_sum(*block(i, middle), jnp.pad(arrived[i], ((lo, rows - hi), (0, 0))))
        for i, (lo, hi) in enumerate(cuts)
    ]
    sent, beside = after(sent, side, 1)
    arrived = [swap(t, d) for t, d in zip(sent, (cube.y, cube.z, cube.x))]
    arrived, near, _ = together((arrived, near, beside()))
    sent = [low_sum(*block(i, near), arrived[i]) for i in range(3)]
    sent, beside = after(sent, side, 2)
    arrived = [swap(t, d) for t, d in zip(sent, (cube.x, cube.y, cube.z))]
    arrived, own, _ = together((arrived, own, beside()))
    total = sum(wide(t) for t in [*own, *arrived])
    for direction in reversed(cube.extra):
        half = total.shape[0] // 2
        total = total[:half] + wide(swap(total[half:].astype(bf16), direction))
    return total


def norm_factor(values):
    return lax.rsqrt(jnp.mean(values * values, axis=1, keepdims=True) + epsilon)


def norm_back(values, factor, gain, grad):
    gain_grad = jnp.sum(grad * values * factor, axis=0, keepdims=True)
    scaled = grad * gain
    inner = jnp.mean(scaled * values, axis=1, keepdims=True)
    return factor * (scaled - values * factor * factor * inner), gain_grad


def stack_heads(rows):
    return jnp.concatenate(
        [rows[:, i : i + HEAD_SIZE] for i in range(0, rows.shape[1], HEAD_SIZE)], axis=0
    )


def spread_heads(stacked, rows):
    return jnp.concatenate(
        [stacked[i : i + rows] for i in range(0, stacked.shape[0], rows)], axis=1
    )


def head_probs(query, key, allowed):
    scores = jnp.where(allowed > 0.0, dot_nt(query, key) * HEAD_SIZE ** (-0.5), masked_value)
    exp_scores = jnp.exp(scores - jnp.max(scores, axis=1, keepdims=True))
    return exp_scores / jnp.sum(exp_scores, axis=1, keepdims=True)


def normed_rows(values, gain):
    return (values * norm_factor(values) * gain).astype(bf16)


def group_probs(qkv, allowed):
    width = qkv.shape[1] - 2 * HEAD_SIZE
    query = stack_heads(qkv[:, :width])
    key, value = qkv[:, width : width + HEAD_SIZE], qkv[:, width + HEAD_SIZE :]
    tiled = jnp.concatenate([allowed] * (width // HEAD_SIZE), axis=0)
    return query, key, value, head_probs(query, key, tiled)


def head_group(normed, allowed, weights, qkv, heads):
    w_query, w_key, w_value, w_out = weights
    width = w_query.shape[1]
    qkv[:, :width] = dot_nn(normed, w_query).astype(bf16)
    qkv[:, width : width + HEAD_SIZE] = dot_nn(normed, w_key).astype(bf16)
    qkv[:, width + HEAD_SIZE :] = dot_nn(normed, w_value).astype(bf16)
    _, _, value, probs = group_probs(qkv[...], allowed)
    heads[...] = spread_heads(dot_nn(probs.astype(bf16), value).astype(bf16), normed.shape[0])
    return dot_nt(heads[...], w_out)


VMEM = pl.BlockSpec(memory_space=pltpu.VMEM)
SMEM = pl.BlockSpec(memory_space=pltpu.SMEM)
KERNEL_VMEM = 62 << 20


def like(shape, dtype):
    return jax.ShapeDtypeStruct(shape, dtype)


def on_device(body, outs, args, flops, scalars=()):
    moved = sum(a.size * a.dtype.itemsize for a in [*args, *outs])
    return pl.pallas_call(
        body,
        out_shape=outs,
        in_specs=[SMEM] * len(scalars) + [VMEM] * len(args),
        out_specs=[VMEM] * len(outs),
        compiler_params=pltpu.CompilerParams(vmem_limit_bytes=KERNEL_VMEM),
        cost_estimate=pl.CostEstimate(flops=flops, bytes_accessed=moved, transcendentals=0),
    )(*scalars, *args)


def geometry(lens, micro, side, rows, block):
    ends, total, best, start = [], 0, lens[micro, 0, 0], 0
    for i in range(lens.shape[2]):
        length = lens[micro, 0, i]
        if i:
            start = jnp.where(length > best, total, start)
            best = jnp.maximum(best, length)
        total = total + length
        ends.append(total)
    return ends, lax.rem(start + rows * side, block)


def positions(shape, axis, begin, block):
    place = lax.broadcasted_iota(jnp.int32, shape, axis) + begin
    return jnp.where(place >= block, place - block, place)


def selection(begin, rows, block):
    wanted = positions((rows, block), 0, begin, block)
    return (wanted == lax.broadcasted_iota(jnp.int32, (rows, block), 1)).astype(f32)


def sequence_mask(ends, begin, rows, block):
    row, col = [positions((rows, rows), axis, begin, block) for axis in (0, 1)]
    inside = sum(jnp.abs((row >= e).astype(jnp.int32) - (col >= e).astype(jnp.int32)) for e in ends)
    return ((inside == 0) & (col <= row)).astype(f32)


def gate_columns(pick, routes, gates):
    peers = lax.axis_size("dp")
    expert = lax.broadcasted_iota(jnp.int32, (128, routes.shape[1]), 0)
    table = jnp.zeros(expert.shape, f32)
    for k in range(routes.shape[0]):
        gate, route = gates[k : k + 1, :], routes[k : k + 1, :]
        high = wide(gate.astype(bf16))
        table += jnp.where(expert == route, high, 0.0) + jnp.where(expert == route + peers, gate - high, 0.0)
    return dot_nt(pick, table.astype(bf16)).astype(bf16)


def opening_body(lens, tokens, grad, routes, gates, gain, wq, wk, wv, wo, *outs):
    inputs, part, qkv, heads, sent, qkv_other, heads_other, mask, extra, cot, cot_other = outs
    block = tokens.shape[0]
    rows = block // 2
    shard = lax.axis_index("shard")
    first = jnp.where(lax.axis_index("section") == 0, 1.0, 0.0)
    weights = [w[...] for w in (wq, wk, wv, wo)]
    for own in (False, True):
        to_qkv, to_heads = (qkv, heads) if own else (qkv_other, heads_other)
        ends, begin = geometry(lens, 0, shard if own else 1 - shard, rows, block)
        pick = selection(begin, rows, block)
        values = dot_nn((pick * first).astype(bf16), tokens[...])
        allowed = sequence_mask(ends, begin, rows, block)
        value = head_group(normed_rows(values, gain[...]), allowed, weights, to_qkv, to_heads)
        cot_rows = dot_nn((pick * (1.0 - first)).astype(bf16), grad[...]).astype(bf16)
        if own:
            inputs[...] = values.astype(bf16)
            part[...] = values + value
            mask[...] = allowed
            extra[...] = gate_columns(pick.astype(bf16), routes[...], gates[...])
            cot[...] = cot_rows
        else:
            sent[...] = value.astype(bf16)
            cot_other[...] = cot_rows


def opening(lens, tokens, grad, routes, gates, gain, weights):
    block, model = tokens.shape
    rows = block // 2
    width, out = sum(w.shape[1] for w in weights[:3]), weights[3].shape[1]
    shapes = [
        like((rows, model), bf16), like((rows, model), f32), like((rows, width), bf16), like((rows, out), bf16),
        like((rows, model), bf16), like((rows, width), bf16), like((rows, out), bf16),
        like((rows, rows), f32), like((rows, 128), bf16), like((rows, model), bf16), like((rows, model), bf16),
    ]
    args = [tokens, grad, routes, gates, gain, *weights]
    outs = on_device(opening_body, shapes, args, 4 * rows * model * (width + out), (lens,))
    return outs[:5], outs[7:]


def settle_body(lens, tokens, grad, routes, gates, fresh, cot, mask, extra):
    block = tokens.shape[0]
    rows = block // 2
    first = jnp.where(lax.axis_index("section") == 0, 1.0, 0.0)
    ends, begin = geometry(lens, 1, lax.axis_index("shard"), rows, block)
    pick = selection(begin, rows, block)
    fresh[...] = dot_nn((pick * first).astype(bf16), tokens[...]).astype(bf16)
    cot[...] = dot_nn((pick * (1.0 - first)).astype(bf16), grad[...]).astype(bf16)
    mask[...] = sequence_mask(ends, begin, rows, block)
    extra[...] = gate_columns(pick.astype(bf16), routes[...], gates[...])


def settle(lens, tokens, grad, routes, gates):
    block, model = tokens.shape
    rows = block // 2
    shapes = [like((rows, model), bf16)] * 2 + [like((rows, rows), f32), like((rows, 128), bf16)]
    args = [tokens, grad, routes, gates]
    return on_device(settle_body, shapes, args, 2 * block * block * model, (lens,))


def joined_body(part, other, gain, extra, hidden, payload):
    total = part[...] + wide(other[...])
    hidden[...] = total
    model = total.shape[1]
    payload[:, :model] = normed_rows(total, gain[...])
    payload[:, model:] = extra[...]


def joined(part, other, gain, extra):
    rows, model = part.shape
    shapes = [like((rows, model), f32), like((rows, model + extra.shape[1]), bf16)]
    return on_device(joined_body, shapes, [part, other, gain, extra], 10 * rows * model)


def split_packed(packed, weights):
    at, parts = 0, []
    for w in weights:
        parts.append(packed[:, at : at + w.shape[1]])
        at += w.shape[1]
    return parts


def other_heads_body(inputs, mask, gain, wq, wk, wv, wo, packed, qkv, heads):
    normed = normed_rows(wide(inputs[...]), gain[...])
    head_group(normed, mask[...], split_packed(packed, (wq, wk, wv, wo)), qkv, heads)


def other_heads(inputs, mask, gain, weights, packed):
    rows = inputs.shape[0]
    width, out = sum(w.shape[1] for w in weights[:3]), weights[3].shape[1]
    shapes = [like((rows, width), bf16), like((rows, out), bf16)]
    args = [inputs, mask, gain, *weights, packed]
    return on_device(other_heads_body, shapes, args, 2 * rows * packed.size)


def attention_body(fresh, arriving, mask, gain, gain_two, extra, wq, wk, wv, wo, packed, *outs):
    inputs, hidden, payload, qkv0, qkv1, heads0, heads1 = outs
    rows = fresh[...] + arriving[...]
    inputs[...] = rows
    total = wide(rows)
    normed = normed_rows(total, gain[...])
    own = [w[...] for w in (wq, wk, wv, wo)]
    total = total + head_group(normed, mask[...], own, qkv0, heads0)
    total = total + head_group(normed, mask[...], split_packed(packed, own), qkv1, heads1)
    hidden[...] = total
    model = total.shape[1]
    payload[:, :model] = normed_rows(total, gain_two[...])
    payload[:, model:] = extra[...]


def attention_forward(fresh, arriving, mask, gain, gain_two, extra, weights, packed):
    rows, model = fresh.shape
    width, out = sum(w.shape[1] for w in weights[:3]), weights[3].shape[1]
    shapes = [
        like((rows, model), bf16), like((rows, model), f32), like((rows, model + extra.shape[1]), bf16),
        like((rows, width), bf16), like((rows, width), bf16), like((rows, out), bf16), like((rows, out), bf16),
    ]
    args = [fresh, arriving, mask, gain, gain_two, extra, *weights, packed]
    outs = on_device(attention_body, shapes, args, 4 * rows * packed.size)
    inputs, hidden, payload, qkv0, qkv1, heads0, heads1 = outs
    return inputs, hidden, payload, [(qkv0, heads0), (qkv1, heads1)]


def attention_back_body(grad, grad_two, inputs, hidden, mask, gain, gain_two, q0, q1, wq, wk, wv, wo, packed, *outs):
    grad_input, grad_input_low, grad_low, normed, g0, g1, gain_grad, gain_two_grad = outs
    rows = inputs.shape[0]
    values = wide(inputs[...])
    normed[...] = normed_rows(values, gain[...])
    total = hidden[...]
    back, gain_two_grad[...] = norm_back(total, norm_factor(total), gain_two[...], grad_two[...])
    grad_hidden = wide(grad[...]) + back
    low = grad_hidden.astype(bf16)
    grad_low[...] = low
    grad_normed = jnp.zeros_like(grad_hidden)
    own = [w[...] for w in (wq, wk, wv, wo)]
    for qkv, weights, grad_qkv in ((q0, own, g0), (q1, split_packed(packed, own), g1)):
        query, key, value, probs = group_probs(qkv[...], mask[...])
        grad_heads = stack_heads(dot_nn(low, weights[3]).astype(bf16))
        grad_probs = dot_nt(grad_heads, value)
        inner = jnp.sum(probs * grad_probs, axis=1, keepdims=True)
        grad_scores = (probs * (grad_probs - inner) * HEAD_SIZE ** (-0.5)).astype(bf16)
        grads = [
            spread_heads(dot_nn(grad_scores, key).astype(bf16), rows),
            dot_tn(grad_scores, query).astype(bf16),
            dot_tn(probs.astype(bf16), grad_heads).astype(bf16),
        ]
        at = 0
        for part, w in zip(grads, weights):
            grad_qkv[:, at : at + part.shape[1]] = part
            at += part.shape[1]
            grad_normed = grad_normed + dot_nt(part, w)
    back, gain_grad[...] = norm_back(values, norm_factor(values), gain[...], grad_normed)
    result = grad_hidden + back
    grad_input[...] = result
    grad_input_low[...] = result.astype(bf16)


def attention_backward(grad, grad_two, inputs, hidden, mask, gain, gain_two, projected, weights, packed):
    rows, model = inputs.shape
    width = projected[0].shape[1]
    shapes = [
        like((rows, model), f32), like((rows, model), bf16), like((rows, model), bf16),
        like((rows, model), bf16), like((rows, width), bf16), like((rows, width), bf16),
        like((1, model), f32), like((1, model), f32),
    ]
    args = [grad, grad_two, inputs, hidden, mask, gain, gain_two, *projected, *weights, packed]
    return on_device(attention_back_body, shapes, args, 8 * rows * packed.size)


def place(pieces, *targets):
    at = 0
    for piece in pieces:
        rows, first = piece.shape[0], 0
        for target in targets:
            target[at : at + rows, :] = piece[:, first : first + target.shape[1]]
            first += target.shape[1]
        at += rows


def own_gate(extra):
    me, peers = lax.axis_index("dp"), lax.axis_size("dp")
    lane = lax.broadcasted_iota(jnp.int32, extra.shape, 1)
    return jnp.sum(jnp.where((lane == me) | (lane == me + peers), wide(extra), 0.0), axis=1, keepdims=True)


def chunked(rows, step):
    count = max(c for c in (128, 192, 256, 384) if rows % c == 0)
    if rows == count:
        step(0, count)
    else:
        pl.loop(0, rows // count)(lambda i: step(pl.multiple_of(i * count, count), count))


def expert_stage_body(pieces, *refs):
    ins, (rows, extra, gate_out, up_out, *parts) = refs[:pieces], refs[pieces + 3 :]
    w_gate, w_up, w_down = refs[pieces : pieces + 3]
    place(ins, rows, extra)
    half = rows.shape[0] // 2
    for i, part in enumerate(parts):

        def step(first, count, i=i, part=part):
            here = pl.ds(first + i * half, count)
            values = rows[here, :]
            gate = dot_nn(values, w_gate[...])
            up = dot_nn(values, w_up[...])
            gate_out[here, :] = gate.astype(bf16)
            up_out[here, :] = up.astype(bf16)
            act = (gate / (1.0 + jnp.exp(-gate)) * up).astype(bf16)
            scale = own_gate(extra[here, :])
            part[pl.ds(first, count), :] = (scale * dot_nn(act, w_down[...])).astype(bf16)

        chunked(half, step)


def expert_stage(pieces, w_gate, w_up, w_down):
    count = sum(p.shape[0] for p in pieces)
    model, units = w_gate.shape
    shapes = [
        like((count, model), bf16), like((count, pieces[0].shape[1] - model), bf16),
        like((count, units), bf16), like((count, units), bf16),
        like((count // 2, model), bf16), like((count // 2, model), bf16),
    ]
    body = functools.partial(expert_stage_body, len(pieces))
    outs = on_device(body, shapes, [*pieces, w_gate, w_up, w_down], 6 * count * w_gate.size)
    return outs[4:], outs[:4]


def expert_back_body(pieces, *refs):
    ins = refs[:pieces]
    extra, gate_in, up_in, w_gate, w_up, w_down, grad_rows, grad_gate, grad_up, act, *parts = refs[pieces:]
    place(ins, grad_rows)
    half = grad_rows.shape[0] // 2
    for i, part in enumerate(parts):

        def step(first, count, i=i, part=part):
            here = pl.ds(first + i * half, count)
            scale = own_gate(extra[here, :])
            scaled = (scale * wide(grad_rows[here, :])).astype(bf16)
            grad_rows[here, :] = scaled
            grad_act = dot_nt(scaled, w_down[...])
            gate, up = wide(gate_in[here, :]), wide(up_in[here, :])
            sig = 1.0 / (1.0 + jnp.exp(-gate))
            silu = gate * sig
            low_gate = (grad_act * up * sig * (1.0 + gate * (1.0 - sig))).astype(bf16)
            low_up = (grad_act * silu).astype(bf16)
            grad_gate[here, :] = low_gate
            grad_up[here, :] = low_up
            act[here, :] = (silu * up).astype(bf16)
            grad_in = dot_nt(low_gate, w_gate[...]) + dot_nt(low_up, w_up[...])
            part[pl.ds(first, count), :] = grad_in.astype(bf16)

        chunked(half, step)


def expert_back_stage(pieces, saved, w_gate, w_up, w_down):
    rows, extra, gate_out, up_out = saved
    count = rows.shape[0]
    model, units = w_gate.shape
    shapes = [
        like((count, model), bf16), like((count, units), bf16), like((count, units), bf16),
        like((count, units), bf16), like((count // 2, model), bf16), like((count // 2, model), bf16),
    ]
    body = functools.partial(expert_back_body, len(pieces))
    args = [*pieces, extra, gate_out, up_out, w_gate, w_up, w_down]
    outs = on_device(body, shapes, args, 6 * count * w_gate.size)
    return outs[4:], outs[:4]


def product_sums_body(stages, products, *refs):
    ins, outs = refs[: -len(products)], refs[-len(products) :]
    fields = 1 + max(max(p) for p in products)
    totals = [ref[...] for ref in ins[fields * stages :]] or [0.0] * len(products)
    for i in range(stages):
        stage = [r[...] for r in ins[fields * i : fields * (i + 1)]]
        totals = [t + dot_tn(stage[a], stage[b]) for t, (a, b) in zip(totals, products)]
    for out, total in zip(outs, totals):
        out[...] = total


def product_sums(stages, products, swept, sums):
    width = stages[0][swept].shape[1]
    step = min(t.shape[1] for t in stages[0])
    rows = sum(stage[0].shape[0] for stage in stages)
    args, specs = [], []
    for stage in stages:
        args += stage
        for i, t in enumerate(stage):
            if i == swept:
                specs.append(pl.BlockSpec((t.shape[0], step), lambda j: (0, j)))
            else:
                specs.append(pl.BlockSpec(t.shape, lambda j: (0, 0)))
    shapes, outs = [], []
    for left, right in products:
        other = stages[0][right if left == swept else left].shape[1]
        if left == swept:
            shapes.append(like((width, other), f32))
            outs.append(pl.BlockSpec((step, other), lambda j: (j, 0)))
        else:
            shapes.append(like((other, width), f32))
            outs.append(pl.BlockSpec((other, step), lambda j: (0, j)))
    first = len(args)
    if sums is not None:
        args += sums
        specs += outs
    return pl.pallas_call(
        functools.partial(product_sums_body, len(stages), products),
        grid=(width // step,),
        out_shape=shapes,
        in_specs=specs,
        out_specs=outs,
        input_output_aliases={} if sums is None else {first + i: i for i in range(len(shapes))},
        compiler_params=pltpu.CompilerParams(vmem_limit_bytes=KERNEL_VMEM),
        cost_estimate=pl.CostEstimate(
            flops=2 * rows * sum(t.size for t in shapes),
            bytes_accessed=sum(a.size * a.dtype.itemsize for a in args),
            transcendentals=0,
        ),
    )(*args)


def expert_forward(rows, w_gate, w_up, w_down):
    gate_out = dot_nn(rows, w_gate)
    up_out = dot_nn(rows, w_up)
    act = (gate_out / (1.0 + jnp.exp(-gate_out)) * up_out).astype(bf16)
    part = dot_nn(act, w_down).astype(bf16)
    return part, (rows, gate_out.astype(bf16), up_out.astype(bf16))


def expert_backward(grad_rows, saved, w_gate, w_up, w_down):
    rows, gate_low, up_low = saved
    gate_out, up_out = wide(gate_low), wide(up_low)
    grad_act = dot_nt(grad_rows, w_down)
    sig = 1.0 / (1.0 + jnp.exp(-gate_out))
    silu = gate_out * sig
    grad_gate = (grad_act * up_out * sig * (1.0 + gate_out * (1.0 - sig))).astype(bf16)
    grad_up = (grad_act * silu).astype(bf16)
    act = (silu * up_out).astype(bf16)
    grad_in = (dot_nt(grad_gate, w_gate) + dot_nt(grad_up, w_up)).astype(bf16)
    return grad_in, (dot_tn(rows, grad_gate), dot_tn(rows, grad_up), dot_tn(act, grad_rows))


def halves(array):
    half = array.shape[0] // 2
    return array[:half], array[half:]


class Blocks:
    def __init__(self, cube, weights):
        self.cube, self.weights = cube, weights

    def forward(self, payload, micro, side=()):
        saved = []

        def work(stage, pieces):
            parts, kept = expert_stage(pieces, *self.weights)
            saved.append(kept)
            return parts

        return gather_rows(self.cube, payload, work, side), saved

    def back_stage(self, stage, pieces, saved):
        parts, kept = expert_back_stage(pieces, saved[stage], *self.weights)
        return parts, [saved[stage][0], *kept]

    def backward(self, grad, micro, saved, side=()):
        keeps = []

        def work(stage, pieces):
            parts, kept = self.back_stage(stage, pieces, saved)
            keeps.append(kept)
            return parts

        return gather_rows(self.cube, grad, work, side), keeps

    def late_backward(self, pieces, saved):
        results, keeps = [None] * 4, [None] * 4

        def run(*stages):
            def work(*gathered):
                for stage, rows in zip(stages, gathered):
                    (mine, other), keeps[stage] = self.back_stage(stage, rows, saved)
                    results[stage] = (mine, swap(other, self.cube.core))
                return [results[stage] for stage in stages]

            return lambda: [pieces[stage] for stage in stages], work

        return [run(3), run(2), run(1, 0)], results, keeps

    def total(self, results, side=()):
        return reduce_rows(self.cube, results, side)

    def weight_sums(self, keeps, sums):
        def hidden(*stages):
            sums[0] = product_sums(stages, ((0, 1), (0, 2)), 0, sums[0])
            return sums[0]

        def back(*stages):
            sums[1] = product_sums(stages, ((0, 1),), 1, sums[1])
            return sums[1]

        return [
            (lambda: [[rows, gate, up] for rows, _, gate, up, _ in keeps], hidden),
            (lambda: [[act, grad] for _, grad, _, _, act in keeps], back),
        ]


def run_all(side):
    for thunk in side:
        if thunk is not None:
            thunk[1](*thunk[0]())


class Buckets:
    def __init__(self, cube, weights, routes, gates, capacity):
        self.cube, self.weights, self.capacity = cube, weights, capacity
        micros, self.rows, self.top = routes.shape
        self.experts = lax.axis_size("dp")
        self.tables = []
        for m in range(micros):
            flat = routes[m].reshape(-1)
            onehot = (flat[:, None] == jnp.arange(self.experts, dtype=jnp.int32)).astype(jnp.int32)
            earlier = jnp.cumsum(onehot, axis=0) - onehot
            target = flat * capacity + jnp.sum(earlier * onehot, axis=1)
            source = jnp.full((self.experts * capacity,), flat.shape[0], jnp.int32)
            source = source.at[target].set(jnp.arange(flat.shape[0], dtype=jnp.int32))
            self.tables.append((target, source, gates[m]))

    def table(self, micro):
        return jax.tree.map(lambda a, b: jnp.where(micro == 0, a, b), self.tables[0], self.tables[1])

    def exchange(self, rows):
        shape = (self.experts, self.capacity, rows.shape[1])
        moved = lax.all_to_all(rows.reshape(shape), "dp", split_axis=0, concat_axis=0, tiled=True)
        return moved.reshape(rows.shape)

    def whole(self, own):
        return jnp.concatenate([own, swap(own, self.cube.z)], axis=0)

    def forward(self, payload, micro, side=()):
        target, source, gates = self.table(micro)
        own = payload[:, : self.weights[0].shape[0]]
        padded = jnp.pad(self.whole(own), ((0, 1), (0, 0)))
        arrived = self.exchange(jnp.take(padded, source // self.top, axis=0))
        part, saved = expert_forward(arrived, *self.weights)
        picked = jnp.take(self.exchange(part), target, axis=0).reshape(self.rows, self.top, -1)
        run_all(side)
        return jnp.sum(gates[:, :, None] * picked, axis=1), saved

    def backward(self, grad, micro, saved, side=()):
        target, source, gates = self.table(micro)
        scaled = (gates[:, :, None] * wide(self.whole(grad))[:, None, :]).astype(bf16)
        padded = jnp.pad(scaled.reshape(self.rows * self.top, -1), ((0, 1), (0, 0)))
        arrived = self.exchange(jnp.take(padded, source, axis=0))
        grad_in, weights = expert_backward(arrived, saved, *self.weights)
        picked = jnp.take(self.exchange(grad_in), target, axis=0).reshape(self.rows, self.top, -1)
        run_all(side)
        return jnp.sum(picked, axis=1, dtype=f32), weights

    def total(self, results, side=()):
        own, other = halves(results.astype(bf16))
        run_all(side)
        return wide(own) + wide(swap(other, self.cube.z))

    def weight_sums(self, weights, sums):
        def add(*weights):
            for i, part in enumerate((list(weights[:2]), list(weights[2:]))):
                sums[i] = part if sums[i] is None else [a + b for a, b in zip(sums[i], part)]

        return [None, (lambda: weights, add)]


def local(
    tokens, lengths, routes, gates, attn_gain, q_weight, key_projection, value_projection,
    o_weight, mlp_gain, expert_gate, expert_up, expert_down, cotangent,
):
    cube = Cube()
    section = lax.axis_index("section")
    shard = lax.axis_index("shard")
    me = lax.axis_index("dp")
    peers, shards = lax.axis_size("dp"), lax.axis_size("shard")
    _, block_rows, model = tokens.shape
    rows = block_rows // shards
    share = model // peers
    first = section == 0
    gain_one, gain_two = attn_gain[0][None], mlp_gain[0][None]
    weights = [q_weight[0], key_projection[0], value_projection[0], o_weight[0]]
    expert_w = (expert_gate[0, 0], expert_up[0, 0], expert_down[0, 0])
    capacity = 2 * block_rows * routes.shape[3] // peers
    whole_blocks = capacity >= block_rows

    def chosen(here, there):
        return jax.tree.map(lambda a, b: jnp.where(first, a, b), here, there)

    def begins(lens):
        lens = lens[:, 0]
        ends, longest = jnp.cumsum(lens, axis=1), jnp.argmax(lens, axis=1)
        return [ends[m, longest[m]] - lens[m, longest[m]] for m in range(2)]

    def turned(array, begin):
        doubled = jnp.concatenate([array, array], axis=0)
        return lax.dynamic_slice_in_dim(doubled, (begin + rows * shard) % block_rows, block_rows, 0)

    if whole_blocks:
        mixture = Blocks(cube, expert_w)
    else:
        early = begins(lengths)
        mixture = Buckets(
            cube,
            expert_w,
            jnp.stack([turned(routes[0, m], early[m]) for m in range(2)]),
            jnp.stack([turned(gates[0, m], early[m]) for m in range(2)]),
            capacity,
        )

    slices = jnp.concatenate([lax.dynamic_slice_in_dim(w, me * share, share, 0) for w in weights], axis=1)
    slices = swap(slices, cube.z)

    route_cols = [routes[0, m].T for m in range(2)]
    gate_cols = [gates[0, m].T for m in range(2)]
    (inputs, part, qkv, heads, sent, *_), (mask0, extra0, cot_own, cot_other) = opening(
        lengths, tokens[0], cotangent[0], route_cols[0], gate_cols[0], gain_one, weights
    )
    settled = [tokens[1], cotangent[1], route_cols[1], gate_cols[1]]
    sent, settled = together((sent, settled))
    moved = [swap(sent, cube.z)]
    if whole_blocks:
        moved += [swap(cot_own, cube.x), swap(cot_own, cube.y)]
    (arrived, *near_cot), slices, settled = together((moved, slices, settle(lengths, *settled)))
    fresh1, cot1, mask1, extra1 = settled
    packed = lax.all_gather(slices, "dp", axis=0, tiled=True)
    hidden, payload = joined(part, arrived, gain_two, extra0)
    results, saved = mixture.forward(payload, 0)
    total = mixture.total(results)
    result0 = (hidden + total).astype(bf16)
    if whole_blocks:
        result0, cot_other, near_cot = together((result0, cot_other, near_cot))
    arriving = lax.ppermute(result0, "section", [(0, 1)])
    state0 = [inputs, hidden, mask0, None, saved]

    mask_mid, extra_mid = chosen((mask1, extra1), (mask0, extra0))
    if whole_blocks:
        x0, y0 = near_cot
        y1 = swap(cot_other, cube.y)
        pieces_cot = [[cot_own], [x0, y0, cot_other], [swap(x0, cube.y), y1, swap(cot_other, cube.x)], [swap(y1, cube.x)]]
        pieces_cot = [[*stage, *[swap(t, cube.core) for t in stage]] for stage in pieces_cot]
    inputs1, hidden1, payload, groups1 = attention_forward(
        fresh1, arriving, mask_mid, gain_one, gain_two, extra_mid, weights, packed
    )
    if whole_blocks:
        payload, pieces_cot = together((payload, pieces_cot))

    def first_groups(*args):
        groups = other_heads(*args)
        state0[3] = [(qkv, heads), tuple(groups)]
        return groups

    micro_mid = 1 - section
    results, saved1 = mixture.forward(
        payload, micro_mid, [(lambda: [inputs, mask0, gain_one, weights, packed], first_groups)]
    )

    grad0 = cot_own
    if whole_blocks:
        thunks, back_results, keeps0 = mixture.late_backward(pieces_cot, saved1)
        total = mixture.total(results, thunks)
    else:
        back_results, keeps0 = mixture.backward(grad0, micro_mid, saved1)
        total = mixture.total(results)
    result1 = (hidden1 + total).astype(bf16)
    arriving = lax.ppermute(result1, "section", [(0, 1)])

    slot2 = []

    def last_attention(arriving):
        zero = jnp.zeros((rows, model), bf16)
        slot2.extend(
            attention_forward(zero, arriving, mask1, gain_one, gain_two, extra1, weights, packed)
        )
        return slot2

    grad_two = mixture.total(back_results, [None, None, (lambda: [arriving], last_attention)])
    inputs2, hidden2, payload, groups2 = slot2

    def attention_turn(grad, grad_two, state):
        inputs, hidden, mask, groups, _ = state
        outs = attention_backward(
            grad, grad_two, inputs, hidden, mask, gain_one, gain_two, [g[0] for g in groups], weights, packed
        )
        grad_input, low, grad_low, normed, g0, g1, attn_g, mlp_g = outs
        factors = (normed, grad_low, (g0, g1), [g[1] for g in groups])
        return grad_input, low, factors, jnp.concatenate([attn_g, mlp_g], axis=0)

    turn0 = []
    state1 = [inputs1, hidden1, mask_mid, groups1, saved1]

    def first_turn(grad_two):
        turn0.extend(attention_turn(grad0, grad_two, state1))
        return turn0

    results2, saved2 = mixture.forward(payload, 1, [(lambda: [grad_two], first_turn)])
    coming = lax.ppermute(turn0[1], "section", [(1, 0)])
    state2 = [inputs2, hidden2, mask1, groups2, saved2]

    sums = [None, None]
    coming, results2, saved2 = together((coming, results2, saved2))
    state2[4] = saved2
    grad1 = coming + cot1
    state_mid = chosen(state0, state2)
    back_results, keeps1 = mixture.backward(grad1, section, state_mid[4])
    grad_two = mixture.total(back_results, [None, *mixture.weight_sums(keeps0, sums)])
    grad_two, results2 = together((grad_two, results2))
    turn1 = attention_turn(grad1, grad_two, state_mid)
    coming = lax.ppermute(turn1[1], "section", [(1, 0)])

    total = mixture.total(results2)
    result2 = (hidden2 + total).astype(bf16)

    grad2, result2 = together((coming, result2))
    back_results, keeps2 = mixture.backward(grad2, 1 - section, saved1)
    grad_two = mixture.total(back_results, [None, *mixture.weight_sums(keeps1, sums)])
    turn2 = attention_turn(grad2, grad_two, state1)

    turns = (turn0, turn1, turn2)
    factors = [t[2] for t in turns]
    starts = begins(together((lengths, turn1[0]))[0])

    def owned(left, rights, side):
        full = [dot_tn(left, right).astype(bf16).reshape(peers, share, -1) for right in rights]

        def blocks(group):
            taken = [jnp.take(full[s], me ^ (m ^ cube.inner), axis=0) for m, s in group]
            return jnp.concatenate(taken, axis=0).reshape(-1, rights[0].shape[1])

        pairs = [(blocks(g), swap(blocks(mate), cube.core)) for g, mate in cube.stages]
        return reduce_rows(cube, pairs, side)

    def placed(own, m):
        half = model // shards
        kept = lax.dynamic_slice_in_dim(own, shard * half, half, 1)
        given = lax.dynamic_slice_in_dim(own, (1 - shard) * half, half, 1)
        got = swap(given, cube.z)
        low = jnp.where(shard == 0, kept, got)
        high = jnp.where(shard == 0, got, kept)
        return lax.dynamic_slice_in_dim(
            jnp.concatenate([low, high, low, high], axis=0), (block_rows - starts[m]) % block_rows, block_rows, 0
        )

    gain_total = [sum(t[3] for t in turns)]

    def gain_step(*directions):
        def step(total):
            for direction in directions:
                total = total + swap(total, direction)
            gain_total.append(total)
            return total

        return lambda: gain_total[-1:], step

    placings = []

    def last_placing(own):
        placings.append(placed(own, 1))
        return placings

    grad_o = owned(
        jnp.concatenate([f[1] for f in factors], axis=0),
        [jnp.concatenate([f[3][g] for f in factors], axis=0) for g in range(shards)],
        [gain_step(*cube.extra, cube.core), *mixture.weight_sums(keeps2, sums)],
    )
    grad_qkv = owned(
        jnp.concatenate([f[0] for f in factors], axis=0),
        [jnp.concatenate([f[2][g] for f in factors], axis=0) for g in range(shards)],
        [gain_step(cube.x), gain_step(cube.y, cube.z), (lambda: [chosen(turn2[0], turn1[0])], last_placing)],
    )
    width = q_weight.shape[2]
    grad_q = grad_qkv[:, :width]
    grad_k = grad_qkv[:, width : width + HEAD_SIZE]
    grad_v = grad_qkv[:, width + HEAD_SIZE :]
    gain_sums = lax.dynamic_slice_in_dim(gain_total[-1], me * share, share, 1)
    section_out = jnp.stack([placed(chosen(result0, result1), 0), placed(chosen(result1, result2), 1)])
    input_grad = jnp.stack([placed(chosen(turn1[0], turn0[0]), 0), placings[0]])
    (gate_total, up_total), (down_total,) = sums
    return (
        section_out[None],
        input_grad[None],
        gain_sums[0][None],
        grad_q[None],
        grad_k[None],
        grad_v[None],
        grad_o[None],
        gain_sums[1][None],
        gate_total[None, None],
        up_total[None, None],
        down_total[None, None],
    )


def solution(mesh):
    in_specs = (
        P(None, "dp", None),
        P(None, "dp", None),
        P("section", None, "dp", None),
        P("section", None, "dp", None),
        P("section", None),
        P("section", None, "shard"),
        P("section", None, "shard"),
        P("section", None, "shard"),
        P("section", None, "shard"),
        P("section", None),
        P("section", "dp", None, "shard"),
        P("section", "dp", None, "shard"),
        P("section", "dp", "shard", None),
        P(None, "dp", None),
    )
    out_specs = (
        P("section", None, "dp", "shard"),
        P("section", None, "dp", "shard"),
        P("section", "dp"),
        P("section", "dp", "shard"),
        P("section", "dp", "shard"),
        P("section", "dp", "shard"),
        P("section", "dp", "shard"),
        P("section", "dp"),
        P("section", "dp", None, "shard"),
        P("section", "dp", None, "shard"),
        P("section", "dp", "shard", None),
    )
    return jax.shard_map(local, mesh=mesh, in_specs=in_specs, out_specs=out_specs, check_vma=False)
```

profile of v0, /device:TPU:0, one launch (start us, length us, event | category | flops | bytes accessed | tf_op | source)
XLA Modules:
  0.0 831.1 jit_solution(5884916852465648875)
XLA Ops:
  16.7 9.1 %shard_map.509 = (bf16[128,1536]{1,0:T(8,128)(2,1)}, f32[128,1536]{1,0:T(8,128)}, bf16[128,1024]{1,0:T(8,128)(2,1)}, bf16[128,768]{1,0:T(8,128)(2,1)}, bf16[128,...) custom-call(s32[2,1,4]{2,1,0:T(1,128)} %lens.3, ...), custom_call_target="tpu_custom_call" | custom-call | flops 1409286144 | bytes 10467328 | tf_op jit(solution)/shard_map/pallas_call | solution.py:197
  67.2 8.8 %shard_map.513 = (bf16[768,1536]{1,0:T(8,128)(2,1)}, bf16[768,128]{1,0:T(8,128)(2,1)}, bf16[768,384]{1,0:T(8,128)(2,1)}, bf16[768,384]{1,0:T(8,128)(2,1)}, bf16[...) custom-call(bf16[128,1664]{1,0:T(8,128)(2,1)} %collective-permute-done.4.refs_0_, ...), custom_call_target="tpu_custom_call" | custom-call | flops 2717908992 | bytes 12189696 | tf_op jit(solution)/shard_map/pallas_call | solution.py:197
  173.4 9.6 %shard_map.516 = (bf16[128,1536]{1,0:T(8,128)(2,1)}, f32[128,1536]{1,0:T(8,128)}, bf16[128,1664]{1,0:T(8,128)(2,1)}, bf16[128,1024]{1,0:T(8,128)(2,1)}, bf16[128...) custom-call(bf16[128,1536]{1,0:T(8,128)(2,1)} %get-tuple-element.682.fresh, ...), custom_call_target="tpu_custom_call" | custom-call | flops 1409286144 | bytes 14430208 | tf_op jit(solution)/shard_map/pallas_call | solution.py:197
  183.5 9.1 %collective-permute-start.51 = (bf16[128,1664]{1,0:T(8,128)(2,1)}, bf16[128,1664]{1,0:T(8,128)(2,1)}, u32[]{:S(2)}, u32[]{:S(2)}) collective-permute-start(bf16[128,1664]{1,0:T(8,128)(2,1)} %get-tuple-element.694.refs_0_), channel_id=1, source_target_pairs={{0,1},{1,0},{2,3},{3,2},{4,5},{5,4},{6,7},{7,6},{8,9},{9,8},{10,11... | collective-permute-start | bytes 1277960 | tf_op jit(solution)/shard_map/ppermute | solution.py:55
  230.0 8.3 %shard_map.520 = (bf16[768,1536]{1,0:T(8,128)(2,1)}, bf16[768,128]{1,0:T(8,128)(2,1)}, bf16[768,384]{1,0:T(8,128)(2,1)}, bf16[768,384]{1,0:T(8,128)(2,1)}, bf16[...) custom-call(bf16[128,1664]{1,0:T(8,128)(2,1)} %copy-done.125, bf16[128,1664]{1,0:T(8,128)(2,1)} %copy-done.128, ...), custom_call_target="tpu_custom_call" | custom-call | flops 2717908992 | bytes 12189696 | tf_op jit(solution)/shard_map/pallas_call | solution.py:197
  264.3 8.7 %shard_map.523 = (bf16[768,1536]{1,0:T(8,128)(2,1)}, bf16[768,384]{1,0:T(8,128)(2,1)}, bf16[768,384]{1,0:T(8,128)(2,1)}, bf16[768,384]{1,0:T(8,128)(2,1)}, bf16[...) custom-call(bf16[128,1536]{1,0:T(8,128)(2,1)} %collective-permute-done.41.refs_0_, ...), custom_call_target="tpu_custom_call" | custom-call | flops 2717908992 | bytes 13762560 | tf_op jit(solution)/shard_map/pallas_call | solution.py:197
  280.7 10.8 %collective-permute-done.87 = bf16[48,1536]{1,0:T(8,128)(2,1)S(1)} collective-permute-done((bf16[48,1536]{1,0:T(8,128)(2,1)S(1)}, bf16[48,1536]{1,0:T(8,128)(2,1)S(1)}, u32[]{:S(2)}, u32[]{:S(2)}) %collective-permute-start.87) | collective-permute-done | bytes 147488 | tf_op jit(solution)/shard_map/ppermute | solution.py:55
  298.6 8.9 %shard_map.524 = (bf16[768,1536]{1,0:T(8,128)(2,1)}, bf16[768,384]{1,0:T(8,128)(2,1)}, bf16[768,384]{1,0:T(8,128)(2,1)}, bf16[768,384]{1,0:T(8,128)(2,1)}, bf16[...) custom-call(bf16[128,1536]{1,0:T(8,128)(2,1)} %collective-permute-done.1.refs_0_, ...), custom_call_target="tpu_custom_call" | custom-call | flops 2717908992 | bytes 13762560 | tf_op jit(solution)/shard_map/pallas_call | solution.py:197
  351.1 9.4 %collective-permute-start.95 = (bf16[128,1536]{1,0:T(8,128)(2,1)S(1)}, bf16[128,1536]{1,0:T(8,128)(2,1)}, u32[]{:S(2)}, u32[]{:S(2)}) collective-permute-start(bf16[128,1536]{1,0:T(8,128)(2,1)S(1)} %get-tuple-element.818), channel_id=1, source_target_pairs={{0,1},{1,0},{2,3},{3,2},{4,5},{5,4},{6,7},{7,6},{8,9},{9,8},{10,11... | collective-permute-start | bytes 1179656 | tf_op jit(solution)/shard_map/ppermute | solution.py:55
  361.3 9.6 %shard_map.526 = (bf16[128,1536]{1,0:T(8,128)(2,1)}, f32[128,1536]{1,0:T(8,128)}, bf16[128,1664]{1,0:T(8,128)(2,1)}, bf16[128,1024]{1,0:T(8,128)(2,1)}, bf16[128...) custom-call(bf16[128,1536]{1,0:T(8,128)(2,1)} %broadcast_in_dim.48.fresh, ...), custom_call_target="tpu_custom_call" | custom-call | flops 1409286144 | bytes 14430208 | tf_op jit(solution)/shard_map/pallas_call | solution.py:197
  375.6 10.8 %shard_map.527 = (f32[128,1536]{1,0:T(8,128)}, bf16[128,1536]{1,0:T(8,128)(2,1)}, bf16[128,1536]{1,0:T(8,128)(2,1)}, bf16[128,1536]{1,0:T(8,128)(2,1)}, bf16[128...) custom-call(bf16[128,1536]{1,0:T(8,128)(2,1)} %get-tuple-element.792.refs_0_.grad, ...), custom_call_target="tpu_custom_call" | custom-call | flops 2818572288 | bytes 16474112 | tf_op jit(solution)/shard_map/pallas_call | solution.py:197
  396.6 8.4 %shard_map.529 = (bf16[768,1536]{1,0:T(8,128)(2,1)}, bf16[768,128]{1,0:T(8,128)(2,1)}, bf16[768,384]{1,0:T(8,128)(2,1)}, bf16[768,384]{1,0:T(8,128)(2,1)}, bf16[...) custom-call(bf16[128,1664]{1,0:T(8,128)(2,1)} %collective-permute-done.97.refs_0_, ...), custom_call_target="tpu_custom_call" | custom-call | flops 2717908992 | bytes 12189696 | tf_op jit(solution)/shard_map/pallas_call | solution.py:197
  432.1 13.1 %collective-permute-done.96 = bf16[128,1536]{1,0:T(8,128)(2,1)S(1)} collective-permute-done((bf16[128,1536]{1,0:T(8,128)(2,1)}, bf16[128,1536]{1,0:T(8,128)(2,1)S(1)}, u32[]{:S(2)}, u32[]{:S(2)}) %collective-permute-start.96) | collective-permute-done | bytes 393248 | tf_op jit(solution)/shard_map/ppermute | solution.py:846
  465.2 8.6 %shard_map.533 = (bf16[768,1536]{1,0:T(8,128)(2,1)}, bf16[768,384]{1,0:T(8,128)(2,1)}, bf16[768,384]{1,0:T(8,128)(2,1)}, bf16[768,384]{1,0:T(8,128)(2,1)}, bf16[...) custom-call(bf16[128,1536]{1,0:T(8,128)(2,1)} %collective-permute-done.120.refs_0_, ...), custom_call_target="tpu_custom_call" | custom-call | flops 2717908992 | bytes 13762560 | tf_op jit(solution)/shard_map/pallas_call | solution.py:197
  487.1 8.8 %shard_map.534 = (bf16[768,1536]{1,0:T(8,128)(2,1)}, bf16[768,384]{1,0:T(8,128)(2,1)}, bf16[768,384]{1,0:T(8,128)(2,1)}, bf16[768,384]{1,0:T(8,128)(2,1)}, bf16[...) custom-call(bf16[128,1536]{1,0:T(8,128)(2,1)} %copy-done.129, bf16[128,1536]{1,0:T(8,128)(2,1)} %copy-done.131, ...), custom_call_target="tpu_custom_call" | custom-call | flops 2717908992 | bytes 13762560 | tf_op jit(solution)/shard_map/pallas_call | solution.py:197
  519.2 10.8 %shard_map.536 = (f32[1536,384]{1,0:T(8,128)}, f32[1536,384]{1,0:T(8,128)}) custom-call(bf16[256,1536]{1,0:T(8,128)(2,1)} %get-tuple-element.1188.refs_0_, bf16[256,384]{1,0:T(8,128)(2,1)} %get-tuple-element.956.refs_1_, bf16[256,384]{1,0:T(8,128)(2,1)} %get-tuple-element.957.refs_2_, bf16[768,1536]{1,0:T(8,128)(2,1)} %get-tuple-element.1191.refs_3_, ...), custom_call_target="tpu_custom_call" | custom-call | flops 4831838208 | bytes 9437184 | tf_op jit(solution)/shard_map/pallas_call | solution.py:550
  579.0 10.8 %shard_map.538 = (f32[128,1536]{1,0:T(8,128)}, bf16[128,1536]{1,0:T(8,128)(2,1)}, bf16[128,1536]{1,0:T(8,128)(2,1)}, bf16[128,1536]{1,0:T(8,128)(2,1)}, bf16[128...) custom-call(bf16[128,1536]{1,0:T(8,128)(2,1)} %copy-done.1, ...), custom_call_target="tpu_custom_call" | custom-call | flops 2818572288 | bytes 16474112 | tf_op jit(solution)/shard_map/pallas_call | solution.py:197
  593.0 11.9 %collective-permute-done.152.refs_0_.grad = bf16[128,1536]{1,0:T(8,128)(2,1)S(1)} collective-permute-done((bf16[128,1536]{1,0:T(8,128)(2,1)}, bf16[128,1536]{1,0:T(8,128)(2,1)S(1)}, u32[]{:S(2)}, u32[]{:S(2)}) %collective-permute-start.152) | collective-permute-done | bytes 393248 | tf_op jit(solution)/shard_map/ppermute | solution.py:858
  626.3 8.7 %shard_map.540 = (bf16[768,1536]{1,0:T(8,128)(2,1)}, bf16[768,384]{1,0:T(8,128)(2,1)}, bf16[768,384]{1,0:T(8,128)(2,1)}, bf16[768,384]{1,0:T(8,128)(2,1)}, bf16[...) custom-call(bf16[128,1536]{1,0:T(8,128)(2,1)} %collective-permute-done.164.refs_0_, ...), custom_call_target="tpu_custom_call" | custom-call | flops 2717908992 | bytes 13762560 | tf_op jit(solution)/shard_map/pallas_call | solution.py:197
  646.1 8.6 %shard_map.541 = (bf16[768,1536]{1,0:T(8,128)(2,1)}, bf16[768,384]{1,0:T(8,128)(2,1)}, bf16[768,384]{1,0:T(8,128)(2,1)}, bf16[768,384]{1,0:T(8,128)(2,1)}, bf16[...) custom-call(bf16[128,1536]{1,0:T(8,128)(2,1)} %collective-permute-done.168.refs_0_, ...), custom_call_target="tpu_custom_call" | custom-call | flops 2717908992 | bytes 13762560 | tf_op jit(solution)/shard_map/pallas_call | solution.py:197
  687.6 11.4 %shard_map.543 = (f32[1536,384]{1,0:T(8,128)}, f32[1536,384]{1,0:T(8,128)}) custom-call(bf16[256,1536]{1,0:T(8,128)(2,1)} %broadcast_select_fusion.3.refs_0_, bf16[256,384]{1,0:T(8,128)(2,1)} %get-tuple-element.1088.refs_1_, bf16[256,384]{1,0:T(8,128)(2,1)} %get-tuple-element.1089.refs_2_, ...), custom_call_target="tpu_custom_call", output_to_operand_aliasing={{0}: (12, {}), {1}: (13, {})} | custom-call | flops 4831838208 | bytes 14155776 | tf_op jit(solution)/shard_map/pallas_call | solution.py:550
  706.8 8.3 %shard_map.544.refs_8_ = f32[384,1536]{1,0:T(8,128)} custom-call(bf16[256,384]{1,0:T(8,128)(2,1)} %get-tuple-element.1119.refs_0_, bf16[256,1536]{1,0:T(8,128)(2,1)} %get-tuple-element.1120.refs_1_, bf16[768,384]{1,0:T(8,128)(2,1)} %get-tuple-element.1121.refs_2_, bf16[768,1536]{1,0:T(8,128)(2,1)} %get-tuple-element.1122.refs_3_, ...), custom_call_target="tpu_custom_call", output_to_operand_aliasing={{}: (8, {})} | custom-call | flops 2415919104 | bytes 10223616 | tf_op jit(solution)/shard_map/pallas_call | solution.py:550
  717.3 10.9 %shard_map.545 = (f32[128,1536]{1,0:T(8,128)}, bf16[128,1536]{1,0:T(8,128)(2,1)}, bf16[128,1536]{1,0:T(8,128)(2,1)}, bf16[128,1536]{1,0:T(8,128)(2,1)}, bf16[128...) custom-call(bf16[128,1536]{1,0:T(8,128)(2,1)} %copy-done.6, ...), custom_call_target="tpu_custom_call" | custom-call | flops 2818572288 | bytes 16474112 | tf_op jit(solution)/shard_map/pallas_call | solution.py:197
  775.4 11.4 %shard_map.546 = (f32[1536,384]{1,0:T(8,128)}, f32[1536,384]{1,0:T(8,128)}) custom-call(bf16[256,1536]{1,0:T(8,128)(2,1)} %get-tuple-element.1188.refs_0_, bf16[256,384]{1,0:T(8,128)(2,1)} %get-tuple-element.1189.refs_1_, bf16[256,384]{1,0:T(8,128)(2,1)} %get-tuple-element.1190.refs_2_, ...), custom_call_target="tpu_custom_call", output_to_operand_aliasing={{0}: (12, {}), {1}: (13, {})} | custom-call | flops 4831838208 | bytes 14155776 | tf_op jit(solution)/shard_map/pallas_call | solution.py:550
  (955 shorter events, 573.3 us)
Async XLA Ops:
  7.2 166.2 %all-gather.2.cloned.1.call-start = ((), (), s32[]{:S(2)}) async-start(), calls=%async_computation | async-start | bytes 6193152 | tf_op jit(solution)/shard_map/all_gather | solution.py:775
  9.4 28.8 %collective-permute-start.3 = (bf16[192,1792]{1,0:T(8,128)(2,1)S(1)}, bf16[192,1792]{1,0:T(8,128)(2,1)S(1)}, u32[]{:S(2)}, u32[]{:S(2)}) collective-permute-start(bf16[192,1792]{1,0:T(8,128)(2,1)S(1)} %pad_maximum_fusion.8), channel_id=1, source_target_pairs={{0,1},{1,0},{2,3},{3,2},{4,5},{5,4},{6,7},{7,6},{8,9},{9,8},{10,11... | collective-permute-start | bytes 2064392 | tf_op jit(solution)/shard_map/ppermute | solution.py:55
  43.5 18.5 %collective-permute-start.4 = (bf16[128,1664]{1,0:T(8,128)(2,1)}, bf16[128,1664]{1,0:T(8,128)(2,1)}, u32[]{:S(2)}, u32[]{:S(2)}) collective-permute-start(bf16[128,1664]{1,0:T(8,128)(2,1)} %get-tuple-element.637.refs_0_), channel_id=1, source_target_pairs={{0,4},{2,6},{4,0},{6,2},{8,12},{10,14},{12,8},{14,10},{1,5},{3,7},... | collective-permute-start | bytes 1277960 | tf_op jit(solution)/shard_map/ppermute | solution.py:55
  64.1 20.6 %collective-permute-start.10 = (bf16[128,1664]{1,0:T(8,128)(2,1)}, bf16[128,1664]{1,0:T(8,128)(2,1)S(1)}, u32[]{:S(2)}, u32[]{:S(2)}) collective-permute-start(bf16[128,1664]{1,0:T(8,128)(2,1)} %collective-permute-done.6.refs_2_), channel_id=1, source_target_pairs={{0,4},{2,6},{4,0},{6,2},{8,12},{10,14},{12,8},{14,10},{1,5},{3,7},... | collective-permute-start | bytes 1277960 | tf_op jit(solution)/shard_map/ppermute | solution.py:55
  162.4 20.5 %collective-permute-start.40 = (bf16[128,1536]{1,0:T(8,128)(2,1)}, bf16[128,1536]{1,0:T(8,128)(2,1)}, u32[]{:S(2)}, u32[]{:S(2)}) collective-permute-start(bf16[128,1536]{1,0:T(8,128)(2,1)} %get-tuple-element.783.refs_2_), channel_id=1, source_target_pairs={{0,2},{2,0},{4,6},{6,4},{8,10},{10,8},{12,14},{14,12},{1,3},{3,1},... | collective-permute-start | bytes 1179656 | tf_op jit(solution)/shard_map/ppermute | solution.py:55
  183.5 23.3 %collective-permute-start.51 = (bf16[128,1664]{1,0:T(8,128)(2,1)}, bf16[128,1664]{1,0:T(8,128)(2,1)}, u32[]{:S(2)}, u32[]{:S(2)}) collective-permute-start(bf16[128,1664]{1,0:T(8,128)(2,1)} %get-tuple-element.694.refs_0_), channel_id=1, source_target_pairs={{0,1},{1,0},{2,3},{3,2},{4,5},{5,4},{6,7},{7,6},{8,9},{9,8},{10,11... | collective-permute-start | bytes 1277960 | tf_op jit(solution)/shard_map/ppermute | solution.py:55
  273.0 23.6 %collective-permute-start.79 = (bf16[384,1536]{1,0:T(8,128)(2,1)}, bf16[384,1536]{1,0:T(8,128)(2,1)}, u32[]{:S(2)}, u32[]{:S(2)}) collective-permute-start(bf16[384,1536]{1,0:T(8,128)(2,1)} %get-tuple-element.762), channel_id=1, source_target_pairs={{0,2},{2,0},{4,6},{6,4},{8,10},{10,8},{12,14},{14,12},{1,3},{3,1},... | collective-permute-start | bytes 3538952 | tf_op jit(solution)/shard_map/ppermute | solution.py:55
  275.8 20.8 %collective-permute-start.76 = (bf16[128,1536]{1,0:T(8,128)(2,1)}, bf16[128,1536]{1,0:T(8,128)(2,1)S(1)}, u32[]{:S(2)}, u32[]{:S(2)}) collective-permute-start(bf16[128,1536]{1,0:T(8,128)(2,1)} %get-tuple-element.747), channel_id=1, source_target_pairs={{0,8},{2,10},{4,12},{6,14},{8,0},{10,2},{12,4},{14,6},{1,9},{3,11}... | collective-permute-start | bytes 1179656 | tf_op jit(solution)/shard_map/ppermute | solution.py:55
  276.4 20.2 %collective-permute-start.77 = (bf16[128,1536]{1,0:T(8,128)(2,1)}, bf16[128,1536]{1,0:T(8,128)(2,1)S(1)}, u32[]{:S(2)}, u32[]{:S(2)}) collective-permute-start(bf16[128,1536]{1,0:T(8,128)(2,1)} %get-tuple-element.748), channel_id=1, source_target_pairs={{0,1},{1,0},{2,3},{3,2},{4,5},{5,4},{6,7},{7,6},{8,9},{9,8},{10,11... | collective-permute-start | bytes 1179656 | tf_op jit(solution)/shard_map/ppermute | solution.py:55
  277.4 19.8 %collective-permute-start.78 = (bf16[128,1536]{1,0:T(8,128)(2,1)}, bf16[128,1536]{1,0:T(8,128)(2,1)S(1)}, u32[]{:S(2)}, u32[]{:S(2)}) collective-permute-start(bf16[128,1536]{1,0:T(8,128)(2,1)} %get-tuple-element.749), channel_id=1, source_target_pairs={{0,4},{2,6},{4,0},{6,2},{8,12},{10,14},{12,8},{14,10},{1,5},{3,7},... | collective-permute-start | bytes 1179656 | tf_op jit(solution)/shard_map/ppermute | solution.py:55
  349.1 21.8 %collective-permute-start.93 = (bf16[128,1536]{1,0:T(8,128)(2,1)}, bf16[128,1536]{1,0:T(8,128)(2,1)}, u32[]{:S(2)}, u32[]{:S(2)}) collective-permute-start(bf16[128,1536]{1,0:T(8,128)(2,1)} %get-tuple-element.816), channel_id=1, source_target_pairs={{0,4},{2,6},{4,0},{6,2},{8,12},{10,14},{12,8},{14,10},{1,5},{3,7},... | collective-permute-start | bytes 1179656 | tf_op jit(solution)/shard_map/ppermute | solution.py:55
  349.4 21.5 %collective-permute-start.94 = (bf16[128,1536]{1,0:T(8,128)(2,1)S(1)}, bf16[128,1536]{1,0:T(8,128)(2,1)}, u32[]{:S(2)}, u32[]{:S(2)}) collective-permute-start(bf16[128,1536]{1,0:T(8,128)(2,1)S(1)} %get-tuple-element.817), channel_id=1, source_target_pairs={{0,8},{2,10},{4,12},{6,14},{8,0},{10,2},{12,4},{14,6},{1,9},{3,11}... | collective-permute-start | bytes 1179656 | tf_op jit(solution)/shard_map/ppermute | solution.py:55
  351.1 19.8 %collective-permute-start.95 = (bf16[128,1536]{1,0:T(8,128)(2,1)S(1)}, bf16[128,1536]{1,0:T(8,128)(2,1)}, u32[]{:S(2)}, u32[]{:S(2)}) collective-permute-start(bf16[128,1536]{1,0:T(8,128)(2,1)S(1)} %get-tuple-element.818), channel_id=1, source_target_pairs={{0,1},{1,0},{2,3},{3,2},{4,5},{5,4},{6,7},{7,6},{8,9},{9,8},{10,11... | collective-permute-start | bytes 1179656 | tf_op jit(solution)/shard_map/ppermute | solution.py:55
  421.5 23.7 %collective-permute-start.115 = (bf16[384,1536]{1,0:T(8,128)(2,1)}, bf16[384,1536]{1,0:T(8,128)(2,1)}, u32[]{:S(2)}, u32[]{:S(2)}) collective-permute-start(bf16[384,1536]{1,0:T(8,128)(2,1)} %get-tuple-element.864), channel_id=1, source_target_pairs={{0,2},{2,0},{4,6},{6,4},{8,10},{10,8},{12,14},{14,12},{1,3},{3,1},... | collective-permute-start | bytes 3538952 | tf_op jit(solution)/shard_map/ppermute | solution.py:55
  422.6 22.6 %collective-permute-start.96 = (bf16[128,1536]{1,0:T(8,128)(2,1)}, bf16[128,1536]{1,0:T(8,128)(2,1)S(1)}, u32[]{:S(2)}, u32[]{:S(2)}) collective-permute-start(bf16[128,1536]{1,0:T(8,128)(2,1)} %get-tuple-element.834), channel_id=1, source_target_pairs={{16,0},{17,1},{18,2},{19,3},{20,4},{21,5},{22,6},{23,7},{24,8},{25... | collective-permute-start | bytes 1179656 | tf_op jit(solution)/shard_map/ppermute | solution.py:846
  474.9 21.0 %collective-permute-start.134 = (bf16[384,1536]{1,0:T(8,128)(2,1)}, bf16[384,1536]{1,0:T(8,128)(2,1)S(1)}, u32[]{:S(2)}, u32[]{:S(2)}) collective-permute-start(bf16[384,1536]{1,0:T(8,128)(2,1)} %get-tuple-element.911), channel_id=1, source_target_pairs={{0,2},{2,0},{4,6},{6,4},{8,10},{10,8},{12,14},{14,12},{1,3},{3,1},... | collective-permute-start | bytes 3538952 | tf_op jit(solution)/shard_map/ppermute | solution.py:55
  635.8 19.0 %collective-permute-start.178 = (bf16[384,1536]{1,0:T(8,128)(2,1)}, bf16[384,1536]{1,0:T(8,128)(2,1)}, u32[]{:S(2)}, u32[]{:S(2)}) collective-permute-start(bf16[384,1536]{1,0:T(8,128)(2,1)} %get-tuple-element.1051), channel_id=1, source_target_pairs={{0,2},{2,0},{4,6},{6,4},{8,10},{10,8},{12,14},{14,12},{1,3},{3,1},... | collective-permute-start | bytes 3538952 | tf_op jit(solution)/shard_map/ppermute | solution.py:55
  730.6 20.4 %collective-permute-start.163 = (f32[128,768]{1,0:T(8,128)S(1)}, f32[128,768]{1,0:T(8,128)S(1)}, u32[]{:S(2)}, u32[]{:S(2)}) collective-permute-start(f32[128,768]{1,0:T(8,128)S(1)} %constant_dynamic-slice_fusion.2), channel_id=1, source_target_pairs={{0,1},{1,0},{2,3},{3,2},{4,5},{5,4},{6,7},{7,6},{8,9},{9,8},{10,11... | collective-permute-start | bytes 1179656 | tf_op jit(solution)/shard_map/ppermute | solution.py:55
  736.4 20.5 %collective-permute-start.218 = (bf16[576,768]{1,0:T(8,128)(2,1)S(1)}, bf16[576,768]{1,0:T(8,128)(2,1)S(1)}, u32[]{:S(2)}, u32[]{:S(2)}) collective-permute-start(bf16[576,768]{1,0:T(8,128)(2,1)S(1)} %bitcast.281), channel_id=1, source_target_pairs={{0,2},{2,0},{4,6},{6,4},{8,10},{10,8},{12,14},{14,12},{1,3},{3,1},... | collective-permute-start | bytes 2654216 | tf_op jit(solution)/shard_map/ppermute | solution.py:55
  743.7 22.8 %collective-permute-start.202 = (bf16[576,1024]{1,0:T(8,128)(2,1)S(1)}, bf16[576,1024]{1,0:T(8,128)(2,1)S(1)}, u32[]{:S(2)}, u32[]{:S(2)}) collective-permute-start(bf16[576,1024]{1,0:T(8,128)(2,1)S(1)} %bitcast.279), channel_id=1, source_target_pairs={{0,2},{2,0},{4,6},{6,4},{8,10},{10,8},{12,14},{14,12},{1,3},{3,1},... | collective-permute-start | bytes 3538952 | tf_op jit(solution)/shard_map/ppermute | solution.py:55
  756.9 34.1 %collective-permute-start.207 = (bf16[576,1024]{1,0:T(8,128)(2,1)}, bf16[576,1024]{1,0:T(8,128)(2,1)}, u32[]{:S(2)}, u32[]{:S(2)}) collective-permute-start(bf16[576,1024]{1,0:T(8,128)(2,1)} %bitcast.77), channel_id=1, source_target_pairs={{0,2},{2,0},{4,6},{6,4},{8,10},{10,8},{12,14},{14,12},{1,3},{3,1},... | collective-permute-start | bytes 3538952 | tf_op jit(solution)/shard_map/ppermute | solution.py:55
  770.6 21.1 %collective-permute-start.204 = (bf16[192,1024]{1,0:T(8,128)(2,1)}, bf16[192,1024]{1,0:T(8,128)(2,1)}, u32[]{:S(2)}, u32[]{:S(2)}) collective-permute-start(bf16[192,1024]{1,0:T(8,128)(2,1)} %get-tuple-element.1151), channel_id=1, source_target_pairs={{0,8},{2,10},{4,12},{6,14},{8,0},{10,2},{12,4},{14,6},{1,9},{3,11}... | collective-permute-start | bytes 1179656 | tf_op jit(solution)/shard_map/ppermute | solution.py:55
  772.9 20.2 %collective-permute-start.205 = (bf16[192,1024]{1,0:T(8,128)(2,1)}, bf16[192,1024]{1,0:T(8,128)(2,1)}, u32[]{:S(2)}, u32[]{:S(2)}) collective-permute-start(bf16[192,1024]{1,0:T(8,128)(2,1)} %get-tuple-element.1152), channel_id=1, source_target_pairs={{0,1},{1,0},{2,3},{3,2},{4,5},{5,4},{6,7},{7,6},{8,9},{9,8},{10,11... | collective-permute-start | bytes 1179656 | tf_op jit(solution)/shard_map/ppermute | solution.py:55
  774.1 19.9 %collective-permute-start.206 = (bf16[192,1024]{1,0:T(8,128)(2,1)}, bf16[192,1024]{1,0:T(8,128)(2,1)}, u32[]{:S(2)}, u32[]{:S(2)}) collective-permute-start(bf16[192,1024]{1,0:T(8,128)(2,1)} %get-tuple-element.1153), channel_id=1, source_target_pairs={{0,4},{2,6},{4,0},{6,2},{8,12},{10,14},{12,8},{14,10},{1,5},{3,7},... | collective-permute-start | bytes 1179656 | tf_op jit(solution)/shard_map/ppermute | solution.py:55
  (374 other events, 3072.6 us)
Sparse Core Ops, SparseCore 0:
  39.1 54.0 all-gather.1
where the time goes:
time: 848 us; the launch traced here: 831 us
  Pallas kernels  295 us (35%)
  starting transfers between devices  188 us (22%)
  waiting for transfers between devices  181 us (21%)
  other arithmetic  90.2 us (11%)
  local copies, waits for them, and re-layouts  47.9 us (6%)
  between operations  22.8 us (3%)
    pallas_call x33, Pallas kernels, on_device(): pl.pallas_call(body, out_shape=outs, in_specs=[SMEM] * len(scalars) + [VM...  237 us
    ppermute x223, starting transfers between devices, swap(): lax.ppermute(value, axis, [(i, i ^ bit) for i in range(lax.axis_size(axis...  175 us
    ppermute x223, waiting for transfers between devices, swap(): lax.ppermute(value, axis, [(i, i ^ bit) for i in range(lax.axis_size(axis...  149 us
    pallas_call x6, Pallas kernels, product_sums(): pl.pallas_call(functools.partial(product_sums_body, len(stages), products...  57.8 us
    convert_element_type x24, other arithmetic, low_sum(): return sum((wide(t) for t in terms)).astype(bf16)  34.6 us
    select_n x26, other arithmetic, chosen(): return jax.tree.map(lambda a, b: jnp.where(first, a, b), here, there)  29.8 us
    unnamed x344, local copies, waits for them, and re-layouts  20.1 us
  transfers between devices with their start and end apart: 228, of which 81 were waited for; matrix products, arithmetic and copies ran while one was open for 11% of the time, Pallas kernels for 29%

commit v1 on v0

v1 whole, which is shorter than its diff:
```python
import functools

import jax
import jax.numpy as jnp
import numpy as np
from jax import lax
from jax.experimental import pallas as pl
from jax.experimental.pallas import tpu as pltpu
from jax.sharding import PartitionSpec as P

HEAD_SIZE = 128
epsilon = 1e-06
masked_value = -1e30
bf16 = jnp.bfloat16
f32 = jnp.float32


def wide(a):
    return a.astype(f32)


def dot_nn(a, b):
    return lax.dot_general(a, b, (((1,), (0,)), ((), ())), preferred_element_type=f32)


def dot_nt(a, b):
    return lax.dot_general(a, b, (((1,), (1,)), ((), ())), preferred_element_type=f32)


def dot_tn(a, b):
    return lax.dot_general(a, b, (((0,), (0,)), ((), ())), preferred_element_type=f32)


class Cube:
    def __init__(self):
        peers = lax.axis_size("dp")
        bits = [1 << i for i in range(peers.bit_length() - 1)]
        rest = bits[1:]
        self.core = ("dp", bits[0])
        self.x = ("dp", rest[0])
        self.y = ("dp", rest[len(rest) // 2])
        self.z = ("shard", 1)
        self.extra = [("dp", b) for b in rest if b not in (self.x[1], self.y[1])]
        inner = [0]
        for _, bit in self.extra:
            inner = inner + [m | bit for m in inner]
        self.inner = np.array(inner)
        x, y = self.x[1], self.y[1]
        self.corner = (x | y, 1)
        stages = [[(0, 0)], [(x, 0), (y, 0), (0, 1)], [(x | y, 0), (y, 1), (x, 1)], [self.corner]]
        self.stages = [(g, [(m | self.core[1], s) for m, s in g]) for g in stages]


def swap(value, direction):
    axis, bit = direction
    return lax.ppermute(value, axis, [(i, i ^ bit) for i in range(lax.axis_size(axis))])


def across(value, cube):
    mask, flip = cube.corner
    shards = lax.axis_size("shard")
    pairs = [
        (d * shards + s, (d ^ mask) * shards + (s ^ flip))
        for d in range(lax.axis_size("dp"))
        for s in range(shards)
    ]
    return lax.ppermute(value, ("dp", "shard"), pairs)


together = lax.optimization_barrier


def both(*thunks):
    def work(*groups):
        return [thunk[1](*group) for thunk, group in zip(thunks, groups)]

    return lambda: [thunk[0]() for thunk in thunks], work


def after(payload, thunks, step):
    if step >= len(thunks) or thunks[step] is None:
        return payload, lambda: ()
    inputs, work = thunks[step]
    payload, inputs = together((payload, inputs()))
    return payload, lambda: work(*inputs)


def gather_rows(cube, own, work, side=()):
    core = cube.core
    own, beside = after(own, side, 0)
    near = [swap(own, d) for d in (cube.x, cube.y, cube.z)]
    mine0, other0 = work(0, [own, swap(own, core)])
    near, mine0, other0, _ = together((near, mine0, other0, beside()))

    near, beside = after(near, side, 1)
    middle = [swap(block, d) for block, d in zip(near, (cube.y, cube.z, cube.x))]
    in0 = swap(other0, core)
    mine1, other1 = work(1, [*near, *[swap(block, core) for block in near]])
    middle, in0, mine1, other1, _ = together((middle, in0, mine1, other1, beside()))

    middle, beside = after(middle, side, 2)
    corner = swap(middle[0], cube.z)
    mine2, other2 = work(2, [*middle, *[swap(block, core) for block in middle]])
    corner, mine2, other2, _ = together((corner, mine2, other2, beside()))
    other2, beside = after(other2, side, 3)
    in2 = swap(other2, core)
    mine3, other3 = work(3, [corner, swap(corner, core)])
    in2, mine3, other3, _ = together((in2, mine3, other3, beside()))
    return [(mine0, in0), (mine1, other1), (mine2, in2), (mine3, other3)]


def low_sum(*terms):
    return sum(wide(t) for t in terms).astype(bf16)


def reduce_start(cube, pairs, side=()):
    own, near, middle, corner = pairs
    rows = corner[0].shape[0]
    sent = [low_sum(*[g[i * rows : (i + 1) * rows] for g in middle]) for i in range(3)]
    (sent, near, corner), beside = after((sent, near, corner), side, 0)
    arrived = [swap(t, d) for t, d in zip(sent, (cube.y, cube.z, cube.x))]
    near, corner = [(mine, swap(other, cube.core)) for mine, other in (near, corner)]
    arrived, own, near, corner, _ = together((arrived, own, near, corner, beside()))
    return own, near, arrived, corner


def reduce_finish(cube, state, side=()):
    own, near, arrived, corner = state
    rows = corner[0].shape[0]
    sent = [low_sum(*corner)] + [low_sum(*[g[i * rows : (i + 1) * rows] for g in near], arrived[i]) for i in range(3)]
    sent, beside = after(sent, side, 0)
    arrived = [swap(t, d) for t, d in zip(sent[1:], (cube.x, cube.y, cube.z))] + [across(sent[0], cube)]
    arrived, own, _ = together((arrived, own, beside()))
    total = sum(wide(t) for t in [*own, *arrived])
    for direction in reversed(cube.extra):
        half = total.shape[0] // 2
        total = total[:half] + wide(swap(total[half:].astype(bf16), direction))
    return total


def norm_factor(values):
    return lax.rsqrt(jnp.mean(values * values, axis=1, keepdims=True) + epsilon)


def norm_back(values, factor, gain, grad):
    gain_grad = jnp.sum(grad * values * factor, axis=0, keepdims=True)
    scaled = grad * gain
    inner = jnp.mean(scaled * values, axis=1, keepdims=True)
    return factor * (scaled - values * factor * factor * inner), gain_grad


def stack_heads(rows):
    return jnp.concatenate(
        [rows[:, i : i + HEAD_SIZE] for i in range(0, rows.shape[1], HEAD_SIZE)], axis=0
    )


def spread_heads(stacked, rows):
    return jnp.concatenate(
        [stacked[i : i + rows] for i in range(0, stacked.shape[0], rows)], axis=1
    )


def head_probs(query, key, allowed):
    scores = jnp.where(allowed > 0.0, dot_nt(query, key) * HEAD_SIZE ** (-0.5), masked_value)
    exp_scores = jnp.exp(scores - jnp.max(scores, axis=1, keepdims=True))
    return exp_scores / jnp.sum(exp_scores, axis=1, keepdims=True)


def normed_rows(values, gain):
    return (values * norm_factor(values) * gain).astype(bf16)


def group_probs(qkv, allowed):
    width = qkv.shape[1] - 2 * HEAD_SIZE
    query = stack_heads(qkv[:, :width])
    key, value = qkv[:, width : width + HEAD_SIZE], qkv[:, width + HEAD_SIZE :]
    tiled = jnp.concatenate([allowed] * (width // HEAD_SIZE), axis=0)
    return query, key, value, head_probs(query, key, tiled)


def head_group(normed, allowed, weights, qkv, heads):
    *projections, w_out = weights
    at = 0
    for w in projections:
        part = dot_nn(normed, w()).astype(bf16)
        qkv[:, at : at + part.shape[1]] = part
        at += part.shape[1]
    _, _, value, probs = group_probs(qkv[...], allowed)
    heads[...] = spread_heads(dot_nn(probs.astype(bf16), value).astype(bf16), normed.shape[0])
    return dot_nt(heads[...], w_out())


VMEM = pl.BlockSpec(memory_space=pltpu.VMEM)
SMEM = pl.BlockSpec(memory_space=pltpu.SMEM)
ANY = pl.BlockSpec(memory_space=pl.ANY)
KERNEL_VMEM = 42 << 20


def held(shape, dtype):
    return pltpu.VMEM(shape, dtype)


def like(shape, dtype):
    return pltpu.HBM(shape, dtype)


def close(value):
    return pltpu.with_memory_space_constraint(value, pltpu.VMEM)


def distant(value):
    return pltpu.with_memory_space_constraint(value, pltpu.HBM)


def pinned(*values):
    def body(*refs):
        ins, outs, sems = refs[: len(values)], refs[len(values) : -1], refs[-1]
        copies = Copies(sems)
        for copy in [copies.start(a, b) for a, b in zip(ins, outs)]:
            copy.wait()

    return pl.pallas_call(
        body,
        out_shape=[held(v.shape, v.dtype) for v in values],
        in_specs=[ANY] * len(values),
        out_specs=[VMEM] * len(values),
        scratch_shapes=[pltpu.SemaphoreType.DMA((len(values),))],
        compiler_params=pltpu.CompilerParams(vmem_limit_bytes=1 << 20),
    )(*values)


def put_together(pieces, spans, shape):
    starts = jnp.stack([first for first, _, _ in spans]).astype(jnp.int32)

    def body(starts, *refs):
        ins, out, sems = refs[:-2], refs[-2], refs[-1]
        copies, waits = Copies(sems), []
        for i, (piece, (_, unit, column)) in enumerate(zip(ins, spans)):
            rows = pl.ds(pl.multiple_of(starts[i] * unit, unit), piece.shape[0])
            waits.append(copies.start(piece, out.at[rows, pl.ds(column, piece.shape[1])]))
        for copy in waits:
            copy.wait()

    return pl.pallas_call(
        body,
        out_shape=held(shape, pieces[0].dtype),
        in_specs=[SMEM] + [ANY] * len(pieces),
        out_specs=VMEM,
        scratch_shapes=[pltpu.SemaphoreType.DMA((len(pieces),))],
        compiler_params=pltpu.CompilerParams(vmem_limit_bytes=KERNEL_VMEM),
    )(starts, *map(distant, pieces))


class Copies:
    def __init__(self, sems):
        self.sems, self.count = sems, 0

    def start(self, source, target):
        copy = pltpu.make_async_copy(source, target, self.sems.at[self.count])
        self.count += 1
        copy.start()
        return copy

    def fetch(self, source, target):
        copy, waited = self.start(source, target), []

        def value():
            if not waited:
                copy.wait()
                waited.append(True)
            return target[...]

        return value


def on_device(body, outs, args, flops, scalars=(), kept=(), far=(), scratch=(), direct=False):
    moved = sum(a.size * a.dtype.itemsize for a in args)
    return pl.pallas_call(
        body,
        out_shape=outs,
        in_specs=[SMEM] * len(scalars) + [VMEM] * (len(args) + len(kept)) + [ANY] * len(far),
        out_specs=[SMEM if o.dtype == jnp.int32 else ANY if direct else VMEM for o in outs],
        scratch_shapes=scratch,
        compiler_params=pltpu.CompilerParams(vmem_limit_bytes=KERNEL_VMEM),
        cost_estimate=pl.CostEstimate(flops=flops // 64, bytes_accessed=moved // 64, transcendentals=0),
    )(*scalars, *map(distant, args), *map(close, kept), *far)


def holders(*arrays):
    return [pltpu.VMEM(a.shape, a.dtype) for a in arrays] + [pltpu.SemaphoreType.DMA((len(arrays) + 1,))]


def geometry(lens, micro, side, rows, block):
    ends, total, best, start = [], 0, lens[micro, 0, 0], 0
    for i in range(lens.shape[2]):
        length = lens[micro, 0, i]
        if i:
            start = jnp.where(length > best, total, start)
            best = jnp.maximum(best, length)
        total = total + length
        ends.append(total)
    return ends, lax.rem(start + rows * side, block)


def positions(shape, axis, begin, block):
    place = lax.broadcasted_iota(jnp.int32, shape, axis) + begin
    return jnp.where(place >= block, place - block, place)


def selection(begin, rows, block):
    wanted = positions((rows, block), 0, begin, block)
    return (wanted == lax.broadcasted_iota(jnp.int32, (rows, block), 1)).astype(f32)


def sequence_mask(ends, begin, rows, block):
    row, col = [positions((rows, rows), axis, begin, block) for axis in (0, 1)]
    inside = sum(jnp.abs((row >= e).astype(jnp.int32) - (col >= e).astype(jnp.int32)) for e in ends)
    return ((inside == 0) & (col <= row)).astype(f32)


def gate_columns(pick, routes, gates):
    peers = lax.axis_size("dp")
    expert = lax.broadcasted_iota(jnp.int32, (128, routes.shape[1]), 0)
    table = jnp.zeros(expert.shape, f32)
    for k in range(routes.shape[0]):
        gate, route = gates[k : k + 1, :], routes[k : k + 1, :]
        high = wide(gate.astype(bf16))
        table += jnp.where(expert == route, high, 0.0) + jnp.where(expert == route + peers, gate - high, 0.0)
    return dot_nt(pick, table.astype(bf16)).astype(bf16)


def turned_body(lens, blocks, own, other, block_rows, sems):
    copy = Copies(sems).fetch(blocks.at[0], block_rows)
    block = block_rows.shape[0]
    here = jnp.where(lax.axis_index("section") == 0, 0.0, 1.0)
    shard = lax.axis_index("shard")
    for side, out in ((shard, own), (1 - shard, other)):
        _, begin = geometry(lens, 0, side, block // 2, block)
        out[...] = dot_nn((selection(begin, block // 2, block) * here).astype(bf16), copy()).astype(bf16)


def turned_block(lens, blocks):
    _, block, model = blocks.shape
    scratch = [pltpu.VMEM((block, model), bf16), pltpu.SemaphoreType.DMA((1,))]
    shapes = [like((block // 2, model), bf16)] * 2
    return on_device(
        turned_body, shapes, [], 2 * block * block * model, (lens,), far=[distant(blocks)], scratch=scratch
    )


def opening_body(lens, gain, tokens, *refs):
    wq, wk, wv, wo, inputs, part, qkv, heads, sent, qkv_other, heads_other, mask, *scratch, sems = refs
    copies = Copies(sems)
    sources = [tokens.at[0], wq, wk, wv, wo]
    block_rows, *weights = [copies.fetch(a, b) for a, b in zip(sources, scratch)]
    block = tokens.shape[1]
    rows = block // 2
    shard = lax.axis_index("shard")
    first = jnp.where(lax.axis_index("section") == 0, 1.0, 0.0)
    for own in (False, True):
        to_qkv, to_heads = (qkv, heads) if own else (qkv_other, heads_other)
        ends, begin = geometry(lens, 0, shard if own else 1 - shard, rows, block)
        pick = selection(begin, rows, block)
        values = dot_nn((pick * first).astype(bf16), block_rows())
        allowed = sequence_mask(ends, begin, rows, block)
        value = head_group(normed_rows(values, gain[...]), allowed, weights, to_qkv, to_heads)
        if own:
            inputs[...] = values.astype(bf16)
            part[...] = values + value
            mask[...] = allowed
        else:
            sent[...] = value.astype(bf16)


def opening(lens, tokens, gain, weights):
    _, block, model = tokens.shape
    rows = block // 2
    width, out = sum(w.shape[1] for w in weights[:3]), weights[3].shape[1]
    shapes = [
        like((rows, model), bf16), like((rows, model), f32), like((rows, width), bf16), like((rows, out), bf16),
        like((rows, model), bf16), like((rows, width), bf16), like((rows, out), bf16), like((rows, rows), f32),
    ]
    scratch = [pltpu.VMEM((block, model), bf16), *holders(*weights)]
    outs = on_device(
        opening_body, shapes, [gain], 4 * rows * model * (width + out), (lens,), far=[distant(t) for t in (tokens, *weights)], scratch=scratch
    )
    return outs[:5], outs[7]


def settle_body(lens, routes0, gates0, routes1, gates1, tokens, grad, *refs):
    fresh, cot, mask, extra0, extra1, starts, token_rows, grad_rows, sems = refs
    copies = Copies(sems)
    for micro in range(2):
        _, starts[micro] = geometry(lens, micro, 0, tokens.shape[1] // 2, tokens.shape[1])
    token_rows = copies.fetch(tokens.at[1], token_rows)
    grad_rows = copies.fetch(grad.at[1], grad_rows)
    block = tokens.shape[1]
    rows = block // 2
    first = jnp.where(lax.axis_index("section") == 0, 1.0, 0.0)
    for micro, routes, gates, extra in ((0, routes0, gates0, extra0), (1, routes1, gates1, extra1)):
        ends, begin = geometry(lens, micro, lax.axis_index("shard"), rows, block)
        pick = selection(begin, rows, block)
        extra[...] = gate_columns(pick.astype(bf16), routes[...], gates[...])
    fresh[...] = dot_nn((pick * first).astype(bf16), token_rows()).astype(bf16)
    cot[...] = dot_nn((pick * (1.0 - first)).astype(bf16), grad_rows()).astype(bf16)
    mask[...] = sequence_mask(ends, begin, rows, block)


def settle(lens, tokens, grad, routes, gates):
    _, block, model = tokens.shape
    rows = block // 2
    shapes = [like((rows, model), bf16)] * 2 + [like((rows, rows), f32)] + [like((rows, 128), bf16)] * 2
    shapes.append(pltpu.SMEM((2,), jnp.int32))
    args = [routes[0], gates[0], routes[1], gates[1]]
    scratch = [pltpu.VMEM((block, model), bf16)] * 2 + [pltpu.SemaphoreType.DMA((2,))]
    return on_device(
        settle_body, shapes, args, 2 * block * block * model, (lens,), far=[distant(tokens), distant(grad)], scratch=scratch
    )


def joined_body(part, other, extra, gain, hidden, payload):
    total = part[...] + wide(other[...])
    hidden[...] = total
    model = total.shape[1]
    payload[:, :model] = normed_rows(total, gain[...])
    payload[:, model:] = extra[...]


def joined(part, other, gain, extra):
    rows, model = part.shape
    shapes = [like((rows, model), f32), like((rows, model + extra.shape[1]), bf16)]
    return on_device(joined_body, shapes, [part, other, extra, gain], 10 * rows * model)


def by_halves(refs):
    *own, packed = refs
    widths = [w.shape[1] for w in own]
    firsts = [sum(widths[:i]) for i in range(4)]
    other = [lambda f=f, w=w: packed[:, f : f + w] for f, w in zip(firsts, widths)]
    return [lambda w=w: w[...] for w in own], other


def other_heads_body(inputs, mask, gain, wq, wk, wv, wo, packed, qkv, heads):
    _, weights = by_halves((wq, wk, wv, wo, packed))
    head_group(normed_rows(wide(inputs[...]), gain[...]), mask[...], weights, qkv, heads)


def other_heads(inputs, mask, gain, weights, packed):
    rows = inputs.shape[0]
    width, out = sum(w.shape[1] for w in weights[:3]), weights[3].shape[1]
    shapes = [like((rows, width), bf16), like((rows, out), bf16)]
    return on_device(
        other_heads_body, shapes, [inputs, mask, gain], 2 * rows * packed.size, kept=[*weights, packed]
    )


def attention_body(fresh, arriving, mask, extra, gain, gain_two, *refs):
    own, other = by_halves(refs[:5])
    inputs, hidden, payload, qkv0, qkv1, heads0, heads1 = refs[5:]
    rows = fresh[...] + arriving[...]
    inputs[...] = rows
    total = wide(rows)
    normed = normed_rows(total, gain[...])
    total = total + head_group(normed, mask[...], own, qkv0, heads0)
    total = total + head_group(normed, mask[...], other, qkv1, heads1)
    hidden[...] = total
    model = total.shape[1]
    payload[:, :model] = normed_rows(total, gain_two[...])
    payload[:, model:] = extra[...]


def attention_forward(fresh, arriving, mask, gain, gain_two, extra, weights, packed):
    rows, model = fresh.shape
    width, out = sum(w.shape[1] for w in weights[:3]), weights[3].shape[1]
    shapes = [
        like((rows, model), bf16), like((rows, model), f32), like((rows, model + extra.shape[1]), bf16),
        like((rows, width), bf16), like((rows, width), bf16), like((rows, out), bf16), like((rows, out), bf16),
    ]
    args = [fresh, arriving, mask, extra, gain, gain_two]
    outs = on_device(attention_body, shapes, args, 4 * rows * packed.size, kept=[*weights, packed])
    inputs, hidden, payload, qkv0, qkv1, heads0, heads1 = outs
    return inputs, hidden, payload, [(qkv0, heads0), (qkv1, heads1)]


def attention_back_body(grad, grad_two, inputs, hidden, mask, q0, q1, gain, gain_two, *refs):
    own, other = by_halves(refs[:5])
    grad_input, grad_input_low, grad_low, normed, g0, g1, gain_grad, gain_two_grad = refs[5:]
    rows = inputs.shape[0]
    values = wide(inputs[...])
    normed[...] = normed_rows(values, gain[...])
    total = hidden[...]
    back, gain_two_grad[...] = norm_back(total, norm_factor(total), gain_two[...], grad_two[...])
    grad_hidden = wide(grad[...]) + back
    low = grad_hidden.astype(bf16)
    grad_low[...] = low
    grad_normed = jnp.zeros_like(grad_hidden)
    for qkv, weights, grad_qkv in ((q0, own, g0), (q1, other, g1)):
        query, key, value, probs = group_probs(qkv[...], mask[...])
        grad_heads = stack_heads(dot_nn(low, weights[3]()).astype(bf16))
        grad_probs = dot_nt(grad_heads, value)
        inner = jnp.sum(probs * grad_probs, axis=1, keepdims=True)
        grad_scores = (probs * (grad_probs - inner) * HEAD_SIZE ** (-0.5)).astype(bf16)
        grads = [
            spread_heads(dot_nn(grad_scores, key).astype(bf16), rows),
            dot_tn(grad_scores, query).astype(bf16),
            dot_tn(probs.astype(bf16), grad_heads).astype(bf16),
        ]
        at = 0
        for part, w in zip(grads, weights):
            grad_qkv[:, at : at + part.shape[1]] = part
            at += part.shape[1]
            grad_normed = grad_normed + dot_nt(part, w())
    back, gain_grad[...] = norm_back(values, norm_factor(values), gain[...], grad_normed)
    result = grad_hidden + back
    grad_input[...] = result
    grad_input_low[...] = result.astype(bf16)


def attention_backward(grad, grad_two, inputs, hidden, mask, gain, gain_two, projected, weights, packed):
    rows, model = inputs.shape
    width = projected[0].shape[1]
    shapes = [
        like((rows, model), f32), like((rows, model), bf16), like((rows, model), bf16),
        like((rows, model), bf16), like((rows, width), bf16), like((rows, width), bf16),
        like((1, model), f32), like((1, model), f32),
    ]
    args = [grad, grad_two, inputs, hidden, mask, *projected, gain, gain_two]
    return on_device(attention_back_body, shapes, args, 8 * rows * packed.size, kept=[*weights, packed])


def ranges(pieces):
    pairs = [p if isinstance(p, tuple) else (p, (0, p.shape[0])) for p in pieces]
    return [p for p, _ in pairs], [r for _, r in pairs]


def place(copies, pieces, spans, *targets):
    halves_of, at = ([], []), 0
    for piece, (lo, hi) in zip(pieces, spans):
        first, count = 0, hi - lo
        for target in targets:
            source = piece.at[pl.ds(lo, count), pl.ds(first, target.shape[1])]
            copy = copies.start(source, target.at[pl.ds(at, count), :])
            halves_of[2 * at // targets[0].shape[0]].append(copy)
            first += target.shape[1]
        at += count
    return halves_of


def own_gate(extra):
    me, peers = lax.axis_index("dp"), lax.axis_size("dp")
    lane = lax.broadcasted_iota(jnp.int32, extra.shape, 1)
    return jnp.sum(jnp.where((lane == me) | (lane == me + peers), wide(extra), 0.0), axis=1, keepdims=True)


def expert_stage_body(spans, *refs):
    pieces = len(spans)
    (w_gate, w_up, w_down), ins = refs[:3], refs[3 : pieces + 3]
    rows_out, extra_out, gate_out, up_out, *part_outs = refs[pieces + 3 : pieces + 9]
    rows, extra, gate_held, up_held, part, sems = refs[pieces + 9 :]
    copies, leaving = Copies(sems), []
    arriving = place(copies, ins, spans, rows, extra)
    half = rows.shape[0] // 2
    for i, part_out in enumerate(part_outs):
        here = pl.ds(i * half, half)
        for copy in arriving[i]:
            copy.wait()
        leaving.append(copies.start(rows.at[here, :], rows_out.at[here, :]))
        leaving.append(copies.start(extra.at[here, :], extra_out.at[here, :]))
        values = rows[here, :]
        gate = dot_nn(values, w_gate[...])
        up = dot_nn(values, w_up[...])
        gate_held[here, :] = gate.astype(bf16)
        up_held[here, :] = up.astype(bf16)
        leaving.append(copies.start(gate_held.at[here, :], gate_out.at[here, :]))
        leaving.append(copies.start(up_held.at[here, :], up_out.at[here, :]))
        act = (gate / (1.0 + jnp.exp(-gate)) * up).astype(bf16)
        part[here, :] = (own_gate(extra[here, :]) * dot_nn(act, w_down[...])).astype(bf16)
        leaving.append(copies.start(part.at[here, :], part_out))
    for copy in leaving:
        copy.wait()


def expert_stage(pieces, *weights):
    pieces, spans = ranges(pieces)
    count = sum(hi - lo for lo, hi in spans)
    model, units = weights[0].shape
    extra = pieces[0].shape[1] - model
    saved = [(count, model), (count, extra), (count, units), (count, units)]
    shapes = [like(t, bf16) for t in [*saved, (count // 2, model), (count // 2, model)]]
    scratch = [pltpu.VMEM(t, bf16) for t in [*saved, (count, model)]]
    scratch.append(pltpu.SemaphoreType.DMA((2 * len(pieces) + 10,)))
    body = functools.partial(expert_stage_body, spans)
    outs = on_device(
        body, shapes, [], 6 * count * weights[0].size, kept=weights, far=pieces, scratch=scratch, direct=True
    )
    return outs[4:], outs[:4]


def expert_back_body(spans, *refs):
    pieces = len(spans)
    (w_gate, w_up, w_down), ins, (extra_in, gate_in, up_in) = refs[:3], refs[3 : pieces + 3], refs[pieces + 3 : pieces + 6]
    outs = refs[pieces + 6 : pieces + 12]
    *held_back, part, extra, gate_held, up_held, sems = refs[pieces + 12 :]
    grad_rows, grad_gate, grad_up, act = held_back
    copies, leaving = Copies(sems), []
    half = grad_rows.shape[0] // 2
    arriving = [[], []]
    for i in range(2):
        here = pl.ds(i * half, half)
        for source, target in ((extra_in, extra), (gate_in, gate_held), (up_in, up_held)):
            arriving[i].append(copies.start(source.at[here, :], target.at[here, :]))
    for i, more in enumerate(place(copies, ins, spans, grad_rows)):
        arriving[i] += more
    for i, part_out in enumerate(outs[4:]):
        here = pl.ds(i * half, half)
        for copy in arriving[i]:
            copy.wait()
        scaled = (own_gate(extra[here, :]) * wide(grad_rows[here, :])).astype(bf16)
        grad_rows[here, :] = scaled
        grad_act = dot_nt(scaled, w_down[...])
        gate, up = wide(gate_held[here, :]), wide(up_held[here, :])
        sig = 1.0 / (1.0 + jnp.exp(-gate))
        silu = gate * sig
        low_gate = (grad_act * up * sig * (1.0 + gate * (1.0 - sig))).astype(bf16)
        low_up = (grad_act * silu).astype(bf16)
        grad_gate[here, :] = low_gate
        grad_up[here, :] = low_up
        act[here, :] = (silu * up).astype(bf16)
        for source, target in zip(held_back, outs):
            leaving.append(copies.start(source.at[here, :], target.at[here, :]))
        grad_in = dot_nt(low_gate, w_gate[...]) + dot_nt(low_up, w_up[...])
        part[here, :] = grad_in.astype(bf16)
        leaving.append(copies.start(part.at[here, :], part_out))
    for copy in leaving:
        copy.wait()


def expert_back_stage(pieces, saved, *weights):
    rows, extra, gate_out, up_out = saved
    pieces, spans = ranges(pieces)
    count = rows.shape[0]
    model, units = weights[0].shape
    back = [(count, model), (count, units), (count, units), (count, units)]
    shapes = [like(t, bf16) for t in [*back, (count // 2, model), (count // 2, model)]]
    scratch = [pltpu.VMEM(t, bf16) for t in [*back, (count, model), extra.shape, gate_out.shape, up_out.shape]]
    scratch.append(pltpu.SemaphoreType.DMA((len(pieces) + 16,)))
    body = functools.partial(expert_back_body, spans)
    far = [*pieces, *map(distant, (extra, gate_out, up_out))]
    outs = on_device(
        body, shapes, [], 6 * count * weights[0].size, kept=weights, far=far, scratch=scratch, direct=True
    )
    return outs[4:], outs[:4]


def product_sums_body(stages, products, *refs):
    ins, outs = refs[: -len(products)], refs[-len(products) :]
    fields = 1 + max(max(p) for p in products)
    totals = [ref[...] for ref in ins[fields * stages :]] or [0.0] * len(products)
    for i in range(stages):
        stage = [r[...] for r in ins[fields * i : fields * (i + 1)]]
        totals = [t + dot_tn(stage[a], stage[b]) for t, (a, b) in zip(totals, products)]
    for out, total in zip(outs, totals):
        out[...] = total


def product_sums(stages, products, swept, sums):
    width = stages[0][swept].shape[1]
    step = min(t.shape[1] for t in stages[0])
    rows = sum(stage[0].shape[0] for stage in stages)
    args, specs = [], []
    for stage in stages:
        args += map(distant, stage)
        for i, t in enumerate(stage):
            if i == swept:
                specs.append(pl.BlockSpec((t.shape[0], step), lambda j: (0, j)))
            else:
                specs.append(pl.BlockSpec(t.shape, lambda j: (0, 0)))
    shapes, outs = [], []
    for left, right in products:
        other = stages[0][right if left == swept else left].shape[1]
        if left == swept:
            shapes.append(like((width, other), f32))
            outs.append(pl.BlockSpec((step, other), lambda j: (j, 0)))
        else:
            shapes.append(like((other, width), f32))
            outs.append(pl.BlockSpec((other, step), lambda j: (0, j)))
    model_work = width * step // 32
    first = len(args)
    if sums is not None:
        args += map(distant, sums)
        specs += outs
    return pl.pallas_call(
        functools.partial(product_sums_body, len(stages), products),
        grid=(width // step,),
        out_shape=shapes,
        in_specs=specs,
        out_specs=outs,
        input_output_aliases={} if sums is None else {first + i: i for i in range(len(shapes))},
        compiler_params=pltpu.CompilerParams(vmem_limit_bytes=KERNEL_VMEM),
        cost_estimate=pl.CostEstimate(flops=rows * model_work, bytes_accessed=rows, transcendentals=0),
    )(*args)


def expert_forward(rows, w_gate, w_up, w_down):
    gate_out = dot_nn(rows, w_gate)
    up_out = dot_nn(rows, w_up)
    act = (gate_out / (1.0 + jnp.exp(-gate_out)) * up_out).astype(bf16)
    part = dot_nn(act, w_down).astype(bf16)
    return part, (rows, gate_out.astype(bf16), up_out.astype(bf16))


def expert_backward(grad_rows, saved, w_gate, w_up, w_down):
    rows, gate_low, up_low = saved
    gate_out, up_out = wide(gate_low), wide(up_low)
    grad_act = dot_nt(grad_rows, w_down)
    sig = 1.0 / (1.0 + jnp.exp(-gate_out))
    silu = gate_out * sig
    grad_gate = (grad_act * up_out * sig * (1.0 + gate_out * (1.0 - sig))).astype(bf16)
    grad_up = (grad_act * silu).astype(bf16)
    act = (silu * up_out).astype(bf16)
    grad_in = (dot_nt(grad_gate, w_gate) + dot_nt(grad_up, w_up)).astype(bf16)
    return grad_in, (dot_tn(rows, grad_gate), dot_tn(rows, grad_up), dot_tn(act, grad_rows))


def halves(array):
    half = array.shape[0] // 2
    return array[:half], array[half:]


def owned_body(turns, groups, blocks, with_last, gains, *refs):
    refs = list(refs)
    lefts = [refs.pop(0) for _ in range(turns)]
    rights = [[refs.pop(0) for _ in range(turns + with_last)] for _ in range(groups)]
    last = [refs.pop(0) for _ in range(4 * with_last)]
    gains = [refs.pop(0)[...] for _ in range(gains)]
    outs, products, sems = refs[: 2 * len(blocks)], refs[-2], refs[-1]
    values = [t[...] for t in lefts]
    if with_last:
        grad, grad_two, hidden, gain = last
        total = hidden[...]
        back, _ = norm_back(total, norm_factor(total), gain[...], grad_two[...])
        values.append((wide(grad[...]) + back).astype(bf16))
    left = jnp.concatenate(values, axis=0)
    for g in range(groups):
        right = jnp.concatenate([t[...] for t in rights[g]], axis=0)
        products[g, :, : right.shape[1]] = dot_tn(left, right).astype(bf16)
        if gains:
            terms, at = [], right.shape[1]
            for gain in gains:
                high = gain.astype(bf16)
                terms += [high, (gain - wide(high)).astype(bf16)]
            rows = jnp.concatenate(terms + [jnp.zeros_like(terms[0])] * (-len(terms) % 16), axis=0)
            which = lax.broadcasted_iota(jnp.int32, (rows.shape[0], 128), 0)
            column = lax.broadcasted_iota(jnp.int32, (rows.shape[0], 128), 1)
            chosen = (column == (which // 2) % 2) & (which < len(terms))
            products[g, :, at : at + 128] = dot_tn(rows, jnp.where(chosen, 1.0, 0.0).astype(bf16)).astype(bf16)
    copies, leaving = Copies(sems), []
    me = lax.axis_index("dp")
    share = products.shape[1] // lax.axis_size("dp")
    for i, group in enumerate(blocks):
        for out, places in zip(outs[2 * i : 2 * i + 2], group):
            for j, (mask, side) in enumerate(places):
                rows = pl.ds(pl.multiple_of((me ^ mask) * share, share), share)
                leaving.append(copies.start(products.at[side, rows, :], out.at[pl.ds(j * share, share), :]))
    for copy in leaving:
        copy.wait()


def owned_products(cube, lefts, rights, last=(), gains=()):
    model, width = lefts[0].shape[1], rights[0][0].shape[1] + (128 if gains else 0)
    share = model // lax.axis_size("dp")
    blocks = [
        [[(m ^ int(i), s) for m, s in side for i in cube.inner] for side in pair] for pair in cube.stages
    ]
    shapes = [like((len(places) * share, width), bf16) for pair in blocks for places in pair]
    scratch = [
        pltpu.VMEM((len(rights), model, width), bf16),
        pltpu.SemaphoreType.DMA((sum(len(places) for pair in blocks for places in pair),)),
    ]
    args = [*lefts, *[t for group in rights for t in group], *last, *gains]
    outs = pl.pallas_call(
        functools.partial(owned_body, len(lefts), len(rights), blocks, 1 if last else 0, len(gains)),
        out_shape=shapes,
        in_specs=[VMEM] * len(args),
        out_specs=[ANY] * len(shapes),
        scratch_shapes=scratch,
        compiler_params=pltpu.CompilerParams(vmem_limit_bytes=KERNEL_VMEM),
    )(*map(distant, args))
    return [(outs[2 * i], outs[2 * i + 1]) for i in range(len(blocks))]


class Blocks:
    def __init__(self, cube, weights):
        self.cube, self.weights = cube, weights

    def forward(self, payload, micro, side=()):
        saved = [None] * 4

        def work(stage, pieces):
            parts, kept = expert_stage(pieces, *self.weights)
            saved[stage] = kept
            return parts

        return gather_rows(self.cube, payload, work, side), saved

    def back_stage(self, stage, pieces, saved):
        parts, kept = expert_back_stage(pieces, saved[stage], *self.weights)
        return parts, [saved[stage][0], *kept]

    def backward(self, grad, micro, saved, side=()):
        keeps = [None] * 4

        def work(stage, pieces):
            parts, kept = self.back_stage(stage, pieces, saved)
            keeps[stage] = kept
            return parts

        return gather_rows(self.cube, grad, work, side), keeps

    def late_backward(self, pieces, saved):
        parts, keeps = [None] * 4, [None] * 4

        def run(*stages):
            def work(*gathered):
                for stage, rows in zip(stages, gathered):
                    parts[stage], keeps[stage] = self.back_stage(stage, rows, saved)
                return [parts[stage] for stage in stages]

            return lambda: [pieces[stage] for stage in stages], work

        return run, parts, keeps

    def total_start(self, results, side=()):
        return reduce_start(self.cube, results, side)

    def total_finish(self, state, side=()):
        return reduce_finish(self.cube, state, side)

    def total(self, results, side=()):
        return self.total_finish(self.total_start(results, side[:1]), side[1:])

    def weight_sums(self, keeps, sums):
        def hidden(*stages):
            sums[0] = product_sums(stages, ((0, 1), (0, 2)), 0, sums[0])
            return sums[0]

        def back(*stages):
            sums[1] = product_sums(stages, ((0, 1),), 1, sums[1])
            return sums[1]

        return [
            (lambda: [[rows, gate, up] for rows, _, gate, up, _ in keeps], hidden),
            (lambda: [[act, grad] for _, grad, _, _, act in keeps], back),
        ]


def run_all(side):
    for thunk in side:
        if thunk is not None:
            thunk[1](*thunk[0]())


class Buckets:
    def __init__(self, cube, weights, routes, gates, capacity):
        self.cube, self.weights, self.capacity = cube, weights, capacity
        micros, self.rows, self.top = routes.shape
        self.experts = lax.axis_size("dp")
        self.tables = []
        for m in range(micros):
            flat = routes[m].reshape(-1)
            onehot = (flat[:, None] == jnp.arange(self.experts, dtype=jnp.int32)).astype(jnp.int32)
            earlier = jnp.cumsum(onehot, axis=0) - onehot
            target = flat * capacity + jnp.sum(earlier * onehot, axis=1)
            source = jnp.full((self.experts * capacity,), flat.shape[0], jnp.int32)
            source = source.at[target].set(jnp.arange(flat.shape[0], dtype=jnp.int32))
            self.tables.append((target, source, gates[m]))

    def table(self, micro):
        return jax.tree.map(lambda a, b: jnp.where(micro == 0, a, b), self.tables[0], self.tables[1])

    def exchange(self, rows):
        shape = (self.experts, self.capacity, rows.shape[1])
        moved = lax.all_to_all(rows.reshape(shape), "dp", split_axis=0, concat_axis=0, tiled=True)
        return moved.reshape(rows.shape)

    def whole(self, own):
        return jnp.concatenate([own, swap(own, self.cube.z)], axis=0)

    def forward(self, payload, micro, side=()):
        target, source, gates = self.table(micro)
        own = payload[:, : self.weights[0].shape[0]]
        padded = jnp.pad(self.whole(own), ((0, 1), (0, 0)))
        arrived = self.exchange(jnp.take(padded, source // self.top, axis=0))
        part, saved = expert_forward(arrived, *self.weights)
        picked = jnp.take(self.exchange(part), target, axis=0).reshape(self.rows, self.top, -1)
        run_all(side)
        return jnp.sum(gates[:, :, None] * picked, axis=1), saved

    def backward(self, grad, micro, saved, side=()):
        target, source, gates = self.table(micro)
        scaled = (gates[:, :, None] * wide(self.whole(grad))[:, None, :]).astype(bf16)
        padded = jnp.pad(scaled.reshape(self.rows * self.top, -1), ((0, 1), (0, 0)))
        arrived = self.exchange(jnp.take(padded, source, axis=0))
        grad_in, weights = expert_backward(arrived, saved, *self.weights)
        picked = jnp.take(self.exchange(grad_in), target, axis=0).reshape(self.rows, self.top, -1)
        run_all(side)
        return jnp.sum(picked, axis=1, dtype=f32), weights

    def total_start(self, results, side=()):
        run_all(side)
        return results

    def total_finish(self, results, side=()):
        own, other = halves(results.astype(bf16))
        run_all(side)
        return wide(own) + wide(swap(other, self.cube.z))

    def total(self, results, side=()):
        return self.total_finish(results, side)

    def weight_sums(self, weights, sums):
        def add(*weights):
            for i, part in enumerate((list(weights[:2]), list(weights[2:]))):
                sums[i] = part if sums[i] is None else [a + b for a, b in zip(sums[i], part)]

        return [None, (lambda: weights, add)]


def local(
    tokens, lengths, routes, gates, attn_gain, q_weight, key_projection, value_projection,
    o_weight, mlp_gain, expert_gate, expert_up, expert_down, cotangent,
):
    cube = Cube()
    section = lax.axis_index("section")
    shard = lax.axis_index("shard")
    me = lax.axis_index("dp")
    peers, shards = lax.axis_size("dp"), lax.axis_size("shard")
    _, block_rows, model = tokens.shape
    rows = block_rows // shards
    share = model // peers
    first = section == 0
    gain_one, gain_two = attn_gain[0][None], mlp_gain[0][None]
    weights = [q_weight[0], key_projection[0], value_projection[0], o_weight[0]]
    expert_w = (expert_gate[0, 0], expert_up[0, 0], expert_down[0, 0])
    capacity = 2 * block_rows * routes.shape[3] // peers
    whole_blocks = capacity >= block_rows

    def chosen(here, there):
        return jax.tree.map(lambda a, b: jnp.where(first, a, b), here, there)

    def begins(lens):
        lens = lens[:, 0]
        ends, longest = jnp.cumsum(lens, axis=1), jnp.argmax(lens, axis=1)
        return [ends[m, longest[m]] - lens[m, longest[m]] for m in range(2)]

    def turned(array, begin):
        doubled = jnp.concatenate([array, array], axis=0)
        return lax.dynamic_slice_in_dim(doubled, (begin + rows * shard) % block_rows, block_rows, 0)

    if not whole_blocks:
        early = begins(lengths)
        mixture = Buckets(
            cube,
            expert_w,
            jnp.stack([turned(routes[0, m], early[m]) for m in range(2)]),
            jnp.stack([turned(gates[0, m], early[m]) for m in range(2)]),
            capacity,
        )

    slices = [lax.dynamic_slice_in_dim(w, me * share, share, 0) for w in weights]
    qkv_slices = swap(jnp.concatenate(slices[:3], axis=1), cube.z)
    out_slices = slices[3]
    half_share = share // 2
    mask = cube.x[1] | cube.y[1]
    far_places = [2 * (me ^ mask), 2 * (me ^ mask) + 1]
    plane_places = [2 * (me ^ m) for m in (0, cube.x[1], cube.y[1])]
    mate_bit = cube.core[1]

    def mate_places(places):
        return [p ^ (2 * mate_bit) for p in places]

    def placed(own, m):
        half = model // shards
        kept = lax.dynamic_slice_in_dim(own, shard * half, half, 1)
        given = lax.dynamic_slice_in_dim(own, (1 - shard) * half, half, 1)
        got = swap(given, cube.z)
        low = jnp.where(shard == 0, kept, got)
        high = jnp.where(shard == 0, got, kept)
        return lax.dynamic_slice_in_dim(
            jnp.concatenate([low, high, low, high], axis=0), (block_rows - starts[m]) % block_rows, block_rows, 0
        )

    route_cols = [routes[0, m].T for m in range(2)]
    gate_cols = [gates[0, m].T for m in range(2)]
    cot_own, cot_other = turned_block(lengths, cotangent)
    opened, mask0 = opening(lengths, tokens, gain_one, weights)
    settled = [tokens, cotangent, route_cols, gate_cols, expert_w]
    own_near = [swap(cot_own, d) for d in (cube.x, cube.y)] if whole_blocks else []
    opened, own_near, qkv_slices, cot_other, settled = together(
        (opened, own_near, qkv_slices, cot_other, settled)
    )
    inputs, part, qkv, heads, sent = opened
    *settled, expert_w = settled
    other_near = [swap(cot_other, d) for d in (cube.x, cube.y)] if whole_blocks else []
    arrived, other_near, settled, expert_w = together(
        (swap(sent, cube.z), other_near, settle(lengths, *settled), pinned(*expert_w))
    )
    fresh1, cot1, mask1, extra0, extra1, starts = settled
    hidden, payload = joined(part, arrived, gain_two, extra0)
    if whole_blocks:
        mixture = Blocks(cube, expert_w)
        plane = []

        def first_plane(qkv_slices, out_slices):
            near = [qkv_slices] + [swap(qkv_slices, d) for d in (cube.x, cube.y, ("dp", mask))]
            plane.extend([near, swap(out_slices, cube.z)])
            return plane

        side = [None, None, (lambda: [qkv_slices, out_slices], first_plane)]
        results, saved = mixture.forward(payload, 0, side)
        qkv_near, out_slices = plane
    else:
        results, saved = mixture.forward(payload, 0)
    first_mates = []

    def first_exchange(*near):
        first_mates.extend(swap(t, cube.core) for t in near)
        return first_mates

    total = mixture.total(results, [(lambda: qkv_near, first_exchange)] if whole_blocks else [])
    result0 = (hidden + total).astype(bf16)
    if whole_blocks:
        result0, qkv_near, out_slices = together((result0, qkv_near, out_slices))
        arriving = lax.ppermute(result0, "section", [(0, 1)])
        out_near = [out_slices] + [swap(out_slices, d) for d in (cube.x, cube.y, ("dp", mask))]
        arriving, out_near, weights = together((arriving, out_near, pinned(*weights)))
        qkv_mates, out_mates = first_mates, [swap(t, cube.core) for t in out_near]
        all_places = [*plane_places, far_places[0]]
        width = qkv_slices.shape[1]
        spans, pieces = [], []
        for group, places, column in (
            (qkv_near, all_places, 0), (qkv_mates, mate_places(all_places), 0),
            (out_near, all_places, width), (out_mates, mate_places(all_places), width),
        ):
            pieces += group
            spans += [(p, half_share, column) for p in places]
        packed = put_together(pieces, spans, (model, width + out_slices.shape[1]))
    else:
        arriving = lax.ppermute(result0, "section", [(0, 1)])
        packed = lax.all_gather(
            jnp.concatenate([qkv_slices, swap(out_slices, cube.z)], axis=1), "dp", axis=0, tiled=True
        )
    state0 = [inputs, hidden, mask0, None, saved]

    mask_mid, extra_mid = chosen((mask1, extra1), (mask0, extra0))

    inputs1, hidden1, payload, groups1 = attention_forward(
        fresh1, arriving, mask_mid, gain_one, gain_two, extra_mid, weights, packed
    )
    def first_groups(*args):
        groups = other_heads(*args)
        state0[3] = [(qkv, heads), tuple(groups)]
        return groups

    micro_mid = 1 - section
    late = []

    def cot_mates(*cots):
        late.append([swap(t, cube.core) for t in cots])
        return late[0]

    def cot_far(x0, y1):
        late.append([swap(x0, cube.y), swap(y1, cube.x)])
        return late[1]

    side = [(lambda: [inputs, mask0, gain_one, weights, packed], first_groups)]
    if whole_blocks:
        (x0, y0), (x1, y1) = own_near, other_near
        side += [(lambda: [cot_own, cot_other, x0, y0, x1, y1], cot_mates), (lambda: [x0, y1], cot_far)]
    results, saved1 = mixture.forward(payload, micro_mid, side)

    grad0 = cot_own
    if whole_blocks:
        (own_c, other_c, x0_c, y0_c, x1_c, y1_c), far = late
        far_c = [swap(t, cube.core) for t in far]
        pieces = [
            [cot_own, own_c],
            [x0, y0, cot_other, x0_c, y0_c, other_c],
            [far[0], y1, x1, far_c[0], y1_c, x1_c],
            [far[1], far_c[1]],
        ]
        run, back_results, keeps0 = mixture.late_backward(pieces, saved1)

        def exchange(*others):
            back_results[2] = (back_results[2][0], swap(others[0], cube.core))
            return back_results[2]

        total = mixture.total(results, [run(2), both((lambda: [back_results[2][1]], exchange), run(3, 1, 0))])
    else:
        back_results, keeps0 = mixture.backward(grad0, micro_mid, saved1)
        total = mixture.total(results)
    result1 = (hidden1 + total).astype(bf16)

    slot2 = []

    def last_attention(arriving):
        zero = jnp.zeros((rows, model), bf16)
        slot2.extend(
            attention_forward(zero, arriving, mask1, gain_one, gain_two, extra1, weights, packed)
        )
        return slot2

    arrived = []

    def second_handoff(result):
        arrived.append(lax.ppermute(result, "section", [(0, 1)]))
        return arrived

    result1, back_results = together((result1, back_results))
    if whole_blocks:
        back_results[0] = (back_results[0][0], swap(back_results[0][1], cube.core))
    state = mixture.total_start(back_results, [(lambda: [result1], second_handoff)])
    grad_two = mixture.total_finish(state, [(lambda: arrived, last_attention)])
    inputs2, hidden2, payload, groups2 = slot2

    def attention_turn(grad, grad_two, state):
        inputs, hidden, mask, groups, _ = state
        outs = attention_backward(
            grad, grad_two, inputs, hidden, mask, gain_one, gain_two, [g[0] for g in groups], weights, packed
        )
        grad_input, low, grad_low, normed, g0, g1, attn_g, mlp_g = outs
        factors = (normed, grad_low, (g0, g1), [g[1] for g in groups])
        return grad_input, low, factors, (attn_g, mlp_g)

    state1 = [inputs1, hidden1, mask_mid, groups1, saved1]
    turn0, returned = [], []

    def first_turn(grad_two):
        turn0.extend(attention_turn(grad0, grad_two, state1))
        return turn0

    def first_return(low):
        returned.append(lax.ppermute(low, "section", [(1, 0)]))
        return returned

    side = [(lambda: [grad_two], first_turn), None, (lambda: [turn0[1]], first_return)]
    results2, saved2 = mixture.forward(payload, 1, side)
    coming = returned[0]
    state2 = [inputs2, hidden2, mask1, groups2, saved2]

    sums = [None, None]
    coming, results2, saved2 = together((coming, results2, saved2))
    state2[4] = saved2
    grad1 = coming + cot1
    state_mid = chosen(state0, state2)
    back_results, keeps1 = mixture.backward(grad1, section, state_mid[4])
    placings = {}

    def placing(name, micro, own):
        def work(rows):
            placings[name, micro] = placed(rows, micro)
            return placings[name, micro]

        return lambda: [own()], work

    work0 = mixture.weight_sums(keeps0, sums)
    work0[0] = both(*[w for w in work0[:1] if w], placing("out", 0, lambda: chosen(result0, result1)))
    grad_two = mixture.total(back_results, work0)
    turn1 = attention_turn(grad1, grad_two, state_mid)
    low, results2 = together((turn1[1], results2))
    coming = lax.ppermute(low, "section", [(1, 0)])
    state = mixture.total_start(results2)
    grad2, state = together((coming, state))

    last_total = []

    def finish_last(*state):
        last_total.append(mixture.total_finish(state[0] if len(state) == 1 else state))
        return last_total

    side = [None, None, (lambda: [state] if not whole_blocks else list(state), finish_last)]
    side.append(placing("grad", 0, lambda: chosen(turn1[0], turn0[0])))
    back_results, keeps2 = mixture.backward(grad2, 1 - section, saved1, side)
    result2 = (hidden2 + last_total[0]).astype(bf16)
    work1 = mixture.weight_sums(keeps1, sums)
    work1[0] = both(*[w for w in work1[:1] if w], placing("out", 1, lambda: chosen(result1, result2)))
    grad_two = mixture.total(back_results, work1)

    inputs, hidden, _, groups, _ = state1
    heads_all = [[t[2][3][g] for t in (turn0, turn1)] + [groups[g][1]] for g in range(shards)]
    out_pairs = owned_products(cube, [turn0[2][1], turn1[2][1]], heads_all, (grad2, grad_two, hidden, gain_two))
    turn2 = []

    def last_turn(grad_two):
        turn2.extend(attention_turn(grad2, grad_two, state1))
        return turn2

    def exchanged(pairs):
        return [(mine, swap(other, cube.core)) if i in (0, 2) else (mine, other) for i, (mine, other) in enumerate(pairs)]

    out_state = reduce_start(cube, exchanged(out_pairs), [(lambda: [grad_two], last_turn)])
    turns = (turn0, turn1, turn2)
    factors = [t[2] for t in turns]
    qkv_pairs = []

    def qkv_products(*_):
        rights = [[f[2][g] for f in factors] for g in range(shards)]
        gains = [g for t in turns for g in t[3]]
        qkv_pairs.extend(owned_products(cube, [f[0] for f in factors], rights, gains=gains))
        return qkv_pairs

    grad_o = reduce_finish(cube, out_state, [(lambda: [], qkv_products)])
    hidden_work, down_work = mixture.weight_sums(keeps2, sums)
    qkv_pairs, grad_o = together((qkv_pairs, grad_o))
    hidden_work = both(*[w for w in [hidden_work] if w], placing("grad", 1, lambda: chosen(turn2[0], turn1[0])))
    qkv_state = reduce_start(cube, exchanged(qkv_pairs), [hidden_work])
    grad_qkv = reduce_finish(cube, qkv_state, [down_work])
    width = q_weight.shape[2]
    grad_q = grad_qkv[:, :width]
    grad_k = grad_qkv[:, width : width + HEAD_SIZE]
    grad_v = grad_qkv[:, width + HEAD_SIZE : width + 2 * HEAD_SIZE]
    gain_pair = [grad_qkv[:, width + 2 * HEAD_SIZE + i] for i in range(2)]
    section_out = jnp.stack([placings["out", 0], placings["out", 1]])
    input_grad = jnp.stack([placings["grad", 0], placings["grad", 1]])
    (gate_total, up_total), (down_total,) = sums
    return (
        section_out[None],
        input_grad[None],
        gain_pair[0][None],
        grad_q[None],
        grad_k[None],
        grad_v[None],
        grad_o[None],
        gain_pair[1][None],
        gate_total[None, None],
        up_total[None, None],
        down_total[None, None],
    )


def solution(mesh):
    in_specs = (
        P(None, "dp", None),
        P(None, "dp", None),
        P("section", None, "dp", None),
        P("section", None, "dp", None),
        P("section", None),
        P("section", None, "shard"),
        P("section", None, "shard"),
        P("section", None, "shard"),
        P("section", None, "shard"),
        P("section", None),
        P("section", "dp", None, "shard"),
        P("section", "dp", None, "shard"),
        P("section", "dp", "shard", None),
        P(None, "dp", None),
    )
    out_specs = (
        P("section", None, "dp", "shard"),
        P("section", None, "dp", "shard"),
        P("section", "dp"),
        P("section", "dp", "shard"),
        P("section", "dp", "shard"),
        P("section", "dp", "shard"),
        P("section", "dp", "shard"),
        P("section", "dp"),
        P("section", "dp", None, "shard"),
        P("section", "dp", None, "shard"),
        P("section", "dp", "shard", None),
    )
    return jax.shard_map(local, mesh=mesh, in_specs=in_specs, out_specs=out_specs, check_vma=False)
```

time: 848 us -> 749 us (0.88)
  waiting for transfers between devices: 181 us -> 235 us
  other arithmetic: 90.2 us -> 54.2 us
  starting transfers between devices: 188 us -> 152 us
  Pallas kernels: 295 us -> 260 us
  between operations: 22.8 us -> 4.67 us
  local copies, waits for them, and re-layouts: 47.9 us -> 32.2 us
    pallas_call x33 -> x34, Pallas kernels: 237 us -> 179 us  [on_device(): pl.pallas_call(body, out_shape=outs, in_specs=[SMEM] * len(scalars) + [VM...]
    ppermute x3 -> x11, waiting for transfers between devices: 28.9 us -> 84.3 us  [the longest x8 52.4 us: across(): return lax.ppermute(value, ('dp', 'shard'), pairs)]
    ppermute x223 -> x190, starting transfers between devices: 175 us -> 125 us  [swap(): lax.ppermute(value, axis, [(i, i ^ bit) for i in range(lax.axis_size(axis...]
    pallas_call x0 -> x5, Pallas kernels: none -> 21.2 us  [the longest x2 15.7 us: owned_products(): pl.pallas_call(functools.partial(owned_body, len(lefts), len(rights), blo...]
    convert_element_type x24, other arithmetic: 34.6 us -> 16.6 us  [low_sum(): return sum((wide(t) for t in terms)).astype(bf16)]
    slice x31 -> x2, local copies, waits for them, and re-layouts: 17 us -> 1.38 us  [the longest x1 0.78 us: local(): gain_pair = [grad_qkv[:, width + 2 * HEAD_SIZE + i] for i in range(2)]]
    ppermute x3 -> x11, starting transfers between devices: 8.07 us -> 21.6 us  [the longest x8 13.8 us: across(): return lax.ppermute(value, ('dp', 'shard'), pairs)]
    select_n x26 -> x28, other arithmetic: 29.8 us -> 23.5 us  [chosen(): return jax.tree.map(lambda a, b: jnp.where(first, a, b), here, there)]
  transfers between devices with their start and end apart: 228 -> 202, of which waited for: 81 -> 78; matrix products, arithmetic and copies ran while one was open for 11% -> 6% of each run, Pallas kernels for 29% -> 31%
where the time goes in v1:
time: 749 us; the launch traced here: 738 us
  Pallas kernels  260 us (35%)
  waiting for transfers between devices  235 us (31%)
  starting transfers between devices  152 us (20%)
  other arithmetic  54.2 us (7%)
  local copies, waits for them, and re-layouts  32.2 us (4%)
    pallas_call x34, Pallas kernels, on_device(): pl.pallas_call(body, out_shape=outs, in_specs=[SMEM] * len(scalars) + [VM...  179 us
    ppermute x190, waiting for transfers between devices, swap(): lax.ppermute(value, axis, [(i, i ^ bit) for i in range(lax.axis_size(axis...  151 us
    ppermute x190, starting transfers between devices, swap(): lax.ppermute(value, axis, [(i, i ^ bit) for i in range(lax.axis_size(axis...  125 us
    pallas_call x6, Pallas kernels, product_sums(): pl.pallas_call(functools.partial(product_sums_body, len(stages), products...  59.2 us
    ppermute x8, waiting for transfers between devices, across(): return lax.ppermute(value, ('dp', 'shard'), pairs)  52.4 us
    unnamed x356, local copies, waits for them, and re-layouts  24.3 us
    select_n x28, other arithmetic, chosen(): return jax.tree.map(lambda a, b: jnp.where(first, a, b), here, there)  23.5 us
    convert_element_type x24, other arithmetic, low_sum(): return sum((wide(t) for t in terms)).astype(bf16)  16.6 us
  transfers between devices with their start and end apart: 202, of which 78 were waited for; matrix products, arithmetic and copies ran while one was open for 6% of the time, Pallas kernels for 31%

profile of v1, /device:TPU:0, one launch (start us, length us, event | category | flops | bytes accessed | tf_op | source)
XLA Modules:
  0.0 737.8 jit_solution(5342486454496136881)
XLA Ops:
  12.3 8.8 %shard_map.221 = (bf16[128,1536]{1,0:T(8,128)(2,1)}, f32[128,1536]{1,0:T(8,128)}, bf16[128,1024]{1,0:T(8,128)(2,1)}, bf16[128,768]{1,0:T(8,128)(2,1)}, bf16[128,...) custom-call(s32[2,1,4]{2,1,0:T(1,128)S(1)} %copy-done.45, ...), custom_call_target="tpu_custom_call" | custom-call | flops 22020096 | bytes 96 | tf_op jit(solution)/shard_map/pallas_call | solution.py:279
  75.5 7.6 %collective-permute-done.24.refs_8_ = bf16[192,768]{1,0:T(8,128)(2,1)} collective-permute-done((bf16[192,768]{1,0:T(8,128)(2,1)S(1)}, bf16[192,768]{1,0:T(8,128)(2,1)}, u32[]{:S(2)}, u32[]{:S(2)}) %collective-permute-start.24) | collective-permute-done | bytes 294944 | tf_op jit(solution)/shard_map/ppermute | solution.py:56
  96.4 8.8 %collective-permute-done.27 = bf16[128,1536]{1,0:T(8,128)(2,1)S(1)} collective-permute-done((bf16[128,1536]{1,0:T(8,128)(2,1)S(1)}, bf16[128,1536]{1,0:T(8,128)(2,1)S(1)}, u32[]{:S(2)}, u32[]{:S(2)}) %collective-permute-start.27) | collective-permute-done | bytes 393248 | tf_op jit(solution)/shard_map/ppermute | solution.py:56
  115.2 8.3 %collective-permute-done.39 = bf16[128,1536]{1,0:T(8,128)(2,1)S(1)} collective-permute-done((bf16[128,1536]{1,0:T(8,128)(2,1)S(1)}, bf16[128,1536]{1,0:T(8,128)(2,1)S(1)}, u32[]{:S(2)}, u32[]{:S(2)}) %collective-permute-start.39) | collective-permute-done | bytes 393248 | tf_op jit(solution)/shard_map/ppermute | solution.py:67
  270.0 8.0 %collective-permute-done.85 = bf16[128,1536]{1,0:T(8,128)(2,1)S(1)} collective-permute-done((bf16[128,1536]{1,0:T(8,128)(2,1)S(1)}, bf16[128,1536]{1,0:T(8,128)(2,1)S(1)}, u32[]{:S(2)}, u32[]{:S(2)}) %collective-permute-start.85) | collective-permute-done | bytes 393248 | tf_op jit(solution)/shard_map/ppermute | solution.py:56
  283.4 8.0 %collective-permute-done.91.arriving = bf16[128,1536]{1,0:T(8,128)(2,1)S(1)} collective-permute-done((bf16[128,1536]{1,0:T(8,128)(2,1)S(1)}, bf16[128,1536]{1,0:T(8,128)(2,1)S(1)}, u32[]{:S(2)}, u32[]{:S(2)}) %collective-permute-start.91) | collective-permute-done | bytes 393248 | tf_op jit(solution)/shard_map/ppermute | solution.py:1117
  294.1 9.8 %collective-permute-start.94 = (bf16[128,1536]{1,0:T(8,128)(2,1)S(1)}, bf16[128,1536]{1,0:T(8,128)(2,1)S(1)}, u32[]{:S(2)}, u32[]{:S(2)}) collective-permute-start(bf16[128,1536]{1,0:T(8,128)(2,1)S(1)} %get-tuple-element.1021), channel_id=1, source_target_pairs={{0,1},{1,0},{2,3},{3,2},{4,5},{5,4},{6,7},{7,6},{8,9},{9,8},{10,11... | collective-permute-start | bytes 1179656 | tf_op jit(solution)/shard_map/ppermute | solution.py:56
  314.0 8.1 %collective-permute-done.95 = bf16[128,1536]{1,0:T(8,128)(2,1)S(1)} collective-permute-done((bf16[128,1536]{1,0:T(8,128)(2,1)S(1)}, bf16[128,1536]{1,0:T(8,128)(2,1)S(1)}, u32[]{:S(2)}, u32[]{:S(2)}) %collective-permute-start.95) | collective-permute-done | bytes 393248 | tf_op jit(solution)/shard_map/ppermute | solution.py:67
  327.0 7.5 %shard_map.244 = (f32[128,1536]{1,0:T(8,128)}, bf16[128,1536]{1,0:T(8,128)(2,1)}, bf16[128,1536]{1,0:T(8,128)(2,1)}, bf16[128,1536]{1,0:T(8,128)(2,1)}, bf16[128...) custom-call(bf16[128,1536]{1,0:T(8,128)(2,1)} %get-tuple-element.980.refs_3_.grad, ...), custom_call_target="tpu_custom_call" | custom-call | flops 44040192 | bytes 46272 | tf_op jit(solution)/shard_map/pallas_call | solution.py:279
  360.6 15.5 %collective-permute-done.107 = bf16[128,1536]{1,0:T(8,128)(2,1)S(1)} collective-permute-done((bf16[128,1536]{1,0:T(8,128)(2,1)S(1)}, bf16[128,1536]{1,0:T(8,128)(2,1)S(1)}, u32[]{:S(2)}, u32[]{:S(2)}) %collective-permute-start.107) | collective-permute-done | bytes 393248 | tf_op jit(solution)/shard_map/ppermute | solution.py:1144
  444.9 11.0 %shard_map.252 = (f32[1536,384]{1,0:T(8,128)}, f32[1536,384]{1,0:T(8,128)}) custom-call(bf16[256,1536]{1,0:T(8,128)(2,1)} %get-tuple-element.1455.refs_0_, bf16[256,384]{1,0:T(8,128)(2,1)} %get-tuple-element.1170.refs_1_, bf16[256,384]{1,0:T(8,128)(2,1)} %get-tuple-element.1171.refs_2_, bf16[768,1536]{1,0:T(8,128)(2,1)} %get-tuple-element.1458.refs_3_, ...), custom_call_target="tpu_custom_call" | custom-call | flops 37748736 | bytes 2048 | tf_op jit(solution)/shard_map/pallas_call | solution.py:693
  464.2 8.2 %shard_map.253.refs_8_ = f32[384,1536]{1,0:T(8,128)} custom-call(bf16[256,384]{1,0:T(8,128)(2,1)} %get-tuple-element.1204.refs_0_, bf16[256,1536]{1,0:T(8,128)(2,1)} %get-tuple-element.1205.refs_1_, bf16[768,384]{1,0:T(8,128)(2,1)} %get-tuple-element.1206.refs_2_, bf16[768,1536]{1,0:T(8,128)(2,1)} %get-tuple-element.1207.refs_3_, ...), custom_call_target="tpu_custom_call" | custom-call | flops 37748736 | bytes 2048 | tf_op jit(solution)/shard_map/pallas_call | solution.py:693
  472.5 8.2 %collective-permute-done.140 = bf16[128,1536]{1,0:T(8,128)(2,1)S(1)} collective-permute-done((bf16[128,1536]{1,0:T(8,128)(2,1)S(1)}, bf16[128,1536]{1,0:T(8,128)(2,1)S(1)}, u32[]{:S(2)}, u32[]{:S(2)}) %collective-permute-start.140) | collective-permute-done | bytes 393248 | tf_op jit(solution)/shard_map/ppermute | solution.py:67
  482.0 7.6 %shard_map.254 = (f32[128,1536]{1,0:T(8,128)}, bf16[128,1536]{1,0:T(8,128)(2,1)}, bf16[128,1536]{1,0:T(8,128)(2,1)}, bf16[128,1536]{1,0:T(8,128)(2,1)}, bf16[128...) custom-call(bf16[128,1536]{1,0:T(8,128)(2,1)} %copy-done.20, ...), custom_call_target="tpu_custom_call" | custom-call | flops 44040192 | bytes 46272 | tf_op jit(solution)/shard_map/pallas_call | solution.py:279
  495.4 7.6 %collective-permute-done.144 = bf16[128,1536]{1,0:T(8,128)(2,1)S(1)} collective-permute-done((bf16[128,1536]{1,0:T(8,128)(2,1)S(1)}, bf16[128,1536]{1,0:T(8,128)(2,1)S(1)}, u32[]{:S(2)}, u32[]{:S(2)}) %collective-permute-start.144) | collective-permute-done | bytes 393248 | tf_op jit(solution)/shard_map/ppermute | solution.py:56
  507.2 8.4 %collective-permute-done.141.refs_3_.refs_8_.grad = bf16[128,1536]{1,0:T(8,128)(2,1)S(1)} collective-permute-done((bf16[128,1536]{1,0:T(8,128)(2,1)S(1)}, bf16[128,1536]{1,0:T(8,128)(2,1)S(1)}, u32[]{:S(2)}, u32[]{:S(2)}) %collective-permute-start.141) | collective-permute-done | bytes 393248 | tf_op jit(solution)/shard_map/ppermute | solution.py:1172
  598.4 11.5 %shard_map.259 = (f32[1536,384]{1,0:T(8,128)}, f32[1536,384]{1,0:T(8,128)}) custom-call(bf16[256,1536]{1,0:T(8,128)(2,1)} %broadcast_select_fusion.3.refs_0_, bf16[256,384]{1,0:T(8,128)(2,1)} %get-tuple-element.1330.refs_1_, bf16[256,384]{1,0:T(8,128)(2,1)} %get-tuple-element.1331.refs_2_, ...), custom_call_target="tpu_custom_call", output_to_operand_aliasing={{0}: (12, {}), {1}: (13, {})} | custom-call | flops 37748736 | bytes 2048 | tf_op jit(solution)/shard_map/pallas_call | solution.py:693
  620.5 8.9 %shard_map.260.refs_8_ = f32[384,1536]{1,0:T(8,128)} custom-call(bf16[256,384]{1,0:T(8,128)(2,1)} %get-tuple-element.1364.refs_0_, bf16[256,1536]{1,0:T(8,128)(2,1)} %get-tuple-element.1365.refs_1_, bf16[768,384]{1,0:T(8,128)(2,1)} %get-tuple-element.1366.refs_2_, bf16[768,1536]{1,0:T(8,128)(2,1)} %get-tuple-element.1367.refs_3_, ...), custom_call_target="tpu_custom_call", output_to_operand_aliasing={{}: (8, {})} | custom-call | flops 37748736 | bytes 2048 | tf_op jit(solution)/shard_map/pallas_call | solution.py:693
  652.4 7.5 %shard_map.262 = (f32[128,1536]{1,0:T(8,128)}, bf16[128,1536]{1,0:T(8,128)(2,1)}, bf16[128,1536]{1,0:T(8,128)(2,1)}, bf16[128,1536]{1,0:T(8,128)(2,1)}, bf16[128...) custom-call(bf16[128,1536]{1,0:T(8,128)(2,1)} %copy-done.19, ...), custom_call_target="tpu_custom_call" | custom-call | flops 44040192 | bytes 46272 | tf_op jit(solution)/shard_map/pallas_call | solution.py:279
  666.5 8.4 %shard_map.263 = (bf16[192,1152]{1,0:T(8,128)(2,1)}, bf16[192,1152]{1,0:T(8,128)(2,1)}, bf16[576,1152]{1,0:T(8,128)(2,1)}, bf16[576,1152]{1,0:T(8,128)(2,1)}, bf...) custom-call(bf16[128,1536]{1,0:T(8,128)(2,1)} %get-tuple-element.104, ...), custom_call_target="tpu_custom_call" | custom-call | tf_op jit(solution)/shard_map/pallas_call | solution.py:782
  689.1 7.8 %collective-permute-done.191 = f32[128,768]{1,0:T(8,128)S(1)} collective-permute-done((f32[128,768]{1,0:T(8,128)S(1)}, f32[128,768]{1,0:T(8,128)S(1)}, u32[]{:S(2)}, u32[]{:S(2)}) %collective-permute-start.191) | collective-permute-done | bytes 393248 | tf_op jit(solution)/shard_map/ppermute | solution.py:56
  697.0 11.4 %shard_map.264 = (f32[1536,384]{1,0:T(8,128)}, f32[1536,384]{1,0:T(8,128)}) custom-call(bf16[256,1536]{1,0:T(8,128)(2,1)} %get-tuple-element.1455.refs_0_, bf16[256,384]{1,0:T(8,128)(2,1)} %get-tuple-element.1456.refs_1_, bf16[256,384]{1,0:T(8,128)(2,1)} %get-tuple-element.1457.refs_2_, ...), custom_call_target="tpu_custom_call", output_to_operand_aliasing={{0}: (12, {}), {1}: (13, {})} | custom-call | flops 37748736 | bytes 2048 | tf_op jit(solution)/shard_map/pallas_call | solution.py:693
  717.6 8.2 %shard_map.265 = f32[384,1536]{1,0:T(8,128)} custom-call(bf16[256,384]{1,0:T(8,128)(2,1)} %get-tuple-element.1490.refs_0_, bf16[256,1536]{1,0:T(8,128)(2,1)} %get-tuple-element.1491.refs_1_, bf16[768,384]{1,0:T(8,128)(2,1)} %get-tuple-element.1492.refs_2_, bf16[768,1536]{1,0:T(8,128)(2,1)} %get-tuple-element.1493.refs_3_, ...), custom_call_target="tpu_custom_call", output_to_operand_aliasing={{}: (8, {})} | custom-call | flops 37748736 | bytes 2048 | tf_op jit(solution)/shard_map/pallas_call | solution.py:693
  725.8 9.1 %collective-permute-done.201 = bf16[192,1152]{1,0:T(8,128)(2,1)S(1)} collective-permute-done((bf16[192,1152]{1,0:T(8,128)(2,1)S(1)}, bf16[192,1152]{1,0:T(8,128)(2,1)S(1)}, u32[]{:S(2)}, u32[]{:S(2)}) %collective-permute-start.201) | collective-permute-done | bytes 442400 | tf_op jit(solution)/shard_map/ppermute | solution.py:67
  (869 shorter events, 518.8 us)
Async XLA Ops:
  64.4 21.8 %collective-permute-start.17 = (bf16[128,1664]{1,0:T(8,128)(2,1)S(1)}, bf16[128,1664]{1,0:T(8,128)(2,1)S(1)}, u32[]{:S(2)}, u32[]{:S(2)}) collective-permute-start(bf16[128,1664]{1,0:T(8,128)(2,1)S(1)} %collective-permute-done.10.refs_3_), channel_id=1, source_target_pairs={{0,1},{1,0},{2,3},{3,2},{4,5},{5,4},{6,7},{7,6},{8,9},{9,8},{10,11... | collective-permute-start | bytes 1277960 | tf_op jit(solution)/shard_map/ppermute | solution.py:56
  132.2 21.4 %collective-permute-start.40 = (bf16[128,1536]{1,0:T(8,128)(2,1)}, bf16[128,1536]{1,0:T(8,128)(2,1)}, u32[]{:S(2)}, u32[]{:S(2)}) collective-permute-start(bf16[128,1536]{1,0:T(8,128)(2,1)} %add_convert_fusion.44), channel_id=1, source_target_pairs={{0,16},{1,17},{2,18},{3,19},{4,20},{5,21},{6,22},{7,23},{8,24},{9,... | collective-permute-start | bytes 1179656 | tf_op jit(solution)/shard_map/ppermute | solution.py:1035
  241.2 22.4 %collective-permute-start.84 = (bf16[384,1536]{1,0:T(8,128)(2,1)}, bf16[384,1536]{1,0:T(8,128)(2,1)S(1)}, u32[]{:S(2)}, u32[]{:S(2)}) collective-permute-start(bf16[384,1536]{1,0:T(8,128)(2,1)} %get-tuple-element.961), channel_id=1, source_target_pairs={{0,2},{2,0},{4,6},{6,4},{8,10},{10,8},{12,14},{14,12},{1,3},{3,1},... | collective-permute-start | bytes 3538952 | tf_op jit(solution)/shard_map/ppermute | solution.py:56
  241.3 21.8 %collective-permute-start.80 = (bf16[128,1536]{1,0:T(8,128)(2,1)}, bf16[128,1536]{1,0:T(8,128)(2,1)S(1)}, u32[]{:S(2)}, u32[]{:S(2)}) collective-permute-start(bf16[128,1536]{1,0:T(8,128)(2,1)} %get-tuple-element.955), channel_id=1, source_target_pairs={{0,4},{2,6},{4,0},{6,2},{8,12},{10,14},{12,8},{14,10},{1,5},{3,7},... | collective-permute-start | bytes 1179656 | tf_op jit(solution)/shard_map/ppermute | solution.py:56
  242.3 20.8 %collective-permute-start.81 = (bf16[128,1536]{1,0:T(8,128)(2,1)S(1)}, bf16[128,1536]{1,0:T(8,128)(2,1)S(1)}, u32[]{:S(2)}, u32[]{:S(2)}) collective-permute-start(bf16[128,1536]{1,0:T(8,128)(2,1)S(1)} %get-tuple-element.956), channel_id=1, source_target_pairs={{0,8},{2,10},{4,12},{6,14},{8,0},{10,2},{12,4},{14,6},{1,9},{3,11}... | collective-permute-start | bytes 1179656 | tf_op jit(solution)/shard_map/ppermute | solution.py:56
  243.3 19.8 %collective-permute-start.82 = (bf16[128,1536]{1,0:T(8,128)(2,1)S(1)}, bf16[128,1536]{1,0:T(8,128)(2,1)S(1)}, u32[]{:S(2)}, u32[]{:S(2)}) collective-permute-start(bf16[128,1536]{1,0:T(8,128)(2,1)S(1)} %get-tuple-element.957), channel_id=1, source_target_pairs={{0,1},{1,0},{2,3},{3,2},{4,5},{5,4},{6,7},{7,6},{8,9},{9,8},{10,11... | collective-permute-start | bytes 1179656 | tf_op jit(solution)/shard_map/ppermute | solution.py:56
  266.5 24.9 %collective-permute-start.89 = (bf16[384,1536]{1,0:T(8,128)(2,1)S(1)}, bf16[384,1536]{1,0:T(8,128)(2,1)S(1)}, u32[]{:S(2)}, u32[]{:S(2)}) collective-permute-start(bf16[384,1536]{1,0:T(8,128)(2,1)S(1)} %copy-done.161), channel_id=1, source_target_pairs={{0,2},{2,0},{4,6},{6,4},{8,10},{10,8},{12,14},{14,12},{1,3},{3,1},... | collective-permute-start | bytes 3538952 | tf_op jit(solution)/shard_map/ppermute | solution.py:56
  292.2 19.8 %collective-permute-start.92 = (bf16[128,1536]{1,0:T(8,128)(2,1)S(1)}, bf16[128,1536]{1,0:T(8,128)(2,1)S(1)}, u32[]{:S(2)}, u32[]{:S(2)}) collective-permute-start(bf16[128,1536]{1,0:T(8,128)(2,1)S(1)} %get-tuple-element.1019), channel_id=1, source_target_pairs={{0,4},{2,6},{4,0},{6,2},{8,12},{10,14},{12,8},{14,10},{1,5},{3,7},... | collective-permute-start | bytes 1179656 | tf_op jit(solution)/shard_map/ppermute | solution.py:56
  294.1 19.8 %collective-permute-start.94 = (bf16[128,1536]{1,0:T(8,128)(2,1)S(1)}, bf16[128,1536]{1,0:T(8,128)(2,1)S(1)}, u32[]{:S(2)}, u32[]{:S(2)}) collective-permute-start(bf16[128,1536]{1,0:T(8,128)(2,1)S(1)} %get-tuple-element.1021), channel_id=1, source_target_pairs={{0,1},{1,0},{2,3},{3,2},{4,5},{5,4},{6,7},{7,6},{8,9},{9,8},{10,11... | collective-permute-start | bytes 1179656 | tf_op jit(solution)/shard_map/ppermute | solution.py:56
  351.7 24.4 %collective-permute-start.108 = (bf16[128,1664]{1,0:T(8,128)(2,1)S(1)}, bf16[128,1664]{1,0:T(8,128)(2,1)}, u32[]{:S(2)}, u32[]{:S(2)}) collective-permute-start(bf16[128,1664]{1,0:T(8,128)(2,1)S(1)} %collective-permute-done.100.refs_3_), channel_id=1, source_target_pairs={{0,1},{1,0},{2,3},{3,2},{4,5},{5,4},{6,7},{7,6},{8,9},{9,8},{10,11... | collective-permute-start | bytes 1277960 | tf_op jit(solution)/shard_map/ppermute | solution.py:56
  353.4 22.6 %collective-permute-start.107 = (bf16[128,1536]{1,0:T(8,128)(2,1)S(1)}, bf16[128,1536]{1,0:T(8,128)(2,1)S(1)}, u32[]{:S(2)}, u32[]{:S(2)}) collective-permute-start(bf16[128,1536]{1,0:T(8,128)(2,1)S(1)} %copy-done.166), channel_id=1, source_target_pairs={{16,0},{17,1},{18,2},{19,3},{20,4},{21,5},{22,6},{23,7},{24,8},{25... | collective-permute-start | bytes 1179656 | tf_op jit(solution)/shard_map/ppermute | solution.py:1144
  434.8 23.0 %collective-permute-start.135 = (bf16[384,1536]{1,0:T(8,128)(2,1)S(1)}, bf16[384,1536]{1,0:T(8,128)(2,1)S(1)}, u32[]{:S(2)}, u32[]{:S(2)}) collective-permute-start(bf16[384,1536]{1,0:T(8,128)(2,1)S(1)} %copy-done.159), channel_id=1, source_target_pairs={{0,2},{2,0},{4,6},{6,4},{8,10},{10,8},{12,14},{14,12},{1,3},{3,1},... | collective-permute-start | bytes 3538952 | tf_op jit(solution)/shard_map/ppermute | solution.py:56
  437.4 20.4 %collective-permute-start.132 = (bf16[128,1536]{1,0:T(8,128)(2,1)S(1)}, bf16[128,1536]{1,0:T(8,128)(2,1)S(1)}, u32[]{:S(2)}, u32[]{:S(2)}) collective-permute-start(bf16[128,1536]{1,0:T(8,128)(2,1)S(1)} %get-tuple-element.1160), channel_id=1, source_target_pairs={{0,8},{2,10},{4,12},{6,14},{8,0},{10,2},{12,4},{14,6},{1,9},{3,11}... | collective-permute-start | bytes 1179656 | tf_op jit(solution)/shard_map/ppermute | solution.py:56
  460.7 20.1 %collective-permute-start.140 = (bf16[128,1536]{1,0:T(8,128)(2,1)S(1)}, bf16[128,1536]{1,0:T(8,128)(2,1)S(1)}, u32[]{:S(2)}, u32[]{:S(2)}) collective-permute-start(bf16[128,1536]{1,0:T(8,128)(2,1)S(1)} %add_convert_fusion.25), channel_id=1, source_target_pairs={{0,13},{1,12},{2,15},{3,14},{4,9},{5,8},{6,11},{7,10},{8,5},{9,4},... | collective-permute-start | bytes 1179656 | tf_op jit(solution)/shard_map/ppermute | solution.py:67
  494.1 21.5 %collective-permute-start.141 = (bf16[128,1536]{1,0:T(8,128)(2,1)S(1)}, bf16[128,1536]{1,0:T(8,128)(2,1)S(1)}, u32[]{:S(2)}, u32[]{:S(2)}) collective-permute-start(bf16[128,1536]{1,0:T(8,128)(2,1)S(1)} %copy-done.171), channel_id=1, source_target_pairs={{16,0},{17,1},{18,2},{19,3},{20,4},{21,5},{22,6},{23,7},{24,8},{25... | collective-permute-start | bytes 1179656 | tf_op jit(solution)/shard_map/ppermute | solution.py:1172
  590.0 21.2 %collective-permute-start.173 = (bf16[384,1536]{1,0:T(8,128)(2,1)}, bf16[384,1536]{1,0:T(8,128)(2,1)S(1)}, u32[]{:S(2)}, u32[]{:S(2)}) collective-permute-start(bf16[384,1536]{1,0:T(8,128)(2,1)} %get-tuple-element.1326), channel_id=1, source_target_pairs={{0,2},{2,0},{4,6},{6,4},{8,10},{10,8},{12,14},{14,12},{1,3},{3,1},... | collective-permute-start | bytes 3538952 | tf_op jit(solution)/shard_map/ppermute | solution.py:56
  590.4 20.7 %collective-permute-start.170 = (bf16[128,1536]{1,0:T(8,128)(2,1)}, bf16[128,1536]{1,0:T(8,128)(2,1)}, u32[]{:S(2)}, u32[]{:S(2)}) collective-permute-start(bf16[128,1536]{1,0:T(8,128)(2,1)} %get-tuple-element.1320), channel_id=1, source_target_pairs={{0,8},{2,10},{4,12},{6,14},{8,0},{10,2},{12,4},{14,6},{1,9},{3,11}... | collective-permute-start | bytes 1179656 | tf_op jit(solution)/shard_map/ppermute | solution.py:56
  591.3 19.8 %collective-permute-start.171 = (bf16[128,1536]{1,0:T(8,128)(2,1)}, bf16[128,1536]{1,0:T(8,128)(2,1)}, u32[]{:S(2)}, u32[]{:S(2)}) collective-permute-start(bf16[128,1536]{1,0:T(8,128)(2,1)} %get-tuple-element.1321), channel_id=1, source_target_pairs={{0,1},{1,0},{2,3},{3,2},{4,5},{5,4},{6,7},{7,6},{8,9},{9,8},{10,11... | collective-permute-start | bytes 1179656 | tf_op jit(solution)/shard_map/ppermute | solution.py:56
  616.5 19.9 %collective-permute-start.178 = (bf16[128,1536]{1,0:T(8,128)(2,1)S(1)}, bf16[128,1536]{1,0:T(8,128)(2,1)S(1)}, u32[]{:S(2)}, u32[]{:S(2)}) collective-permute-start(bf16[128,1536]{1,0:T(8,128)(2,1)S(1)} %add_convert_fusion.10), channel_id=1, source_target_pairs={{0,13},{1,12},{2,15},{3,14},{4,9},{5,8},{6,11},{7,10},{8,5},{9,4},... | collective-permute-start | bytes 1179656 | tf_op jit(solution)/shard_map/ppermute | solution.py:67
  684.3 24.8 %collective-permute-start.196 = (bf16[576,1152]{1,0:T(8,128)(2,1)S(1)}, bf16[576,1152]{1,0:T(8,128)(2,1)S(1)}, u32[]{:S(2)}, u32[]{:S(2)}) collective-permute-start(bf16[576,1152]{1,0:T(8,128)(2,1)S(1)} %copy-done.157), channel_id=1, source_target_pairs={{0,2},{2,0},{4,6},{6,4},{8,10},{10,8},{12,14},{14,12},{1,3},{3,1},... | collective-permute-start | bytes 3981320 | tf_op jit(solution)/shard_map/ppermute | solution.py:56
  686.6 22.5 %collective-permute-start.192 = (bf16[192,1152]{1,0:T(8,128)(2,1)S(1)}, bf16[192,1152]{1,0:T(8,128)(2,1)S(1)}, u32[]{:S(2)}, u32[]{:S(2)}) collective-permute-start(bf16[192,1152]{1,0:T(8,128)(2,1)S(1)} %get-tuple-element.1446), channel_id=1, source_target_pairs={{0,8},{2,10},{4,12},{6,14},{8,0},{10,2},{12,4},{14,6},{1,9},{3,11}... | collective-permute-start | bytes 1327112 | tf_op jit(solution)/shard_map/ppermute | solution.py:56
  687.4 21.7 %collective-permute-start.193 = (bf16[192,1152]{1,0:T(8,128)(2,1)S(1)}, bf16[192,1152]{1,0:T(8,128)(2,1)S(1)}, u32[]{:S(2)}, u32[]{:S(2)}) collective-permute-start(bf16[192,1152]{1,0:T(8,128)(2,1)S(1)} %get-tuple-element.1447), channel_id=1, source_target_pairs={{0,1},{1,0},{2,3},{3,2},{4,5},{5,4},{6,7},{7,6},{8,9},{9,8},{10,11... | collective-permute-start | bytes 1327112 | tf_op jit(solution)/shard_map/ppermute | solution.py:56
  688.1 21.0 %collective-permute-start.194 = (bf16[192,1152]{1,0:T(8,128)(2,1)S(1)}, bf16[192,1152]{1,0:T(8,128)(2,1)S(1)}, u32[]{:S(2)}, u32[]{:S(2)}) collective-permute-start(bf16[192,1152]{1,0:T(8,128)(2,1)S(1)} %get-tuple-element.1448), channel_id=1, source_target_pairs={{0,4},{2,6},{4,0},{6,2},{8,12},{10,14},{12,8},{14,10},{1,5},{3,7},... | collective-permute-start | bytes 1327112 | tf_op jit(solution)/shard_map/ppermute | solution.py:56
  714.0 20.9 %collective-permute-start.201 = (bf16[192,1152]{1,0:T(8,128)(2,1)S(1)}, bf16[192,1152]{1,0:T(8,128)(2,1)S(1)}, u32[]{:S(2)}, u32[]{:S(2)}) collective-permute-start(bf16[192,1152]{1,0:T(8,128)(2,1)S(1)} %add_convert_fusion.3), channel_id=1, source_target_pairs={{0,13},{1,12},{2,15},{3,14},{4,9},{5,8},{6,11},{7,10},{8,5},{9,4},... | collective-permute-start | bytes 1327112 | tf_op jit(solution)/shard_map/ppermute | solution.py:67
  (356 other events, 3234.7 us)

commit v2 on v1

--- a/solution.py
+++ b/solution.py
@@ -86,48 +86,36 @@
 
 
 def gather_rows(cube, own, work, side=()):
-    core = cube.core
     own, beside = after(own, side, 0)
     near = [swap(own, d) for d in (cube.x, cube.y, cube.z)]
-    mine0, other0 = work(0, [own, swap(own, core)])
-    near, mine0, other0, _ = together((near, mine0, other0, beside()))
+    first = work(0, [own])
+    near, first, _ = together((near, first, beside()))
 
     near, beside = after(near, side, 1)
     middle = [swap(block, d) for block, d in zip(near, (cube.y, cube.z, cube.x))]
-    in0 = swap(other0, core)
-    mine1, other1 = work(1, [*near, *[swap(block, core) for block in near]])
-    middle, in0, mine1, other1, _ = together((middle, in0, mine1, other1, beside()))
+    second = work(1, near)
+    middle, second, _ = together((middle, second, beside()))
 
     middle, beside = after(middle, side, 2)
     corner = swap(middle[0], cube.z)
-    mine2, other2 = work(2, [*middle, *[swap(block, core) for block in middle]])
-    corner, mine2, other2, _ = together((corner, mine2, other2, beside()))
-    other2, beside = after(other2, side, 3)
-    in2 = swap(other2, core)
-    mine3, other3 = work(3, [corner, swap(corner, core)])
-    in2, mine3, other3, _ = together((in2, mine3, other3, beside()))
-    return [(mine0, in0), (mine1, other1), (mine2, in2), (mine3, other3)]
+    third = work(2, middle)
+    corner, third, _ = together((corner, third, beside()))
+    return first, second, third, (lambda: [corner], lambda *blocks: work(3, list(blocks)))
 
 
 def low_sum(*terms):
     return sum(wide(t) for t in terms).astype(bf16)
 
 
-def reduce_start(cube, pairs, side=()):
-    own, near, middle, corner = pairs
-    rows = corner[0].shape[0]
-    sent = [low_sum(*[g[i * rows : (i + 1) * rows] for g in middle]) for i in range(3)]
-    (sent, near, corner), beside = after((sent, near, corner), side, 0)
-    arrived = [swap(t, d) for t, d in zip(sent, (cube.y, cube.z, cube.x))]
-    near, corner = [(mine, swap(other, cube.core)) for mine, other in (near, corner)]
-    arrived, own, near, corner, _ = together((arrived, own, near, corner, beside()))
-    return own, near, arrived, corner
-
-
-def reduce_finish(cube, state, side=()):
-    own, near, arrived, corner = state
-    rows = corner[0].shape[0]
-    sent = [low_sum(*corner)] + [low_sum(*[g[i * rows : (i + 1) * rows] for g in near], arrived[i]) for i in range(3)]
+def reduce_start(cube, middle, corner, rest, side=()):
+    (middle, rest), beside = after((middle, rest), side, 0)
+    middle, inputs = together((middle, corner[0]()))
+    arrived = [swap(t, d) for t, d in zip(middle, (cube.y, cube.z, cube.x))]
+    return together((arrived, corner[1](*inputs), rest, beside()))[:3]
+
+
+def reduce_finish(cube, arrived, corner, near, own, side=()):
+    sent = [low_sum(*corner)] + [low_sum(*terms, a) for terms, a in zip(near, arrived)]
     sent, beside = after(sent, side, 0)
     arrived = [swap(t, d) for t, d in zip(sent[1:], (cube.x, cube.y, cube.z))] + [across(sent[0], cube)]
     arrived, own, _ = together((arrived, own, beside()))
@@ -213,21 +201,33 @@
     return pltpu.with_memory_space_constraint(value, pltpu.HBM)
 
 
-def pinned(*values):
+def pinned(groups, axes=None):
+    groups = [g if isinstance(g, (list, tuple)) else (g,) for g in groups]
+    axes = axes or [0] * len(groups)
+    values = [v for g in groups for v in g]
+    shapes = [
+        tuple(n * len(g) if i == axis else n for i, n in enumerate(g[0].shape)) for g, axis in zip(groups, axes)
+    ]
+
     def body(*refs):
-        ins, outs, sems = refs[: len(values)], refs[len(values) : -1], refs[-1]
-        copies = Copies(sems)
-        for copy in [copies.start(a, b) for a, b in zip(ins, outs)]:
+        ins, outs, sems = list(refs[: len(values)]), refs[len(values) : -1], refs[-1]
+        copies, waits = Copies(sems), []
+        for group, axis, out in zip(groups, axes, outs):
+            for i, value in enumerate(group):
+                size = value.shape[axis]
+                place = [slice(None)] * axis + [pl.ds(i * size, size)]
+                waits.append(copies.start(ins.pop(0), out.at[tuple(place)]))
+        for copy in waits:
             copy.wait()
 
     return pl.pallas_call(
         body,
-        out_shape=[held(v.shape, v.dtype) for v in values],
+        out_shape=[held(shape, g[0].dtype) for g, shape in zip(groups, shapes)],
         in_specs=[ANY] * len(values),
-        out_specs=[VMEM] * len(values),
+        out_specs=[VMEM] * len(groups),
         scratch_shapes=[pltpu.SemaphoreType.DMA((len(values),))],
         compiler_params=pltpu.CompilerParams(vmem_limit_bytes=1 << 20),
-    )(*values)
+    )(*map(distant, values))
 
 
 def put_together(pieces, spans, shape):
@@ -529,177 +529,159 @@
     return on_device(attention_back_body, shapes, args, 8 * rows * packed.size, kept=[*weights, packed])
 
 
-def ranges(pieces):
-    pairs = [p if isinstance(p, tuple) else (p, (0, p.shape[0])) for p in pieces]
-    return [p for p, _ in pairs], [r for _, r in pairs]
-
-
-def place(copies, pieces, spans, *targets):
-    halves_of, at = ([], []), 0
-    for piece, (lo, hi) in zip(pieces, spans):
-        first, count = 0, hi - lo
+def place(copies, pieces, *targets):
+    started, at = [], 0
+    for piece in pieces:
+        first, count = 0, piece.shape[0]
         for target in targets:
-            source = piece.at[pl.ds(lo, count), pl.ds(first, target.shape[1])]
-            copy = copies.start(source, target.at[pl.ds(at, count), :])
-            halves_of[2 * at // targets[0].shape[0]].append(copy)
+            source = piece.at[:, pl.ds(first, target.shape[1])]
+            started.append(copies.start(source, target.at[pl.ds(at, count), :]))
             first += target.shape[1]
         at += count
-    return halves_of
-
-
-def own_gate(extra):
+    return started
+
+
+def pair_gates(extra, width):
     me, peers = lax.axis_index("dp"), lax.axis_size("dp")
     lane = lax.broadcasted_iota(jnp.int32, extra.shape, 1)
-    return jnp.sum(jnp.where((lane == me) | (lane == me + peers), wide(extra), 0.0), axis=1, keepdims=True)
-
-
-def expert_stage_body(spans, *refs):
-    pieces = len(spans)
-    (w_gate, w_up, w_down), ins = refs[:3], refs[3 : pieces + 3]
-    rows_out, extra_out, gate_out, up_out, *part_outs = refs[pieces + 3 : pieces + 9]
-    rows, extra, gate_held, up_held, part, sems = refs[pieces + 9 :]
+
+    def gate(expert):
+        return jnp.sum(jnp.where((lane == expert) | (lane == expert + peers), wide(extra), 0.0), axis=1, keepdims=True)
+
+    column = lax.broadcasted_iota(jnp.int32, (extra.shape[0], width), 1)
+    return jnp.where(column < width // 2, gate(me), gate(me ^ 1))
+
+
+def expert_stage_body(count, w_gate, w_up, w_down, *refs):
+    ins, (gate_out, up_out), outs = refs[:count], refs[count : count + 2], refs[count + 2 : 2 * count + 2]
+    rows, extra, gate_held, up_held, part, sems = refs[2 * count + 2 :]
     copies, leaving = Copies(sems), []
-    arriving = place(copies, ins, spans, rows, extra)
-    half = rows.shape[0] // 2
-    for i, part_out in enumerate(part_outs):
-        here = pl.ds(i * half, half)
-        for copy in arriving[i]:
-            copy.wait()
-        leaving.append(copies.start(rows.at[here, :], rows_out.at[here, :]))
-        leaving.append(copies.start(extra.at[here, :], extra_out.at[here, :]))
-        values = rows[here, :]
-        gate = dot_nn(values, w_gate[...])
-        up = dot_nn(values, w_up[...])
-        gate_held[here, :] = gate.astype(bf16)
-        up_held[here, :] = up.astype(bf16)
-        leaving.append(copies.start(gate_held.at[here, :], gate_out.at[here, :]))
-        leaving.append(copies.start(up_held.at[here, :], up_out.at[here, :]))
-        act = (gate / (1.0 + jnp.exp(-gate)) * up).astype(bf16)
-        part[here, :] = (own_gate(extra[here, :]) * dot_nn(act, w_down[...])).astype(bf16)
-        leaving.append(copies.start(part.at[here, :], part_out))
+    for copy in place(copies, ins, rows, extra):
+        copy.wait()
+    values = rows[...]
+    gate = dot_nn(values, w_gate[...])
+    up = dot_nn(values, w_up[...])
+    gate_held[...] = gate.astype(bf16)
+    leaving.append(copies.start(gate_held, gate_out))
+    up_held[...] = up.astype(bf16)
+    leaving.append(copies.start(up_held, up_out))
+    act = gate / (1.0 + jnp.exp(-gate)) * up * pair_gates(extra[...], gate.shape[1])
+    part[...] = dot_nn(act.astype(bf16), w_down[...]).astype(bf16)
+    at = 0
+    for out in outs:
+        leaving.append(copies.start(part.at[pl.ds(at, out.shape[0]), :], out))
+        at += out.shape[0]
     for copy in leaving:
         copy.wait()
 
 
 def expert_stage(pieces, *weights):
-    pieces, spans = ranges(pieces)
-    count = sum(hi - lo for lo, hi in spans)
+    count = sum(p.shape[0] for p in pieces)
     model, units = weights[0].shape
     extra = pieces[0].shape[1] - model
-    saved = [(count, model), (count, extra), (count, units), (count, units)]
-    shapes = [like(t, bf16) for t in [*saved, (count // 2, model), (count // 2, model)]]
-    scratch = [pltpu.VMEM(t, bf16) for t in [*saved, (count, model)]]
-    scratch.append(pltpu.SemaphoreType.DMA((2 * len(pieces) + 10,)))
-    body = functools.partial(expert_stage_body, spans)
+    shapes = [like((count, units), bf16)] * 2 + [like((p.shape[0], model), bf16) for p in pieces]
+    scratch = [pltpu.VMEM((count, n), bf16) for n in (model, extra, units, units, model)]
+    scratch.append(pltpu.SemaphoreType.DMA((3 * len(pieces) + 2,)))
+    body = functools.partial(expert_stage_body, len(pieces))
     outs = on_device(
         body, shapes, [], 6 * count * weights[0].size, kept=weights, far=pieces, scratch=scratch, direct=True
     )
-    return outs[4:], outs[:4]
-
-
-def expert_back_body(spans, *refs):
-    pieces = len(spans)
-    (w_gate, w_up, w_down), ins, (extra_in, gate_in, up_in) = refs[:3], refs[3 : pieces + 3], refs[pieces + 3 : pieces + 6]
-    outs = refs[pieces + 6 : pieces + 12]
-    *held_back, part, extra, gate_held, up_held, sems = refs[pieces + 12 :]
-    grad_rows, grad_gate, grad_up, act = held_back
-    copies, leaving = Copies(sems), []
-    half = grad_rows.shape[0] // 2
-    arriving = [[], []]
-    for i in range(2):
-        here = pl.ds(i * half, half)
-        for source, target in ((extra_in, extra), (gate_in, gate_held), (up_in, up_held)):
-            arriving[i].append(copies.start(source.at[here, :], target.at[here, :]))
-    for i, more in enumerate(place(copies, ins, spans, grad_rows)):
-        arriving[i] += more
-    for i, part_out in enumerate(outs[4:]):
-        here = pl.ds(i * half, half)
-        for copy in arriving[i]:
-            copy.wait()
-        scaled = (own_gate(extra[here, :]) * wide(grad_rows[here, :])).astype(bf16)
-        grad_rows[here, :] = scaled
-        grad_act = dot_nt(scaled, w_down[...])
-        gate, up = wide(gate_held[here, :]), wide(up_held[here, :])
-        sig = 1.0 / (1.0 + jnp.exp(-gate))
-        silu = gate * sig
-        low_gate = (grad_act * up * sig * (1.0 + gate * (1.0 - sig))).astype(bf16)
-        low_up = (grad_act * silu).astype(bf16)
-        grad_gate[here, :] = low_gate
-        grad_up[here, :] = low_up
-        act[here, :] = (silu * up).astype(bf16)
-        for source, target in zip(held_back, outs):
-            leaving.append(copies.start(source.at[here, :], target.at[here, :]))
-        grad_in = dot_nt(low_gate, w_gate[...]) + dot_nt(low_up, w_up[...])
-        part[here, :] = grad_in.astype(bf16)
-        leaving.append(copies.start(part.at[here, :], part_out))
+    return outs[2:], (pieces, *outs[:2])
+
+
+def expert_back_body(count, w_gate, w_up, w_down, *refs):
+    ins, payloads, (gate_in, up_in) = refs[:count], refs[count : 2 * count], refs[2 * count : 2 * count + 2]
+    grad_outs, outs = refs[2 * count + 2 : 2 * count + 5], refs[2 * count + 5 : 3 * count + 5]
+    grads, extra, gate_held, up_held, *held_back, part, sems = refs[3 * count + 5 :]
+    copies, leaving, first = Copies(sems), [], w_gate.shape[0]
+    arriving = place(copies, ins, grads)
+    at = 0
+    for payload in payloads:
+        size = payload.shape[0]
+        arriving.append(
+            copies.start(payload.at[:, pl.ds(first, extra.shape[1])], extra.at[pl.ds(at, size), :])
+        )
+        at += size
+    arriving += [copies.start(gate_in, gate_held), copies.start(up_in, up_held)]
+    for copy in arriving:
+        copy.wait()
+    scale = pair_gates(extra[...], w_gate.shape[1])
+    grad_act = scale * dot_nt(grads[...], w_down[...])
+    gate, up = wide(gate_held[...]), wide(up_held[...])
+    sig = 1.0 / (1.0 + jnp.exp(-gate))
+    silu = gate * sig
+    low_gate = (grad_act * up * sig * (1.0 + gate * (1.0 - sig))).astype(bf16)
+    low_up = (grad_act * silu).astype(bf16)
+    for value, held_value, out in zip((low_gate, low_up, (scale * silu * up).astype(bf16)), held_back, grad_outs):
+        held_value[...] = value
+        leaving.append(copies.start(held_value, out))
+    part[...] = (dot_nt(low_gate, w_gate[...]) + dot_nt(low_up, w_up[...])).astype(bf16)
+    at = 0
+    for out in outs:
+        leaving.append(copies.start(part.at[pl.ds(at, out.shape[0]), :], out))
+        at += out.shape[0]
     for copy in leaving:
         copy.wait()
 
 
 def expert_back_stage(pieces, saved, *weights):
-    rows, extra, gate_out, up_out = saved
-    pieces, spans = ranges(pieces)
-    count = rows.shape[0]
+    payloads, gate_out, up_out = saved
+    count = sum(p.shape[0] for p in pieces)
     model, units = weights[0].shape
-    back = [(count, model), (count, units), (count, units), (count, units)]
-    shapes = [like(t, bf16) for t in [*back, (count // 2, model), (count // 2, model)]]
-    scratch = [pltpu.VMEM(t, bf16) for t in [*back, (count, model), extra.shape, gate_out.shape, up_out.shape]]
-    scratch.append(pltpu.SemaphoreType.DMA((len(pieces) + 16,)))
-    body = functools.partial(expert_back_body, spans)
-    far = [*pieces, *map(distant, (extra, gate_out, up_out))]
+    extra = payloads[0].shape[1] - model
+    shapes = [like((count, units), bf16)] * 3 + [like((p.shape[0], model), bf16) for p in pieces]
+    scratch = [pltpu.VMEM((count, n), bf16) for n in (model, extra, units, units, units, units, units, model)]
+    scratch.append(pltpu.SemaphoreType.DMA((3 * len(pieces) + 5,)))
+    body = functools.partial(expert_back_body, len(pieces))
+    far = [*pieces, *payloads, gate_out, up_out]
     outs = on_device(
         body, shapes, [], 6 * count * weights[0].size, kept=weights, far=far, scratch=scratch, direct=True
     )
-    return outs[4:], outs[:4]
-
-
-def product_sums_body(stages, products, *refs):
-    ins, outs = refs[: -len(products)], refs[-len(products) :]
-    fields = 1 + max(max(p) for p in products)
-    totals = [ref[...] for ref in ins[fields * stages :]] or [0.0] * len(products)
-    for i in range(stages):
-        stage = [r[...] for r in ins[fields * i : fields * (i + 1)]]
-        totals = [t + dot_tn(stage[a], stage[b]) for t, (a, b) in zip(totals, products)]
-    for out, total in zip(outs, totals):
-        out[...] = total
-
-
-def product_sums(stages, products, swept, sums):
-    width = stages[0][swept].shape[1]
-    step = min(t.shape[1] for t in stages[0])
-    rows = sum(stage[0].shape[0] for stage in stages)
-    args, specs = [], []
-    for stage in stages:
-        args += map(distant, stage)
-        for i, t in enumerate(stage):
-            if i == swept:
-                specs.append(pl.BlockSpec((t.shape[0], step), lambda j: (0, j)))
+    return outs[3:], (payloads, pieces, *outs[:3])
+
+
+def swept_products(swept, fixed, sums, swept_left, final):
+    width = fixed[0][0].shape[1]
+    step, steps = width // 2, 4
+    rows = sum(t.shape[0] for t in swept)
+
+    def body(*refs):
+        refs = list(refs)
+        left = jnp.concatenate([refs.pop(0)[...] for _ in swept], axis=0)
+        rights = [jnp.concatenate([refs.pop(0)[...] for _ in group], axis=0) for group in fixed]
+        totals = [refs.pop(0)[...] for _ in sums or ()] or [0.0] * len(fixed)
+        for total, right in zip(totals, rights):
+            total = total + (dot_tn(left, right) if swept_left else dot_tn(right, left))
+            if final:
+                parts = (total[:, :step], total[:, step:]) if swept_left else (total[:step], total[step:])
+                refs.pop(0)[...] = parts[0]
+                refs.pop(0)[...] = parts[1].astype(bf16)
             else:
-                specs.append(pl.BlockSpec(t.shape, lambda j: (0, 0)))
-    shapes, outs = [], []
-    for left, right in products:
-        other = stages[0][right if left == swept else left].shape[1]
-        if left == swept:
-            shapes.append(like((width, other), f32))
-            outs.append(pl.BlockSpec((step, other), lambda j: (j, 0)))
-        else:
-            shapes.append(like((other, width), f32))
-            outs.append(pl.BlockSpec((other, step), lambda j: (0, j)))
-    model_work = width * step // 32
-    first = len(args)
-    if sums is not None:
-        args += map(distant, sums)
-        specs += outs
+                refs.pop(0)[...] = total
+
+    def spec(size):
+        return pl.BlockSpec((step, size), lambda j: (j, 0)) if swept_left else pl.BlockSpec((size, step), lambda j: (0, j))
+
+    def shape(size):
+        return (step * steps, size) if swept_left else (size, step * steps)
+
+    shapes, out_specs = [], []
+    for _ in fixed:
+        for size, dtype in ((step, f32), (step, bf16)) if final else ((width, f32),):
+            shapes.append(like(shape(size), dtype))
+            out_specs.append(spec(size))
+    in_specs = [pl.BlockSpec((t.shape[0], step), lambda j: (0, j)) for t in swept]
+    in_specs += [pl.BlockSpec(t.shape, lambda j: (0, 0)) for group in fixed for t in group]
+    in_specs += [spec(width) for _ in sums or ()]
     return pl.pallas_call(
-        functools.partial(product_sums_body, len(stages), products),
-        grid=(width // step,),
+        body,
+        grid=(steps,),
         out_shape=shapes,
-        in_specs=specs,
-        out_specs=outs,
-        input_output_aliases={} if sums is None else {first + i: i for i in range(len(shapes))},
+        in_specs=in_specs,
+        out_specs=out_specs,
         compiler_params=pltpu.CompilerParams(vmem_limit_bytes=KERNEL_VMEM),
-        cost_estimate=pl.CostEstimate(flops=rows * model_work, bytes_accessed=rows, transcendentals=0),
-    )(*args)
+        cost_estimate=pl.CostEstimate(flops=rows * width, bytes_accessed=rows, transcendentals=0),
+    )(*map(distant, [*swept, *[t for group in fixed for t in group], *(sums or ())]))
 
 
 def expert_forward(rows, w_gate, w_up, w_down):
@@ -798,22 +780,16 @@
         saved = [None] * 4
 
         def work(stage, pieces):
-            parts, kept = expert_stage(pieces, *self.weights)
-            saved[stage] = kept
+            parts, saved[stage] = expert_stage(pieces, *self.weights)
             return parts
 
         return gather_rows(self.cube, payload, work, side), saved
-
-    def back_stage(self, stage, pieces, saved):
-        parts, kept = expert_back_stage(pieces, saved[stage], *self.weights)
-        return parts, [saved[stage][0], *kept]
 
     def backward(self, grad, micro, saved, side=()):
         keeps = [None] * 4
 
         def work(stage, pieces):
-            parts, kept = self.back_stage(stage, pieces, saved)
-            keeps[stage] = kept
+            parts, keeps[stage] = expert_back_stage(pieces, saved[stage], *self.weights)
             return parts
 
         return gather_rows(self.cube, grad, work, side), keeps
@@ -824,34 +800,41 @@
         def run(*stages):
             def work(*gathered):
                 for stage, rows in zip(stages, gathered):
-                    parts[stage], keeps[stage] = self.back_stage(stage, rows, saved)
-                return [parts[stage] for stage in stages]
+                    parts[stage], keeps[stage] = expert_back_stage(rows, saved[stage], *self.weights)
+                return [t for stage in stages for t in parts[stage]]
 
             return lambda: [pieces[stage] for stage in stages], work
 
         return run, parts, keeps
 
     def total_start(self, results, side=()):
-        return reduce_start(self.cube, results, side)
+        own, near, middle, corner = results
+        arrived, corner, (own, near) = reduce_start(self.cube, middle, corner, (own, near), side)
+        return arrived, corner, [[t] for t in near], own
 
     def total_finish(self, state, side=()):
-        return reduce_finish(self.cube, state, side)
+        return reduce_finish(self.cube, *state, side)
 
     def total(self, results, side=()):
         return self.total_finish(self.total_start(results, side[:1]), side[1:])
 
-    def weight_sums(self, keeps, sums):
-        def hidden(*stages):
-            sums[0] = product_sums(stages, ((0, 1), (0, 2)), 0, sums[0])
+    def weight_sums(self, slots, sums, final=False):
+        def stages():
+            return [stage for keeps in slots for stage in keeps]
+
+        def hidden(*args):
+            payloads, gates, ups = args
+            sums[0] = swept_products(payloads, [gates, ups], sums[0], True, final)
             return sums[0]
 
-        def back(*stages):
-            sums[1] = product_sums(stages, ((0, 1),), 1, sums[1])
+        def down(*args):
+            grads, acts = args
+            sums[1] = swept_products(grads, [acts], sums[1], False, final)
             return sums[1]
 
         return [
-            (lambda: [[rows, gate, up] for rows, _, gate, up, _ in keeps], hidden),
-            (lambda: [[act, grad] for _, grad, _, _, act in keeps], back),
+            (lambda: [[t for s in stages() for t in s[0]], [s[2] for s in stages()], [s[3] for s in stages()]], hidden),
+            (lambda: [[t for s in stages() for t in s[1]], [s[4] for s in stages()]], down),
         ]
 
 
@@ -919,12 +902,13 @@
     def total(self, results, side=()):
         return self.total_finish(results, side)
 
-    def weight_sums(self, weights, sums):
-        def add(*weights):
-            for i, part in enumerate((list(weights[:2]), list(weights[2:]))):
-                sums[i] = part if sums[i] is None else [a + b for a, b in zip(sums[i], part)]
-
-        return [None, (lambda: weights, add)]
+    def weight_sums(self, slots, sums, final=False):
+        def add(*slots):
+            for weights in slots:
+                for i, part in enumerate((list(weights[:2]), list(weights[2:]))):
+                    sums[i] = part if sums[i] is None else [a + b for a, b in zip(sums[i], part)]
+
+        return [None, (lambda: slots, add)]
 
 
 def local(
@@ -995,16 +979,18 @@
     gate_cols = [gates[0, m].T for m in range(2)]
     cot_own, cot_other = turned_block(lengths, cotangent)
     opened, mask0 = opening(lengths, tokens, gain_one, weights)
-    settled = [tokens, cotangent, route_cols, gate_cols, expert_w]
+    settled = [tokens, cotangent, route_cols, gate_cols]
     own_near = [swap(cot_own, d) for d in (cube.x, cube.y)] if whole_blocks else []
-    opened, own_near, qkv_slices, cot_other, settled = together(
-        (opened, own_near, qkv_slices, cot_other, settled)
+    mate_w = [swap(w, cube.core) for w in expert_w] if whole_blocks else []
+    opened, own_near, qkv_slices, cot_other, settled, mate_w = together(
+        (opened, own_near, qkv_slices, cot_other, settled, mate_w)
     )
     inputs, part, qkv, heads, sent = opened
-    *settled, expert_w = settled
     other_near = [swap(cot_other, d) for d in (cube.x, cube.y)] if whole_blocks else []
+    if whole_blocks:
+        expert_w = pinned(list(zip(expert_w, mate_w)), (1, 1, 0))
     arrived, other_near, settled, expert_w = together(
-        (swap(sent, cube.z), other_near, settle(lengths, *settled), pinned(*expert_w))
+        (swap(sent, cube.z), other_near, settle(lengths, *settled), expert_w)
     )
     fresh1, cot1, mask1, extra0, extra1, starts = settled
     hidden, payload = joined(part, arrived, gain_two, extra0)
@@ -1034,7 +1020,7 @@
         result0, qkv_near, out_slices = together((result0, qkv_near, out_slices))
         arriving = lax.ppermute(result0, "section", [(0, 1)])
         out_near = [out_slices] + [swap(out_slices, d) for d in (cube.x, cube.y, ("dp", mask))]
-        arriving, out_near, weights = together((arriving, out_near, pinned(*weights)))
+        arriving, out_near, weights = together((arriving, out_near, pinned(weights)))
         qkv_mates, out_mates = first_mates, [swap(t, cube.core) for t in out_near]
         all_places = [*plane_places, far_places[0]]
         width = qkv_slices.shape[1]
@@ -1066,37 +1052,22 @@
     micro_mid = 1 - section
     late = []
 
-    def cot_mates(*cots):
-        late.append([swap(t, cube.core) for t in cots])
-        return late[0]
-
     def cot_far(x0, y1):
-        late.append([swap(x0, cube.y), swap(y1, cube.x)])
-        return late[1]
+        late.extend([swap(x0, cube.y), swap(y1, cube.x)])
+        return late
 
     side = [(lambda: [inputs, mask0, gain_one, weights, packed], first_groups)]
     if whole_blocks:
         (x0, y0), (x1, y1) = own_near, other_near
-        side += [(lambda: [cot_own, cot_other, x0, y0, x1, y1], cot_mates), (lambda: [x0, y1], cot_far)]
+        side += [None, (lambda: [x0, y1], cot_far)]
     results, saved1 = mixture.forward(payload, micro_mid, side)
 
     grad0 = cot_own
     if whole_blocks:
-        (own_c, other_c, x0_c, y0_c, x1_c, y1_c), far = late
-        far_c = [swap(t, cube.core) for t in far]
-        pieces = [
-            [cot_own, own_c],
-            [x0, y0, cot_other, x0_c, y0_c, other_c],
-            [far[0], y1, x1, far_c[0], y1_c, x1_c],
-            [far[1], far_c[1]],
-        ]
+        pieces = [[cot_own], [x0, y0, cot_other], [late[0], y1, x1], [late[1]]]
         run, back_results, keeps0 = mixture.late_backward(pieces, saved1)
-
-        def exchange(*others):
-            back_results[2] = (back_results[2][0], swap(others[0], cube.core))
-            return back_results[2]
-
-        total = mixture.total(results, [run(2), both((lambda: [back_results[2][1]], exchange), run(3, 1, 0))])
+        total = mixture.total(results, [run(2), run(1, 0)])
+        back_results[3] = run(3)
     else:
         back_results, keeps0 = mixture.backward(grad0, micro_mid, saved1)
         total = mixture.total(results)
@@ -1117,9 +1088,10 @@
         arrived.append(lax.ppermute(result, "section", [(0, 1)]))
         return arrived
 
-    result1, back_results = together((result1, back_results))
     if whole_blocks:
-        back_results[0] = (back_results[0][0], swap(back_results[0][1], cube.core))
+        result1, back_results[:3] = together((result1, back_results[:3]))
+    else:
+        result1, back_results = together((result1, back_results))
     state = mixture.total_start(back_results, [(lambda: [result1], second_handoff)])
     grad_two = mixture.total_finish(state, [(lambda: arrived, last_attention)])
     inputs2, hidden2, payload, groups2 = slot2
@@ -1150,7 +1122,13 @@
     state2 = [inputs2, hidden2, mask1, groups2, saved2]
 
     sums = [None, None]
-    coming, results2, saved2 = together((coming, results2, saved2))
+    if whole_blocks:
+        *results2, corner = results2
+        coming, results2, inputs = together((coming, results2, corner[0]()))
+        corner = corner[1](*inputs)
+        results2 = [*results2, (lambda: [corner], lambda t: t)]
+    else:
+        coming, results2, saved2 = together((coming, results2, saved2))
     state2[4] = saved2
     grad1 = coming + cot1
     state_mid = chosen(state0, state2)
@@ -1164,11 +1142,13 @@
 
         return lambda: [own()], work
 
-    work0 = mixture.weight_sums(keeps0, sums)
-    work0[0] = both(*[w for w in work0[:1] if w], placing("out", 0, lambda: chosen(result0, result1)))
-    grad_two = mixture.total(back_results, work0)
+    hidden_work, down_work = mixture.weight_sums([keeps0, keeps1], sums)
+    grad_two = mixture.total(back_results, [placing("out", 0, lambda: chosen(result0, result1)), hidden_work])
     turn1 = attention_turn(grad1, grad_two, state_mid)
-    low, results2 = together((turn1[1], results2))
+    if whole_blocks:
+        low, results2[:3] = together((turn1[1], list(results2[:3])))
+    else:
+        low, results2 = together((turn1[1], results2))
     coming = lax.ppermute(low, "section", [(1, 0)])
     state = mixture.total_start(results2)
     grad2, state = together((coming, state))
@@ -1180,12 +1160,11 @@
         return last_total
 
     side = [None, None, (lambda: [state] if not whole_blocks else list(state), finish_last)]
-    side.append(placing("grad", 0, lambda: chosen(turn1[0], turn0[0])))
     back_results, keeps2 = mixture.backward(grad2, 1 - section, saved1, side)
     result2 = (hidden2 + last_total[0]).astype(bf16)
-    work1 = mixture.weight_sums(keeps1, sums)
-    work1[0] = both(*[w for w in work1[:1] if w], placing("out", 1, lambda: chosen(result1, result2)))
-    grad_two = mixture.total(back_results, work1)
+    placing_out = placing("out", 1, lambda: chosen(result1, result2))
+    placing_grad = placing("grad", 0, lambda: chosen(turn1[0], turn0[0]))
+    grad_two = mixture.total(back_results, [both(placing_out, placing_grad), down_work])
 
     inputs, hidden, _, groups, _ = state1
     heads_all = [[t[2][3][g] for t in (turn0, turn1)] + [groups[g][1]] for g in range(shards)]
@@ -1196,10 +1175,27 @@
         turn2.extend(attention_turn(grad2, grad_two, state1))
         return turn2
 
-    def exchanged(pairs):
-        return [(mine, swap(other, cube.core)) if i in (0, 2) else (mine, other) for i, (mine, other) in enumerate(pairs)]
-
-    out_state = reduce_start(cube, exchanged(out_pairs), [(lambda: [grad_two], last_turn)])
+    def exchange(*others):
+        return [swap(t, cube.core) for t in others]
+
+    def sums_start(pairs, side):
+        own, near, middle, corner = pairs
+        size = corner[0].shape[0]
+
+        def blocks(*terms):
+            return [[t[i * size : (i + 1) * size] for t in terms] for i in range(3)]
+
+        middle = [low_sum(*terms) for terms in blocks(middle[0], swap(middle[1], cube.core))]
+        others = (lambda: [own[1], near[1], corner[1]], exchange)
+        arrived, others, mine = reduce_start(cube, middle, others, (own[0], near[0], corner[0]), side)
+        return arrived, [mine[2], others[2]], blocks(mine[1], others[1]), [mine[0], others[0]]
+
+    def run_both(*works):
+        works = [w for w in works if w]
+        return both(*works) if works else None
+
+    hidden_end, down_end = mixture.weight_sums([keeps2], sums, True)
+    out_state = sums_start(out_pairs, [run_both((lambda: [grad_two], last_turn), down_end)])
     turns = (turn0, turn1, turn2)
     factors = [t[2] for t in turns]
     qkv_pairs = []
@@ -1210,12 +1206,29 @@
         qkv_pairs.extend(owned_products(cube, [f[0] for f in factors], rights, gains=gains))
         return qkv_pairs
 
-    grad_o = reduce_finish(cube, out_state, [(lambda: [], qkv_products)])
-    hidden_work, down_work = mixture.weight_sums(keeps2, sums)
+    grad_o = reduce_finish(cube, *out_state, [run_both((lambda: [], qkv_products), hidden_end)])
     qkv_pairs, grad_o = together((qkv_pairs, grad_o))
-    hidden_work = both(*[w for w in [hidden_work] if w], placing("grad", 1, lambda: chosen(turn2[0], turn1[0])))
-    qkv_state = reduce_start(cube, exchanged(qkv_pairs), [hidden_work])
-    grad_qkv = reduce_finish(cube, qkv_state, [down_work])
+    last_rows = placing("grad", 1, lambda: chosen(turn2[0], turn1[0]))
+    if whole_blocks:
+        (gate_total, gate_other, up_total, up_other), (down_total, down_other) = sums
+        arrived_sums = []
+
+        def last_exchange(*others):
+            arrived_sums.extend(exchange(*others))
+            return arrived_sums
+
+        last_rows = both(last_rows, (lambda: [gate_other, up_other, down_other], last_exchange))
+    else:
+        (gate_total, up_total), (down_total,) = sums
+    qkv_state = sums_start(qkv_pairs, [last_rows])
+    expert_sums = [gate_total, up_total, down_total]
+
+    def last_sums(*arrived):
+        expert_sums[:] = [mine + wide(other) for mine, other in zip(expert_sums, arrived)]
+        return expert_sums
+
+    grad_qkv = reduce_finish(cube, *qkv_state, [(lambda: arrived_sums, last_sums)] if whole_blocks else [])
+    gate_total, up_total, down_total = expert_sums
     width = q_weight.shape[2]
     grad_q = grad_qkv[:, :width]
     grad_k = grad_qkv[:, width : width + HEAD_SIZE]
@@ -1223,7 +1236,6 @@
     gain_pair = [grad_qkv[:, width + 2 * HEAD_SIZE + i] for i in range(2)]
     section_out = jnp.stack([placings["out", 0], placings["out", 1]])
     input_grad = jnp.stack([placings["grad", 0], placings["grad", 1]])
-    (gate_total, up_total), (down_total,) = sums
     return (
         section_out[None],
         input_grad[None],

time: 749 us -> 651 us (0.87)
  waiting for transfers between devices: 235 us -> 168 us
  Pallas kernels: 260 us -> 233 us
  other arithmetic: 54.2 us -> 40 us
  local copies, waits for them, and re-layouts: 32.2 us -> 41.1 us
    ppermute x8, waiting for transfers between devices: 52.4 us -> 13.5 us  [across(): return lax.ppermute(value, ('dp', 'shard'), pairs)]
    pallas_call x34, Pallas kernels: 179 us -> 161 us  [on_device(): pl.pallas_call(body, out_shape=outs, in_specs=[SMEM] * len(scalars) + [VM...]
    select_n x28, other arithmetic: 23.5 us -> 12.1 us  [chosen(): return jax.tree.map(lambda a, b: jnp.where(first, a, b), here, there)]
    convert_element_type x24, other arithmetic: 16.6 us -> 6.67 us  [low_sum(): return sum((wide(t) for t in terms)).astype(bf16)]
    ppermute x1, waiting for transfers between devices: 15.5 us -> 6.13 us  [first_return(): returned.append(lax.ppermute(low, 'section', [(1, 0)]))]
    pallas_call x8 -> x6, Pallas kernels: 61.2 us -> 52.6 us  [the longest x4 46.8 us: swept_products(): pl.pallas_call(body, grid=(steps,), out_shape=shapes, in_specs=in_specs,...]
    ppermute x1, waiting for transfers between devices: 7.97 us -> 0.01 us  [second_handoff(): arrived.append(lax.ppermute(result, 'section', [(0, 1)]))]
    unnamed x356 -> x462, local copies, waits for them, and re-layouts: 24.3 us -> 31.7 us
  transfers between devices with their start and end apart: 202 -> 136, of which waited for: 78 -> 53; matrix products, arithmetic and copies ran while one was open for 6% -> 5% of each run, Pallas kernels for 31% -> 32%
where the time goes in v2:
time: 651 us; the launch traced here: 642 us
  Pallas kernels  233 us (36%)
  waiting for transfers between devices  168 us (26%)
  starting transfers between devices  155 us (24%)
  local copies, waits for them, and re-layouts  41.1 us (6%)
  other arithmetic  40 us (6%)
    pallas_call x34, Pallas kernels, on_device(): pl.pallas_call(body, out_shape=outs, in_specs=[SMEM] * len(scalars) + [VM...  161 us
    ppermute x124, waiting for transfers between devices, swap(): lax.ppermute(value, axis, [(i, i ^ bit) for i in range(lax.axis_size(axis...  147 us
    ppermute x124, starting transfers between devices, swap(): lax.ppermute(value, axis, [(i, i ^ bit) for i in range(lax.axis_size(axis...  128 us
    pallas_call x4, Pallas kernels, swept_products(): pl.pallas_call(body, grid=(steps,), out_shape=shapes, in_specs=in_specs,...  46.8 us
    unnamed x462, local copies, waits for them, and re-layouts  31.7 us
    pallas_call x2, Pallas kernels, owned_products(): pl.pallas_call(functools.partial(owned_body, len(lefts), len(rights), blo...  15.7 us
    ppermute x8, starting transfers between devices, across(): return lax.ppermute(value, ('dp', 'shard'), pairs)  13.5 us
    ppermute x8, waiting for transfers between devices, across(): return lax.ppermute(value, ('dp', 'shard'), pairs)  13.5 us
  transfers between devices with their start and end apart: 136, of which 53 were waited for; matrix products, arithmetic and copies ran while one was open for 5% of the time, Pallas kernels for 32%

profile of v2, /device:TPU:0, one launch (start us, length us, event | category | flops | bytes accessed | tf_op | source)
XLA Modules:
  0.0 641.8 jit_solution(9050221149722602371)
XLA Ops:
  10.7 8.4 %shard_map.221 = (bf16[128,1536]{1,0:T(8,128)(2,1)}, f32[128,1536]{1,0:T(8,128)}, bf16[128,1024]{1,0:T(8,128)(2,1)}, bf16[128,768]{1,0:T(8,128)(2,1)}, bf16[128,...) custom-call(s32[2,1,4]{2,1,0:T(1,128)S(1)} %copy-done.115, ...), custom_call_target="tpu_custom_call" | custom-call | flops 22020096 | bytes 96 | tf_op jit(solution)/shard_map/pallas_call | solution.py:279
  22.6 7.5 %collective-permute-done.refs_0_.refs_1_ = bf16[128,1536]{1,0:T(8,128)(2,1)S(1)} collective-permute-done((bf16[128,1536]{1,0:T(8,128)(2,1)S(1)}, bf16[128,1536]{1,0:T(8,128)(2,1)S(1)}, u32[]{:S(2)}, u32[]{:S(2)}) %collective-permute-start) | collective-permute-done | bytes 393248 | tf_op jit(solution)/shard_map/ppermute | solution.py:56
  100.3 6.6 %collective-permute-done.29 = bf16[128,1536]{1,0:T(8,128)(2,1)S(1)} collective-permute-done((bf16[128,1536]{1,0:T(8,128)(2,1)S(1)}, bf16[128,1536]{1,0:T(8,128)(2,1)S(1)}, u32[]{:S(2)}, u32[]{:S(2)}) %collective-permute-start.29) | collective-permute-done | bytes 393248 | tf_op jit(solution)/shard_map/ppermute | solution.py:56
  106.9 9.9 %collective-permute-done.28 = bf16[128,1536]{1,0:T(8,128)(2,1)S(1)} collective-permute-done((bf16[128,1536]{1,0:T(8,128)(2,1)S(1)}, bf16[128,1536]{1,0:T(8,128)(2,1)S(1)}, u32[]{:S(2)}, u32[]{:S(2)}) %collective-permute-start.28) | collective-permute-done | bytes 393248 | tf_op jit(solution)/shard_map/ppermute | solution.py:56
  148.9 7.0 %shard_map.232 = (bf16[128,1536]{1,0:T(8,128)(2,1)}, f32[128,1536]{1,0:T(8,128)}, bf16[128,1664]{1,0:T(8,128)(2,1)}, bf16[128,1024]{1,0:T(8,128)(2,1)}, bf16[128...) custom-call(bf16[128,1536]{1,0:T(8,128)(2,1)} %get-tuple-element.748.fresh, ...), custom_call_target="tpu_custom_call" | custom-call | flops 22020096 | bytes 14016 | tf_op jit(solution)/shard_map/pallas_call | solution.py:279
  196.6 6.4 shard_map.238
  223.6 6.4 %shard_map.239 = (bf16[384,768]{1,0:T(8,128)(2,1)}, bf16[384,768]{1,0:T(8,128)(2,1)}, bf16[384,768]{1,0:T(8,128)(2,1)}, bf16[128,1536]{1,0:T(8,128)(2,1)}, bf16[...) custom-call(bf16[1536,768]{1,0:T(8,128)(2,1)S(1)} %get-tuple-element.754.w_gate, bf16[1536,768]{1,0:T(8,128)(2,1)S(1)} %copy-done.2, ...), custom_call_target="tpu_custom_call" | custom-call | flops 42467328 | tf_op jit(solution)/shard_map/pallas_call | solution.py:279
  280.2 7.5 %shard_map.244 = (f32[128,1536]{1,0:T(8,128)}, bf16[128,1536]{1,0:T(8,128)(2,1)}, bf16[128,1536]{1,0:T(8,128)(2,1)}, bf16[128,1536]{1,0:T(8,128)(2,1)}, bf16[128...) custom-call(bf16[128,1536]{1,0:T(8,128)(2,1)} %get-tuple-element.1251.refs_0_.grad, ...), custom_call_target="tpu_custom_call" | custom-call | flops 44040192 | bytes 46272 | tf_op jit(solution)/shard_map/pallas_call | solution.py:279
  316.2 7.4 %collective-permute-start.73 = (bf16[128,1536]{1,0:T(8,128)(2,1)S(1)}, bf16[128,1536]{1,0:T(8,128)(2,1)S(1)}, u32[]{:S(2)}, u32[]{:S(2)}) collective-permute-start(bf16[128,1536]{1,0:T(8,128)(2,1)S(1)} %add.296.refs_0_.grad.refs_8_), channel_id=1, source_target_pairs={{0,1},{1,0},{2,3},{3,2},{4,5},{5,4},{6,7},{7,6},{8,9},{9,8},{10,11... | collective-permute-start | bytes 1179656 | tf_op jit(solution)/shard_map/ppermute | solution.py:56
  338.2 6.4 %shard_map.248 = (bf16[384,768]{1,0:T(8,128)(2,1)}, bf16[384,768]{1,0:T(8,128)(2,1)}, bf16[384,768]{1,0:T(8,128)(2,1)}, bf16[128,1536]{1,0:T(8,128)(2,1)}, bf16[...) custom-call(bf16[1536,768]{1,0:T(8,128)(2,1)S(1)} %get-tuple-element.754.w_gate, bf16[1536,768]{1,0:T(8,128)(2,1)S(1)} %copy-done.3, ...), custom_call_target="tpu_custom_call" | custom-call | flops 42467328 | tf_op jit(solution)/shard_map/pallas_call | solution.py:279
  346.9 6.5 %shard_map.249 = (bf16[384,768]{1,0:T(8,128)(2,1)}, bf16[384,768]{1,0:T(8,128)(2,1)}, bf16[384,768]{1,0:T(8,128)(2,1)}, bf16[128,1536]{1,0:T(8,128)(2,1)}, bf16[...) custom-call(bf16[1536,768]{1,0:T(8,128)(2,1)S(1)} %get-tuple-element.754.w_gate, bf16[1536,768]{1,0:T(8,128)(2,1)S(1)} %copy-done.3, ...), custom_call_target="tpu_custom_call" | custom-call | flops 42467328 | tf_op jit(solution)/shard_map/pallas_call | solution.py:279
  374.5 16.0 %shard_map.252 = (f32[1536,768]{1,0:T(8,128)}, f32[1536,768]{1,0:T(8,128)}) custom-call(bf16[128,1664]{1,0:T(8,128)(2,1)} %get-tuple-element.1358.refs_0_.refs_1_, bf16[128,1664]{1,0:T(8,128)(2,1)} %copy-done.32, bf16[128,1664]{1,0:T(8,128)(2,1)} %copy-done.29, bf16[128,1664]{1,0:T(8,128)(2,1)} %copy-done.26, bf16[128,1664]{1,0:T(8,128)(2,1)} %copy-done.35, ...), custom_call_target="tpu_custom_call" | custom-call | flops 1572864 | bytes 2048 | tf_op jit(solution)/shard_map/pallas_call | solution.py:676
  391.7 7.6 %shard_map.253 = (f32[128,1536]{1,0:T(8,128)}, bf16[128,1536]{1,0:T(8,128)(2,1)}, bf16[128,1536]{1,0:T(8,128)(2,1)}, bf16[128,1536]{1,0:T(8,128)(2,1)}, bf16[128...) custom-call(bf16[128,1536]{1,0:T(8,128)(2,1)} %copy-done.41, ...), custom_call_target="tpu_custom_call" | custom-call | flops 44040192 | bytes 46272 | tf_op jit(solution)/shard_map/pallas_call | solution.py:279
  436.6 6.4 shard_map.255
  453.4 6.4 shard_map.256
  461.5 7.5 %collective-permute-done.96.refs_0_.refs_7_ = bf16[128,1536]{1,0:T(8,128)(2,1)S(1)} collective-permute-done((bf16[128,1536]{1,0:T(8,128)(2,1)S(1)}, bf16[128,1536]{1,0:T(8,128)(2,1)S(1)}, u32[]{:S(2)}, u32[]{:S(2)}) %collective-permute-start.96) | collective-permute-done | bytes 393248 | tf_op jit(solution)/shard_map/ppermute | solution.py:56
  497.8 11.1 %shard_map.258.refs_12_ = f32[768,1536]{1,0:T(8,128)} custom-call(bf16[128,1536]{1,0:T(8,128)(2,1)} %get-tuple-element.1251.refs_0_.grad, bf16[128,1536]{1,0:T(8,128)(2,1)} %copy-done.84, bf16[128,1536]{1,0:T(8,128)(2,1)} %copy-done.82, bf16[128,1536]{1,0:T(8,128)(2,1)} %get-tuple-element.1254.refs_2_.refs_3_, bf16[128,1536]{1,0:T(8,128)(2,1)} %copy-done.91, ...), custom_call_target="tpu_custom_call" | custom-call | flops 1572864 | bytes 2048 | tf_op jit(solution)/shard_map/pallas_call | solution.py:676
  510.0 7.3 %shard_map.259 = (bf16[192,768]{1,0:T(8,128)(2,1)}, bf16[192,768]{1,0:T(8,128)(2,1)}, bf16[576,768]{1,0:T(8,128)(2,1)}, bf16[576,768]{1,0:T(8,128)(2,1)}, bf16[5...) custom-call(bf16[128,1536]{1,0:T(8,128)(2,1)} %get-tuple-element.985.refs_0_, ...), custom_call_target="tpu_custom_call" | custom-call | tf_op jit(solution)/shard_map/pallas_call | solution.py:764
  531.0 8.4 %shard_map.262 = (f32[384,1536]{1,0:T(8,128)}, bf16[384,1536]{1,0:T(8,128)(2,1)}) custom-call(bf16[128,1536]{1,0:T(8,128)(2,1)} %copy-done.42, bf16[128,1536]{1,0:T(8,128)(2,1)} %copy-done.101, bf16[128,1536]{1,0:T(8,128)(2,1)} %copy-done.100, bf16[128,1536]{1,0:T(8,128)(2,1)} %copy-done.99, bf16[128,1536]{1,0:T(8,128)(2,1)} %copy-done.102, ...), custom_call_target="tpu_custom_call" | custom-call | flops 786432 | bytes 1024 | tf_op jit(solution)/shard_map/pallas_call | solution.py:676
  539.5 7.6 %shard_map.260 = (f32[128,1536]{1,0:T(8,128)}, bf16[128,1536]{1,0:T(8,128)(2,1)}, bf16[128,1536]{1,0:T(8,128)(2,1)}, bf16[128,1536]{1,0:T(8,128)(2,1)}, bf16[128...) custom-call(bf16[128,1536]{1,0:T(8,128)(2,1)} %copy-done.42, ...), custom_call_target="tpu_custom_call" | custom-call | flops 44040192 | bytes 46272 | tf_op jit(solution)/shard_map/pallas_call | solution.py:279
  552.5 8.4 %shard_map.261 = (bf16[192,1152]{1,0:T(8,128)(2,1)}, bf16[192,1152]{1,0:T(8,128)(2,1)}, bf16[576,1152]{1,0:T(8,128)(2,1)}, bf16[576,1152]{1,0:T(8,128)(2,1)}, bf...) custom-call(bf16[128,1536]{1,0:T(8,128)(2,1)} %get-tuple-element.984, ...), custom_call_target="tpu_custom_call" | custom-call | tf_op jit(solution)/shard_map/pallas_call | solution.py:764
  561.0 11.4 %shard_map.263 = (f32[1536,384]{1,0:T(8,128)}, bf16[1536,384]{1,0:T(8,128)(2,1)}, f32[1536,384]{1,0:T(8,128)}, bf16[1536,384]{1,0:T(8,128)(2,1)}) custom-call(bf16[128,1664]{1,0:T(8,128)(2,1)} %get-tuple-element.1358.refs_0_.refs_1_, bf16[128,1664]{1,0:T(8,128)(2,1)} %copy-done.32, bf16[128,1664]{1,0:T(8,128)(2,1)} %copy-done.29, ...), custom_call_target="tpu_custom_call" | custom-call | flops 786432 | bytes 1024 | tf_op jit(solution)/shard_map/pallas_call | solution.py:676
  582.6 16.4 %collective-permute-done.122 = f32[128,768]{1,0:T(8,128)S(1)} collective-permute-done((f32[128,768]{1,0:T(8,128)S(1)}, f32[128,768]{1,0:T(8,128)S(1)}, u32[]{:S(2)}, u32[]{:S(2)}) %collective-permute-start.122) | collective-permute-done | bytes 393248 | tf_op jit(solution)/shard_map/ppermute | solution.py:56
  629.8 9.1 %collective-permute-done.135 = bf16[192,1152]{1,0:T(8,128)(2,1)S(1)} collective-permute-done((bf16[192,1152]{1,0:T(8,128)(2,1)S(1)}, bf16[192,1152]{1,0:T(8,128)(2,1)S(1)}, u32[]{:S(2)}, u32[]{:S(2)}) %collective-permute-start.135) | collective-permute-done | bytes 442400 | tf_op jit(solution)/shard_map/ppermute | solution.py:67
  (845 shorter events, 432.9 us)
Async XLA Ops:
  0.7 29.5 %collective-permute-start.3 = (bf16[1536,384]{1,0:T(8,128)(2,1)}, bf16[1536,384]{1,0:T(8,128)(2,1)S(1)}, u32[]{:S(2)}, u32[]{:S(2)}) collective-permute-start(bf16[1536,384]{1,0:T(8,128)(2,1)} %bitcast.82), channel_id=1, source_target_pairs={{0,2},{2,0},{4,6},{6,4},{8,10},{10,8},{12,14},{14,12},{1,3},{3,1},... | collective-permute-start | bytes 3538952 | tf_op jit(solution)/shard_map/ppermute | solution.py:56
  1.2 28.9 %collective-permute-start.4 = (bf16[1536,384]{1,0:T(8,128)(2,1)}, bf16[1536,384]{1,0:T(8,128)(2,1)S(1)}, u32[]{:S(2)}, u32[]{:S(2)}) collective-permute-start(bf16[1536,384]{1,0:T(8,128)(2,1)} %bitcast.84), channel_id=1, source_target_pairs={{0,2},{2,0},{4,6},{6,4},{8,10},{10,8},{12,14},{14,12},{1,3},{3,1},... | collective-permute-start | bytes 3538952 | tf_op jit(solution)/shard_map/ppermute | solution.py:56
  1.3 28.9 %collective-permute-start.5 = (bf16[384,1536]{1,0:T(8,128)(2,1)}, bf16[384,1536]{1,0:T(8,128)(2,1)}, u32[]{:S(2)}, u32[]{:S(2)}) collective-permute-start(bf16[384,1536]{1,0:T(8,128)(2,1)} %bitcast.86), channel_id=1, source_target_pairs={{0,2},{2,0},{4,6},{6,4},{8,10},{10,8},{12,14},{14,12},{1,3},{3,1},... | collective-permute-start | bytes 3538952 | tf_op jit(solution)/shard_map/ppermute | solution.py:56
  118.3 21.0 %collective-permute-start.31 = (bf16[128,1536]{1,0:T(8,128)(2,1)}, bf16[128,1536]{1,0:T(8,128)(2,1)}, u32[]{:S(2)}, u32[]{:S(2)}) collective-permute-start(bf16[128,1536]{1,0:T(8,128)(2,1)} %add_convert_fusion.24), channel_id=1, source_target_pairs={{0,16},{1,17},{2,18},{3,19},{4,20},{5,21},{6,22},{7,23},{8,24},{9,... | collective-permute-start | bytes 1179656 | tf_op jit(solution)/shard_map/ppermute | solution.py:1021
  206.4 23.6 %collective-permute-start.51 = (bf16[128,1536]{1,0:T(8,128)(2,1)}, bf16[128,1536]{1,0:T(8,128)(2,1)}, u32[]{:S(2)}, u32[]{:S(2)}) collective-permute-start(bf16[128,1536]{1,0:T(8,128)(2,1)} %add_convert_fusion.23), channel_id=1, source_target_pairs={{0,4},{2,6},{4,0},{6,2},{8,12},{10,14},{12,8},{14,10},{1,5},{3,7},... | collective-permute-start | bytes 1179656 | tf_op jit(solution)/shard_map/ppermute | solution.py:56
  207.7 22.3 %collective-permute-start.52 = (bf16[128,1536]{1,0:T(8,128)(2,1)}, bf16[128,1536]{1,0:T(8,128)(2,1)}, u32[]{:S(2)}, u32[]{:S(2)}) collective-permute-start(bf16[128,1536]{1,0:T(8,128)(2,1)} %add_convert_fusion.22), channel_id=1, source_target_pairs={{0,8},{2,10},{4,12},{6,14},{8,0},{10,2},{12,4},{14,6},{1,9},{3,11}... | collective-permute-start | bytes 1179656 | tf_op jit(solution)/shard_map/ppermute | solution.py:56
  208.6 21.4 %collective-permute-start.53 = (bf16[128,1536]{1,0:T(8,128)(2,1)}, bf16[128,1536]{1,0:T(8,128)(2,1)}, u32[]{:S(2)}, u32[]{:S(2)}) collective-permute-start(bf16[128,1536]{1,0:T(8,128)(2,1)} %add_convert_fusion.21), channel_id=1, source_target_pairs={{0,1},{1,0},{2,3},{3,2},{4,5},{5,4},{6,7},{7,6},{8,9},{9,8},{10,11... | collective-permute-start | bytes 1179656 | tf_op jit(solution)/shard_map/ppermute | solution.py:56
  209.7 20.3 %collective-permute-start.54 = (bf16[128,1536]{1,0:T(8,128)(2,1)}, bf16[128,1536]{1,0:T(8,128)(2,1)}, u32[]{:S(2)}, u32[]{:S(2)}) collective-permute-start(bf16[128,1536]{1,0:T(8,128)(2,1)} %get-tuple-element.909), channel_id=1, source_target_pairs={{0,13},{1,12},{2,15},{3,14},{4,9},{5,8},{6,11},{7,10},{8,5},{9,4},... | collective-permute-start | bytes 1179656 | tf_op jit(solution)/shard_map/ppermute | solution.py:67
  368.6 21.8 %collective-permute-start.82 = (bf16[128,1536]{1,0:T(8,128)(2,1)S(1)}, bf16[128,1536]{1,0:T(8,128)(2,1)S(1)}, u32[]{:S(2)}, u32[]{:S(2)}) collective-permute-start(bf16[128,1536]{1,0:T(8,128)(2,1)S(1)} %add_convert_fusion.16), channel_id=1, source_target_pairs={{0,4},{2,6},{4,0},{6,2},{8,12},{10,14},{12,8},{14,10},{1,5},{3,7},... | collective-permute-start | bytes 1179656 | tf_op jit(solution)/shard_map/ppermute | solution.py:56
  370.1 20.4 %collective-permute-start.83 = (bf16[128,1536]{1,0:T(8,128)(2,1)S(1)}, bf16[128,1536]{1,0:T(8,128)(2,1)S(1)}, u32[]{:S(2)}, u32[]{:S(2)}) collective-permute-start(bf16[128,1536]{1,0:T(8,128)(2,1)S(1)} %add_convert_fusion.15), channel_id=1, source_target_pairs={{0,8},{2,10},{4,12},{6,14},{8,0},{10,2},{12,4},{14,6},{1,9},{3,11}... | collective-permute-start | bytes 1179656 | tf_op jit(solution)/shard_map/ppermute | solution.py:56
  370.7 19.8 %collective-permute-start.84 = (bf16[128,1536]{1,0:T(8,128)(2,1)S(1)}, bf16[128,1536]{1,0:T(8,128)(2,1)S(1)}, u32[]{:S(2)}, u32[]{:S(2)}) collective-permute-start(bf16[128,1536]{1,0:T(8,128)(2,1)S(1)} %add_convert_fusion.14), channel_id=1, source_target_pairs={{0,1},{1,0},{2,3},{3,2},{4,5},{5,4},{6,7},{7,6},{8,9},{9,8},{10,11... | collective-permute-start | bytes 1179656 | tf_op jit(solution)/shard_map/ppermute | solution.py:56
  521.4 25.7 %collective-permute-start.115 = (bf16[576,768]{1,0:T(8,128)(2,1)S(1)}, bf16[576,768]{1,0:T(8,128)(2,1)S(1)}, u32[]{:S(2)}, u32[]{:S(2)}) collective-permute-start(bf16[576,768]{1,0:T(8,128)(2,1)S(1)} %copy-done.209), channel_id=1, source_target_pairs={{0,2},{2,0},{4,6},{6,4},{8,10},{10,8},{12,14},{14,12},{1,3},{3,1},... | collective-permute-start | bytes 2654216 | tf_op jit(solution)/shard_map/ppermute | solution.py:56
  523.5 23.6 %collective-permute-start.112 = (bf16[192,768]{1,0:T(8,128)(2,1)S(1)}, bf16[192,768]{1,0:T(8,128)(2,1)S(1)}, u32[]{:S(2)}, u32[]{:S(2)}) collective-permute-start(bf16[192,768]{1,0:T(8,128)(2,1)S(1)} %get-tuple-element.1314), channel_id=1, source_target_pairs={{0,1},{1,0},{2,3},{3,2},{4,5},{5,4},{6,7},{7,6},{8,9},{9,8},{10,11... | collective-permute-start | bytes 884744 | tf_op jit(solution)/shard_map/ppermute | solution.py:56
  523.8 23.3 %collective-permute-start.113 = (bf16[192,768]{1,0:T(8,128)(2,1)S(1)}, bf16[192,768]{1,0:T(8,128)(2,1)S(1)}, u32[]{:S(2)}, u32[]{:S(2)}) collective-permute-start(bf16[192,768]{1,0:T(8,128)(2,1)S(1)} %get-tuple-element.1315), channel_id=1, source_target_pairs={{0,4},{2,6},{4,0},{6,2},{8,12},{10,14},{12,8},{14,10},{1,5},{3,7},... | collective-permute-start | bytes 884744 | tf_op jit(solution)/shard_map/ppermute | solution.py:56
  525.6 21.5 %collective-permute-start.114 = (bf16[192,768]{1,0:T(8,128)(2,1)S(1)}, bf16[192,768]{1,0:T(8,128)(2,1)S(1)}, u32[]{:S(2)}, u32[]{:S(2)}) collective-permute-start(bf16[192,768]{1,0:T(8,128)(2,1)S(1)} %copy-done.224), channel_id=1, source_target_pairs={{0,2},{2,0},{4,6},{6,4},{8,10},{10,8},{12,14},{14,12},{1,3},{3,1},... | collective-permute-start | bytes 884744 | tf_op jit(solution)/shard_map/ppermute | solution.py:56
  547.5 24.9 %collective-permute-start.117 = (bf16[192,768]{1,0:T(8,128)(2,1)S(1)}, bf16[192,768]{1,0:T(8,128)(2,1)S(1)}, u32[]{:S(2)}, u32[]{:S(2)}) collective-permute-start(bf16[192,768]{1,0:T(8,128)(2,1)S(1)} %get-tuple-element.1352), channel_id=1, source_target_pairs={{0,4},{2,6},{4,0},{6,2},{8,12},{10,14},{12,8},{14,10},{1,5},{3,7},... | collective-permute-start | bytes 884744 | tf_op jit(solution)/shard_map/ppermute | solution.py:56
  549.4 23.0 %collective-permute-start.118 = (bf16[192,768]{1,0:T(8,128)(2,1)S(1)}, bf16[192,768]{1,0:T(8,128)(2,1)S(1)}, u32[]{:S(2)}, u32[]{:S(2)}) collective-permute-start(bf16[192,768]{1,0:T(8,128)(2,1)S(1)} %get-tuple-element.1353), channel_id=1, source_target_pairs={{0,8},{2,10},{4,12},{6,14},{8,0},{10,2},{12,4},{14,6},{1,9},{3,11}... | collective-permute-start | bytes 884744 | tf_op jit(solution)/shard_map/ppermute | solution.py:56
  551.2 21.3 %collective-permute-start.119 = (bf16[192,768]{1,0:T(8,128)(2,1)S(1)}, bf16[192,768]{1,0:T(8,128)(2,1)S(1)}, u32[]{:S(2)}, u32[]{:S(2)}) collective-permute-start(bf16[192,768]{1,0:T(8,128)(2,1)S(1)} %get-tuple-element.1354), channel_id=1, source_target_pairs={{0,1},{1,0},{2,3},{3,2},{4,5},{5,4},{6,7},{7,6},{8,9},{9,8},{10,11... | collective-permute-start | bytes 884744 | tf_op jit(solution)/shard_map/ppermute | solution.py:56
  551.5 20.9 %collective-permute-start.120 = (bf16[192,768]{1,0:T(8,128)(2,1)S(1)}, bf16[192,768]{1,0:T(8,128)(2,1)S(1)}, u32[]{:S(2)}, u32[]{:S(2)}) collective-permute-start(bf16[192,768]{1,0:T(8,128)(2,1)S(1)} %add_convert_fusion.31), channel_id=1, source_target_pairs={{0,13},{1,12},{2,15},{3,14},{4,9},{5,8},{6,11},{7,10},{8,5},{9,4},... | collective-permute-start | bytes 884744 | tf_op jit(solution)/shard_map/ppermute | solution.py:67
  576.9 22.2 %collective-permute-start.123 = (bf16[192,1152]{1,0:T(8,128)(2,1)S(1)}, bf16[192,1152]{1,0:T(8,128)(2,1)S(1)}, u32[]{:S(2)}, u32[]{:S(2)}) collective-permute-start(bf16[192,1152]{1,0:T(8,128)(2,1)S(1)} %get-tuple-element.1396), channel_id=1, source_target_pairs={{0,8},{2,10},{4,12},{6,14},{8,0},{10,2},{12,4},{14,6},{1,9},{3,11}... | collective-permute-start | bytes 1327112 | tf_op jit(solution)/shard_map/ppermute | solution.py:56
  578.7 20.9 %collective-permute-start.124 = (bf16[192,1152]{1,0:T(8,128)(2,1)S(1)}, bf16[192,1152]{1,0:T(8,128)(2,1)S(1)}, u32[]{:S(2)}, u32[]{:S(2)}) collective-permute-start(bf16[192,1152]{1,0:T(8,128)(2,1)S(1)} %get-tuple-element.1397), channel_id=1, source_target_pairs={{0,1},{1,0},{2,3},{3,2},{4,5},{5,4},{6,7},{7,6},{8,9},{9,8},{10,11... | collective-permute-start | bytes 1327112 | tf_op jit(solution)/shard_map/ppermute | solution.py:56
  579.1 20.0 %collective-permute-start.122 = (f32[128,768]{1,0:T(8,128)S(1)}, f32[128,768]{1,0:T(8,128)S(1)}, u32[]{:S(2)}, u32[]{:S(2)}) collective-permute-start(f32[128,768]{1,0:T(8,128)S(1)} %constant_dynamic-slice_fusion), channel_id=1, source_target_pairs={{0,1},{1,0},{2,3},{3,2},{4,5},{5,4},{6,7},{7,6},{8,9},{9,8},{10,11... | collective-permute-start | bytes 1179656 | tf_op jit(solution)/shard_map/ppermute | solution.py:56
  582.6 25.4 %collective-permute-start.127 = (bf16[576,1152]{1,0:T(8,128)(2,1)S(1)}, bf16[576,1152]{1,0:T(8,128)(2,1)S(1)}, u32[]{:S(2)}, u32[]{:S(2)}) collective-permute-start(bf16[576,1152]{1,0:T(8,128)(2,1)S(1)} %copy-done.204), channel_id=1, source_target_pairs={{0,2},{2,0},{4,6},{6,4},{8,10},{10,8},{12,14},{14,12},{1,3},{3,1},... | collective-permute-start | bytes 3981320 | tf_op jit(solution)/shard_map/ppermute | solution.py:56
  617.1 21.8 %collective-permute-start.135 = (bf16[192,1152]{1,0:T(8,128)(2,1)S(1)}, bf16[192,1152]{1,0:T(8,128)(2,1)S(1)}, u32[]{:S(2)}, u32[]{:S(2)}) collective-permute-start(bf16[192,1152]{1,0:T(8,128)(2,1)S(1)} %add_convert_fusion.3), channel_id=1, source_target_pairs={{0,13},{1,12},{2,15},{3,14},{4,9},{5,8},{6,11},{7,10},{8,5},{9,4},... | collective-permute-start | bytes 1327112 | tf_op jit(solution)/shard_map/ppermute | solution.py:67
  (343 other events, 3754.2 us)

commit v3 on v2

--- a/solution.py
+++ b/solution.py
@@ -183,6 +183,7 @@
 SMEM = pl.BlockSpec(memory_space=pltpu.SMEM)
 ANY = pl.BlockSpec(memory_space=pl.ANY)
 KERNEL_VMEM = 42 << 20
+COST = 16
 
 
 def held(shape, dtype):
@@ -283,7 +284,7 @@
         out_specs=[SMEM if o.dtype == jnp.int32 else ANY if direct else VMEM for o in outs],
         scratch_shapes=scratch,
         compiler_params=pltpu.CompilerParams(vmem_limit_bytes=KERNEL_VMEM),
-        cost_estimate=pl.CostEstimate(flops=flops // 64, bytes_accessed=moved // 64, transcendentals=0),
+        cost_estimate=pl.CostEstimate(flops=COST * flops, bytes_accessed=moved, transcendentals=0),
     )(*scalars, *map(distant, args), *map(close, kept), *far)
 
 
@@ -650,14 +651,17 @@
         left = jnp.concatenate([refs.pop(0)[...] for _ in swept], axis=0)
         rights = [jnp.concatenate([refs.pop(0)[...] for _ in group], axis=0) for group in fixed]
         totals = [refs.pop(0)[...] for _ in sums or ()] or [0.0] * len(fixed)
+        others = []
         for total, right in zip(totals, rights):
             total = total + (dot_tn(left, right) if swept_left else dot_tn(right, left))
             if final:
                 parts = (total[:, :step], total[:, step:]) if swept_left else (total[:step], total[step:])
                 refs.pop(0)[...] = parts[0]
-                refs.pop(0)[...] = parts[1].astype(bf16)
+                others.append(parts[1].astype(bf16))
             else:
                 refs.pop(0)[...] = total
+        if final:
+            refs.pop(0)[...] = jnp.concatenate(others, axis=1 if swept_left else 0)
 
     def spec(size):
         return pl.BlockSpec((step, size), lambda j: (j, 0)) if swept_left else pl.BlockSpec((size, step), lambda j: (0, j))
@@ -665,11 +669,9 @@
     def shape(size):
         return (step * steps, size) if swept_left else (size, step * steps)
 
-    shapes, out_specs = [], []
-    for _ in fixed:
-        for size, dtype in ((step, f32), (step, bf16)) if final else ((width, f32),):
-            shapes.append(like(shape(size), dtype))
-            out_specs.append(spec(size))
+    sizes = [(step if final else width, f32)] * len(fixed) + [(step * len(fixed), bf16)] * final
+    shapes = [like(shape(size), dtype) for size, dtype in sizes]
+    out_specs = [spec(size) for size, _ in sizes]
     in_specs = [pl.BlockSpec((t.shape[0], step), lambda j: (0, j)) for t in swept]
     in_specs += [pl.BlockSpec(t.shape, lambda j: (0, 0)) for group in fixed for t in group]
     in_specs += [spec(width) for _ in sums or ()]
@@ -680,7 +682,7 @@
         in_specs=in_specs,
         out_specs=out_specs,
         compiler_params=pltpu.CompilerParams(vmem_limit_bytes=KERNEL_VMEM),
-        cost_estimate=pl.CostEstimate(flops=rows * width, bytes_accessed=rows, transcendentals=0),
+        cost_estimate=pl.CostEstimate(flops=COST * 2 * rows * width * step * steps * len(fixed), bytes_accessed=rows, transcendentals=0),
     )(*map(distant, [*swept, *[t for group in fixed for t in group], *(sums or ())]))
 
 
@@ -752,9 +754,9 @@
 def owned_products(cube, lefts, rights, last=(), gains=()):
     model, width = lefts[0].shape[1], rights[0][0].shape[1] + (128 if gains else 0)
     share = model // lax.axis_size("dp")
-    blocks = [
-        [[(m ^ int(i), s) for m, s in side for i in cube.inner] for side in pair] for pair in cube.stages
-    ]
+    stages = [[[(m ^ int(i), s) for m, s in side for i in cube.inner] for side in pair] for pair in cube.stages]
+    own, near, middle, corner = stages
+    blocks = [middle, [a + b + c for a, b, c in zip(own, near, corner)]]
     shapes = [like((len(places) * share, width), bf16) for pair in blocks for places in pair]
     scratch = [
         pltpu.VMEM((len(rights), model, width), bf16),
@@ -980,17 +982,17 @@
     cot_own, cot_other = turned_block(lengths, cotangent)
     opened, mask0 = opening(lengths, tokens, gain_one, weights)
     settled = [tokens, cotangent, route_cols, gate_cols]
+    mate_w = [swap(w, cube.core) for w in expert_w] if whole_blocks else []
+    opened, qkv_slices, cots, settled, mate_w = together(
+        (opened, qkv_slices, (cot_own, cot_other), settled, mate_w)
+    )
+    inputs, part, qkv, heads, sent = opened
+    cot_own, cot_other = cots
     own_near = [swap(cot_own, d) for d in (cube.x, cube.y)] if whole_blocks else []
-    mate_w = [swap(w, cube.core) for w in expert_w] if whole_blocks else []
-    opened, own_near, qkv_slices, cot_other, settled, mate_w = together(
-        (opened, own_near, qkv_slices, cot_other, settled, mate_w)
-    )
-    inputs, part, qkv, heads, sent = opened
-    other_near = [swap(cot_other, d) for d in (cube.x, cube.y)] if whole_blocks else []
     if whole_blocks:
         expert_w = pinned(list(zip(expert_w, mate_w)), (1, 1, 0))
-    arrived, other_near, settled, expert_w = together(
-        (swap(sent, cube.z), other_near, settle(lengths, *settled), expert_w)
+    arrived, own_near, settled, expert_w = together(
+        (swap(sent, cube.z), own_near, settle(lengths, *settled), expert_w)
     )
     fresh1, cot1, mask1, extra0, extra1, starts = settled
     hidden, payload = joined(part, arrived, gain_two, extra0)
@@ -1014,13 +1016,21 @@
         first_mates.extend(swap(t, cube.core) for t in near)
         return first_mates
 
-    total = mixture.total(results, [(lambda: qkv_near, first_exchange)] if whole_blocks else [])
+    mids = []
+
+    def first_choice(*both_micros):
+        mids.append(chosen(both_micros[2:], both_micros[:2]))
+        return mids
+
+    choice = (lambda: [mask0, extra0, mask1, extra1], first_choice)
+    total = mixture.total(results, [both((lambda: qkv_near, first_exchange), choice) if whole_blocks else choice])
     result0 = (hidden + total).astype(bf16)
     if whole_blocks:
-        result0, qkv_near, out_slices = together((result0, qkv_near, out_slices))
+        result0, qkv_near, out_slices, cot_other = together((result0, qkv_near, out_slices, cot_other))
         arriving = lax.ppermute(result0, "section", [(0, 1)])
         out_near = [out_slices] + [swap(out_slices, d) for d in (cube.x, cube.y, ("dp", mask))]
-        arriving, out_near, weights = together((arriving, out_near, pinned(weights)))
+        other_near = [swap(cot_other, d) for d in (cube.x, cube.y)]
+        arriving, out_near, other_near, weights = together((arriving, out_near, other_near, pinned(weights)))
         qkv_mates, out_mates = first_mates, [swap(t, cube.core) for t in out_near]
         all_places = [*plane_places, far_places[0]]
         width = qkv_slices.shape[1]
@@ -1039,7 +1049,7 @@
         )
     state0 = [inputs, hidden, mask0, None, saved]
 
-    mask_mid, extra_mid = chosen((mask1, extra1), (mask0, extra0))
+    mask_mid, extra_mid = mids[0]
 
     inputs1, hidden1, payload, groups1 = attention_forward(
         fresh1, arriving, mask_mid, gain_one, gain_two, extra_mid, weights, packed
@@ -1144,6 +1154,7 @@
 
     hidden_work, down_work = mixture.weight_sums([keeps0, keeps1], sums)
     grad_two = mixture.total(back_results, [placing("out", 0, lambda: chosen(result0, result1)), hidden_work])
+    grad_two, down_inputs = together((grad_two, down_work[0]())) if down_work else (grad_two, ())
     turn1 = attention_turn(grad1, grad_two, state_mid)
     if whole_blocks:
         low, results2[:3] = together((turn1[1], list(results2[:3])))
@@ -1151,7 +1162,7 @@
         low, results2 = together((turn1[1], results2))
     coming = lax.ppermute(low, "section", [(1, 0)])
     state = mixture.total_start(results2)
-    grad2, state = together((coming, state))
+    grad2, state, _ = together((coming, state, down_work[1](*down_inputs) if down_work else ()))
 
     last_total = []
 
@@ -1164,11 +1175,18 @@
     result2 = (hidden2 + last_total[0]).astype(bf16)
     placing_out = placing("out", 1, lambda: chosen(result1, result2))
     placing_grad = placing("grad", 0, lambda: chosen(turn1[0], turn0[0]))
-    grad_two = mixture.total(back_results, [both(placing_out, placing_grad), down_work])
+    hidden_end, down_end = mixture.weight_sums([keeps2], sums, True)
+    ends = [w for w in (hidden_end, down_end) if w]
+    grad_two = mixture.total(back_results, [both(placing_out, placing_grad), both(*ends)])
+    expert_sums = [*sums[0][:2], sums[1][0]]
+    others = [t for group in sums for t in group if t.dtype == bf16]
 
     inputs, hidden, _, groups, _ = state1
     heads_all = [[t[2][3][g] for t in (turn0, turn1)] + [groups[g][1]] for g in range(shards)]
+    grad_two, others = together((grad_two, others))
+    others = [swap(t, cube.core) for t in others]
     out_pairs = owned_products(cube, [turn0[2][1], turn1[2][1]], heads_all, (grad2, grad_two, hidden, gain_two))
+    out_pairs, others = together((out_pairs, others))
     turn2 = []
 
     def last_turn(grad_two):
@@ -1179,23 +1197,23 @@
         return [swap(t, cube.core) for t in others]
 
     def sums_start(pairs, side):
-        own, near, middle, corner = pairs
-        size = corner[0].shape[0]
+        middle, rest = pairs
+        size = middle[0].shape[0] // 3
 
         def blocks(*terms):
-            return [[t[i * size : (i + 1) * size] for t in terms] for i in range(3)]
+            return [[t[i : i + size] for t in terms] for i in range(0, terms[0].shape[0], size)]
 
         middle = [low_sum(*terms) for terms in blocks(middle[0], swap(middle[1], cube.core))]
-        others = (lambda: [own[1], near[1], corner[1]], exchange)
-        arrived, others, mine = reduce_start(cube, middle, others, (own[0], near[0], corner[0]), side)
-        return arrived, [mine[2], others[2]], blocks(mine[1], others[1]), [mine[0], others[0]]
+        other = (lambda: [rest[1]], lambda t: [swap(t, cube.core)])
+        arrived, other, mine = reduce_start(cube, middle, other, rest[0], side)
+        own, *near, corner = blocks(mine, *other)
+        return arrived, corner, near, own
 
     def run_both(*works):
         works = [w for w in works if w]
         return both(*works) if works else None
 
-    hidden_end, down_end = mixture.weight_sums([keeps2], sums, True)
-    out_state = sums_start(out_pairs, [run_both((lambda: [grad_two], last_turn), down_end)])
+    out_state = sums_start(out_pairs, [(lambda: [grad_two], last_turn)])
     turns = (turn0, turn1, turn2)
     factors = [t[2] for t in turns]
     qkv_pairs = []
@@ -1206,28 +1224,18 @@
         qkv_pairs.extend(owned_products(cube, [f[0] for f in factors], rights, gains=gains))
         return qkv_pairs
 
-    grad_o = reduce_finish(cube, *out_state, [run_both((lambda: [], qkv_products), hidden_end)])
+    grad_o = reduce_finish(cube, *out_state, [(lambda: [], qkv_products)])
     qkv_pairs, grad_o = together((qkv_pairs, grad_o))
+
+    def last_sums(*others):
+        if others:
+            (gate, up), down = jnp.split(others[0], 2, axis=1), others[1]
+            expert_sums[:] = [mine + wide(other) for mine, other in zip(expert_sums, (gate, up, down))]
+        return expert_sums
+
     last_rows = placing("grad", 1, lambda: chosen(turn2[0], turn1[0]))
-    if whole_blocks:
-        (gate_total, gate_other, up_total, up_other), (down_total, down_other) = sums
-        arrived_sums = []
-
-        def last_exchange(*others):
-            arrived_sums.extend(exchange(*others))
-            return arrived_sums
-
-        last_rows = both(last_rows, (lambda: [gate_other, up_other, down_other], last_exchange))
-    else:
-        (gate_total, up_total), (down_total,) = sums
-    qkv_state = sums_start(qkv_pairs, [last_rows])
-    expert_sums = [gate_total, up_total, down_total]
-
-    def last_sums(*arrived):
-        expert_sums[:] = [mine + wide(other) for mine, other in zip(expert_sums, arrived)]
-        return expert_sums
-
-    grad_qkv = reduce_finish(cube, *qkv_state, [(lambda: arrived_sums, last_sums)] if whole_blocks else [])
+    qkv_state = sums_start(qkv_pairs, [both(last_rows, (lambda: others, last_sums))])
+    grad_qkv = reduce_finish(cube, *qkv_state)
     gate_total, up_total, down_total = expert_sums
     width = q_weight.shape[2]
     grad_q = grad_qkv[:, :width]

time: 651 us -> 611 us (0.939)
  waiting for transfers between devices: 168 us -> 149 us
  local copies, waits for them, and re-layouts: 41.1 us -> 27.7 us
  starting transfers between devices: 155 us -> 146 us
    ppermute x124 -> x119, waiting for transfers between devices: 147 us -> 112 us  [swap(): lax.ppermute(value, axis, [(i, i ^ bit) for i in range(lax.axis_size(axis...]
    unnamed x462 -> x412, local copies, waits for them, and re-layouts: 31.7 us -> 19.7 us
    ppermute x124 -> x119, starting transfers between devices: 128 us -> 118 us  [swap(): lax.ppermute(value, axis, [(i, i ^ bit) for i in range(lax.axis_size(axis...]
    ppermute x8, waiting for transfers between devices: 13.5 us -> 21.8 us  [across(): return lax.ppermute(value, ('dp', 'shard'), pairs)]
  transfers between devices with their start and end apart: 136 -> 131, of which waited for: 53 -> 52; matrix products, arithmetic and copies ran while one was open for 5% -> 5% of each run, Pallas kernels for 32% -> 35%
where the time goes in v3:
time: 611 us; the launch traced here: 604 us
  Pallas kernels  233 us (38%)
  waiting for transfers between devices  149 us (24%)
  starting transfers between devices  146 us (24%)
  other arithmetic  43.3 us (7%)
  local copies, waits for them, and re-layouts  27.7 us (5%)
    pallas_call x34, Pallas kernels, on_device(): pl.pallas_call(body, out_shape=outs, in_specs=[SMEM] * len(scalars) + [VM...  161 us
    ppermute x119, starting transfers between devices, swap(): lax.ppermute(value, axis, [(i, i ^ bit) for i in range(lax.axis_size(axis...  118 us
    ppermute x119, waiting for transfers between devices, swap(): lax.ppermute(value, axis, [(i, i ^ bit) for i in range(lax.axis_size(axis...  112 us
    pallas_call x4, Pallas kernels, swept_products(): pl.pallas_call(body, grid=(steps,), out_shape=shapes, in_specs=in_specs,...  46.7 us
    ppermute x8, waiting for transfers between devices, across(): return lax.ppermute(value, ('dp', 'shard'), pairs)  21.8 us
    unnamed x412, local copies, waits for them, and re-layouts  19.7 us
    pallas_call x2, Pallas kernels, owned_products(): pl.pallas_call(functools.partial(owned_body, len(lefts), len(rights), blo...  15.7 us
    ppermute x8, starting transfers between devices, across(): return lax.ppermute(value, ('dp', 'shard'), pairs)  13.3 us
  transfers between devices with their start and end apart: 131, of which 52 were waited for; matrix products, arithmetic and copies ran while one was open for 5% of the time, Pallas kernels for 35%

profile of v3, /device:TPU:0, one launch (start us, length us, event | category | flops | bytes accessed | tf_op | source)
XLA Modules:
  0.0 604.1 jit_solution(785363031229448156)
XLA Ops:
  7.5 8.3 %shard_map.221 = (bf16[128,1536]{1,0:T(8,128)(2,1)}, f32[128,1536]{1,0:T(8,128)}, bf16[128,1024]{1,0:T(8,128)(2,1)}, bf16[128,768]{1,0:T(8,128)(2,1)}, bf16[128,...) custom-call(s32[2,1,4]{2,1,0:T(1,128)S(1)} %copy-done.94, ...), custom_call_target="tpu_custom_call" | custom-call | flops 22548578304 | bytes 6144 | tf_op jit(solution)/shard_map/pallas_call | solution.py:280
  95.1 6.7 %collective-permute-done.27 = bf16[128,1536]{1,0:T(8,128)(2,1)S(1)} collective-permute-done((bf16[128,1536]{1,0:T(8,128)(2,1)S(1)}, bf16[128,1536]{1,0:T(8,128)(2,1)S(1)}, u32[]{:S(2)}, u32[]{:S(2)}) %collective-permute-start.27) | collective-permute-done | bytes 393248 | tf_op jit(solution)/shard_map/ppermute | solution.py:56
  101.8 8.6 %collective-permute-done.26 = bf16[128,1536]{1,0:T(8,128)(2,1)S(1)} collective-permute-done((bf16[128,1536]{1,0:T(8,128)(2,1)S(1)}, bf16[128,1536]{1,0:T(8,128)(2,1)S(1)}, u32[]{:S(2)}, u32[]{:S(2)}) %collective-permute-start.26) | collective-permute-done | bytes 393248 | tf_op jit(solution)/shard_map/ppermute | solution.py:56
  128.8 6.8 %collective-permute-done.31.refs_10_ = bf16[192,768]{1,0:T(8,128)(2,1)} collective-permute-done((bf16[192,768]{1,0:T(8,128)(2,1)}, bf16[192,768]{1,0:T(8,128)(2,1)}, u32[]{:S(2)}, u32[]{:S(2)}) %collective-permute-start.31) | collective-permute-done | bytes 294944 | tf_op jit(solution)/shard_map/ppermute | solution.py:56
  144.1 6.4 %shard_map.232 = (bf16[128,1536]{1,0:T(8,128)(2,1)}, f32[128,1536]{1,0:T(8,128)}, bf16[128,1664]{1,0:T(8,128)(2,1)}, bf16[128,1024]{1,0:T(8,128)(2,1)}, bf16[128...) custom-call(bf16[128,1536]{1,0:T(8,128)(2,1)} %get-tuple-element.727.fresh, ...), custom_call_target="tpu_custom_call" | custom-call | flops 22548578304 | bytes 897024 | tf_op jit(solution)/shard_map/pallas_call | solution.py:280
  192.3 6.9 %shard_map.238 = (bf16[384,768]{1,0:T(8,128)(2,1)}, bf16[384,768]{1,0:T(8,128)(2,1)}, bf16[384,768]{1,0:T(8,128)(2,1)}, bf16[128,1536]{1,0:T(8,128)(2,1)}, bf16[...) custom-call(bf16[1536,768]{1,0:T(8,128)(2,1)S(1)} %get-tuple-element.733.w_gate, bf16[1536,768]{1,0:T(8,128)(2,1)S(1)} %copy-done.31, ...), custom_call_target="tpu_custom_call" | custom-call | flops 43486543872 | tf_op jit(solution)/shard_map/pallas_call | solution.py:280
  211.8 6.4 %shard_map.239 = (bf16[384,768]{1,0:T(8,128)(2,1)}, bf16[384,768]{1,0:T(8,128)(2,1)}, bf16[384,768]{1,0:T(8,128)(2,1)}, bf16[128,1536]{1,0:T(8,128)(2,1)}, bf16[...) custom-call(bf16[1536,768]{1,0:T(8,128)(2,1)S(1)} %get-tuple-element.733.w_gate, bf16[1536,768]{1,0:T(8,128)(2,1)S(1)} %copy-done.31, ...), custom_call_target="tpu_custom_call" | custom-call | flops 43486543872 | tf_op jit(solution)/shard_map/pallas_call | solution.py:280
  228.3 6.8 %collective-permute-start.58 = (bf16[128,1536]{1,0:T(8,128)(2,1)S(1)}, bf16[128,1536]{1,0:T(8,128)(2,1)S(1)}, u32[]{:S(2)}, u32[]{:S(2)}) collective-permute-start(bf16[128,1536]{1,0:T(8,128)(2,1)S(1)} %add_convert_fusion.20), channel_id=1, source_target_pairs={{0,16},{1,17},{2,18},{3,19},{4,20},{5,21},{6,22},{7,23},{8,24},{9,... | collective-permute-start | bytes 1179656 | tf_op jit(solution)/shard_map/ppermute | solution.py:1098
  270.6 7.5 %shard_map.244 = (f32[128,1536]{1,0:T(8,128)}, bf16[128,1536]{1,0:T(8,128)(2,1)}, bf16[128,1536]{1,0:T(8,128)(2,1)}, bf16[128,1536]{1,0:T(8,128)(2,1)}, bf16[128...) custom-call(bf16[128,1536]{1,0:T(8,128)(2,1)} %get-tuple-element.1161.refs_0_.grad, ...), custom_call_target="tpu_custom_call" | custom-call | flops 45097156608 | bytes 2961408 | tf_op jit(solution)/shard_map/pallas_call | solution.py:280
  300.5 10.8 %collective-permute-done.69 = bf16[128,1536]{1,0:T(8,128)(2,1)S(1)} collective-permute-done((bf16[128,1536]{1,0:T(8,128)(2,1)S(1)}, bf16[128,1536]{1,0:T(8,128)(2,1)S(1)}, u32[]{:S(2)}, u32[]{:S(2)}) %collective-permute-start.69) | collective-permute-done | bytes 393248 | tf_op jit(solution)/shard_map/ppermute | solution.py:1126
  325.2 6.4 %shard_map.248 = (bf16[384,768]{1,0:T(8,128)(2,1)}, bf16[384,768]{1,0:T(8,128)(2,1)}, bf16[384,768]{1,0:T(8,128)(2,1)}, bf16[128,1536]{1,0:T(8,128)(2,1)}, bf16[...) custom-call(bf16[1536,768]{1,0:T(8,128)(2,1)S(1)} %copy-done.28, bf16[1536,768]{1,0:T(8,128)(2,1)S(1)} %copy-done.32, ...), custom_call_target="tpu_custom_call" | custom-call | flops 43486543872 | tf_op jit(solution)/shard_map/pallas_call | solution.py:280
  333.4 6.6 %shard_map.249 = (bf16[384,768]{1,0:T(8,128)(2,1)}, bf16[384,768]{1,0:T(8,128)(2,1)}, bf16[384,768]{1,0:T(8,128)(2,1)}, bf16[128,1536]{1,0:T(8,128)(2,1)}, bf16[...) custom-call(bf16[1536,768]{1,0:T(8,128)(2,1)S(1)} %copy-done.28, bf16[1536,768]{1,0:T(8,128)(2,1)S(1)} %copy-done.32, ...), custom_call_target="tpu_custom_call" | custom-call | flops 43486543872 | tf_op jit(solution)/shard_map/pallas_call | solution.py:280
  363.5 15.5 %shard_map.252 = (f32[1536,768]{1,0:T(8,128)}, f32[1536,768]{1,0:T(8,128)}) custom-call(bf16[128,1664]{1,0:T(8,128)(2,1)} %get-tuple-element.1273.refs_0_.refs_1_, bf16[128,1664]{1,0:T(8,128)(2,1)} %copy-done.56, bf16[128,1664]{1,0:T(8,128)(2,1)} %copy-done.54, bf16[128,1664]{1,0:T(8,128)(2,1)} %copy-done.52, bf16[128,1664]{1,0:T(8,128)(2,1)} %copy-done.58, ...), custom_call_target="tpu_custom_call" | custom-call | flops 154618822656 | bytes 2048 | tf_op jit(solution)/shard_map/pallas_call | solution.py:678
  384.4 7.6 %shard_map.253 = (f32[128,1536]{1,0:T(8,128)}, bf16[128,1536]{1,0:T(8,128)(2,1)}, bf16[128,1536]{1,0:T(8,128)(2,1)}, bf16[128,1536]{1,0:T(8,128)(2,1)}, bf16[128...) custom-call(bf16[128,1536]{1,0:T(8,128)(2,1)} %copy-done.26, ...), custom_call_target="tpu_custom_call" | custom-call | flops 45097156608 | bytes 2961408 | tf_op jit(solution)/shard_map/pallas_call | solution.py:280
  397.9 11.7 %shard_map.254.refs_12_ = f32[768,1536]{1,0:T(8,128)} custom-call(bf16[128,1536]{1,0:T(8,128)(2,1)} %get-tuple-element.1161.refs_0_.grad, bf16[128,1536]{1,0:T(8,128)(2,1)} %copy-done.78, bf16[128,1536]{1,0:T(8,128)(2,1)} %copy-done.76, bf16[128,1536]{1,0:T(8,128)(2,1)} %get-tuple-element.1164.refs_2_.refs_3_, ...), custom_call_target="tpu_custom_call" | custom-call | flops 77309411328 | bytes 2048 | tf_op jit(solution)/shard_map/pallas_call | solution.py:678
  447.2 6.4 %shard_map.257 = (bf16[384,768]{1,0:T(8,128)(2,1)}, bf16[384,768]{1,0:T(8,128)(2,1)}, bf16[384,768]{1,0:T(8,128)(2,1)}, bf16[128,1536]{1,0:T(8,128)(2,1)}, bf16[...) custom-call(bf16[1536,768]{1,0:T(8,128)(2,1)S(1)} %copy-done.29, bf16[1536,768]{1,0:T(8,128)(2,1)S(1)} %copy-done.33, ...), custom_call_target="tpu_custom_call" | custom-call | flops 43486543872 | tf_op jit(solution)/shard_map/pallas_call | solution.py:280
  457.0 7.2 %collective-permute-done.96.refs_0_.refs_7_ = bf16[128,1536]{1,0:T(8,128)(2,1)S(1)} collective-permute-done((bf16[128,1536]{1,0:T(8,128)(2,1)S(1)}, bf16[128,1536]{1,0:T(8,128)(2,1)S(1)}, u32[]{:S(2)}, u32[]{:S(2)}) %collective-permute-start.96) | collective-permute-done | bytes 393248 | tf_op jit(solution)/shard_map/ppermute | solution.py:56
  487.3 11.3 %shard_map.259 = (f32[1536,384]{1,0:T(8,128)}, f32[1536,384]{1,0:T(8,128)}, bf16[1536,768]{1,0:T(8,128)(2,1)}) custom-call(bf16[128,1664]{1,0:T(8,128)(2,1)} %get-tuple-element.1273.refs_0_.refs_1_, bf16[128,1664]{1,0:T(8,128)(2,1)} %copy-done.56, bf16[128,1664]{1,0:T(8,128)(2,1)} %copy-done.54, bf16[128,1664]{1,0:T(8,128)(2,1)} %copy-done.52, ...), custom_call_target="tpu_custom_call" | custom-call | flops 77309411328 | bytes 1024 | tf_op jit(solution)/shard_map/pallas_call | solution.py:678
  498.6 8.2 %shard_map.260 = (f32[384,1536]{1,0:T(8,128)}, bf16[384,1536]{1,0:T(8,128)(2,1)}) custom-call(bf16[128,1536]{1,0:T(8,128)(2,1)} %copy-done.25, bf16[128,1536]{1,0:T(8,128)(2,1)} %copy-done.85, bf16[128,1536]{1,0:T(8,128)(2,1)} %copy-done.84, bf16[128,1536]{1,0:T(8,128)(2,1)} %copy-done.83, bf16[128,1536]{1,0:T(8,128)(2,1)} %copy-done.88, ...), custom_call_target="tpu_custom_call" | custom-call | flops 38654705664 | bytes 1024 | tf_op jit(solution)/shard_map/pallas_call | solution.py:678
  510.0 7.3 %shard_map.261 = (bf16[576,768]{1,0:T(8,128)(2,1)}, bf16[576,768]{1,0:T(8,128)(2,1)}, bf16[960,768]{1,0:T(8,128)(2,1)}, bf16[960,768]{1,0:T(8,128)(2,1)}) custom-call(bf16[128,1536]{1,0:T(8,128)(2,1)} %get-tuple-element.970.refs_0_, bf16[128,1536]{1,0:T(8,128)(2,1)} %get-tuple-element.1234.refs_1_, bf16[128,768]{1,0:T(8,128)(2,1)} %get-tuple-element.973.refs_2_.refs_4_, ...), custom_call_target="tpu_custom_call" | custom-call | tf_op jit(solution)/shard_map/pallas_call | solution.py:766
  525.5 7.5 %shard_map.262 = (f32[128,1536]{1,0:T(8,128)}, bf16[128,1536]{1,0:T(8,128)(2,1)}, bf16[128,1536]{1,0:T(8,128)(2,1)}, bf16[128,1536]{1,0:T(8,128)(2,1)}, bf16[128...) custom-call(bf16[128,1536]{1,0:T(8,128)(2,1)} %copy-done.25, ...), custom_call_target="tpu_custom_call" | custom-call | flops 45097156608 | bytes 2961408 | tf_op jit(solution)/shard_map/pallas_call | solution.py:280
  538.4 8.4 %shard_map.263 = (bf16[576,1152]{1,0:T(8,128)(2,1)}, bf16[576,1152]{1,0:T(8,128)(2,1)}, bf16[960,1152]{1,0:T(8,128)(2,1)}, bf16[960,1152]{1,0:T(8,128)(2,1)}) custom-call(bf16[128,1536]{1,0:T(8,128)(2,1)} %get-tuple-element.969.refs_0_, bf16[128,1536]{1,0:T(8,128)(2,1)} %get-tuple-element.1233.refs_1_, bf16[128,1536]{1,0:T(8,128)(2,1)} %get-tuple-element.1322.refs_2_, ...), custom_call_target="tpu_custom_call" | custom-call | tf_op jit(solution)/shard_map/pallas_call | solution.py:766
  570.8 7.0 %collective-permute-done.124 = bf16[192,1152]{1,0:T(8,128)(2,1)S(1)} collective-permute-done((bf16[192,1152]{1,0:T(8,128)(2,1)S(1)}, bf16[192,1152]{1,0:T(8,128)(2,1)S(1)}, u32[]{:S(2)}, u32[]{:S(2)}) %collective-permute-start.124) | collective-permute-done | bytes 442400 | tf_op jit(solution)/shard_map/ppermute | solution.py:56
  585.8 7.7 %collective-permute-done.130 = bf16[192,1152]{1,0:T(8,128)(2,1)S(1)} collective-permute-done((bf16[192,1152]{1,0:T(8,128)(2,1)S(1)}, bf16[192,1152]{1,0:T(8,128)(2,1)S(1)}, u32[]{:S(2)}, u32[]{:S(2)}) %collective-permute-start.130) | collective-permute-done | bytes 442400 | tf_op jit(solution)/shard_map/ppermute | solution.py:67
  (784 shorter events, 405.1 us)
Async XLA Ops:
  3.3 16.6 %collective-permute-start = (bf16[192,1024]{1,0:T(8,128)(2,1)}, bf16[192,1024]{1,0:T(8,128)(2,1)}, u32[]{:S(2)}, u32[]{:S(2)}) collective-permute-start(bf16[192,1024]{1,0:T(8,128)(2,1)} %pad_maximum_fusion), channel_id=1, source_target_pairs={{0,1},{1,0},{2,3},{3,2},{4,5},{5,4},{6,7},{7,6},{8,9},{9,8},{10,11... | collective-permute-start | bytes 1179656 | tf_op jit(solution)/shard_map/ppermute | solution.py:56
  91.0 19.4 %collective-permute-start.26 = (bf16[128,1536]{1,0:T(8,128)(2,1)S(1)}, bf16[128,1536]{1,0:T(8,128)(2,1)S(1)}, u32[]{:S(2)}, u32[]{:S(2)}) collective-permute-start(bf16[128,1536]{1,0:T(8,128)(2,1)S(1)} %add_convert_fusion.26), channel_id=1, source_target_pairs={{0,8},{2,10},{4,12},{6,14},{8,0},{10,2},{12,4},{14,6},{1,9},{3,11}... | collective-permute-start | bytes 1179656 | tf_op jit(solution)/shard_map/ppermute | solution.py:56
  92.1 19.1 %collective-permute-start.25 = (bf16[128,1536]{1,0:T(8,128)(2,1)S(1)}, bf16[128,1536]{1,0:T(8,128)(2,1)S(1)}, u32[]{:S(2)}, u32[]{:S(2)}) collective-permute-start(bf16[128,1536]{1,0:T(8,128)(2,1)S(1)} %add_convert_fusion.27), channel_id=1, source_target_pairs={{0,4},{2,6},{4,0},{6,2},{8,12},{10,14},{12,8},{14,10},{1,5},{3,7},... | collective-permute-start | bytes 1179656 | tf_op jit(solution)/shard_map/ppermute | solution.py:56
  93.3 17.9 %collective-permute-start.28 = (bf16[128,1536]{1,0:T(8,128)(2,1)S(1)}, bf16[128,1536]{1,0:T(8,128)(2,1)S(1)}, u32[]{:S(2)}, u32[]{:S(2)}) collective-permute-start(bf16[128,1536]{1,0:T(8,128)(2,1)S(1)} %copy-done.203), channel_id=1, source_target_pairs={{0,13},{1,12},{2,15},{3,14},{4,9},{5,8},{6,11},{7,10},{8,5},{9,4},... | collective-permute-start | bytes 1179656 | tf_op jit(solution)/shard_map/ppermute | solution.py:67
  113.8 21.8 %collective-permute-start.29 = (bf16[128,1536]{1,0:T(8,128)(2,1)}, bf16[128,1536]{1,0:T(8,128)(2,1)}, u32[]{:S(2)}, u32[]{:S(2)}) collective-permute-start(bf16[128,1536]{1,0:T(8,128)(2,1)} %add_convert_fusion.24), channel_id=1, source_target_pairs={{0,16},{1,17},{2,18},{3,19},{4,20},{5,21},{6,22},{7,23},{8,24},{9,... | collective-permute-start | bytes 1179656 | tf_op jit(solution)/shard_map/ppermute | solution.py:1030
  119.1 16.5 %collective-permute-start.34 = (bf16[128,1536]{1,0:T(8,128)(2,1)S(1)}, bf16[128,1536]{1,0:T(8,128)(2,1)}, u32[]{:S(2)}, u32[]{:S(2)}) collective-permute-start(bf16[128,1536]{1,0:T(8,128)(2,1)S(1)} %copy-done.75), channel_id=1, source_target_pairs={{0,8},{2,10},{4,12},{6,14},{8,0},{10,2},{12,4},{14,6},{1,9},{3,11}... | collective-permute-start | bytes 1179656 | tf_op jit(solution)/shard_map/ppermute | solution.py:56
  225.3 16.6 %collective-permute-start.55 = (bf16[128,1536]{1,0:T(8,128)(2,1)}, bf16[128,1536]{1,0:T(8,128)(2,1)S(1)}, u32[]{:S(2)}, u32[]{:S(2)}) collective-permute-start(bf16[128,1536]{1,0:T(8,128)(2,1)} %get-tuple-element.924), channel_id=1, source_target_pairs={{0,8},{2,10},{4,12},{6,14},{8,0},{10,2},{12,4},{14,6},{1,9},{3,11}... | collective-permute-start | bytes 1179656 | tf_op jit(solution)/shard_map/ppermute | solution.py:56
  246.0 18.5 %collective-permute-start.62 = (bf16[128,1536]{1,0:T(8,128)(2,1)S(1)}, bf16[128,1536]{1,0:T(8,128)(2,1)S(1)}, u32[]{:S(2)}, u32[]{:S(2)}) collective-permute-start(bf16[128,1536]{1,0:T(8,128)(2,1)S(1)} %copy-done.202), channel_id=1, source_target_pairs={{0,13},{1,12},{2,15},{3,14},{4,9},{5,8},{6,11},{7,10},{8,5},{9,4},... | collective-permute-start | bytes 1179656 | tf_op jit(solution)/shard_map/ppermute | solution.py:67
  292.7 18.5 %collective-permute-start.70 = (bf16[128,1664]{1,0:T(8,128)(2,1)S(1)}, bf16[128,1664]{1,0:T(8,128)(2,1)S(1)}, u32[]{:S(2)}, u32[]{:S(2)}) collective-permute-start(bf16[128,1664]{1,0:T(8,128)(2,1)S(1)} %collective-permute-done.66.refs_0_), channel_id=1, source_target_pairs={{0,1},{1,0},{2,3},{3,2},{4,5},{5,4},{6,7},{7,6},{8,9},{9,8},{10,11... | collective-permute-start | bytes 1277960 | tf_op jit(solution)/shard_map/ppermute | solution.py:56
  293.7 17.5 %collective-permute-start.69 = (bf16[128,1536]{1,0:T(8,128)(2,1)S(1)}, bf16[128,1536]{1,0:T(8,128)(2,1)S(1)}, u32[]{:S(2)}, u32[]{:S(2)}) collective-permute-start(bf16[128,1536]{1,0:T(8,128)(2,1)S(1)} %copy-done.200), channel_id=1, source_target_pairs={{16,0},{17,1},{18,2},{19,3},{20,4},{21,5},{22,6},{23,7},{24,8},{25... | collective-permute-start | bytes 1179656 | tf_op jit(solution)/shard_map/ppermute | solution.py:1126
  358.2 20.9 %collective-permute-start.82 = (bf16[128,1536]{1,0:T(8,128)(2,1)}, bf16[128,1536]{1,0:T(8,128)(2,1)}, u32[]{:S(2)}, u32[]{:S(2)}) collective-permute-start(bf16[128,1536]{1,0:T(8,128)(2,1)} %add_convert_fusion.16), channel_id=1, source_target_pairs={{0,4},{2,6},{4,0},{6,2},{8,12},{10,14},{12,8},{14,10},{1,5},{3,7},... | collective-permute-start | bytes 1179656 | tf_op jit(solution)/shard_map/ppermute | solution.py:56
  360.1 18.9 %collective-permute-start.83 = (bf16[128,1536]{1,0:T(8,128)(2,1)}, bf16[128,1536]{1,0:T(8,128)(2,1)}, u32[]{:S(2)}, u32[]{:S(2)}) collective-permute-start(bf16[128,1536]{1,0:T(8,128)(2,1)} %add_convert_fusion.15), channel_id=1, source_target_pairs={{0,8},{2,10},{4,12},{6,14},{8,0},{10,2},{12,4},{14,6},{1,9},{3,11}... | collective-permute-start | bytes 1179656 | tf_op jit(solution)/shard_map/ppermute | solution.py:56
  392.0 17.8 %collective-permute-start.87 = (bf16[128,1536]{1,0:T(8,128)(2,1)S(1)}, bf16[128,1536]{1,0:T(8,128)(2,1)S(1)}, u32[]{:S(2)}, u32[]{:S(2)}) collective-permute-start(bf16[128,1536]{1,0:T(8,128)(2,1)S(1)} %copy-done.195), channel_id=1, source_target_pairs={{0,8},{2,10},{4,12},{6,14},{8,0},{10,2},{12,4},{14,6},{1,9},{3,11}... | collective-permute-start | bytes 1179656 | tf_op jit(solution)/shard_map/ppermute | solution.py:56
  445.1 19.0 %collective-permute-start.96 = (bf16[128,1536]{1,0:T(8,128)(2,1)S(1)}, bf16[128,1536]{1,0:T(8,128)(2,1)S(1)}, u32[]{:S(2)}, u32[]{:S(2)}) collective-permute-start(bf16[128,1536]{1,0:T(8,128)(2,1)S(1)} %collective-permute-done.93.refs_0_.refs_4_), channel_id=1, source_target_pairs={{0,1},{1,0},{2,3},{3,2},{4,5},{5,4},{6,7},{7,6},{8,9},{9,8},{10,11... | collective-permute-start | bytes 1179656 | tf_op jit(solution)/shard_map/ppermute | solution.py:56
  482.2 24.7 %collective-permute-start.106 = (bf16[128,1536]{1,0:T(8,128)(2,1)S(1)}, bf16[128,1536]{1,0:T(8,128)(2,1)S(1)}, u32[]{:S(2)}, u32[]{:S(2)}) collective-permute-start(bf16[128,1536]{1,0:T(8,128)(2,1)S(1)} %add_convert_fusion.9), channel_id=1, source_target_pairs={{0,4},{2,6},{4,0},{6,2},{8,12},{10,14},{12,8},{14,10},{1,5},{3,7},... | collective-permute-start | bytes 1179656 | tf_op jit(solution)/shard_map/ppermute | solution.py:56
  484.3 22.6 %collective-permute-start.107 = (bf16[128,1536]{1,0:T(8,128)(2,1)S(1)}, bf16[128,1536]{1,0:T(8,128)(2,1)S(1)}, u32[]{:S(2)}, u32[]{:S(2)}) collective-permute-start(bf16[128,1536]{1,0:T(8,128)(2,1)S(1)} %add_convert_fusion.8), channel_id=1, source_target_pairs={{0,8},{2,10},{4,12},{6,14},{8,0},{10,2},{12,4},{14,6},{1,9},{3,11}... | collective-permute-start | bytes 1179656 | tf_op jit(solution)/shard_map/ppermute | solution.py:56
  486.2 20.7 %collective-permute-start.108 = (bf16[128,1536]{1,0:T(8,128)(2,1)S(1)}, bf16[128,1536]{1,0:T(8,128)(2,1)S(1)}, u32[]{:S(2)}, u32[]{:S(2)}) collective-permute-start(bf16[128,1536]{1,0:T(8,128)(2,1)S(1)} %add_convert_fusion.7), channel_id=1, source_target_pairs={{0,1},{1,0},{2,3},{3,2},{4,5},{5,4},{6,7},{7,6},{8,9},{9,8},{10,11... | collective-permute-start | bytes 1179656 | tf_op jit(solution)/shard_map/ppermute | solution.py:56
  486.3 20.6 %collective-permute-start.109 = (bf16[128,1536]{1,0:T(8,128)(2,1)S(1)}, bf16[128,1536]{1,0:T(8,128)(2,1)S(1)}, u32[]{:S(2)}, u32[]{:S(2)}) collective-permute-start(bf16[128,1536]{1,0:T(8,128)(2,1)S(1)} %copy-done.196), channel_id=1, source_target_pairs={{0,13},{1,12},{2,15},{3,14},{4,9},{5,8},{6,11},{7,10},{8,5},{9,4},... | collective-permute-start | bytes 1179656 | tf_op jit(solution)/shard_map/ppermute | solution.py:67
  556.6 21.2 %collective-permute-start.126 = (bf16[960,1152]{1,0:T(8,128)(2,1)S(1)}, bf16[960,1152]{1,0:T(8,128)(2,1)S(1)}, u32[]{:S(2)}, u32[]{:S(2)}) collective-permute-start(bf16[960,1152]{1,0:T(8,128)(2,1)S(1)} %copy-done.191), channel_id=1, source_target_pairs={{0,2},{2,0},{4,6},{6,4},{8,10},{10,8},{12,14},{14,12},{1,3},{3,1},... | collective-permute-start | bytes 6635528 | tf_op jit(solution)/shard_map/ppermute | solution.py:56
  558.9 18.8 %collective-permute-start.124 = (bf16[192,1152]{1,0:T(8,128)(2,1)S(1)}, bf16[192,1152]{1,0:T(8,128)(2,1)S(1)}, u32[]{:S(2)}, u32[]{:S(2)}) collective-permute-start(bf16[192,1152]{1,0:T(8,128)(2,1)S(1)} %get-tuple-element.1371), channel_id=1, source_target_pairs={{0,1},{1,0},{2,3},{3,2},{4,5},{5,4},{6,7},{7,6},{8,9},{9,8},{10,11... | collective-permute-start | bytes 1327112 | tf_op jit(solution)/shard_map/ppermute | solution.py:56
  559.2 18.6 %collective-permute-start.125 = (bf16[192,1152]{1,0:T(8,128)(2,1)S(1)}, bf16[192,1152]{1,0:T(8,128)(2,1)S(1)}, u32[]{:S(2)}, u32[]{:S(2)}) collective-permute-start(bf16[192,1152]{1,0:T(8,128)(2,1)S(1)} %get-tuple-element.1372), channel_id=1, source_target_pairs={{0,4},{2,6},{4,0},{6,2},{8,12},{10,14},{12,8},{14,10},{1,5},{3,7},... | collective-permute-start | bytes 1327112 | tf_op jit(solution)/shard_map/ppermute | solution.py:56
  579.9 19.8 %collective-permute-start.129 = (bf16[192,1152]{1,0:T(8,128)(2,1)S(1)}, bf16[192,1152]{1,0:T(8,128)(2,1)S(1)}, u32[]{:S(2)}, u32[]{:S(2)}) collective-permute-start(bf16[192,1152]{1,0:T(8,128)(2,1)S(1)} %get-tuple-element.1394), channel_id=1, source_target_pairs={{0,1},{1,0},{2,3},{3,2},{4,5},{5,4},{6,7},{7,6},{8,9},{9,8},{10,11... | collective-permute-start | bytes 1327112 | tf_op jit(solution)/shard_map/ppermute | solution.py:56
  580.4 20.8 %collective-permute-start.128 = (bf16[192,1152]{1,0:T(8,128)(2,1)S(1)}, bf16[192,1152]{1,0:T(8,128)(2,1)S(1)}, u32[]{:S(2)}, u32[]{:S(2)}) collective-permute-start(bf16[192,1152]{1,0:T(8,128)(2,1)S(1)} %get-tuple-element.1395), channel_id=1, source_target_pairs={{0,8},{2,10},{4,12},{6,14},{8,0},{10,2},{12,4},{14,6},{1,9},{3,11}... | collective-permute-start | bytes 1327112 | tf_op jit(solution)/shard_map/ppermute | solution.py:56
  581.8 19.4 %collective-permute-start.127 = (bf16[192,1152]{1,0:T(8,128)(2,1)S(1)}, bf16[192,1152]{1,0:T(8,128)(2,1)S(1)}, u32[]{:S(2)}, u32[]{:S(2)}) collective-permute-start(bf16[192,1152]{1,0:T(8,128)(2,1)S(1)} %get-tuple-element.1396), channel_id=1, source_target_pairs={{0,4},{2,6},{4,0},{6,2},{8,12},{10,14},{12,8},{14,10},{1,5},{3,7},... | collective-permute-start | bytes 1327112 | tf_op jit(solution)/shard_map/ppermute | solution.py:56
  (313 other events, 3782.1 us)

commit v4 on v3

--- a/solution.py
+++ b/solution.py
@@ -359,19 +359,25 @@
     rows = block // 2
     shard = lax.axis_index("shard")
     first = jnp.where(lax.axis_index("section") == 0, 1.0, 0.0)
-    for own in (False, True):
-        to_qkv, to_heads = (qkv, heads) if own else (qkv_other, heads_other)
-        ends, begin = geometry(lens, 0, shard if own else 1 - shard, rows, block)
-        pick = selection(begin, rows, block)
-        values = dot_nn((pick * first).astype(bf16), block_rows())
-        allowed = sequence_mask(ends, begin, rows, block)
-        value = head_group(normed_rows(values, gain[...]), allowed, weights, to_qkv, to_heads)
-        if own:
-            inputs[...] = values.astype(bf16)
-            part[...] = values + value
-            mask[...] = allowed
-        else:
-            sent[...] = value.astype(bf16)
+    sides = []
+    for side in (shard, 1 - shard):
+        ends, begin = geometry(lens, 0, side, rows, block)
+        sides.append((selection(begin, rows, block) * first, sequence_mask(ends, begin, rows, block)))
+    values = dot_nn(jnp.concatenate([pick for pick, _ in sides], axis=0).astype(bf16), block_rows())
+    inputs[...] = values[:rows].astype(bf16)
+    mask[...] = sides[0][1]
+    normed = normed_rows(values, gain[...])
+    *projections, w_out = weights
+    projected = jnp.concatenate([dot_nn(normed, w()).astype(bf16) for w in projections], axis=1)
+    both_heads = []
+    for i, (to_qkv, to_heads) in enumerate(((qkv, heads), (qkv_other, heads_other))):
+        to_qkv[...] = projected[i * rows : (i + 1) * rows]
+        _, _, value, probs = group_probs(to_qkv[...], sides[i][1])
+        to_heads[...] = spread_heads(dot_nn(probs.astype(bf16), value).astype(bf16), rows)
+        both_heads.append(to_heads[...])
+    result = dot_nt(jnp.concatenate(both_heads, axis=0), w_out())
+    part[...] = values[:rows] + result[:rows]
+    sent[...] = result[rows:].astype(bf16)
 
 
 def opening(lens, tokens, gain, weights):
@@ -435,30 +441,16 @@
 
 
 def by_halves(refs):
-    *own, packed = refs
-    widths = [w.shape[1] for w in own]
-    firsts = [sum(widths[:i]) for i in range(4)]
+    *own, packed, packed_out = refs
+    widths = [w.shape[1] for w in own[:3]]
+    firsts = [sum(widths[:i]) for i in range(3)]
     other = [lambda f=f, w=w: packed[:, f : f + w] for f, w in zip(firsts, widths)]
-    return [lambda w=w: w[...] for w in own], other
-
-
-def other_heads_body(inputs, mask, gain, wq, wk, wv, wo, packed, qkv, heads):
-    _, weights = by_halves((wq, wk, wv, wo, packed))
-    head_group(normed_rows(wide(inputs[...]), gain[...]), mask[...], weights, qkv, heads)
-
-
-def other_heads(inputs, mask, gain, weights, packed):
-    rows = inputs.shape[0]
-    width, out = sum(w.shape[1] for w in weights[:3]), weights[3].shape[1]
-    shapes = [like((rows, width), bf16), like((rows, out), bf16)]
-    return on_device(
-        other_heads_body, shapes, [inputs, mask, gain], 2 * rows * packed.size, kept=[*weights, packed]
-    )
+    return [lambda w=w: w[...] for w in own], [*other, lambda: packed_out[...]]
 
 
 def attention_body(fresh, arriving, mask, extra, gain, gain_two, *refs):
-    own, other = by_halves(refs[:5])
-    inputs, hidden, payload, qkv0, qkv1, heads0, heads1 = refs[5:]
+    own, other = by_halves(refs[:6])
+    inputs, hidden, payload, qkv0, qkv1, heads0, heads1 = refs[6:]
     rows = fresh[...] + arriving[...]
     inputs[...] = rows
     total = wide(rows)
@@ -479,14 +471,14 @@
         like((rows, width), bf16), like((rows, width), bf16), like((rows, out), bf16), like((rows, out), bf16),
     ]
     args = [fresh, arriving, mask, extra, gain, gain_two]
-    outs = on_device(attention_body, shapes, args, 4 * rows * packed.size, kept=[*weights, packed])
+    outs = on_device(attention_body, shapes, args, 6 * rows * packed[0].size, kept=[*weights, *packed])
     inputs, hidden, payload, qkv0, qkv1, heads0, heads1 = outs
     return inputs, hidden, payload, [(qkv0, heads0), (qkv1, heads1)]
 
 
 def attention_back_body(grad, grad_two, inputs, hidden, mask, q0, q1, gain, gain_two, *refs):
-    own, other = by_halves(refs[:5])
-    grad_input, grad_input_low, grad_low, normed, g0, g1, gain_grad, gain_two_grad = refs[5:]
+    own, other = by_halves(refs[:6])
+    grad_input, grad_input_low, grad_low, normed, g0, g1, gain_grad, gain_two_grad = refs[6:]
     rows = inputs.shape[0]
     values = wide(inputs[...])
     normed[...] = normed_rows(values, gain[...])
@@ -527,7 +519,7 @@
         like((1, model), f32), like((1, model), f32),
     ]
     args = [grad, grad_two, inputs, hidden, mask, *projected, gain, gain_two]
-    return on_device(attention_back_body, shapes, args, 8 * rows * packed.size, kept=[*weights, packed])
+    return on_device(attention_back_body, shapes, args, 12 * rows * packed[0].size, kept=[*weights, *packed])
 
 
 def place(copies, pieces, *targets):
@@ -966,37 +958,43 @@
     def mate_places(places):
         return [p ^ (2 * mate_bit) for p in places]
 
-    def placed(own, m):
+    def parted(own):
         half = model // shards
-        kept = lax.dynamic_slice_in_dim(own, shard * half, half, 1)
         given = lax.dynamic_slice_in_dim(own, (1 - shard) * half, half, 1)
-        got = swap(given, cube.z)
+        return lax.dynamic_slice_in_dim(own, shard * half, half, 1), given.astype(bf16)
+
+    def placed(parts, m):
+        kept, given = parts
+        got = swap(given, cube.z).astype(kept.dtype)
         low = jnp.where(shard == 0, kept, got)
         high = jnp.where(shard == 0, got, kept)
         return lax.dynamic_slice_in_dim(
             jnp.concatenate([low, high, low, high], axis=0), (block_rows - starts[m]) % block_rows, block_rows, 0
         )
 
-    route_cols = [routes[0, m].T for m in range(2)]
-    gate_cols = [gates[0, m].T for m in range(2)]
     cot_own, cot_other = turned_block(lengths, cotangent)
+    own_near = [swap(cot_own, d) for d in (cube.x, cube.y)] if whole_blocks else []
     opened, mask0 = opening(lengths, tokens, gain_one, weights)
-    settled = [tokens, cotangent, route_cols, gate_cols]
-    mate_w = [swap(w, cube.core) for w in expert_w] if whole_blocks else []
-    opened, qkv_slices, cots, settled, mate_w = together(
-        (opened, qkv_slices, (cot_own, cot_other), settled, mate_w)
+    settled = [tokens, cotangent, routes, gates]
+    mates = [swap(expert_w[0], cube.core)] if whole_blocks else []
+    opened, qkv_slices, own_near, cot_other, settled, mates, expert_w = together(
+        (opened, qkv_slices, own_near, cot_other, settled, mates, expert_w)
     )
     inputs, part, qkv, heads, sent = opened
-    cot_own, cot_other = cots
-    own_near = [swap(cot_own, d) for d in (cube.x, cube.y)] if whole_blocks else []
+    *settled, route_rows, gate_rows = settled
+    settled += [[t[0, m].T for m in range(2)] for t in (route_rows, gate_rows)]
+    other_near = [swap(cot_other, d) for d in (cube.x, cube.y)] if whole_blocks else []
     if whole_blocks:
-        expert_w = pinned(list(zip(expert_w, mate_w)), (1, 1, 0))
-    arrived, own_near, settled, expert_w = together(
-        (swap(sent, cube.z), own_near, settle(lengths, *settled), expert_w)
+        mates.append(swap(expert_w[1], cube.core))
+    arrived, other_near, settled, mates, expert_w = together(
+        (swap(sent, cube.z), other_near, settle(lengths, *settled), mates, expert_w)
     )
     fresh1, cot1, mask1, extra0, extra1, starts = settled
     hidden, payload = joined(part, arrived, gain_two, extra0)
     if whole_blocks:
+        payload, expert_w, mates = together((payload, expert_w, mates))
+        mates.append(swap(expert_w[2], cube.core))
+        expert_w = pinned(list(zip(expert_w, mates)), (1, 1, 0))
         mixture = Blocks(cube, expert_w)
         plane = []
 
@@ -1020,45 +1018,38 @@
 
     def first_choice(*both_micros):
         mids.append(chosen(both_micros[2:], both_micros[:2]))
+        mids.append(chosen(both_micros[:2], both_micros[2:]))
         return mids
 
     choice = (lambda: [mask0, extra0, mask1, extra1], first_choice)
     total = mixture.total(results, [both((lambda: qkv_near, first_exchange), choice) if whole_blocks else choice])
     result0 = (hidden + total).astype(bf16)
     if whole_blocks:
-        result0, qkv_near, out_slices, cot_other = together((result0, qkv_near, out_slices, cot_other))
+        result0, qkv_near, out_slices = together((result0, qkv_near, out_slices))
         arriving = lax.ppermute(result0, "section", [(0, 1)])
         out_near = [out_slices] + [swap(out_slices, d) for d in (cube.x, cube.y, ("dp", mask))]
-        other_near = [swap(cot_other, d) for d in (cube.x, cube.y)]
-        arriving, out_near, other_near, weights = together((arriving, out_near, other_near, pinned(weights)))
-        qkv_mates, out_mates = first_mates, [swap(t, cube.core) for t in out_near]
         all_places = [*plane_places, far_places[0]]
-        width = qkv_slices.shape[1]
-        spans, pieces = [], []
-        for group, places, column in (
-            (qkv_near, all_places, 0), (qkv_mates, mate_places(all_places), 0),
-            (out_near, all_places, width), (out_mates, mate_places(all_places), width),
-        ):
-            pieces += group
-            spans += [(p, half_share, column) for p in places]
-        packed = put_together(pieces, spans, (model, width + out_slices.shape[1]))
+        places = [*all_places, *mate_places(all_places)]
+
+        def assembled(pieces):
+            spans = [(p, half_share, 0) for p in places]
+            return put_together(pieces, spans, (model, pieces[0].shape[1]))
+
+        arriving, out_near, weights, qkv_packed = together(
+            (arriving, out_near, pinned(weights), assembled([*qkv_near, *first_mates]))
+        )
+        packed = [qkv_packed, assembled([*out_near, *[swap(t, cube.core) for t in out_near]])]
     else:
         arriving = lax.ppermute(result0, "section", [(0, 1)])
-        packed = lax.all_gather(
-            jnp.concatenate([qkv_slices, swap(out_slices, cube.z)], axis=1), "dp", axis=0, tiled=True
-        )
-    state0 = [inputs, hidden, mask0, None, saved]
-
-    mask_mid, extra_mid = mids[0]
+        packed = [
+            lax.all_gather(t, "dp", axis=0, tiled=True) for t in (qkv_slices, swap(out_slices, cube.z))
+        ]
+
+    (mask_mid, extra_mid), (mask_last, extra_last) = mids
 
     inputs1, hidden1, payload, groups1 = attention_forward(
         fresh1, arriving, mask_mid, gain_one, gain_two, extra_mid, weights, packed
     )
-    def first_groups(*args):
-        groups = other_heads(*args)
-        state0[3] = [(qkv, heads), tuple(groups)]
-        return groups
-
     micro_mid = 1 - section
     late = []
 
@@ -1066,10 +1057,10 @@
         late.extend([swap(x0, cube.y), swap(y1, cube.x)])
         return late
 
-    side = [(lambda: [inputs, mask0, gain_one, weights, packed], first_groups)]
+    side = []
     if whole_blocks:
         (x0, y0), (x1, y1) = own_near, other_near
-        side += [None, (lambda: [x0, y1], cot_far)]
+        side = [None, None, (lambda: [x0, y1], cot_far)]
     results, saved1 = mixture.forward(payload, micro_mid, side)
 
     grad0 = cot_own
@@ -1086,9 +1077,8 @@
     slot2 = []
 
     def last_attention(arriving):
-        zero = jnp.zeros((rows, model), bf16)
         slot2.extend(
-            attention_forward(zero, arriving, mask1, gain_one, gain_two, extra1, weights, packed)
+            attention_forward(inputs, arriving, mask_last, gain_one, gain_two, extra_last, weights, packed)
         )
         return slot2
 
@@ -1127,9 +1117,8 @@
         return returned
 
     side = [(lambda: [grad_two], first_turn), None, (lambda: [turn0[1]], first_return)]
-    results2, saved2 = mixture.forward(payload, 1, side)
+    results2, saved2 = mixture.forward(payload, section, side)
     coming = returned[0]
-    state2 = [inputs2, hidden2, mask1, groups2, saved2]
 
     sums = [None, None]
     if whole_blocks:
@@ -1139,23 +1128,28 @@
         results2 = [*results2, (lambda: [corner], lambda t: t)]
     else:
         coming, results2, saved2 = together((coming, results2, saved2))
-    state2[4] = saved2
     grad1 = coming + cot1
-    state_mid = chosen(state0, state2)
-    back_results, keeps1 = mixture.backward(grad1, section, state_mid[4])
+    state2 = [inputs2, hidden2, mask_last, groups2, saved2]
+    back_results, keeps1 = mixture.backward(grad1, section, saved2)
+    def run_both(*works):
+        works = [w for w in works if w]
+        return both(*works) if works else None
+
     placings = {}
 
     def placing(name, micro, own):
         def work(rows):
-            placings[name, micro] = placed(rows, micro)
+            placings[name, micro] = placed(parted(rows), micro)
             return placings[name, micro]
 
         return lambda: [own()], work
 
-    hidden_work, down_work = mixture.weight_sums([keeps0, keeps1], sums)
-    grad_two = mixture.total(back_results, [placing("out", 0, lambda: chosen(result0, result1)), hidden_work])
+    hidden_work, _ = mixture.weight_sums([keeps0], sums)
+    _, down_work = mixture.weight_sums([keeps0, keeps1], sums)
+    place_first = placing("out", 0, lambda: chosen(result0, result1))
+    grad_two = mixture.total(back_results, [run_both(place_first, hidden_work)])
     grad_two, down_inputs = together((grad_two, down_work[0]())) if down_work else (grad_two, ())
-    turn1 = attention_turn(grad1, grad_two, state_mid)
+    turn1 = attention_turn(grad1, grad_two, state2)
     if whole_blocks:
         low, results2[:3] = together((turn1[1], list(results2[:3])))
     else:
@@ -1170,23 +1164,30 @@
         last_total.append(mixture.total_finish(state[0] if len(state) == 1 else state))
         return last_total
 
-    side = [None, None, (lambda: [state] if not whole_blocks else list(state), finish_last)]
+    hidden_work, _ = mixture.weight_sums([keeps1], sums)
+    side = [None, None, run_both((lambda: [state] if not whole_blocks else list(state), finish_last), hidden_work)]
     back_results, keeps2 = mixture.backward(grad2, 1 - section, saved1, side)
     result2 = (hidden2 + last_total[0]).astype(bf16)
     placing_out = placing("out", 1, lambda: chosen(result1, result2))
     placing_grad = placing("grad", 0, lambda: chosen(turn1[0], turn0[0]))
     hidden_end, down_end = mixture.weight_sums([keeps2], sums, True)
-    ends = [w for w in (hidden_end, down_end) if w]
-    grad_two = mixture.total(back_results, [both(placing_out, placing_grad), both(*ends)])
-    expert_sums = [*sums[0][:2], sums[1][0]]
-    others = [t for group in sums for t in group if t.dtype == bf16]
-
-    inputs, hidden, _, groups, _ = state1
-    heads_all = [[t[2][3][g] for t in (turn0, turn1)] + [groups[g][1]] for g in range(shards)]
-    grad_two, others = together((grad_two, others))
+    waiting = []
+
+    def part_both(out, grad):
+        waiting.extend([parted(out), parted(grad)])
+        return waiting
+
+    part_work = (lambda: [chosen(result1, result2), chosen(turn1[0], turn0[0])], part_both)
+    grad_two = mixture.total(back_results, [part_work, run_both(hidden_end or down_end)])
+
+    _, hidden, _, groups, _ = state1
+    others = [t for t in sums[0] if t.dtype == bf16]
+    grad_two, others, waiting = together((grad_two, others, waiting))
     others = [swap(t, cube.core) for t in others]
+    placings["out", 1], placings["grad", 0] = placed(waiting[0], 1), placed(waiting[1], 0)
+    heads_all = [[groups1[g][1], groups2[g][1], groups1[g][1]] for g in range(shards)]
     out_pairs = owned_products(cube, [turn0[2][1], turn1[2][1]], heads_all, (grad2, grad_two, hidden, gain_two))
-    out_pairs, others = together((out_pairs, others))
+    out_pairs, others, placings = together((out_pairs, others, placings))
     turn2 = []
 
     def last_turn(grad_two):
@@ -1209,10 +1210,6 @@
         own, *near, corner = blocks(mine, *other)
         return arrived, corner, near, own
 
-    def run_both(*works):
-        works = [w for w in works if w]
-        return both(*works) if works else None
-
     out_state = sums_start(out_pairs, [(lambda: [grad_two], last_turn)])
     turns = (turn0, turn1, turn2)
     factors = [t[2] for t in turns]
@@ -1227,15 +1224,23 @@
     grad_o = reduce_finish(cube, *out_state, [(lambda: [], qkv_products)])
     qkv_pairs, grad_o = together((qkv_pairs, grad_o))
 
-    def last_sums(*others):
-        if others:
-            (gate, up), down = jnp.split(others[0], 2, axis=1), others[1]
-            expert_sums[:] = [mine + wide(other) for mine, other in zip(expert_sums, (gate, up, down))]
+    expert_sums = list(sums[0][:2])
+
+    def hidden_sums(*others):
+        for other in others:
+            expert_sums[:] = [mine + wide(t) for mine, t in zip(expert_sums, jnp.split(other, 2, axis=1))]
         return expert_sums
 
+    def down_sums(*others):
+        for other in others:
+            expert_sums[2] = expert_sums[2] + wide(swap(other, cube.core))
+        return expert_sums[2]
+
     last_rows = placing("grad", 1, lambda: chosen(turn2[0], turn1[0]))
-    qkv_state = sums_start(qkv_pairs, [both(last_rows, (lambda: others, last_sums))])
-    grad_qkv = reduce_finish(cube, *qkv_state)
+    last_end = down_end if whole_blocks else None
+    qkv_state = sums_start(qkv_pairs, [run_both(last_rows, (lambda: others, hidden_sums), last_end)])
+    expert_sums.append(sums[1][0])
+    grad_qkv = reduce_finish(cube, *qkv_state, [(lambda: sums[1][1:], down_sums)])
     gate_total, up_total, down_total = expert_sums
     width = q_weight.shape[2]
     grad_q = grad_qkv[:, :width]

time: 611 us -> 596 us (0.975)
  other arithmetic: 43.3 us -> 34.9 us
  starting transfers between devices: 146 us -> 139 us
    ppermute x8, waiting for transfers between devices: 21.8 us -> 36.5 us  [across(): return lax.ppermute(value, ('dp', 'shard'), pairs)]
    ppermute x119, waiting for transfers between devices: 112 us -> 104 us  [swap(): lax.ppermute(value, axis, [(i, i ^ bit) for i in range(lax.axis_size(axis...]
    ppermute x119, starting transfers between devices: 118 us -> 110 us  [swap(): lax.ppermute(value, axis, [(i, i ^ bit) for i in range(lax.axis_size(axis...]
    pallas_call x34 -> x33, Pallas kernels: 161 us -> 156 us  [on_device(): pl.pallas_call(body, out_shape=outs, in_specs=[SMEM] * len(scalars) + [VM...]
    pallas_call x4 -> x5, Pallas kernels: 46.7 us -> 51.3 us  [swept_products(): pl.pallas_call(body, grid=(steps,), out_shape=shapes, in_specs=in_specs,...]
    unnamed x412 -> x370, local copies, waits for them, and re-layouts: 19.7 us -> 18.5 us
  transfers between devices with their start and end apart: 131 -> 131, of which waited for: 52 -> 53; matrix products, arithmetic and copies ran while one was open for 5% -> 4% of each run, Pallas kernels for 35% -> 36%
where the time goes in v4:
time: 596 us; the launch traced here: 590 us
  Pallas kernels  234 us (39%)
  waiting for transfers between devices  149 us (25%)
  starting transfers between devices  139 us (23%)
  other arithmetic  34.9 us (6%)
  local copies, waits for them, and re-layouts  27.9 us (5%)
    pallas_call x33, Pallas kernels, on_device(): pl.pallas_call(body, out_shape=outs, in_specs=[SMEM] * len(scalars) + [VM...  156 us
    ppermute x119, starting transfers between devices, swap(): lax.ppermute(value, axis, [(i, i ^ bit) for i in range(lax.axis_size(axis...  110 us
    ppermute x119, waiting for transfers between devices, swap(): lax.ppermute(value, axis, [(i, i ^ bit) for i in range(lax.axis_size(axis...  104 us
    pallas_call x5, Pallas kernels, swept_products(): pl.pallas_call(body, grid=(steps,), out_shape=shapes, in_specs=in_specs,...  51.3 us
    ppermute x8, waiting for transfers between devices, across(): return lax.ppermute(value, ('dp', 'shard'), pairs)  36.5 us
    unnamed x370, local copies, waits for them, and re-layouts  18.5 us
    ppermute x8, starting transfers between devices, across(): return lax.ppermute(value, ('dp', 'shard'), pairs)  16.7 us
    pallas_call x2, Pallas kernels, owned_products(): pl.pallas_call(functools.partial(owned_body, len(lefts), len(rights), blo...  15.8 us
  transfers between devices with their start and end apart: 131, of which 53 were waited for; matrix products, arithmetic and copies ran while one was open for 4% of the time, Pallas kernels for 36%

profile of v4, /device:TPU:0, one launch (start us, length us, event | category | flops | bytes accessed | tf_op | source)
XLA Modules:
  0.0 589.9 jit_solution(10852773283304634320)
XLA Ops:
  12.3 7.3 %shard_map.222 = (bf16[128,1536]{1,0:T(8,128)(2,1)}, f32[128,1536]{1,0:T(8,128)}, bf16[128,1024]{1,0:T(8,128)(2,1)}, bf16[128,768]{1,0:T(8,128)(2,1)}, bf16[128,...) custom-call(s32[2,1,4]{2,1,0:T(1,128)S(1)} %copy-done.78, ...), custom_call_target="tpu_custom_call" | custom-call | flops 22548578304 | bytes 6144 | tf_op jit(solution)/shard_map/pallas_call | solution.py:280
  76.9 8.7 %collective-permute-done.19.refs_0_ = bf16[192,768]{1,0:T(8,128)(2,1)} collective-permute-done((bf16[192,768]{1,0:T(8,128)(2,1)S(1)}, bf16[192,768]{1,0:T(8,128)(2,1)}, u32[]{:S(2)}, u32[]{:S(2)}) %collective-permute-start.19) | collective-permute-done | bytes 294944 | tf_op jit(solution)/shard_map/ppermute | solution.py:56
  111.0 8.7 %collective-permute-done.30 = bf16[128,1536]{1,0:T(8,128)(2,1)S(1)} collective-permute-done((bf16[128,1536]{1,0:T(8,128)(2,1)S(1)}, bf16[128,1536]{1,0:T(8,128)(2,1)S(1)}, u32[]{:S(2)}, u32[]{:S(2)}) %collective-permute-start.30) | collective-permute-done | bytes 393248 | tf_op jit(solution)/shard_map/ppermute | solution.py:67
  146.8 7.0 %shard_map.233 = (bf16[128,1536]{1,0:T(8,128)(2,1)}, f32[128,1536]{1,0:T(8,128)}, bf16[128,1664]{1,0:T(8,128)(2,1)}, bf16[128,1024]{1,0:T(8,128)(2,1)}, bf16[128...) custom-call(bf16[128,1536]{1,0:T(8,128)(2,1)} %get-tuple-element.712.fresh, ...), custom_call_target="tpu_custom_call" | custom-call | flops 19327352832 | bytes 897024 | tf_op jit(solution)/shard_map/pallas_call | solution.py:280
  194.6 6.4 %shard_map.238 = (bf16[384,768]{1,0:T(8,128)(2,1)}, bf16[384,768]{1,0:T(8,128)(2,1)}, bf16[384,768]{1,0:T(8,128)(2,1)}, bf16[128,1536]{1,0:T(8,128)(2,1)}, bf16[...) custom-call(bf16[1536,768]{1,0:T(8,128)(2,1)S(1)} %copy-done.7, bf16[1536,768]{1,0:T(8,128)(2,1)S(1)} %copy-done.9, ...), custom_call_target="tpu_custom_call" | custom-call | flops 43486543872 | tf_op jit(solution)/shard_map/pallas_call | solution.py:280
  213.9 6.6 %shard_map.239 = (bf16[384,768]{1,0:T(8,128)(2,1)}, bf16[384,768]{1,0:T(8,128)(2,1)}, bf16[384,768]{1,0:T(8,128)(2,1)}, bf16[128,1536]{1,0:T(8,128)(2,1)}, bf16[...) custom-call(bf16[1536,768]{1,0:T(8,128)(2,1)S(1)} %copy-done.7, bf16[1536,768]{1,0:T(8,128)(2,1)S(1)} %copy-done.9, ...), custom_call_target="tpu_custom_call" | custom-call | flops 43486543872 | tf_op jit(solution)/shard_map/pallas_call | solution.py:280
  256.6 7.7 %collective-permute-done.62 = bf16[128,1536]{1,0:T(8,128)(2,1)S(1)} collective-permute-done((bf16[128,1536]{1,0:T(8,128)(2,1)}, bf16[128,1536]{1,0:T(8,128)(2,1)S(1)}, u32[]{:S(2)}, u32[]{:S(2)}) %collective-permute-start.62) | collective-permute-done | bytes 393248 | tf_op jit(solution)/shard_map/ppermute | solution.py:67
  270.7 7.5 %shard_map.243 = (f32[128,1536]{1,0:T(8,128)}, bf16[128,1536]{1,0:T(8,128)(2,1)}, bf16[128,1536]{1,0:T(8,128)(2,1)}, bf16[128,1536]{1,0:T(8,128)(2,1)}, bf16[128...) custom-call(bf16[128,1536]{1,0:T(8,128)(2,1)} %get-tuple-element.1108.refs_0_.grad, ...), custom_call_target="tpu_custom_call" | custom-call | flops 38654705664 | bytes 2961408 | tf_op jit(solution)/shard_map/pallas_call | solution.py:280
  288.5 6.8 %collective-permute-done.67.refs_1_.refs_4_.refs_5_ = bf16[128,1664]{1,0:T(8,128)(2,1)S(1)} collective-permute-done((bf16[128,1664]{1,0:T(8,128)(2,1)S(1)}, bf16[128,1664]{1,0:T(8,128)(2,1)S(1)}, u32[]{:S(2)}, u32[]{:S(2)}) %collective-permute-start.67) | collective-permute-done | bytes 426016 | tf_op jit(solution)/shard_map/ppermute | solution.py:56
  301.2 8.2 %collective-permute-done.69 = bf16[128,1536]{1,0:T(8,128)(2,1)S(1)} collective-permute-done((bf16[128,1536]{1,0:T(8,128)(2,1)S(1)}, bf16[128,1536]{1,0:T(8,128)(2,1)S(1)}, u32[]{:S(2)}, u32[]{:S(2)}) %collective-permute-start.69) | collective-permute-done | bytes 393248 | tf_op jit(solution)/shard_map/ppermute | solution.py:1116
  327.1 6.4 %shard_map.248 = (bf16[384,768]{1,0:T(8,128)(2,1)}, bf16[384,768]{1,0:T(8,128)(2,1)}, bf16[384,768]{1,0:T(8,128)(2,1)}, bf16[128,1536]{1,0:T(8,128)(2,1)}, bf16[...) custom-call(bf16[1536,768]{1,0:T(8,128)(2,1)S(1)} %copy-done.7, bf16[1536,768]{1,0:T(8,128)(2,1)S(1)} %copy-done.9, ...), custom_call_target="tpu_custom_call" | custom-call | flops 43486543872 | tf_op jit(solution)/shard_map/pallas_call | solution.py:280
  338.0 6.6 %shard_map.249 = (bf16[384,768]{1,0:T(8,128)(2,1)}, bf16[384,768]{1,0:T(8,128)(2,1)}, bf16[384,768]{1,0:T(8,128)(2,1)}, bf16[128,1536]{1,0:T(8,128)(2,1)}, bf16[...) custom-call(bf16[1536,768]{1,0:T(8,128)(2,1)S(1)} %copy-done.7, bf16[1536,768]{1,0:T(8,128)(2,1)S(1)} %copy-done.9, ...), custom_call_target="tpu_custom_call" | custom-call | flops 43486543872 | tf_op jit(solution)/shard_map/pallas_call | solution.py:280
  351.0 9.2 %shard_map.252 = (f32[1536,768]{1,0:T(8,128)}, f32[1536,768]{1,0:T(8,128)}) custom-call(bf16[128,1664]{1,0:T(8,128)(2,1)} %get-tuple-element.1239.refs_0_.refs_1_, bf16[128,1664]{1,0:T(8,128)(2,1)} %copy-done.20, bf16[128,1664]{1,0:T(8,128)(2,1)} %copy-done.22, bf16[128,1664]{1,0:T(8,128)(2,1)} %copy-done.24, bf16[128,1664]{1,0:T(8,128)(2,1)} %copy-done.26, ...), custom_call_target="tpu_custom_call" | custom-call | flops 77309411328 | bytes 1024 | tf_op jit(solution)/shard_map/pallas_call | solution.py:670
  383.2 7.7 %shard_map.253 = (f32[128,1536]{1,0:T(8,128)}, bf16[128,1536]{1,0:T(8,128)(2,1)}, bf16[128,1536]{1,0:T(8,128)(2,1)}, bf16[128,1536]{1,0:T(8,128)(2,1)}, bf16[128...) custom-call(bf16[128,1536]{1,0:T(8,128)(2,1)} %copy-done.5, ...), custom_call_target="tpu_custom_call" | custom-call | flops 38654705664 | bytes 2961408 | tf_op jit(solution)/shard_map/pallas_call | solution.py:280
  395.9 11.1 %shard_map.254.refs_12_ = f32[768,1536]{1,0:T(8,128)} custom-call(bf16[128,1536]{1,0:T(8,128)(2,1)} %get-tuple-element.1108.refs_0_.grad, bf16[128,1536]{1,0:T(8,128)(2,1)} %copy-done.53, bf16[128,1536]{1,0:T(8,128)(2,1)} %copy-done.55, bf16[128,1536]{1,0:T(8,128)(2,1)} %get-tuple-element.1111.refs_2_.refs_3_, bf16[128,1536]{1,0:T(8,128)(2,1)} %copy-done.64, ...), custom_call_target="tpu_custom_call" | custom-call | flops 77309411328 | bytes 2048 | tf_op jit(solution)/shard_map/pallas_call | solution.py:670
  424.1 6.4 %shard_map.256 = (bf16[384,768]{1,0:T(8,128)(2,1)}, bf16[384,768]{1,0:T(8,128)(2,1)}, bf16[384,768]{1,0:T(8,128)(2,1)}, bf16[128,1536]{1,0:T(8,128)(2,1)}, bf16[...) custom-call(bf16[1536,768]{1,0:T(8,128)(2,1)S(1)} %copy-done.7, bf16[1536,768]{1,0:T(8,128)(2,1)S(1)} %copy-done.9, ...), custom_call_target="tpu_custom_call" | custom-call | flops 43486543872 | tf_op jit(solution)/shard_map/pallas_call | solution.py:280
  441.4 11.6 %shard_map.258 = (f32[1536,768]{1,0:T(8,128)}, f32[1536,768]{1,0:T(8,128)}) custom-call(bf16[128,1664]{1,0:T(8,128)(2,1)} %get-tuple-element.1178.refs_0_.refs_1_, bf16[128,1664]{1,0:T(8,128)(2,1)} %copy-done.35, bf16[128,1664]{1,0:T(8,128)(2,1)} %copy-done.36, bf16[128,1664]{1,0:T(8,128)(2,1)} %copy-done.37, bf16[128,1664]{1,0:T(8,128)(2,1)} %copy-done.39, ...), custom_call_target="tpu_custom_call" | custom-call | flops 77309411328 | bytes 1024 | tf_op jit(solution)/shard_map/pallas_call | solution.py:670
  453.1 6.4 %shard_map.257 = (bf16[384,768]{1,0:T(8,128)(2,1)}, bf16[384,768]{1,0:T(8,128)(2,1)}, bf16[384,768]{1,0:T(8,128)(2,1)}, bf16[128,1536]{1,0:T(8,128)(2,1)}, bf16[...) custom-call(bf16[1536,768]{1,0:T(8,128)(2,1)S(1)} %copy-done.7, bf16[1536,768]{1,0:T(8,128)(2,1)S(1)} %copy-done.9, ...), custom_call_target="tpu_custom_call" | custom-call | flops 43486543872 | tf_op jit(solution)/shard_map/pallas_call | solution.py:280
  478.2 11.4 %shard_map.260 = (f32[1536,384]{1,0:T(8,128)}, f32[1536,384]{1,0:T(8,128)}, bf16[1536,768]{1,0:T(8,128)(2,1)}) custom-call(bf16[128,1664]{1,0:T(8,128)(2,1)} %get-tuple-element.1239.refs_0_.refs_1_, bf16[128,1664]{1,0:T(8,128)(2,1)} %copy-done.20, bf16[128,1664]{1,0:T(8,128)(2,1)} %copy-done.22, bf16[128,1664]{1,0:T(8,128)(2,1)} %copy-done.24, ...), custom_call_target="tpu_custom_call" | custom-call | flops 77309411328 | bytes 1024 | tf_op jit(solution)/shard_map/pallas_call | solution.py:670
  493.6 7.2 %shard_map.261 = (bf16[576,768]{1,0:T(8,128)(2,1)}, bf16[576,768]{1,0:T(8,128)(2,1)}, bf16[960,768]{1,0:T(8,128)(2,1)}, bf16[960,768]{1,0:T(8,128)(2,1)}) custom-call(bf16[128,1536]{1,0:T(8,128)(2,1)} %get-tuple-element.948.refs_0_, bf16[128,1536]{1,0:T(8,128)(2,1)} %get-tuple-element.1078.refs_1_, bf16[128,768]{1,0:T(8,128)(2,1)} %get-tuple-element.956.refs_2_.refs_4_, ...), custom_call_target="tpu_custom_call" | custom-call | tf_op jit(solution)/shard_map/pallas_call | solution.py:758
  510.3 7.5 %shard_map.262 = (f32[128,1536]{1,0:T(8,128)}, bf16[128,1536]{1,0:T(8,128)(2,1)}, bf16[128,1536]{1,0:T(8,128)(2,1)}, bf16[128,1536]{1,0:T(8,128)(2,1)}, bf16[128...) custom-call(bf16[128,1536]{1,0:T(8,128)(2,1)} %copy-done.4, ...), custom_call_target="tpu_custom_call" | custom-call | flops 38654705664 | bytes 2961408 | tf_op jit(solution)/shard_map/pallas_call | solution.py:280
  523.8 8.6 %shard_map.263 = (bf16[576,1152]{1,0:T(8,128)(2,1)}, bf16[576,1152]{1,0:T(8,128)(2,1)}, bf16[960,1152]{1,0:T(8,128)(2,1)}, bf16[960,1152]{1,0:T(8,128)(2,1)}) custom-call(bf16[128,1536]{1,0:T(8,128)(2,1)} %get-tuple-element.953.refs_0_, bf16[128,1536]{1,0:T(8,128)(2,1)} %get-tuple-element.1276.refs_1_, bf16[128,1536]{1,0:T(8,128)(2,1)} %get-tuple-element.1281.refs_2_, ...), custom_call_target="tpu_custom_call" | custom-call | tf_op jit(solution)/shard_map/pallas_call | solution.py:758
  545.0 8.0 %shard_map.264 = (f32[384,1536]{1,0:T(8,128)}, bf16[384,1536]{1,0:T(8,128)(2,1)}) custom-call(bf16[128,1536]{1,0:T(8,128)(2,1)} %copy-done.4, bf16[128,1536]{1,0:T(8,128)(2,1)} %copy-done.61, bf16[128,1536]{1,0:T(8,128)(2,1)} %copy-done.62, bf16[128,1536]{1,0:T(8,128)(2,1)} %copy-done.63, bf16[128,1536]{1,0:T(8,128)(2,1)} %copy-done.66, ...), custom_call_target="tpu_custom_call" | custom-call | flops 38654705664 | bytes 1024 | tf_op jit(solution)/shard_map/pallas_call | solution.py:670
  578.1 8.9 %collective-permute-done.129 = bf16[192,1152]{1,0:T(8,128)(2,1)S(1)} collective-permute-done((bf16[192,1152]{1,0:T(8,128)(2,1)S(1)}, bf16[192,1152]{1,0:T(8,128)(2,1)S(1)}, u32[]{:S(2)}, u32[]{:S(2)}) %collective-permute-start.129) | collective-permute-done | bytes 442400 | tf_op jit(solution)/shard_map/ppermute | solution.py:67
  (721 shorter events, 393.1 us)
Async XLA Ops:
  4.2 16.8 %collective-permute-start.1 = (bf16[128,1536]{1,0:T(8,128)(2,1)}, bf16[128,1536]{1,0:T(8,128)(2,1)S(1)}, u32[]{:S(2)}, u32[]{:S(2)}) collective-permute-start(bf16[128,1536]{1,0:T(8,128)(2,1)} %get-tuple-element.1108.refs_0_.grad), channel_id=1, source_target_pairs={{0,4},{2,6},{4,0},{6,2},{8,12},{10,14},{12,8},{14,10},{1,5},{3,7},... | collective-permute-start | bytes 1179656 | tf_op jit(solution)/shard_map/ppermute | solution.py:56
  67.1 18.5 %collective-permute-start.16 = (bf16[192,1024]{1,0:T(8,128)(2,1)S(1)}, bf16[192,1024]{1,0:T(8,128)(2,1)S(1)}, u32[]{:S(2)}, u32[]{:S(2)}) collective-permute-start(bf16[192,1024]{1,0:T(8,128)(2,1)S(1)} %collective-permute-done.refs_0_), channel_id=1, source_target_pairs={{0,4},{2,6},{4,0},{6,2},{8,12},{10,14},{12,8},{14,10},{1,5},{3,7},... | collective-permute-start | bytes 1179656 | tf_op jit(solution)/shard_map/ppermute | solution.py:56
  67.7 17.9 %collective-permute-start.17 = (bf16[192,1024]{1,0:T(8,128)(2,1)S(1)}, bf16[192,1024]{1,0:T(8,128)(2,1)S(1)}, u32[]{:S(2)}, u32[]{:S(2)}) collective-permute-start(bf16[192,1024]{1,0:T(8,128)(2,1)S(1)} %collective-permute-done.refs_0_), channel_id=1, source_target_pairs={{0,8},{2,10},{4,12},{6,14},{8,0},{10,2},{12,4},{14,6},{1,9},{3,11}... | collective-permute-start | bytes 1179656 | tf_op jit(solution)/shard_map/ppermute | solution.py:56
  69.1 16.6 %collective-permute-start.18 = (bf16[192,1024]{1,0:T(8,128)(2,1)S(1)}, bf16[192,1024]{1,0:T(8,128)(2,1)S(1)}, u32[]{:S(2)}, u32[]{:S(2)}) collective-permute-start(bf16[192,1024]{1,0:T(8,128)(2,1)S(1)} %collective-permute-done.refs_0_), channel_id=1, source_target_pairs={{0,12},{2,14},{4,8},{6,10},{8,4},{10,6},{12,0},{14,2},{1,13},{3,15... | collective-permute-start | bytes 1179656 | tf_op jit(solution)/shard_map/ppermute | solution.py:56
  99.5 20.2 %collective-permute-start.30 = (bf16[128,1536]{1,0:T(8,128)(2,1)S(1)}, bf16[128,1536]{1,0:T(8,128)(2,1)S(1)}, u32[]{:S(2)}, u32[]{:S(2)}) collective-permute-start(bf16[128,1536]{1,0:T(8,128)(2,1)S(1)} %copy-done.177), channel_id=1, source_target_pairs={{0,13},{1,12},{2,15},{3,14},{4,9},{5,8},{6,11},{7,10},{8,5},{9,4},... | collective-permute-start | bytes 1179656 | tf_op jit(solution)/shard_map/ppermute | solution.py:67
  120.7 19.7 %collective-permute-start.31 = (bf16[128,1536]{1,0:T(8,128)(2,1)}, bf16[128,1536]{1,0:T(8,128)(2,1)}, u32[]{:S(2)}, u32[]{:S(2)}) collective-permute-start(bf16[128,1536]{1,0:T(8,128)(2,1)} %add_convert_fusion.24), channel_id=1, source_target_pairs={{0,16},{1,17},{2,18},{3,19},{4,20},{5,21},{6,22},{7,23},{8,24},{9,... | collective-permute-start | bytes 1179656 | tf_op jit(solution)/shard_map/ppermute | solution.py:1029
  208.9 16.1 %collective-permute-start.51 = (bf16[128,1536]{1,0:T(8,128)(2,1)}, bf16[128,1536]{1,0:T(8,128)(2,1)S(1)}, u32[]{:S(2)}, u32[]{:S(2)}) collective-permute-start(bf16[128,1536]{1,0:T(8,128)(2,1)} %add_convert_fusion.23), channel_id=1, source_target_pairs={{0,4},{2,6},{4,0},{6,2},{8,12},{10,14},{12,8},{14,10},{1,5},{3,7},... | collective-permute-start | bytes 1179656 | tf_op jit(solution)/shard_map/ppermute | solution.py:56
  296.8 16.4 %collective-permute-start.70 = (bf16[128,1664]{1,0:T(8,128)(2,1)S(1)}, bf16[128,1664]{1,0:T(8,128)(2,1)S(1)}, u32[]{:S(2)}, u32[]{:S(2)}) collective-permute-start(bf16[128,1664]{1,0:T(8,128)(2,1)S(1)} %collective-permute-done.66.refs_0_.refs_3_.refs_4_), channel_id=1, source_target_pairs={{0,1},{1,0},{2,3},{3,2},{4,5},{5,4},{6,7},{7,6},{8,9},{9,8},{10,11... | collective-permute-start | bytes 1277960 | tf_op jit(solution)/shard_map/ppermute | solution.py:56
  346.1 20.4 %collective-permute-start.78 = (bf16[128,1536]{1,0:T(8,128)(2,1)}, bf16[128,1536]{1,0:T(8,128)(2,1)S(1)}, u32[]{:S(2)}, u32[]{:S(2)}) collective-permute-start(bf16[128,1536]{1,0:T(8,128)(2,1)} %get-tuple-element.1024), channel_id=1, source_target_pairs={{0,8},{2,10},{4,12},{6,14},{8,0},{10,2},{12,4},{14,6},{1,9},{3,11}... | collective-permute-start | bytes 1179656 | tf_op jit(solution)/shard_map/ppermute | solution.py:56
  348.6 17.9 %collective-permute-start.79 = (bf16[128,1536]{1,0:T(8,128)(2,1)}, bf16[128,1536]{1,0:T(8,128)(2,1)S(1)}, u32[]{:S(2)}, u32[]{:S(2)}) collective-permute-start(bf16[128,1536]{1,0:T(8,128)(2,1)} %get-tuple-element.1025), channel_id=1, source_target_pairs={{0,1},{1,0},{2,3},{3,2},{4,5},{5,4},{6,7},{7,6},{8,9},{9,8},{10,11... | collective-permute-start | bytes 1179656 | tf_op jit(solution)/shard_map/ppermute | solution.py:56
  349.0 17.5 %collective-permute-start.80 = (bf16[128,1536]{1,0:T(8,128)(2,1)}, bf16[128,1536]{1,0:T(8,128)(2,1)S(1)}, u32[]{:S(2)}, u32[]{:S(2)}) collective-permute-start(bf16[128,1536]{1,0:T(8,128)(2,1)} %get-tuple-element.1026), channel_id=1, source_target_pairs={{0,4},{2,6},{4,0},{6,2},{8,12},{10,14},{12,8},{14,10},{1,5},{3,7},... | collective-permute-start | bytes 1179656 | tf_op jit(solution)/shard_map/ppermute | solution.py:56
  390.8 18.5 %collective-permute-start.86 = (bf16[128,1536]{1,0:T(8,128)(2,1)}, bf16[128,1536]{1,0:T(8,128)(2,1)S(1)}, u32[]{:S(2)}, u32[]{:S(2)}) collective-permute-start(bf16[128,1536]{1,0:T(8,128)(2,1)} %get-tuple-element.1087), channel_id=1, source_target_pairs={{16,0},{17,1},{18,2},{19,3},{20,4},{21,5},{22,6},{23,7},{24,8},{25... | collective-permute-start | bytes 1179656 | tf_op jit(solution)/shard_map/ppermute | solution.py:1157
  392.5 15.5 %collective-permute-start.87 = (bf16[128,1536]{1,0:T(8,128)(2,1)S(1)}, bf16[128,1536]{1,0:T(8,128)(2,1)S(1)}, u32[]{:S(2)}, u32[]{:S(2)}) collective-permute-start(bf16[128,1536]{1,0:T(8,128)(2,1)S(1)} %copy-done.175), channel_id=1, source_target_pairs={{0,8},{2,10},{4,12},{6,14},{8,0},{10,2},{12,4},{14,6},{1,9},{3,11}... | collective-permute-start | bytes 1179656 | tf_op jit(solution)/shard_map/ppermute | solution.py:56
  393.4 15.9 %collective-permute-start.88 = (bf16[128,1536]{1,0:T(8,128)(2,1)S(1)}, bf16[128,1536]{1,0:T(8,128)(2,1)S(1)}, u32[]{:S(2)}, u32[]{:S(2)}) collective-permute-start(bf16[128,1536]{1,0:T(8,128)(2,1)S(1)} %copy-done.174), channel_id=1, source_target_pairs={{0,1},{1,0},{2,3},{3,2},{4,5},{5,4},{6,7},{7,6},{8,9},{9,8},{10,11... | collective-permute-start | bytes 1179656 | tf_op jit(solution)/shard_map/ppermute | solution.py:56
  434.1 25.9 %collective-permute-start.96 = (bf16[128,1536]{1,0:T(8,128)(2,1)S(1)}, bf16[128,1536]{1,0:T(8,128)(2,1)S(1)}, u32[]{:S(2)}, u32[]{:S(2)}) collective-permute-start(bf16[128,1536]{1,0:T(8,128)(2,1)S(1)} %collective-permute-done.93.refs_0_.refs_4_), channel_id=1, source_target_pairs={{0,1},{1,0},{2,3},{3,2},{4,5},{5,4},{6,7},{7,6},{8,9},{9,8},{10,11... | collective-permute-start | bytes 1179656 | tf_op jit(solution)/shard_map/ppermute | solution.py:56
  436.0 23.6 %collective-permute-start.97 = (bf16[128,1536]{1,0:T(8,128)(2,1)S(1)}, bf16[128,1536]{1,0:T(8,128)(2,1)S(1)}, u32[]{:S(2)}, u32[]{:S(2)}) collective-permute-start(bf16[128,1536]{1,0:T(8,128)(2,1)S(1)} %add_convert_fusion.13), channel_id=1, source_target_pairs={{0,4},{2,6},{4,0},{6,2},{8,12},{10,14},{12,8},{14,10},{1,5},{3,7},... | collective-permute-start | bytes 1179656 | tf_op jit(solution)/shard_map/ppermute | solution.py:56
  436.4 23.1 %collective-permute-start.98 = (bf16[128,1536]{1,0:T(8,128)(2,1)S(1)}, bf16[128,1536]{1,0:T(8,128)(2,1)S(1)}, u32[]{:S(2)}, u32[]{:S(2)}) collective-permute-start(bf16[128,1536]{1,0:T(8,128)(2,1)S(1)} %add_convert_fusion.12), channel_id=1, source_target_pairs={{0,8},{2,10},{4,12},{6,14},{8,0},{10,2},{12,4},{14,6},{1,9},{3,11}... | collective-permute-start | bytes 1179656 | tf_op jit(solution)/shard_map/ppermute | solution.py:56
  436.7 22.8 %collective-permute-start.99 = (bf16[128,1536]{1,0:T(8,128)(2,1)S(1)}, bf16[128,1536]{1,0:T(8,128)(2,1)S(1)}, u32[]{:S(2)}, u32[]{:S(2)}) collective-permute-start(bf16[128,1536]{1,0:T(8,128)(2,1)S(1)} %add_convert_fusion.11), channel_id=1, source_target_pairs={{0,1},{1,0},{2,3},{3,2},{4,5},{5,4},{6,7},{7,6},{8,9},{9,8},{10,11... | collective-permute-start | bytes 1179656 | tf_op jit(solution)/shard_map/ppermute | solution.py:56
  437.5 22.1 %collective-permute-start.100 = (bf16[128,1536]{1,0:T(8,128)(2,1)S(1)}, bf16[128,1536]{1,0:T(8,128)(2,1)S(1)}, u32[]{:S(2)}, u32[]{:S(2)}) collective-permute-start(bf16[128,1536]{1,0:T(8,128)(2,1)S(1)} %copy-done.172), channel_id=1, source_target_pairs={{0,13},{1,12},{2,15},{3,14},{4,9},{5,8},{6,11},{7,10},{8,5},{9,4},... | collective-permute-start | bytes 1179656 | tf_op jit(solution)/shard_map/ppermute | solution.py:67
  473.2 16.5 %collective-permute-start.104 = (bf16[128,1536]{1,0:T(8,128)(2,1)S(1)}, bf16[128,1536]{1,0:T(8,128)(2,1)S(1)}, u32[]{:S(2)}, u32[]{:S(2)}) collective-permute-start(bf16[128,1536]{1,0:T(8,128)(2,1)S(1)} %add_convert_fusion.9), channel_id=1, source_target_pairs={{0,4},{2,6},{4,0},{6,2},{8,12},{10,14},{12,8},{14,10},{1,5},{3,7},... | collective-permute-start | bytes 1179656 | tf_op jit(solution)/shard_map/ppermute | solution.py:56
  473.3 16.4 %collective-permute-start.105 = (bf16[128,1536]{1,0:T(8,128)(2,1)S(1)}, bf16[128,1536]{1,0:T(8,128)(2,1)S(1)}, u32[]{:S(2)}, u32[]{:S(2)}) collective-permute-start(bf16[128,1536]{1,0:T(8,128)(2,1)S(1)} %add_convert_fusion.8), channel_id=1, source_target_pairs={{0,8},{2,10},{4,12},{6,14},{8,0},{10,2},{12,4},{14,6},{1,9},{3,11}... | collective-permute-start | bytes 1179656 | tf_op jit(solution)/shard_map/ppermute | solution.py:56
  540.9 16.4 %collective-permute-start.121 = (bf16[128,768]{1,0:T(8,128)(2,1)S(1)}, bf16[128,768]{1,0:T(8,128)(2,1)S(1)}, u32[]{:S(2)}, u32[]{:S(2)}) collective-permute-start(bf16[128,768]{1,0:T(8,128)(2,1)S(1)} %dynamic-slice_convert_fusion), channel_id=1, source_target_pairs={{0,1},{1,0},{2,3},{3,2},{4,5},{5,4},{6,7},{7,6},{8,9},{9,8},{10,11... | collective-permute-start | bytes 589832 | tf_op jit(solution)/shard_map/ppermute | solution.py:56
  542.6 15.3 %collective-permute-start.122 = (bf16[192,1152]{1,0:T(8,128)(2,1)S(1)}, bf16[192,1152]{1,0:T(8,128)(2,1)S(1)}, u32[]{:S(2)}, u32[]{:S(2)}) collective-permute-start(bf16[192,1152]{1,0:T(8,128)(2,1)S(1)} %get-tuple-element.1332), channel_id=1, source_target_pairs={{0,8},{2,10},{4,12},{6,14},{8,0},{10,2},{12,4},{14,6},{1,9},{3,11}... | collective-permute-start | bytes 1327112 | tf_op jit(solution)/shard_map/ppermute | solution.py:56
  566.7 20.3 %collective-permute-start.129 = (bf16[192,1152]{1,0:T(8,128)(2,1)S(1)}, bf16[192,1152]{1,0:T(8,128)(2,1)S(1)}, u32[]{:S(2)}, u32[]{:S(2)}) collective-permute-start(bf16[192,1152]{1,0:T(8,128)(2,1)S(1)} %get-tuple-element.1360), channel_id=1, source_target_pairs={{0,13},{1,12},{2,15},{3,14},{4,9},{5,8},{6,11},{7,10},{8,5},{9,4},... | collective-permute-start | bytes 1327112 | tf_op jit(solution)/shard_map/ppermute | solution.py:67
  (293 other events, 3383.8 us)

commit v5 on v4

--- a/solution.py
+++ b/solution.py
@@ -115,9 +115,10 @@
 
 
 def reduce_finish(cube, arrived, corner, near, own, side=()):
-    sent = [low_sum(*corner)] + [low_sum(*terms, a) for terms, a in zip(near, arrived)]
+    sent = [low_sum(*terms) for terms in [*([corner] if corner else []), *[[*t, a] for t, a in zip(near, arrived)]]]
     sent, beside = after(sent, side, 0)
-    arrived = [swap(t, d) for t, d in zip(sent[1:], (cube.x, cube.y, cube.z))] + [across(sent[0], cube)]
+    arrived = [swap(t, d) for t, d in zip(sent[-3:], (cube.x, cube.y, cube.z))]
+    arrived += [across(t, cube) for t in sent[:-3]]
     arrived, own, _ = together((arrived, own, beside()))
     total = sum(wide(t) for t in [*own, *arrived])
     for direction in reversed(cube.extra):
@@ -184,6 +185,7 @@
 ANY = pl.BlockSpec(memory_space=pl.ANY)
 KERNEL_VMEM = 42 << 20
 COST = 16
+HELD = True
 
 
 def held(shape, dtype):
@@ -572,7 +574,8 @@
     count = sum(p.shape[0] for p in pieces)
     model, units = weights[0].shape
     extra = pieces[0].shape[1] - model
-    shapes = [like((count, units), bf16)] * 2 + [like((p.shape[0], model), bf16) for p in pieces]
+    kind = held if HELD and len(pieces) == 3 else like
+    shapes = [like((count, units), bf16)] * 2 + [kind((p.shape[0], model), bf16) for p in pieces]
     scratch = [pltpu.VMEM((count, n), bf16) for n in (model, extra, units, units, model)]
     scratch.append(pltpu.SemaphoreType.DMA((3 * len(pieces) + 2,)))
     body = functools.partial(expert_stage_body, len(pieces))
@@ -622,7 +625,8 @@
     count = sum(p.shape[0] for p in pieces)
     model, units = weights[0].shape
     extra = payloads[0].shape[1] - model
-    shapes = [like((count, units), bf16)] * 3 + [like((p.shape[0], model), bf16) for p in pieces]
+    kind = held if HELD and len(pieces) == 3 else like
+    shapes = [like((count, units), bf16)] * 3 + [kind((p.shape[0], model), bf16) for p in pieces]
     scratch = [pltpu.VMEM((count, n), bf16) for n in (model, extra, units, units, units, units, units, model)]
     scratch.append(pltpu.SemaphoreType.DMA((3 * len(pieces) + 5,)))
     body = functools.partial(expert_back_body, len(pieces))
@@ -946,9 +950,8 @@
             capacity,
         )
 
-    slices = [lax.dynamic_slice_in_dim(w, me * share, share, 0) for w in weights]
-    qkv_slices = swap(jnp.concatenate(slices[:3], axis=1), cube.z)
-    out_slices = slices[3]
+    slices = [lax.dynamic_slice_in_dim(w, me * share, share, 0) for w in weights[:3]]
+    qkv_slices = swap(jnp.concatenate(slices, axis=1), cube.z)
     half_share = share // 2
     mask = cube.x[1] | cube.y[1]
     far_places = [2 * (me ^ mask), 2 * (me ^ mask) + 1]
@@ -963,9 +966,9 @@
         given = lax.dynamic_slice_in_dim(own, (1 - shard) * half, half, 1)
         return lax.dynamic_slice_in_dim(own, shard * half, half, 1), given.astype(bf16)
 
-    def placed(parts, m):
+    def placed(parts, m, got=None):
         kept, given = parts
-        got = swap(given, cube.z).astype(kept.dtype)
+        got = (swap(given, cube.z) if got is None else got).astype(kept.dtype)
         low = jnp.where(shard == 0, kept, got)
         high = jnp.where(shard == 0, got, kept)
         return lax.dynamic_slice_in_dim(
@@ -976,18 +979,20 @@
     own_near = [swap(cot_own, d) for d in (cube.x, cube.y)] if whole_blocks else []
     opened, mask0 = opening(lengths, tokens, gain_one, weights)
     settled = [tokens, cotangent, routes, gates]
+    out_raw = weights[3]
     mates = [swap(expert_w[0], cube.core)] if whole_blocks else []
-    opened, qkv_slices, own_near, cot_other, settled, mates, expert_w = together(
-        (opened, qkv_slices, own_near, cot_other, settled, mates, expert_w)
+    opened, qkv_slices, own_near, cot_other, settled, mates, expert_w, out_raw = together(
+        (opened, qkv_slices, own_near, cot_other, settled, mates, expert_w, out_raw)
     )
+    out_slices = lax.dynamic_slice_in_dim(out_raw, me * share, share, 0)
     inputs, part, qkv, heads, sent = opened
     *settled, route_rows, gate_rows = settled
     settled += [[t[0, m].T for m in range(2)] for t in (route_rows, gate_rows)]
     other_near = [swap(cot_other, d) for d in (cube.x, cube.y)] if whole_blocks else []
     if whole_blocks:
         mates.append(swap(expert_w[1], cube.core))
-    arrived, other_near, settled, mates, expert_w = together(
-        (swap(sent, cube.z), other_near, settle(lengths, *settled), mates, expert_w)
+    arrived, other_near, settled, mates, expert_w, out_slices = together(
+        (swap(sent, cube.z), other_near, settle(lengths, *settled), mates, expert_w, out_slices)
     )
     fresh1, cot1, mask1, extra0, extra1, starts = settled
     hidden, payload = joined(part, arrived, gain_two, extra0)
@@ -1184,10 +1189,10 @@
     others = [t for t in sums[0] if t.dtype == bf16]
     grad_two, others, waiting = together((grad_two, others, waiting))
     others = [swap(t, cube.core) for t in others]
-    placings["out", 1], placings["grad", 0] = placed(waiting[0], 1), placed(waiting[1], 0)
+    received = [swap(given, cube.z) for _, given in waiting]
     heads_all = [[groups1[g][1], groups2[g][1], groups1[g][1]] for g in range(shards)]
     out_pairs = owned_products(cube, [turn0[2][1], turn1[2][1]], heads_all, (grad2, grad_two, hidden, gain_two))
-    out_pairs, others, placings = together((out_pairs, others, placings))
+    out_pairs, others, received = together((out_pairs, others, received))
     turn2 = []
 
     def last_turn(grad_two):
@@ -1228,7 +1233,7 @@
 
     def hidden_sums(*others):
         for other in others:
-            expert_sums[:] = [mine + wide(t) for mine, t in zip(expert_sums, jnp.split(other, 2, axis=1))]
+            expert_sums[:2] = [mine + wide(t) for mine, t in zip(expert_sums, jnp.split(other, 2, axis=1))]
         return expert_sums
 
     def down_sums(*others):
@@ -1236,11 +1241,16 @@
             expert_sums[2] = expert_sums[2] + wide(swap(other, cube.core))
         return expert_sums[2]
 
+    def waited(*got):
+        placings["out", 1], placings["grad", 0] = placed(waiting[0], 1, got[0]), placed(waiting[1], 0, got[1])
+        return placings["out", 1], placings["grad", 0]
+
     last_rows = placing("grad", 1, lambda: chosen(turn2[0], turn1[0]))
     last_end = down_end if whole_blocks else None
-    qkv_state = sums_start(qkv_pairs, [run_both(last_rows, (lambda: others, hidden_sums), last_end)])
+    qkv_state = sums_start(qkv_pairs, [run_both(last_rows, last_end)])
     expert_sums.append(sums[1][0])
-    grad_qkv = reduce_finish(cube, *qkv_state, [(lambda: sums[1][1:], down_sums)])
+    last_side = run_both((lambda: sums[1][1:], down_sums), (lambda: others, hidden_sums), (lambda: received, waited))
+    grad_qkv = reduce_finish(cube, *qkv_state, [last_side])
     gate_total, up_total, down_total = expert_sums
     width = q_weight.shape[2]
     grad_q = grad_qkv[:, :width]

time: 596 us -> 589 us (0.988)
  waiting for transfers between devices: 149 us -> 140 us
  starting transfers between devices: 139 us -> 146 us
    unnamed x370 -> x372, local copies, waits for them, and re-layouts: 18.5 us -> 20.6 us
  transfers between devices with their start and end apart: 131 -> 131, of which waited for: 53 -> 54; matrix products, arithmetic and copies ran while one was open for 4% -> 4% of each run, Pallas kernels for 36% -> 36%
where the time goes in v5:
time: 589 us; the launch traced here: 583 us
  Pallas kernels  231 us (39%)
  starting transfers between devices  146 us (25%)
  waiting for transfers between devices  140 us (24%)
  other arithmetic  30.9 us (5%)
  local copies, waits for them, and re-layouts  29.9 us (5%)
    pallas_call x33, Pallas kernels, on_device(): pl.pallas_call(body, out_shape=outs, in_specs=[SMEM] * len(scalars) + [VM...  154 us
    ppermute x119, starting transfers between devices, swap(): lax.ppermute(value, axis, [(i, i ^ bit) for i in range(lax.axis_size(axis...  116 us
    ppermute x119, waiting for transfers between devices, swap(): lax.ppermute(value, axis, [(i, i ^ bit) for i in range(lax.axis_size(axis...  99.8 us
    pallas_call x5, Pallas kernels, swept_products(): pl.pallas_call(body, grid=(steps,), out_shape=shapes, in_specs=in_specs,...  51.2 us
    ppermute x8, waiting for transfers between devices, across(): return lax.ppermute(value, ('dp', 'shard'), pairs)  32.9 us
    unnamed x372, local copies, waits for them, and re-layouts  20.6 us
    ppermute x8, starting transfers between devices, across(): return lax.ppermute(value, ('dp', 'shard'), pairs)  16.5 us
    pallas_call x2, Pallas kernels, owned_products(): pl.pallas_call(functools.partial(owned_body, len(lefts), len(rights), blo...  15.7 us
  transfers between devices with their start and end apart: 131, of which 54 were waited for; matrix products, arithmetic and copies ran while one was open for 4% of the time, Pallas kernels for 36%

profile of v5, /device:TPU:0, one launch (start us, length us, event | category | flops | bytes accessed | tf_op | source)
XLA Modules:
  0.0 582.5 jit_solution(2865776437700101368)
XLA Ops:
  12.3 7.3 %shard_map.221 = (bf16[128,1536]{1,0:T(8,128)(2,1)}, f32[128,1536]{1,0:T(8,128)}, bf16[128,1024]{1,0:T(8,128)(2,1)}, bf16[128,768]{1,0:T(8,128)(2,1)}, bf16[128,...) custom-call(s32[2,1,4]{2,1,0:T(1,128)S(1)} %copy-done.96, ...), custom_call_target="tpu_custom_call" | custom-call | flops 22548578304 | bytes 6144 | tf_op jit(solution)/shard_map/pallas_call | solution.py:282
  75.4 9.4 %collective-permute-done.19.refs_0_ = bf16[192,768]{1,0:T(8,128)(2,1)} collective-permute-done((bf16[192,768]{1,0:T(8,128)(2,1)S(1)}, bf16[192,768]{1,0:T(8,128)(2,1)}, u32[]{:S(2)}, u32[]{:S(2)}) %collective-permute-start.19) | collective-permute-done | bytes 294944 | tf_op jit(solution)/shard_map/ppermute | solution.py:56
  109.9 8.7 %collective-permute-done.30 = bf16[128,1536]{1,0:T(8,128)(2,1)S(1)} collective-permute-done((bf16[128,1536]{1,0:T(8,128)(2,1)S(1)}, bf16[128,1536]{1,0:T(8,128)(2,1)S(1)}, u32[]{:S(2)}, u32[]{:S(2)}) %collective-permute-start.30) | collective-permute-done | bytes 393248 | tf_op jit(solution)/shard_map/ppermute | solution.py:67
  145.4 7.0 %shard_map.233 = (bf16[128,1536]{1,0:T(8,128)(2,1)}, f32[128,1536]{1,0:T(8,128)}, bf16[128,1664]{1,0:T(8,128)(2,1)}, bf16[128,1024]{1,0:T(8,128)(2,1)}, bf16[128...) custom-call(bf16[128,1536]{1,0:T(8,128)(2,1)} %get-tuple-element.716.fresh, ...), custom_call_target="tpu_custom_call" | custom-call | flops 19327352832 | bytes 897024 | tf_op jit(solution)/shard_map/pallas_call | solution.py:282
  193.6 6.2 %shard_map.238 = (bf16[384,768]{1,0:T(8,128)(2,1)}, bf16[384,768]{1,0:T(8,128)(2,1)}, bf16[384,768]{1,0:T(8,128)(2,1)}, bf16[128,1536]{1,0:T(8,128)(2,1)S(1)}, b...) custom-call(bf16[1536,768]{1,0:T(8,128)(2,1)S(1)} %copy-done.7, bf16[1536,768]{1,0:T(8,128)(2,1)S(1)} %copy-done.9, ...), custom_call_target="tpu_custom_call" | custom-call | flops 43486543872 | tf_op jit(solution)/shard_map/pallas_call | solution.py:282
  209.2 6.3 %shard_map.239 = (bf16[384,768]{1,0:T(8,128)(2,1)}, bf16[384,768]{1,0:T(8,128)(2,1)}, bf16[384,768]{1,0:T(8,128)(2,1)}, bf16[128,1536]{1,0:T(8,128)(2,1)S(1)}, b...) custom-call(bf16[1536,768]{1,0:T(8,128)(2,1)S(1)} %copy-done.7, bf16[1536,768]{1,0:T(8,128)(2,1)S(1)} %copy-done.9, ...), custom_call_target="tpu_custom_call" | custom-call | flops 43486543872 | tf_op jit(solution)/shard_map/pallas_call | solution.py:282
  246.5 6.2 %shard_map.242 = (bf16[128,1536]{1,0:T(8,128)(2,1)}, f32[128,1536]{1,0:T(8,128)}, bf16[128,1664]{1,0:T(8,128)(2,1)}, bf16[128,1024]{1,0:T(8,128)(2,1)}, bf16[128...) custom-call(bf16[128,1536]{1,0:T(8,128)(2,1)} %get-tuple-element.698.fresh, ...), custom_call_target="tpu_custom_call" | custom-call | flops 19327352832 | bytes 897024 | tf_op jit(solution)/shard_map/pallas_call | solution.py:282
  266.0 7.7 %shard_map.244 = (f32[128,1536]{1,0:T(8,128)}, bf16[128,1536]{1,0:T(8,128)(2,1)}, bf16[128,1536]{1,0:T(8,128)(2,1)}, bf16[128,1536]{1,0:T(8,128)(2,1)}, bf16[128...) custom-call(bf16[128,1536]{1,0:T(8,128)(2,1)} %get-tuple-element.1112.refs_0_.grad, ...), custom_call_target="tpu_custom_call" | custom-call | flops 38654705664 | bytes 2961408 | tf_op jit(solution)/shard_map/pallas_call | solution.py:282
  284.1 7.0 %collective-permute-done.67.refs_1_.refs_4_.refs_5_ = bf16[128,1664]{1,0:T(8,128)(2,1)S(1)} collective-permute-done((bf16[128,1664]{1,0:T(8,128)(2,1)S(1)}, bf16[128,1664]{1,0:T(8,128)(2,1)S(1)}, u32[]{:S(2)}, u32[]{:S(2)}) %collective-permute-start.67) | collective-permute-done | bytes 426016 | tf_op jit(solution)/shard_map/ppermute | solution.py:56
  297.3 7.7 %collective-permute-done.69 = bf16[128,1536]{1,0:T(8,128)(2,1)S(1)} collective-permute-done((bf16[128,1536]{1,0:T(8,128)(2,1)S(1)}, bf16[128,1536]{1,0:T(8,128)(2,1)S(1)}, u32[]{:S(2)}, u32[]{:S(2)}) %collective-permute-start.69) | collective-permute-done | bytes 393248 | tf_op jit(solution)/shard_map/ppermute | solution.py:1121
  322.4 6.5 %shard_map.248 = (bf16[384,768]{1,0:T(8,128)(2,1)}, bf16[384,768]{1,0:T(8,128)(2,1)}, bf16[384,768]{1,0:T(8,128)(2,1)}, bf16[128,1536]{1,0:T(8,128)(2,1)S(1)}, b...) custom-call(bf16[1536,768]{1,0:T(8,128)(2,1)S(1)} %copy-done.7, bf16[1536,768]{1,0:T(8,128)(2,1)S(1)} %copy-done.9, ...), custom_call_target="tpu_custom_call" | custom-call | flops 43486543872 | tf_op jit(solution)/shard_map/pallas_call | solution.py:282
  334.7 6.3 %shard_map.249 = (bf16[384,768]{1,0:T(8,128)(2,1)}, bf16[384,768]{1,0:T(8,128)(2,1)}, bf16[384,768]{1,0:T(8,128)(2,1)}, bf16[128,1536]{1,0:T(8,128)(2,1)S(1)}, b...) custom-call(bf16[1536,768]{1,0:T(8,128)(2,1)S(1)} %copy-done.7, bf16[1536,768]{1,0:T(8,128)(2,1)S(1)} %copy-done.9, ...), custom_call_target="tpu_custom_call" | custom-call | flops 43486543872 | tf_op jit(solution)/shard_map/pallas_call | solution.py:282
  346.7 9.2 %shard_map.252 = (f32[1536,768]{1,0:T(8,128)}, f32[1536,768]{1,0:T(8,128)}) custom-call(bf16[128,1664]{1,0:T(8,128)(2,1)} %get-tuple-element.1243.refs_0_.refs_1_, bf16[128,1664]{1,0:T(8,128)(2,1)} %copy-done.25, bf16[128,1664]{1,0:T(8,128)(2,1)} %copy-done.27, bf16[128,1664]{1,0:T(8,128)(2,1)} %copy-done.29, bf16[128,1664]{1,0:T(8,128)(2,1)} %copy-done.31, ...), custom_call_target="tpu_custom_call" | custom-call | flops 77309411328 | bytes 1024 | tf_op jit(solution)/shard_map/pallas_call | solution.py:674
  379.0 7.7 %shard_map.253 = (f32[128,1536]{1,0:T(8,128)}, bf16[128,1536]{1,0:T(8,128)(2,1)}, bf16[128,1536]{1,0:T(8,128)(2,1)}, bf16[128,1536]{1,0:T(8,128)(2,1)}, bf16[128...) custom-call(bf16[128,1536]{1,0:T(8,128)(2,1)} %copy-done.5, ...), custom_call_target="tpu_custom_call" | custom-call | flops 38654705664 | bytes 2961408 | tf_op jit(solution)/shard_map/pallas_call | solution.py:282
  393.7 11.1 %shard_map.254.refs_12_ = f32[768,1536]{1,0:T(8,128)} custom-call(bf16[128,1536]{1,0:T(8,128)(2,1)} %get-tuple-element.1112.refs_0_.grad, bf16[128,1536]{1,0:T(8,128)(2,1)} %copy-done.58, bf16[128,1536]{1,0:T(8,128)(2,1)} %copy-done.60, bf16[128,1536]{1,0:T(8,128)(2,1)} %get-tuple-element.1115.refs_2_.refs_3_, ...), custom_call_target="tpu_custom_call" | custom-call | flops 77309411328 | bytes 2048 | tf_op jit(solution)/shard_map/pallas_call | solution.py:674
  418.9 6.0 %shard_map.256 = (bf16[384,768]{1,0:T(8,128)(2,1)}, bf16[384,768]{1,0:T(8,128)(2,1)}, bf16[384,768]{1,0:T(8,128)(2,1)}, bf16[128,1536]{1,0:T(8,128)(2,1)S(1)}, b...) custom-call(bf16[1536,768]{1,0:T(8,128)(2,1)S(1)} %copy-done.7, bf16[1536,768]{1,0:T(8,128)(2,1)S(1)} %copy-done.9, ...), custom_call_target="tpu_custom_call" | custom-call | flops 43486543872 | tf_op jit(solution)/shard_map/pallas_call | solution.py:282
  436.2 11.5 %shard_map.258 = (f32[1536,768]{1,0:T(8,128)}, f32[1536,768]{1,0:T(8,128)}) custom-call(bf16[128,1664]{1,0:T(8,128)(2,1)} %get-tuple-element.1182.refs_0_.refs_1_, bf16[128,1664]{1,0:T(8,128)(2,1)} %copy-done.41, bf16[128,1664]{1,0:T(8,128)(2,1)} %copy-done.43, bf16[128,1664]{1,0:T(8,128)(2,1)} %copy-done.45, bf16[128,1664]{1,0:T(8,128)(2,1)} %copy-done.47, ...), custom_call_target="tpu_custom_call" | custom-call | flops 77309411328 | bytes 1024 | tf_op jit(solution)/shard_map/pallas_call | solution.py:674
  447.8 6.0 %shard_map.257 = (bf16[384,768]{1,0:T(8,128)(2,1)}, bf16[384,768]{1,0:T(8,128)(2,1)}, bf16[384,768]{1,0:T(8,128)(2,1)}, bf16[128,1536]{1,0:T(8,128)(2,1)S(1)}, b...) custom-call(bf16[1536,768]{1,0:T(8,128)(2,1)S(1)} %copy-done.7, bf16[1536,768]{1,0:T(8,128)(2,1)S(1)} %copy-done.9, ...), custom_call_target="tpu_custom_call" | custom-call | flops 43486543872 | tf_op jit(solution)/shard_map/pallas_call | solution.py:282
  473.6 11.3 %shard_map.260 = (f32[1536,384]{1,0:T(8,128)}, f32[1536,384]{1,0:T(8,128)}, bf16[1536,768]{1,0:T(8,128)(2,1)}) custom-call(bf16[128,1664]{1,0:T(8,128)(2,1)} %get-tuple-element.1243.refs_0_.refs_1_, bf16[128,1664]{1,0:T(8,128)(2,1)} %copy-done.25, bf16[128,1664]{1,0:T(8,128)(2,1)} %copy-done.27, bf16[128,1664]{1,0:T(8,128)(2,1)} %copy-done.29, ...), custom_call_target="tpu_custom_call" | custom-call | flops 77309411328 | bytes 1024 | tf_op jit(solution)/shard_map/pallas_call | solution.py:674
  488.9 7.3 %shard_map.261 = (bf16[576,768]{1,0:T(8,128)(2,1)}, bf16[576,768]{1,0:T(8,128)(2,1)}, bf16[960,768]{1,0:T(8,128)(2,1)}, bf16[960,768]{1,0:T(8,128)(2,1)}) custom-call(bf16[128,1536]{1,0:T(8,128)(2,1)} %get-tuple-element.958.refs_0_, bf16[128,1536]{1,0:T(8,128)(2,1)} %get-tuple-element.1269.refs_1_, bf16[128,768]{1,0:T(8,128)(2,1)} %get-tuple-element.961.refs_2_.refs_4_, ...), custom_call_target="tpu_custom_call" | custom-call | tf_op jit(solution)/shard_map/pallas_call | solution.py:762
  506.1 7.5 %shard_map.262 = (f32[128,1536]{1,0:T(8,128)}, bf16[128,1536]{1,0:T(8,128)(2,1)}, bf16[128,1536]{1,0:T(8,128)(2,1)}, bf16[128,1536]{1,0:T(8,128)(2,1)}, bf16[128...) custom-call(bf16[128,1536]{1,0:T(8,128)(2,1)} %copy-done.4, ...), custom_call_target="tpu_custom_call" | custom-call | flops 38654705664 | bytes 2961408 | tf_op jit(solution)/shard_map/pallas_call | solution.py:282
  519.7 8.4 %shard_map.263 = (bf16[576,1152]{1,0:T(8,128)(2,1)}, bf16[576,1152]{1,0:T(8,128)(2,1)}, bf16[960,1152]{1,0:T(8,128)(2,1)}, bf16[960,1152]{1,0:T(8,128)(2,1)}) custom-call(bf16[128,1536]{1,0:T(8,128)(2,1)} %get-tuple-element.957.refs_0_, bf16[128,1536]{1,0:T(8,128)(2,1)} %get-tuple-element.1268.refs_1_, bf16[128,1536]{1,0:T(8,128)(2,1)} %get-tuple-element.1282.refs_2_, ...), custom_call_target="tpu_custom_call" | custom-call | tf_op jit(solution)/shard_map/pallas_call | solution.py:762
  541.7 8.0 %shard_map.264 = (f32[384,1536]{1,0:T(8,128)}, bf16[384,1536]{1,0:T(8,128)(2,1)}) custom-call(bf16[128,1536]{1,0:T(8,128)(2,1)} %copy-done.4, bf16[128,1536]{1,0:T(8,128)(2,1)} %copy-done.73, bf16[128,1536]{1,0:T(8,128)(2,1)} %copy-done.74, bf16[128,1536]{1,0:T(8,128)(2,1)} %copy-done.75, bf16[128,1536]{1,0:T(8,128)(2,1)} %copy-done.76, ...), custom_call_target="tpu_custom_call" | custom-call | flops 38654705664 | bytes 1024 | tf_op jit(solution)/shard_map/pallas_call | solution.py:674
  572.2 7.4 %collective-permute-done.129 = bf16[192,1152]{1,0:T(8,128)(2,1)S(1)} collective-permute-done((bf16[192,1152]{1,0:T(8,128)(2,1)S(1)}, bf16[192,1152]{1,0:T(8,128)(2,1)S(1)}, u32[]{:S(2)}, u32[]{:S(2)}) %collective-permute-start.129) | collective-permute-done | bytes 442400 | tf_op jit(solution)/shard_map/ppermute | solution.py:67
  (723 shorter events, 390.0 us)
Async XLA Ops:
  4.2 16.8 %collective-permute-start.1 = (bf16[128,1536]{1,0:T(8,128)(2,1)}, bf16[128,1536]{1,0:T(8,128)(2,1)S(1)}, u32[]{:S(2)}, u32[]{:S(2)}) collective-permute-start(bf16[128,1536]{1,0:T(8,128)(2,1)} %get-tuple-element.1112.refs_0_.grad), channel_id=1, source_target_pairs={{0,4},{2,6},{4,0},{6,2},{8,12},{10,14},{12,8},{14,10},{1,5},{3,7},... | collective-permute-start | bytes 1179656 | tf_op jit(solution)/shard_map/ppermute | solution.py:56
  66.0 18.8 %collective-permute-start.16 = (bf16[192,1024]{1,0:T(8,128)(2,1)S(1)}, bf16[192,1024]{1,0:T(8,128)(2,1)S(1)}, u32[]{:S(2)}, u32[]{:S(2)}) collective-permute-start(bf16[192,1024]{1,0:T(8,128)(2,1)S(1)} %collective-permute-done.refs_0_), channel_id=1, source_target_pairs={{0,4},{2,6},{4,0},{6,2},{8,12},{10,14},{12,8},{14,10},{1,5},{3,7},... | collective-permute-start | bytes 1179656 | tf_op jit(solution)/shard_map/ppermute | solution.py:56
  66.7 18.1 %collective-permute-start.17 = (bf16[192,1024]{1,0:T(8,128)(2,1)S(1)}, bf16[192,1024]{1,0:T(8,128)(2,1)S(1)}, u32[]{:S(2)}, u32[]{:S(2)}) collective-permute-start(bf16[192,1024]{1,0:T(8,128)(2,1)S(1)} %collective-permute-done.refs_0_), channel_id=1, source_target_pairs={{0,8},{2,10},{4,12},{6,14},{8,0},{10,2},{12,4},{14,6},{1,9},{3,11}... | collective-permute-start | bytes 1179656 | tf_op jit(solution)/shard_map/ppermute | solution.py:56
  68.0 16.8 %collective-permute-start.18 = (bf16[192,1024]{1,0:T(8,128)(2,1)S(1)}, bf16[192,1024]{1,0:T(8,128)(2,1)S(1)}, u32[]{:S(2)}, u32[]{:S(2)}) collective-permute-start(bf16[192,1024]{1,0:T(8,128)(2,1)S(1)} %collective-permute-done.refs_0_), channel_id=1, source_target_pairs={{0,12},{2,14},{4,8},{6,10},{8,4},{10,6},{12,0},{14,2},{1,13},{3,15... | collective-permute-start | bytes 1179656 | tf_op jit(solution)/shard_map/ppermute | solution.py:56
  98.3 20.3 %collective-permute-start.30 = (bf16[128,1536]{1,0:T(8,128)(2,1)S(1)}, bf16[128,1536]{1,0:T(8,128)(2,1)S(1)}, u32[]{:S(2)}, u32[]{:S(2)}) collective-permute-start(bf16[128,1536]{1,0:T(8,128)(2,1)S(1)} %copy-done.181), channel_id=1, source_target_pairs={{0,13},{1,12},{2,15},{3,14},{4,9},{5,8},{6,11},{7,10},{8,5},{9,4},... | collective-permute-start | bytes 1179656 | tf_op jit(solution)/shard_map/ppermute | solution.py:67
  119.6 19.3 %collective-permute-start.31 = (bf16[128,1536]{1,0:T(8,128)(2,1)}, bf16[128,1536]{1,0:T(8,128)(2,1)}, u32[]{:S(2)}, u32[]{:S(2)}) collective-permute-start(bf16[128,1536]{1,0:T(8,128)(2,1)} %add_convert_fusion.24), channel_id=1, source_target_pairs={{0,16},{1,17},{2,18},{3,19},{4,20},{5,21},{6,22},{7,23},{8,24},{9,... | collective-permute-start | bytes 1179656 | tf_op jit(solution)/shard_map/ppermute | solution.py:1034
  207.0 16.1 %collective-permute-start.54 = (bf16[128,1536]{1,0:T(8,128)(2,1)S(1)}, bf16[128,1536]{1,0:T(8,128)(2,1)S(1)}, u32[]{:S(2)}, u32[]{:S(2)}) collective-permute-start(bf16[128,1536]{1,0:T(8,128)(2,1)S(1)} %copy-done.184), channel_id=1, source_target_pairs={{0,13},{1,12},{2,15},{3,14},{4,9},{5,8},{6,11},{7,10},{8,5},{9,4},... | collective-permute-start | bytes 1179656 | tf_op jit(solution)/shard_map/ppermute | solution.py:67
  259.5 16.3 %collective-permute-start.63 = (bf16[128,1664]{1,0:T(8,128)(2,1)S(1)}, bf16[128,1664]{1,0:T(8,128)(2,1)S(1)}, u32[]{:S(2)}, u32[]{:S(2)}) collective-permute-start(bf16[128,1664]{1,0:T(8,128)(2,1)S(1)} %copy-done.40), channel_id=1, source_target_pairs={{0,4},{2,6},{4,0},{6,2},{8,12},{10,14},{12,8},{14,10},{1,5},{3,7},... | collective-permute-start | bytes 1277960 | tf_op jit(solution)/shard_map/ppermute | solution.py:56
  342.9 19.3 %collective-permute-start.79 = (bf16[128,1536]{1,0:T(8,128)(2,1)S(1)}, bf16[128,1536]{1,0:T(8,128)(2,1)S(1)}, u32[]{:S(2)}, u32[]{:S(2)}) collective-permute-start(bf16[128,1536]{1,0:T(8,128)(2,1)S(1)} %get-tuple-element.1031), channel_id=1, source_target_pairs={{0,8},{2,10},{4,12},{6,14},{8,0},{10,2},{12,4},{14,6},{1,9},{3,11}... | collective-permute-start | bytes 1179656 | tf_op jit(solution)/shard_map/ppermute | solution.py:56
  344.6 17.7 %collective-permute-start.80 = (bf16[128,1536]{1,0:T(8,128)(2,1)S(1)}, bf16[128,1536]{1,0:T(8,128)(2,1)S(1)}, u32[]{:S(2)}, u32[]{:S(2)}) collective-permute-start(bf16[128,1536]{1,0:T(8,128)(2,1)S(1)} %get-tuple-element.1032), channel_id=1, source_target_pairs={{0,1},{1,0},{2,3},{3,2},{4,5},{5,4},{6,7},{7,6},{8,9},{9,8},{10,11... | collective-permute-start | bytes 1179656 | tf_op jit(solution)/shard_map/ppermute | solution.py:56
  345.4 16.9 %collective-permute-start.81 = (bf16[128,1536]{1,0:T(8,128)(2,1)S(1)}, bf16[128,1536]{1,0:T(8,128)(2,1)S(1)}, u32[]{:S(2)}, u32[]{:S(2)}) collective-permute-start(bf16[128,1536]{1,0:T(8,128)(2,1)S(1)} %get-tuple-element.1033), channel_id=1, source_target_pairs={{0,4},{2,6},{4,0},{6,2},{8,12},{10,14},{12,8},{14,10},{1,5},{3,7},... | collective-permute-start | bytes 1179656 | tf_op jit(solution)/shard_map/ppermute | solution.py:56
  386.6 19.2 %collective-permute-start.86 = (bf16[128,1536]{1,0:T(8,128)(2,1)}, bf16[128,1536]{1,0:T(8,128)(2,1)S(1)}, u32[]{:S(2)}, u32[]{:S(2)}) collective-permute-start(bf16[128,1536]{1,0:T(8,128)(2,1)} %get-tuple-element.1091), channel_id=1, source_target_pairs={{16,0},{17,1},{18,2},{19,3},{20,4},{21,5},{22,6},{23,7},{24,8},{25... | collective-permute-start | bytes 1179656 | tf_op jit(solution)/shard_map/ppermute | solution.py:1162
  388.4 17.5 %collective-permute-start.87 = (bf16[128,1536]{1,0:T(8,128)(2,1)S(1)}, bf16[128,1536]{1,0:T(8,128)(2,1)S(1)}, u32[]{:S(2)}, u32[]{:S(2)}) collective-permute-start(bf16[128,1536]{1,0:T(8,128)(2,1)S(1)} %copy-done.85), channel_id=1, source_target_pairs={{0,8},{2,10},{4,12},{6,14},{8,0},{10,2},{12,4},{14,6},{1,9},{3,11}... | collective-permute-start | bytes 1179656 | tf_op jit(solution)/shard_map/ppermute | solution.py:56
  389.4 16.4 %collective-permute-start.88 = (bf16[128,1536]{1,0:T(8,128)(2,1)S(1)}, bf16[128,1536]{1,0:T(8,128)(2,1)S(1)}, u32[]{:S(2)}, u32[]{:S(2)}) collective-permute-start(bf16[128,1536]{1,0:T(8,128)(2,1)S(1)} %copy-done.83), channel_id=1, source_target_pairs={{0,1},{1,0},{2,3},{3,2},{4,5},{5,4},{6,7},{7,6},{8,9},{9,8},{10,11... | collective-permute-start | bytes 1179656 | tf_op jit(solution)/shard_map/ppermute | solution.py:56
  428.9 26.8 %collective-permute-start.96 = (bf16[128,1536]{1,0:T(8,128)(2,1)S(1)}, bf16[128,1536]{1,0:T(8,128)(2,1)S(1)}, u32[]{:S(2)}, u32[]{:S(2)}) collective-permute-start(bf16[128,1536]{1,0:T(8,128)(2,1)S(1)} %collective-permute-done.93.refs_0_.refs_4_), channel_id=1, source_target_pairs={{0,1},{1,0},{2,3},{3,2},{4,5},{5,4},{6,7},{7,6},{8,9},{9,8},{10,11... | collective-permute-start | bytes 1179656 | tf_op jit(solution)/shard_map/ppermute | solution.py:56
  430.8 23.1 %collective-permute-start.97 = (bf16[128,1536]{1,0:T(8,128)(2,1)S(1)}, bf16[128,1536]{1,0:T(8,128)(2,1)}, u32[]{:S(2)}, u32[]{:S(2)}) collective-permute-start(bf16[128,1536]{1,0:T(8,128)(2,1)S(1)} %add_convert_fusion.13), channel_id=1, source_target_pairs={{0,4},{2,6},{4,0},{6,2},{8,12},{10,14},{12,8},{14,10},{1,5},{3,7},... | collective-permute-start | bytes 1179656 | tf_op jit(solution)/shard_map/ppermute | solution.py:56
  431.2 22.7 %collective-permute-start.98 = (bf16[128,1536]{1,0:T(8,128)(2,1)S(1)}, bf16[128,1536]{1,0:T(8,128)(2,1)}, u32[]{:S(2)}, u32[]{:S(2)}) collective-permute-start(bf16[128,1536]{1,0:T(8,128)(2,1)S(1)} %add_convert_fusion.12), channel_id=1, source_target_pairs={{0,8},{2,10},{4,12},{6,14},{8,0},{10,2},{12,4},{14,6},{1,9},{3,11}... | collective-permute-start | bytes 1179656 | tf_op jit(solution)/shard_map/ppermute | solution.py:56
  433.3 20.5 %collective-permute-start.99 = (bf16[128,1536]{1,0:T(8,128)(2,1)S(1)}, bf16[128,1536]{1,0:T(8,128)(2,1)}, u32[]{:S(2)}, u32[]{:S(2)}) collective-permute-start(bf16[128,1536]{1,0:T(8,128)(2,1)S(1)} %add_convert_fusion.11), channel_id=1, source_target_pairs={{0,1},{1,0},{2,3},{3,2},{4,5},{5,4},{6,7},{7,6},{8,9},{9,8},{10,11... | collective-permute-start | bytes 1179656 | tf_op jit(solution)/shard_map/ppermute | solution.py:56
  433.4 20.5 %collective-permute-start.100 = (bf16[128,1536]{1,0:T(8,128)(2,1)}, bf16[128,1536]{1,0:T(8,128)(2,1)}, u32[]{:S(2)}, u32[]{:S(2)}) collective-permute-start(bf16[128,1536]{1,0:T(8,128)(2,1)} %get-tuple-element.1175), channel_id=1, source_target_pairs={{0,13},{1,12},{2,15},{3,14},{4,9},{5,8},{6,11},{7,10},{8,5},{9,4},... | collective-permute-start | bytes 1179656 | tf_op jit(solution)/shard_map/ppermute | solution.py:67
  468.4 16.4 %collective-permute-start.104 = (bf16[128,1536]{1,0:T(8,128)(2,1)S(1)}, bf16[128,1536]{1,0:T(8,128)(2,1)S(1)}, u32[]{:S(2)}, u32[]{:S(2)}) collective-permute-start(bf16[128,1536]{1,0:T(8,128)(2,1)S(1)} %add_convert_fusion.9), channel_id=1, source_target_pairs={{0,4},{2,6},{4,0},{6,2},{8,12},{10,14},{12,8},{14,10},{1,5},{3,7},... | collective-permute-start | bytes 1179656 | tf_op jit(solution)/shard_map/ppermute | solution.py:56
  537.1 18.2 %collective-permute-start.121 = (bf16[192,1152]{1,0:T(8,128)(2,1)S(1)}, bf16[192,1152]{1,0:T(8,128)(2,1)S(1)}, u32[]{:S(2)}, u32[]{:S(2)}) collective-permute-start(bf16[192,1152]{1,0:T(8,128)(2,1)S(1)} %get-tuple-element.1331), channel_id=1, source_target_pairs={{0,8},{2,10},{4,12},{6,14},{8,0},{10,2},{12,4},{14,6},{1,9},{3,11}... | collective-permute-start | bytes 1327112 | tf_op jit(solution)/shard_map/ppermute | solution.py:56
  538.5 16.8 %collective-permute-start.122 = (bf16[192,1152]{1,0:T(8,128)(2,1)S(1)}, bf16[192,1152]{1,0:T(8,128)(2,1)S(1)}, u32[]{:S(2)}, u32[]{:S(2)}) collective-permute-start(bf16[192,1152]{1,0:T(8,128)(2,1)S(1)} %get-tuple-element.1332), channel_id=1, source_target_pairs={{0,1},{1,0},{2,3},{3,2},{4,5},{5,4},{6,7},{7,6},{8,9},{9,8},{10,11... | collective-permute-start | bytes 1327112 | tf_op jit(solution)/shard_map/ppermute | solution.py:56
  538.8 16.6 %collective-permute-start.123 = (bf16[192,1152]{1,0:T(8,128)(2,1)S(1)}, bf16[192,1152]{1,0:T(8,128)(2,1)S(1)}, u32[]{:S(2)}, u32[]{:S(2)}) collective-permute-start(bf16[192,1152]{1,0:T(8,128)(2,1)S(1)} %get-tuple-element.1333), channel_id=1, source_target_pairs={{0,4},{2,6},{4,0},{6,2},{8,12},{10,14},{12,8},{14,10},{1,5},{3,7},... | collective-permute-start | bytes 1327112 | tf_op jit(solution)/shard_map/ppermute | solution.py:56
  559.4 20.3 %collective-permute-start.129 = (bf16[192,1152]{1,0:T(8,128)(2,1)S(1)}, bf16[192,1152]{1,0:T(8,128)(2,1)S(1)}, u32[]{:S(2)}, u32[]{:S(2)}) collective-permute-start(bf16[192,1152]{1,0:T(8,128)(2,1)S(1)} %get-tuple-element.1365), channel_id=1, source_target_pairs={{0,13},{1,12},{2,15},{3,14},{4,9},{5,8},{6,11},{7,10},{8,5},{9,4},... | collective-permute-start | bytes 1327112 | tf_op jit(solution)/shard_map/ppermute | solution.py:67
  (294 other events, 3189.1 us)

commit v6 on v5

--- a/solution.py
+++ b/solution.py
@@ -353,7 +353,7 @@
 
 
 def opening_body(lens, gain, tokens, *refs):
-    wq, wk, wv, wo, inputs, part, qkv, heads, sent, qkv_other, heads_other, mask, *scratch, sems = refs
+    wq, wk, wv, wo, inputs, part, sent, mask, qkv, heads, *scratch, sems = refs
     copies = Copies(sems)
     sources = [tokens.at[0], wq, wk, wv, wo]
     block_rows, *weights = [copies.fetch(a, b) for a, b in zip(sources, scratch)]
@@ -371,13 +371,12 @@
     normed = normed_rows(values, gain[...])
     *projections, w_out = weights
     projected = jnp.concatenate([dot_nn(normed, w()).astype(bf16) for w in projections], axis=1)
-    both_heads = []
-    for i, (to_qkv, to_heads) in enumerate(((qkv, heads), (qkv_other, heads_other))):
-        to_qkv[...] = projected[i * rows : (i + 1) * rows]
-        _, _, value, probs = group_probs(to_qkv[...], sides[i][1])
-        to_heads[...] = spread_heads(dot_nn(probs.astype(bf16), value).astype(bf16), rows)
-        both_heads.append(to_heads[...])
-    result = dot_nt(jnp.concatenate(both_heads, axis=0), w_out())
+    for i, (_, allowed) in enumerate(sides):
+        here = pl.ds(i * rows, rows)
+        qkv[here, :] = projected[i * rows : (i + 1) * rows]
+        _, _, value, probs = group_probs(qkv[here, :], allowed)
+        heads[here, :] = spread_heads(dot_nn(probs.astype(bf16), value).astype(bf16), rows)
+    result = dot_nt(heads[...], w_out())
     part[...] = values[:rows] + result[:rows]
     sent[...] = result[rows:].astype(bf16)
 
@@ -387,14 +386,13 @@
     rows = block // 2
     width, out = sum(w.shape[1] for w in weights[:3]), weights[3].shape[1]
     shapes = [
-        like((rows, model), bf16), like((rows, model), f32), like((rows, width), bf16), like((rows, out), bf16),
-        like((rows, model), bf16), like((rows, width), bf16), like((rows, out), bf16), like((rows, rows), f32),
+        like((rows, model), bf16), like((rows, model), f32), like((rows, model), bf16), like((rows, rows), f32)
     ]
-    scratch = [pltpu.VMEM((block, model), bf16), *holders(*weights)]
-    outs = on_device(
-        opening_body, shapes, [gain], 4 * rows * model * (width + out), (lens,), far=[distant(t) for t in (tokens, *weights)], scratch=scratch
+    scratch = [pltpu.VMEM((block, n), bf16) for n in (width, out, model)] + holders(*weights)
+    return on_device(
+        opening_body, shapes, [gain], 4 * rows * model * (width + out), (lens,),
+        far=[distant(t) for t in (tokens, *weights)], scratch=scratch,
     )
-    return outs[:5], outs[7]
 
 
 def settle_body(lens, routes0, gates0, routes1, gates1, tokens, grad, *refs):
@@ -977,7 +975,7 @@
 
     cot_own, cot_other = turned_block(lengths, cotangent)
     own_near = [swap(cot_own, d) for d in (cube.x, cube.y)] if whole_blocks else []
-    opened, mask0 = opening(lengths, tokens, gain_one, weights)
+    opened = opening(lengths, tokens, gain_one, weights)
     settled = [tokens, cotangent, routes, gates]
     out_raw = weights[3]
     mates = [swap(expert_w[0], cube.core)] if whole_blocks else []
@@ -985,7 +983,7 @@
         (opened, qkv_slices, own_near, cot_other, settled, mates, expert_w, out_raw)
     )
     out_slices = lax.dynamic_slice_in_dim(out_raw, me * share, share, 0)
-    inputs, part, qkv, heads, sent = opened
+    inputs, part, sent, mask0 = opened
     *settled, route_rows, gate_rows = settled
     settled += [[t[0, m].T for m in range(2)] for t in (route_rows, gate_rows)]
     other_near = [swap(cot_other, d) for d in (cube.x, cube.y)] if whole_blocks else []
@@ -1130,12 +1128,11 @@
         *results2, corner = results2
         coming, results2, inputs = together((coming, results2, corner[0]()))
         corner = corner[1](*inputs)
-        results2 = [*results2, (lambda: [corner], lambda t: t)]
+        results2 = [*results2, (lambda: [], lambda: [])]
     else:
         coming, results2, saved2 = together((coming, results2, saved2))
     grad1 = coming + cot1
     state2 = [inputs2, hidden2, mask_last, groups2, saved2]
-    back_results, keeps1 = mixture.backward(grad1, section, saved2)
     def run_both(*works):
         works = [w for w in works if w]
         return both(*works) if works else None
@@ -1149,10 +1146,19 @@
 
         return lambda: [own()], work
 
+    place_first = placing("out", 0, lambda: chosen(result0, result1))
+    back_results, keeps1 = mixture.backward(grad1, section, saved2, [None, None, place_first])
+    corner_sums = []
+
+    def corner_sum(t):
+        corner_sums.append(across(t, cube))
+        return corner_sums
+
+    corner_work = (lambda: corner, corner_sum) if whole_blocks else None
     hidden_work, _ = mixture.weight_sums([keeps0], sums)
     _, down_work = mixture.weight_sums([keeps0, keeps1], sums)
-    place_first = placing("out", 0, lambda: chosen(result0, result1))
-    grad_two = mixture.total(back_results, [run_both(place_first, hidden_work)])
+    hidden_next, _ = mixture.weight_sums([keeps1], sums)
+    grad_two = mixture.total(back_results, [run_both(hidden_work, corner_work), run_both(hidden_next)])
     grad_two, down_inputs = together((grad_two, down_work[0]())) if down_work else (grad_two, ())
     turn1 = attention_turn(grad1, grad_two, state2)
     if whole_blocks:
@@ -1161,6 +1167,8 @@
         low, results2 = together((turn1[1], results2))
     coming = lax.ppermute(low, "section", [(1, 0)])
     state = mixture.total_start(results2)
+    if whole_blocks:
+        state = (*state[:3], [*state[3], *corner_sums])
     grad2, state, _ = together((coming, state, down_work[1](*down_inputs) if down_work else ()))
 
     last_total = []
@@ -1169,8 +1177,7 @@
         last_total.append(mixture.total_finish(state[0] if len(state) == 1 else state))
         return last_total
 
-    hidden_work, _ = mixture.weight_sums([keeps1], sums)
-    side = [None, None, run_both((lambda: [state] if not whole_blocks else list(state), finish_last), hidden_work)]
+    side = [None, None, (lambda: [state] if not whole_blocks else list(state), finish_last)]
     back_results, keeps2 = mixture.backward(grad2, 1 - section, saved1, side)
     result2 = (hidden2 + last_total[0]).astype(bf16)
     placing_out = placing("out", 1, lambda: chosen(result1, result2))

time: 589 us -> 585 us (level)
    ppermute x119, waiting for transfers between devices: 99.8 us -> 91.1 us  [swap(): lax.ppermute(value, axis, [(i, i ^ bit) for i in range(lax.axis_size(axis...]
    ppermute x119, starting transfers between devices: 116 us -> 109 us  [swap(): lax.ppermute(value, axis, [(i, i ^ bit) for i in range(lax.axis_size(axis...]
    unnamed x372 -> x376, local copies, waits for them, and re-layouts: 20.6 us -> 21.4 us
  transfers between devices with their start and end apart: 131 -> 131, of which waited for: 54 -> 55; matrix products, arithmetic and copies ran while one was open for 4% -> 5% of each run, Pallas kernels for 36% -> 36%
where the time goes in v6:
time: 585 us; the launch traced here: 579 us
  Pallas kernels  231 us (39%)
  starting transfers between devices  142 us (24%)
  waiting for transfers between devices  135 us (23%)
  other arithmetic  34.7 us (6%)
  local copies, waits for them, and re-layouts  30.8 us (5%)
    pallas_call x33, Pallas kernels, on_device(): pl.pallas_call(body, out_shape=outs, in_specs=[SMEM] * len(scalars) + [VM...  154 us
    ppermute x119, starting transfers between devices, swap(): lax.ppermute(value, axis, [(i, i ^ bit) for i in range(lax.axis_size(axis...  109 us
    ppermute x119, waiting for transfers between devices, swap(): lax.ppermute(value, axis, [(i, i ^ bit) for i in range(lax.axis_size(axis...  91.1 us
    pallas_call x5, Pallas kernels, swept_products(): pl.pallas_call(body, grid=(steps,), out_shape=shapes, in_specs=in_specs,...  51.7 us
    ppermute x8, waiting for transfers between devices, across(): return lax.ppermute(value, ('dp', 'shard'), pairs)  33.2 us
    unnamed x376, local copies, waits for them, and re-layouts  21.4 us
    ppermute x8, starting transfers between devices, across(): return lax.ppermute(value, ('dp', 'shard'), pairs)  18.3 us
    pallas_call x2, Pallas kernels, owned_products(): pl.pallas_call(functools.partial(owned_body, len(lefts), len(rights), blo...  15.7 us
  transfers between devices with their start and end apart: 131, of which 55 were waited for; matrix products, arithmetic and copies ran while one was open for 5% of the time, Pallas kernels for 36%

profile of v6, /device:TPU:0, one launch (start us, length us, event | category | flops | bytes accessed | tf_op | source)
XLA Modules:
  0.0 578.7 jit_solution(15168826513201752360)
XLA Ops:
  12.3 7.1 %shard_map.221 = (bf16[128,1536]{1,0:T(8,128)(2,1)}, f32[128,1536]{1,0:T(8,128)}, bf16[128,1536]{1,0:T(8,128)(2,1)}, f32[128,128]{1,0:T(8,128)}) custom-call(s32[2,1,4]{2,1,0:T(1,128)S(1)} %copy-done.96, f32[1,1536]{1,0:T(1,128)} %gain.13, bf16[2,256,1536]{2,1,0:T(8,128)(2,1)} %tokens.2, bf16[1536,768]{1,0:T(8,128)(2,1)} %bitcast.61, ...), custom_call_target="tpu_custom_call" | custom-call | flops 22548578304 | bytes 6144 | tf_op jit(solution)/shard_map/pallas_call | solution.py:282
  102.4 6.7 %collective-permute-done.29 = bf16[128,1536]{1,0:T(8,128)(2,1)S(1)} collective-permute-done((bf16[128,1536]{1,0:T(8,128)(2,1)S(1)}, bf16[128,1536]{1,0:T(8,128)(2,1)S(1)}, u32[]{:S(2)}, u32[]{:S(2)}) %collective-permute-start.29) | collective-permute-done | bytes 393248 | tf_op jit(solution)/shard_map/ppermute | solution.py:56
  109.0 9.0 %collective-permute-done.28 = bf16[128,1536]{1,0:T(8,128)(2,1)S(1)} collective-permute-done((bf16[128,1536]{1,0:T(8,128)(2,1)S(1)}, bf16[128,1536]{1,0:T(8,128)(2,1)S(1)}, u32[]{:S(2)}, u32[]{:S(2)}) %collective-permute-start.28) | collective-permute-done | bytes 393248 | tf_op jit(solution)/shard_map/ppermute | solution.py:56
  146.2 7.0 %shard_map.233 = (bf16[128,1536]{1,0:T(8,128)(2,1)}, f32[128,1536]{1,0:T(8,128)}, bf16[128,1664]{1,0:T(8,128)(2,1)}, bf16[128,1024]{1,0:T(8,128)(2,1)}, bf16[128...) custom-call(bf16[128,1536]{1,0:T(8,128)(2,1)} %get-tuple-element.724.fresh, ...), custom_call_target="tpu_custom_call" | custom-call | flops 19327352832 | bytes 897024 | tf_op jit(solution)/shard_map/pallas_call | solution.py:282
  195.6 6.2 %shard_map.238 = (bf16[384,768]{1,0:T(8,128)(2,1)}, bf16[384,768]{1,0:T(8,128)(2,1)}, bf16[384,768]{1,0:T(8,128)(2,1)}, bf16[128,1536]{1,0:T(8,128)(2,1)S(1)}, b...) custom-call(bf16[1536,768]{1,0:T(8,128)(2,1)S(1)} %copy-done.7, bf16[1536,768]{1,0:T(8,128)(2,1)S(1)} %copy-done.9, ...), custom_call_target="tpu_custom_call" | custom-call | flops 43486543872 | tf_op jit(solution)/shard_map/pallas_call | solution.py:282
  227.6 7.4 %collective-permute-start.58 = (bf16[128,1536]{1,0:T(8,128)(2,1)S(1)}, bf16[128,1536]{1,0:T(8,128)(2,1)}, u32[]{:S(2)}, u32[]{:S(2)}) collective-permute-start(bf16[128,1536]{1,0:T(8,128)(2,1)S(1)} %add_convert_fusion.20), channel_id=1, source_target_pairs={{0,16},{1,17},{2,18},{3,19},{4,20},{5,21},{6,22},{7,23},{8,24},{9,... | collective-permute-start | bytes 1179656 | tf_op jit(solution)/shard_map/ppermute | solution.py:1091
  249.3 6.2 %shard_map.242 = (bf16[128,1536]{1,0:T(8,128)(2,1)}, f32[128,1536]{1,0:T(8,128)}, bf16[128,1664]{1,0:T(8,128)(2,1)}, bf16[128,1024]{1,0:T(8,128)(2,1)}, bf16[128...) custom-call(bf16[128,1536]{1,0:T(8,128)(2,1)} %get-tuple-element.706.fresh, ...), custom_call_target="tpu_custom_call" | custom-call | flops 19327352832 | bytes 897024 | tf_op jit(solution)/shard_map/pallas_call | solution.py:282
  255.5 8.4 %collective-permute-done.62 = bf16[128,1536]{1,0:T(8,128)(2,1)S(1)} collective-permute-done((bf16[128,1536]{1,0:T(8,128)(2,1)}, bf16[128,1536]{1,0:T(8,128)(2,1)S(1)}, u32[]{:S(2)}, u32[]{:S(2)}) %collective-permute-start.62) | collective-permute-done | bytes 393248 | tf_op jit(solution)/shard_map/ppermute | solution.py:67
  267.5 7.7 %shard_map.244 = (f32[128,1536]{1,0:T(8,128)}, bf16[128,1536]{1,0:T(8,128)(2,1)}, bf16[128,1536]{1,0:T(8,128)(2,1)}, bf16[128,1536]{1,0:T(8,128)(2,1)}, bf16[128...) custom-call(bf16[128,1536]{1,0:T(8,128)(2,1)} %get-tuple-element.1152.refs_0_.grad, ...), custom_call_target="tpu_custom_call" | custom-call | flops 38654705664 | bytes 2961408 | tf_op jit(solution)/shard_map/pallas_call | solution.py:282
  285.5 7.8 %collective-permute-done.67.refs_1_.refs_4_.refs_5_ = bf16[128,1664]{1,0:T(8,128)(2,1)S(1)} collective-permute-done((bf16[128,1664]{1,0:T(8,128)(2,1)S(1)}, bf16[128,1664]{1,0:T(8,128)(2,1)S(1)}, u32[]{:S(2)}, u32[]{:S(2)}) %collective-permute-start.67) | collective-permute-done | bytes 426016 | tf_op jit(solution)/shard_map/ppermute | solution.py:56
  299.6 8.2 %collective-permute-done.69 = bf16[128,1536]{1,0:T(8,128)(2,1)S(1)} collective-permute-done((bf16[128,1536]{1,0:T(8,128)(2,1)S(1)}, bf16[128,1536]{1,0:T(8,128)(2,1)S(1)}, u32[]{:S(2)}, u32[]{:S(2)}) %collective-permute-start.69) | collective-permute-done | bytes 393248 | tf_op jit(solution)/shard_map/ppermute | solution.py:1119
  323.3 6.6 %shard_map.248 = (bf16[384,768]{1,0:T(8,128)(2,1)}, bf16[384,768]{1,0:T(8,128)(2,1)}, bf16[384,768]{1,0:T(8,128)(2,1)}, bf16[128,1536]{1,0:T(8,128)(2,1)S(1)}, b...) custom-call(bf16[1536,768]{1,0:T(8,128)(2,1)S(1)} %copy-done.7, bf16[1536,768]{1,0:T(8,128)(2,1)S(1)} %copy-done.9, ...), custom_call_target="tpu_custom_call" | custom-call | flops 43486543872 | tf_op jit(solution)/shard_map/pallas_call | solution.py:282
  349.4 9.2 %shard_map.252 = (f32[1536,768]{1,0:T(8,128)}, f32[1536,768]{1,0:T(8,128)}) custom-call(bf16[128,1664]{1,0:T(8,128)(2,1)} %get-tuple-element.1257.refs_0_.refs_1_, bf16[128,1664]{1,0:T(8,128)(2,1)} %copy-done.29, bf16[128,1664]{1,0:T(8,128)(2,1)} %copy-done.27, bf16[128,1664]{1,0:T(8,128)(2,1)} %copy-done.25, bf16[128,1664]{1,0:T(8,128)(2,1)} %copy-done.31, ...), custom_call_target="tpu_custom_call" | custom-call | flops 77309411328 | bytes 1024 | tf_op jit(solution)/shard_map/pallas_call | solution.py:672
  370.3 11.6 %shard_map.253 = (f32[1536,768]{1,0:T(8,128)}, f32[1536,768]{1,0:T(8,128)}) custom-call(bf16[128,1664]{1,0:T(8,128)(2,1)} %get-tuple-element.1094.refs_0_.refs_1_, bf16[128,1664]{1,0:T(8,128)(2,1)} %copy-done.45, bf16[128,1664]{1,0:T(8,128)(2,1)} %copy-done.43, bf16[128,1664]{1,0:T(8,128)(2,1)} %copy-done.41, bf16[128,1664]{1,0:T(8,128)(2,1)} %copy-done.47, ...), custom_call_target="tpu_custom_call" | custom-call | flops 77309411328 | bytes 1024 | tf_op jit(solution)/shard_map/pallas_call | solution.py:672
  382.0 6.7 %collective-permute-done.86 = bf16[128,1536]{1,0:T(8,128)(2,1)S(1)} collective-permute-done((bf16[128,1536]{1,0:T(8,128)(2,1)S(1)}, bf16[128,1536]{1,0:T(8,128)(2,1)S(1)}, u32[]{:S(2)}, u32[]{:S(2)}) %collective-permute-start.86) | collective-permute-done | bytes 393248 | tf_op jit(solution)/shard_map/ppermute | solution.py:67
  389.8 7.6 %shard_map.254 = (f32[128,1536]{1,0:T(8,128)}, bf16[128,1536]{1,0:T(8,128)(2,1)}, bf16[128,1536]{1,0:T(8,128)(2,1)}, bf16[128,1536]{1,0:T(8,128)(2,1)}, bf16[128...) custom-call(bf16[128,1536]{1,0:T(8,128)(2,1)} %copy-done.5, ...), custom_call_target="tpu_custom_call" | custom-call | flops 38654705664 | bytes 2961408 | tf_op jit(solution)/shard_map/pallas_call | solution.py:282
  399.9 11.5 %shard_map.255.refs_12_ = f32[768,1536]{1,0:T(8,128)} custom-call(bf16[128,1536]{1,0:T(8,128)(2,1)} %get-tuple-element.1152.refs_0_.grad, bf16[128,1536]{1,0:T(8,128)(2,1)} %copy-done.60, bf16[128,1536]{1,0:T(8,128)(2,1)} %copy-done.58, bf16[128,1536]{1,0:T(8,128)(2,1)} %get-tuple-element.1155.refs_2_.refs_3_, ...), custom_call_target="tpu_custom_call" | custom-call | flops 77309411328 | bytes 2048 | tf_op jit(solution)/shard_map/pallas_call | solution.py:672
  412.5 6.3 %collective-permute-start.93 = (bf16[128,1536]{1,0:T(8,128)(2,1)S(1)}, bf16[128,1536]{1,0:T(8,128)(2,1)S(1)}, u32[]{:S(2)}, u32[]{:S(2)}) collective-permute-start(bf16[128,1536]{1,0:T(8,128)(2,1)S(1)} %collective-permute-done.87.refs_0_.refs_8_.grad), channel_id=1, source_target_pairs={{0,1},{1,0},{2,3},{3,2},{4,5},{5,4},{6,7},{7,6},{8,9},{9,8},{10,11... | collective-permute-start | bytes 1179656 | tf_op jit(solution)/shard_map/ppermute | solution.py:56
  470.6 11.3 %shard_map.260 = (f32[1536,384]{1,0:T(8,128)}, f32[1536,384]{1,0:T(8,128)}, bf16[1536,768]{1,0:T(8,128)(2,1)}) custom-call(bf16[128,1664]{1,0:T(8,128)(2,1)} %get-tuple-element.1257.refs_0_.refs_1_, bf16[128,1664]{1,0:T(8,128)(2,1)} %copy-done.29, bf16[128,1664]{1,0:T(8,128)(2,1)} %copy-done.27, bf16[128,1664]{1,0:T(8,128)(2,1)} %copy-done.25, ...), custom_call_target="tpu_custom_call" | custom-call | flops 77309411328 | bytes 1024 | tf_op jit(solution)/shard_map/pallas_call | solution.py:672
  485.8 7.3 %shard_map.261 = (bf16[576,768]{1,0:T(8,128)(2,1)}, bf16[576,768]{1,0:T(8,128)(2,1)}, bf16[960,768]{1,0:T(8,128)(2,1)}, bf16[960,768]{1,0:T(8,128)(2,1)}) custom-call(bf16[128,1536]{1,0:T(8,128)(2,1)} %get-tuple-element.966.refs_0_, bf16[128,1536]{1,0:T(8,128)(2,1)} %get-tuple-element.1283.refs_1_, bf16[128,768]{1,0:T(8,128)(2,1)} %get-tuple-element.969.refs_2_.refs_4_, ...), custom_call_target="tpu_custom_call" | custom-call | tf_op jit(solution)/shard_map/pallas_call | solution.py:760
  503.7 7.5 %shard_map.262 = (f32[128,1536]{1,0:T(8,128)}, bf16[128,1536]{1,0:T(8,128)(2,1)}, bf16[128,1536]{1,0:T(8,128)(2,1)}, bf16[128,1536]{1,0:T(8,128)(2,1)}, bf16[128...) custom-call(bf16[128,1536]{1,0:T(8,128)(2,1)} %copy-done.4, ...), custom_call_target="tpu_custom_call" | custom-call | flops 38654705664 | bytes 2961408 | tf_op jit(solution)/shard_map/pallas_call | solution.py:282
  516.7 8.4 %shard_map.263 = (bf16[576,1152]{1,0:T(8,128)(2,1)}, bf16[576,1152]{1,0:T(8,128)(2,1)}, bf16[960,1152]{1,0:T(8,128)(2,1)}, bf16[960,1152]{1,0:T(8,128)(2,1)}) custom-call(bf16[128,1536]{1,0:T(8,128)(2,1)} %get-tuple-element.965.refs_0_, bf16[128,1536]{1,0:T(8,128)(2,1)} %get-tuple-element.1282.refs_1_, bf16[128,1536]{1,0:T(8,128)(2,1)} %get-tuple-element.1296.refs_2_, ...), custom_call_target="tpu_custom_call" | custom-call | tf_op jit(solution)/shard_map/pallas_call | solution.py:760
  537.7 8.0 %shard_map.264 = (f32[384,1536]{1,0:T(8,128)}, bf16[384,1536]{1,0:T(8,128)(2,1)}) custom-call(bf16[128,1536]{1,0:T(8,128)(2,1)} %copy-done.4, bf16[128,1536]{1,0:T(8,128)(2,1)} %copy-done.75, bf16[128,1536]{1,0:T(8,128)(2,1)} %copy-done.74, bf16[128,1536]{1,0:T(8,128)(2,1)} %copy-done.73, bf16[128,1536]{1,0:T(8,128)(2,1)} %copy-done.76, ...), custom_call_target="tpu_custom_call" | custom-call | flops 38654705664 | bytes 1024 | tf_op jit(solution)/shard_map/pallas_call | solution.py:672
  566.9 8.9 %collective-permute-done.129 = bf16[192,1152]{1,0:T(8,128)(2,1)S(1)} collective-permute-done((bf16[192,1152]{1,0:T(8,128)(2,1)S(1)}, bf16[192,1152]{1,0:T(8,128)(2,1)S(1)}, u32[]{:S(2)}, u32[]{:S(2)}) %collective-permute-start.129) | collective-permute-done | bytes 442400 | tf_op jit(solution)/shard_map/ppermute | solution.py:67
  (727 shorter events, 381.1 us)
Async XLA Ops:
  4.2 16.8 %collective-permute-start.2 = (bf16[128,1536]{1,0:T(8,128)(2,1)}, bf16[128,1536]{1,0:T(8,128)(2,1)S(1)}, u32[]{:S(2)}, u32[]{:S(2)}) collective-permute-start(bf16[128,1536]{1,0:T(8,128)(2,1)} %get-tuple-element.1152.refs_0_.grad), channel_id=1, source_target_pairs={{0,8},{2,10},{4,12},{6,14},{8,0},{10,2},{12,4},{14,6},{1,9},{3,11}... | collective-permute-start | bytes 1179656 | tf_op jit(solution)/shard_map/ppermute | solution.py:56
  67.3 16.2 %collective-permute-start.17 = (bf16[192,1024]{1,0:T(8,128)(2,1)S(1)}, bf16[192,1024]{1,0:T(8,128)(2,1)S(1)}, u32[]{:S(2)}, u32[]{:S(2)}) collective-permute-start(bf16[192,1024]{1,0:T(8,128)(2,1)S(1)} %collective-permute-done.refs_0_), channel_id=1, source_target_pairs={{0,8},{2,10},{4,12},{6,14},{8,0},{10,2},{12,4},{14,6},{1,9},{3,11}... | collective-permute-start | bytes 1179656 | tf_op jit(solution)/shard_map/ppermute | solution.py:56
  98.6 19.4 %collective-permute-start.28 = (bf16[128,1536]{1,0:T(8,128)(2,1)S(1)}, bf16[128,1536]{1,0:T(8,128)(2,1)S(1)}, u32[]{:S(2)}, u32[]{:S(2)}) collective-permute-start(bf16[128,1536]{1,0:T(8,128)(2,1)S(1)} %add_convert_fusion.26), channel_id=1, source_target_pairs={{0,8},{2,10},{4,12},{6,14},{8,0},{10,2},{12,4},{14,6},{1,9},{3,11}... | collective-permute-start | bytes 1179656 | tf_op jit(solution)/shard_map/ppermute | solution.py:56
  99.7 19.1 %collective-permute-start.27 = (bf16[128,1536]{1,0:T(8,128)(2,1)S(1)}, bf16[128,1536]{1,0:T(8,128)(2,1)S(1)}, u32[]{:S(2)}, u32[]{:S(2)}) collective-permute-start(bf16[128,1536]{1,0:T(8,128)(2,1)S(1)} %add_convert_fusion.27), channel_id=1, source_target_pairs={{0,4},{2,6},{4,0},{6,2},{8,12},{10,14},{12,8},{14,10},{1,5},{3,7},... | collective-permute-start | bytes 1179656 | tf_op jit(solution)/shard_map/ppermute | solution.py:56
  101.1 17.7 %collective-permute-start.30 = (bf16[128,1536]{1,0:T(8,128)(2,1)S(1)}, bf16[128,1536]{1,0:T(8,128)(2,1)S(1)}, u32[]{:S(2)}, u32[]{:S(2)}) collective-permute-start(bf16[128,1536]{1,0:T(8,128)(2,1)S(1)} %copy-done.184), channel_id=1, source_target_pairs={{0,13},{1,12},{2,15},{3,14},{4,9},{5,8},{6,11},{7,10},{8,5},{9,4},... | collective-permute-start | bytes 1179656 | tf_op jit(solution)/shard_map/ppermute | solution.py:67
  119.8 19.9 %collective-permute-start.31 = (bf16[128,1536]{1,0:T(8,128)(2,1)}, bf16[128,1536]{1,0:T(8,128)(2,1)}, u32[]{:S(2)}, u32[]{:S(2)}) collective-permute-start(bf16[128,1536]{1,0:T(8,128)(2,1)} %add_convert_fusion.24), channel_id=1, source_target_pairs={{0,16},{1,17},{2,18},{3,19},{4,20},{5,21},{6,22},{7,23},{8,24},{9,... | collective-permute-start | bytes 1179656 | tf_op jit(solution)/shard_map/ppermute | solution.py:1032
  206.1 15.8 %collective-permute-start.51 = (bf16[128,1536]{1,0:T(8,128)(2,1)S(1)}, bf16[128,1536]{1,0:T(8,128)(2,1)S(1)}, u32[]{:S(2)}, u32[]{:S(2)}) collective-permute-start(bf16[128,1536]{1,0:T(8,128)(2,1)S(1)} %add_convert_fusion.23), channel_id=1, source_target_pairs={{0,4},{2,6},{4,0},{6,2},{8,12},{10,14},{12,8},{14,10},{1,5},{3,7},... | collective-permute-start | bytes 1179656 | tf_op jit(solution)/shard_map/ppermute | solution.py:56
  206.4 15.5 %collective-permute-start.52 = (bf16[128,1536]{1,0:T(8,128)(2,1)S(1)}, bf16[128,1536]{1,0:T(8,128)(2,1)S(1)}, u32[]{:S(2)}, u32[]{:S(2)}) collective-permute-start(bf16[128,1536]{1,0:T(8,128)(2,1)S(1)} %add_convert_fusion.22), channel_id=1, source_target_pairs={{0,8},{2,10},{4,12},{6,14},{8,0},{10,2},{12,4},{14,6},{1,9},{3,11}... | collective-permute-start | bytes 1179656 | tf_op jit(solution)/shard_map/ppermute | solution.py:56
  208.6 16.0 %collective-permute-start.54 = (bf16[128,1536]{1,0:T(8,128)(2,1)S(1)}, bf16[128,1536]{1,0:T(8,128)(2,1)S(1)}, u32[]{:S(2)}, u32[]{:S(2)}) collective-permute-start(bf16[128,1536]{1,0:T(8,128)(2,1)S(1)} %copy-done.186), channel_id=1, source_target_pairs={{0,13},{1,12},{2,15},{3,14},{4,9},{5,8},{6,11},{7,10},{8,5},{9,4},... | collective-permute-start | bytes 1179656 | tf_op jit(solution)/shard_map/ppermute | solution.py:67
  224.9 16.8 %collective-permute-start.55 = (bf16[128,1536]{1,0:T(8,128)(2,1)S(1)}, bf16[128,1536]{1,0:T(8,128)(2,1)S(1)}, u32[]{:S(2)}, u32[]{:S(2)}) collective-permute-start(bf16[128,1536]{1,0:T(8,128)(2,1)S(1)} %copy-done.94), channel_id=1, source_target_pairs={{0,8},{2,10},{4,12},{6,14},{8,0},{10,2},{12,4},{14,6},{1,9},{3,11}... | collective-permute-start | bytes 1179656 | tf_op jit(solution)/shard_map/ppermute | solution.py:56
  225.4 16.3 %collective-permute-start.56 = (bf16[128,1536]{1,0:T(8,128)(2,1)S(1)}, bf16[128,1536]{1,0:T(8,128)(2,1)S(1)}, u32[]{:S(2)}, u32[]{:S(2)}) collective-permute-start(bf16[128,1536]{1,0:T(8,128)(2,1)S(1)} %copy-done.92), channel_id=1, source_target_pairs={{0,1},{1,0},{2,3},{3,2},{4,5},{5,4},{6,7},{7,6},{8,9},{9,8},{10,11... | collective-permute-start | bytes 1179656 | tf_op jit(solution)/shard_map/ppermute | solution.py:56
  227.6 15.4 %collective-permute-start.58 = (bf16[128,1536]{1,0:T(8,128)(2,1)S(1)}, bf16[128,1536]{1,0:T(8,128)(2,1)}, u32[]{:S(2)}, u32[]{:S(2)}) collective-permute-start(bf16[128,1536]{1,0:T(8,128)(2,1)S(1)} %add_convert_fusion.20), channel_id=1, source_target_pairs={{0,16},{1,17},{2,18},{3,19},{4,20},{5,21},{6,22},{7,23},{8,24},{9,... | collective-permute-start | bytes 1179656 | tf_op jit(solution)/shard_map/ppermute | solution.py:1091
  246.8 17.2 %collective-permute-start.62 = (bf16[128,1536]{1,0:T(8,128)(2,1)}, bf16[128,1536]{1,0:T(8,128)(2,1)S(1)}, u32[]{:S(2)}, u32[]{:S(2)}) collective-permute-start(bf16[128,1536]{1,0:T(8,128)(2,1)} %get-tuple-element.944), channel_id=1, source_target_pairs={{0,13},{1,12},{2,15},{3,14},{4,9},{5,8},{6,11},{7,10},{8,5},{9,4},... | collective-permute-start | bytes 1179656 | tf_op jit(solution)/shard_map/ppermute | solution.py:67
  344.4 18.6 %collective-permute-start.79 = (bf16[128,1536]{1,0:T(8,128)(2,1)S(1)}, bf16[128,1536]{1,0:T(8,128)(2,1)S(1)}, u32[]{:S(2)}, u32[]{:S(2)}) collective-permute-start(bf16[128,1536]{1,0:T(8,128)(2,1)S(1)} %get-tuple-element.1044), channel_id=1, source_target_pairs={{0,8},{2,10},{4,12},{6,14},{8,0},{10,2},{12,4},{14,6},{1,9},{3,11}... | collective-permute-start | bytes 1179656 | tf_op jit(solution)/shard_map/ppermute | solution.py:56
  344.9 18.2 %collective-permute-start.80 = (bf16[128,1536]{1,0:T(8,128)(2,1)S(1)}, bf16[128,1536]{1,0:T(8,128)(2,1)S(1)}, u32[]{:S(2)}, u32[]{:S(2)}) collective-permute-start(bf16[128,1536]{1,0:T(8,128)(2,1)S(1)} %get-tuple-element.1045), channel_id=1, source_target_pairs={{0,1},{1,0},{2,3},{3,2},{4,5},{5,4},{6,7},{7,6},{8,9},{9,8},{10,11... | collective-permute-start | bytes 1179656 | tf_op jit(solution)/shard_map/ppermute | solution.py:56
  346.0 17.1 %collective-permute-start.81 = (bf16[128,1536]{1,0:T(8,128)(2,1)S(1)}, bf16[128,1536]{1,0:T(8,128)(2,1)S(1)}, u32[]{:S(2)}, u32[]{:S(2)}) collective-permute-start(bf16[128,1536]{1,0:T(8,128)(2,1)S(1)} %get-tuple-element.1046), channel_id=1, source_target_pairs={{0,4},{2,6},{4,0},{6,2},{8,12},{10,14},{12,8},{14,10},{1,5},{3,7},... | collective-permute-start | bytes 1179656 | tf_op jit(solution)/shard_map/ppermute | solution.py:56
  347.7 17.3 %collective-permute-start.82 = (bf16[128,1536]{1,0:T(8,128)(2,1)S(1)}, bf16[128,1536]{1,0:T(8,128)(2,1)S(1)}, u32[]{:S(2)}, u32[]{:S(2)}) collective-permute-start(bf16[128,1536]{1,0:T(8,128)(2,1)S(1)} %copy-done.182), channel_id=1, source_target_pairs={{0,13},{1,12},{2,15},{3,14},{4,9},{5,8},{6,11},{7,10},{8,5},{9,4},... | collective-permute-start | bytes 1179656 | tf_op jit(solution)/shard_map/ppermute | solution.py:67
  365.3 16.7 %collective-permute-start.83 = (bf16[128,1536]{1,0:T(8,128)(2,1)S(1)}, bf16[128,1536]{1,0:T(8,128)(2,1)S(1)}, u32[]{:S(2)}, u32[]{:S(2)}) collective-permute-start(bf16[128,1536]{1,0:T(8,128)(2,1)S(1)} %add_convert_fusion.16), channel_id=1, source_target_pairs={{0,4},{2,6},{4,0},{6,2},{8,12},{10,14},{12,8},{14,10},{1,5},{3,7},... | collective-permute-start | bytes 1179656 | tf_op jit(solution)/shard_map/ppermute | solution.py:56
  365.7 16.3 %collective-permute-start.84 = (bf16[128,1536]{1,0:T(8,128)(2,1)S(1)}, bf16[128,1536]{1,0:T(8,128)(2,1)S(1)}, u32[]{:S(2)}, u32[]{:S(2)}) collective-permute-start(bf16[128,1536]{1,0:T(8,128)(2,1)S(1)} %add_convert_fusion.15), channel_id=1, source_target_pairs={{0,8},{2,10},{4,12},{6,14},{8,0},{10,2},{12,4},{14,6},{1,9},{3,11}... | collective-permute-start | bytes 1179656 | tf_op jit(solution)/shard_map/ppermute | solution.py:56
  366.6 15.4 %collective-permute-start.85 = (bf16[128,1536]{1,0:T(8,128)(2,1)S(1)}, bf16[128,1536]{1,0:T(8,128)(2,1)S(1)}, u32[]{:S(2)}, u32[]{:S(2)}) collective-permute-start(bf16[128,1536]{1,0:T(8,128)(2,1)S(1)} %add_convert_fusion.14), channel_id=1, source_target_pairs={{0,1},{1,0},{2,3},{3,2},{4,5},{5,4},{6,7},{7,6},{8,9},{9,8},{10,11... | collective-permute-start | bytes 1179656 | tf_op jit(solution)/shard_map/ppermute | solution.py:56
  367.0 21.7 %collective-permute-start.86 = (bf16[128,1536]{1,0:T(8,128)(2,1)S(1)}, bf16[128,1536]{1,0:T(8,128)(2,1)S(1)}, u32[]{:S(2)}, u32[]{:S(2)}) collective-permute-start(bf16[128,1536]{1,0:T(8,128)(2,1)S(1)} %copy-done.185), channel_id=1, source_target_pairs={{0,13},{1,12},{2,15},{3,14},{4,9},{5,8},{6,11},{7,10},{8,5},{9,4},... | collective-permute-start | bytes 1179656 | tf_op jit(solution)/shard_map/ppermute | solution.py:67
  465.5 16.3 %collective-permute-start.104 = (bf16[128,1536]{1,0:T(8,128)(2,1)S(1)}, bf16[128,1536]{1,0:T(8,128)(2,1)S(1)}, u32[]{:S(2)}, u32[]{:S(2)}) collective-permute-start(bf16[128,1536]{1,0:T(8,128)(2,1)S(1)} %add_convert_fusion.9), channel_id=1, source_target_pairs={{0,4},{2,6},{4,0},{6,2},{8,12},{10,14},{12,8},{14,10},{1,5},{3,7},... | collective-permute-start | bytes 1179656 | tf_op jit(solution)/shard_map/ppermute | solution.py:56
  513.7 16.1 %collective-permute-start.119 = (bf16[192,768]{1,0:T(8,128)(2,1)S(1)}, bf16[192,768]{1,0:T(8,128)(2,1)S(1)}, u32[]{:S(2)}, u32[]{:S(2)}) collective-permute-start(bf16[192,768]{1,0:T(8,128)(2,1)S(1)} %get-tuple-element.1327), channel_id=1, source_target_pairs={{0,13},{1,12},{2,15},{3,14},{4,9},{5,8},{6,11},{7,10},{8,5},{9,4},... | collective-permute-start | bytes 884744 | tf_op jit(solution)/shard_map/ppermute | solution.py:67
  554.5 21.3 %collective-permute-start.129 = (bf16[192,1152]{1,0:T(8,128)(2,1)S(1)}, bf16[192,1152]{1,0:T(8,128)(2,1)S(1)}, u32[]{:S(2)}, u32[]{:S(2)}) collective-permute-start(bf16[192,1152]{1,0:T(8,128)(2,1)S(1)} %get-tuple-element.1379), channel_id=1, source_target_pairs={{0,13},{1,12},{2,15},{3,14},{4,9},{5,8},{6,11},{7,10},{8,5},{9,4},... | collective-permute-start | bytes 1327112 | tf_op jit(solution)/shard_map/ppermute | solution.py:67
  (296 other events, 3247.9 us)

commit v7 on v6

--- a/solution.py
+++ b/solution.py
@@ -386,7 +386,7 @@
     rows = block // 2
     width, out = sum(w.shape[1] for w in weights[:3]), weights[3].shape[1]
     shapes = [
-        like((rows, model), bf16), like((rows, model), f32), like((rows, model), bf16), like((rows, rows), f32)
+        like((rows, model), bf16), held((rows, model), f32), like((rows, model), bf16), like((rows, rows), f32)
     ]
     scratch = [pltpu.VMEM((block, n), bf16) for n in (width, out, model)] + holders(*weights)
     return on_device(
@@ -426,7 +426,7 @@
     )
 
 
-def joined_body(part, other, extra, gain, hidden, payload):
+def joined_body(other, extra, gain, part, hidden, payload):
     total = part[...] + wide(other[...])
     hidden[...] = total
     model = total.shape[1]
@@ -437,7 +437,7 @@
 def joined(part, other, gain, extra):
     rows, model = part.shape
     shapes = [like((rows, model), f32), like((rows, model + extra.shape[1]), bf16)]
-    return on_device(joined_body, shapes, [part, other, extra, gain], 10 * rows * model)
+    return on_device(joined_body, shapes, [other, extra, gain], 10 * rows * model, kept=[part])
 
 
 def by_halves(refs):
@@ -572,7 +572,7 @@
     count = sum(p.shape[0] for p in pieces)
     model, units = weights[0].shape
     extra = pieces[0].shape[1] - model
-    kind = held if HELD and len(pieces) == 3 else like
+    kind = held if HELD else like
     shapes = [like((count, units), bf16)] * 2 + [kind((p.shape[0], model), bf16) for p in pieces]
     scratch = [pltpu.VMEM((count, n), bf16) for n in (model, extra, units, units, model)]
     scratch.append(pltpu.SemaphoreType.DMA((3 * len(pieces) + 2,)))
@@ -623,7 +623,7 @@
     count = sum(p.shape[0] for p in pieces)
     model, units = weights[0].shape
     extra = payloads[0].shape[1] - model
-    kind = held if HELD and len(pieces) == 3 else like
+    kind = held if HELD else like
     shapes = [like((count, units), bf16)] * 3 + [kind((p.shape[0], model), bf16) for p in pieces]
     scratch = [pltpu.VMEM((count, n), bf16) for n in (model, extra, units, units, units, units, units, model)]
     scratch.append(pltpu.SemaphoreType.DMA((3 * len(pieces) + 5,)))

time: 585 us -> 581 us (level)
  starting transfers between devices: 142 us -> 150 us
  other arithmetic: 34.7 us -> 28.5 us
    ppermute x119, starting transfers between devices: 109 us -> 121 us  [swap(): lax.ppermute(value, axis, [(i, i ^ bit) for i in range(lax.axis_size(axis...]
    ppermute x119, waiting for transfers between devices: 91.1 us -> 99.7 us  [swap(): lax.ppermute(value, axis, [(i, i ^ bit) for i in range(lax.axis_size(axis...]
    ppermute x8, waiting for transfers between devices: 33.2 us -> 25.3 us  [across(): return lax.ppermute(value, ('dp', 'shard'), pairs)]
    unnamed x376 -> x356, local copies, waits for them, and re-layouts: 21.4 us -> 18 us
  transfers between devices with their start and end apart: 131 -> 131, of which waited for: 55 -> 60; matrix products, arithmetic and copies ran while one was open for 5% -> 4% of each run, Pallas kernels for 36% -> 36%
where the time goes in v7:
time: 581 us; the launch traced here: 575 us
  Pallas kernels  228 us (39%)
  starting transfers between devices  150 us (26%)
  waiting for transfers between devices  137 us (24%)
  other arithmetic  28.5 us (5%)
  local copies, waits for them, and re-layouts  27.4 us (5%)
    pallas_call x33, Pallas kernels, on_device(): pl.pallas_call(body, out_shape=outs, in_specs=[SMEM] * len(scalars) + [VM...  150 us
    ppermute x119, starting transfers between devices, swap(): lax.ppermute(value, axis, [(i, i ^ bit) for i in range(lax.axis_size(axis...  121 us
    ppermute x119, waiting for transfers between devices, swap(): lax.ppermute(value, axis, [(i, i ^ bit) for i in range(lax.axis_size(axis...  99.7 us
    pallas_call x5, Pallas kernels, swept_products(): pl.pallas_call(body, grid=(steps,), out_shape=shapes, in_specs=in_specs,...  52.2 us
    ppermute x8, waiting for transfers between devices, across(): return lax.ppermute(value, ('dp', 'shard'), pairs)  25.3 us
    unnamed x356, local copies, waits for them, and re-layouts  18 us
    pallas_call x2, Pallas kernels, owned_products(): pl.pallas_call(functools.partial(owned_body, len(lefts), len(rights), blo...  15.7 us
    ppermute x8, starting transfers between devices, across(): return lax.ppermute(value, ('dp', 'shard'), pairs)  13.8 us
  transfers between devices with their start and end apart: 131, of which 60 were waited for; matrix products, arithmetic and copies ran while one was open for 4% of the time, Pallas kernels for 36%

profile of v7, /device:TPU:0, one launch (start us, length us, event | category | flops | bytes accessed | tf_op | source)
XLA Modules:
  0.0 575.3 jit_solution(2875614860036067819)
XLA Ops:
  12.3 6.9 %shard_map.221 = (bf16[128,1536]{1,0:T(8,128)(2,1)}, f32[128,1536]{1,0:T(8,128)S(1)}, bf16[128,1536]{1,0:T(8,128)(2,1)}, f32[128,128]{1,0:T(8,128)}) custom-call(s32[2,1,4]{2,1,0:T(1,128)S(1)} %copy-done.98, f32[1,1536]{1,0:T(1,128)} %gain.13, bf16[2,256,1536]{2,1,0:T(8,128)(2,1)} %tokens.2, bf16[1536,768]{1,0:T(8,128)(2,1)} %bitcast.61, ...), custom_call_target="tpu_custom_call" | custom-call | flops 22548578304 | bytes 6144 | tf_op jit(solution)/shard_map/pallas_call | solution.py:282
  101.0 6.7 %collective-permute-done.29 = bf16[128,1536]{1,0:T(8,128)(2,1)S(1)} collective-permute-done((bf16[128,1536]{1,0:T(8,128)(2,1)S(1)}, bf16[128,1536]{1,0:T(8,128)(2,1)S(1)}, u32[]{:S(2)}, u32[]{:S(2)}) %collective-permute-start.29) | collective-permute-done | bytes 393248 | tf_op jit(solution)/shard_map/ppermute | solution.py:56
  107.6 9.0 %collective-permute-done.28 = bf16[128,1536]{1,0:T(8,128)(2,1)S(1)} collective-permute-done((bf16[128,1536]{1,0:T(8,128)(2,1)S(1)}, bf16[128,1536]{1,0:T(8,128)(2,1)S(1)}, u32[]{:S(2)}, u32[]{:S(2)}) %collective-permute-start.28) | collective-permute-done | bytes 393248 | tf_op jit(solution)/shard_map/ppermute | solution.py:56
  144.7 7.0 %shard_map.233 = (bf16[128,1536]{1,0:T(8,128)(2,1)}, f32[128,1536]{1,0:T(8,128)}, bf16[128,1664]{1,0:T(8,128)(2,1)}, bf16[128,1024]{1,0:T(8,128)(2,1)}, bf16[128...) custom-call(bf16[128,1536]{1,0:T(8,128)(2,1)} %get-tuple-element.724.fresh, ...), custom_call_target="tpu_custom_call" | custom-call | flops 19327352832 | bytes 897024 | tf_op jit(solution)/shard_map/pallas_call | solution.py:282
  194.5 6.3 %shard_map.238 = (bf16[384,768]{1,0:T(8,128)(2,1)}, bf16[384,768]{1,0:T(8,128)(2,1)}, bf16[384,768]{1,0:T(8,128)(2,1)}, bf16[128,1536]{1,0:T(8,128)(2,1)}, bf16[...) custom-call(bf16[1536,768]{1,0:T(8,128)(2,1)S(1)} %copy-done.7, bf16[1536,768]{1,0:T(8,128)(2,1)S(1)} %copy-done.10, ...), custom_call_target="tpu_custom_call" | custom-call | flops 43486543872 | tf_op jit(solution)/shard_map/pallas_call | solution.py:282
  210.3 6.2 %shard_map.239 = (bf16[384,768]{1,0:T(8,128)(2,1)}, bf16[384,768]{1,0:T(8,128)(2,1)}, bf16[384,768]{1,0:T(8,128)(2,1)}, bf16[128,1536]{1,0:T(8,128)(2,1)S(1)}, b...) custom-call(bf16[1536,768]{1,0:T(8,128)(2,1)S(1)} %copy-done.7, bf16[1536,768]{1,0:T(8,128)(2,1)S(1)} %copy-done.10, ...), custom_call_target="tpu_custom_call" | custom-call | flops 43486543872 | tf_op jit(solution)/shard_map/pallas_call | solution.py:282
  226.7 7.1 %collective-permute-start.58 = (bf16[128,1536]{1,0:T(8,128)(2,1)S(1)}, bf16[128,1536]{1,0:T(8,128)(2,1)S(1)}, u32[]{:S(2)}, u32[]{:S(2)}) collective-permute-start(bf16[128,1536]{1,0:T(8,128)(2,1)S(1)} %add_convert_fusion.20), channel_id=1, source_target_pairs={{0,16},{1,17},{2,18},{3,19},{4,20},{5,21},{6,22},{7,23},{8,24},{9,... | collective-permute-start | bytes 1179656 | tf_op jit(solution)/shard_map/ppermute | solution.py:1091
  248.6 6.2 %shard_map.242 = (bf16[128,1536]{1,0:T(8,128)(2,1)}, f32[128,1536]{1,0:T(8,128)}, bf16[128,1664]{1,0:T(8,128)(2,1)}, bf16[128,1024]{1,0:T(8,128)(2,1)}, bf16[128...) custom-call(bf16[128,1536]{1,0:T(8,128)(2,1)} %get-tuple-element.706.fresh, ...), custom_call_target="tpu_custom_call" | custom-call | flops 19327352832 | bytes 897024 | tf_op jit(solution)/shard_map/pallas_call | solution.py:282
  255.9 7.2 %collective-permute-done.62 = bf16[128,1536]{1,0:T(8,128)(2,1)S(1)} collective-permute-done((bf16[128,1536]{1,0:T(8,128)(2,1)S(1)}, bf16[128,1536]{1,0:T(8,128)(2,1)S(1)}, u32[]{:S(2)}, u32[]{:S(2)}) %collective-permute-start.62) | collective-permute-done | bytes 393248 | tf_op jit(solution)/shard_map/ppermute | solution.py:67
  266.4 7.7 %shard_map.244 = (f32[128,1536]{1,0:T(8,128)}, bf16[128,1536]{1,0:T(8,128)(2,1)}, bf16[128,1536]{1,0:T(8,128)(2,1)}, bf16[128,1536]{1,0:T(8,128)(2,1)}, bf16[128...) custom-call(bf16[128,1536]{1,0:T(8,128)(2,1)} %get-tuple-element.1152.refs_0_.grad, ...), custom_call_target="tpu_custom_call" | custom-call | flops 38654705664 | bytes 2961408 | tf_op jit(solution)/shard_map/pallas_call | solution.py:282
  295.6 8.4 %collective-permute-done.69 = bf16[128,1536]{1,0:T(8,128)(2,1)S(1)} collective-permute-done((bf16[128,1536]{1,0:T(8,128)(2,1)S(1)}, bf16[128,1536]{1,0:T(8,128)(2,1)S(1)}, u32[]{:S(2)}, u32[]{:S(2)}) %collective-permute-start.69) | collective-permute-done | bytes 393248 | tf_op jit(solution)/shard_map/ppermute | solution.py:1119
  331.5 6.2 %shard_map.249 = (bf16[384,768]{1,0:T(8,128)(2,1)}, bf16[384,768]{1,0:T(8,128)(2,1)}, bf16[384,768]{1,0:T(8,128)(2,1)}, bf16[128,1536]{1,0:T(8,128)(2,1)S(1)}, b...) custom-call(bf16[1536,768]{1,0:T(8,128)(2,1)S(1)} %copy-done.7, bf16[1536,768]{1,0:T(8,128)(2,1)S(1)} %copy-done.12, ...), custom_call_target="tpu_custom_call" | custom-call | flops 43486543872 | tf_op jit(solution)/shard_map/pallas_call | solution.py:282
  340.0 8.6 %collective-permute-start.79 = (bf16[128,1536]{1,0:T(8,128)(2,1)S(1)}, bf16[128,1536]{1,0:T(8,128)(2,1)S(1)}, u32[]{:S(2)}, u32[]{:S(2)}) collective-permute-start(bf16[128,1536]{1,0:T(8,128)(2,1)S(1)} %get-tuple-element.1044), channel_id=1, source_target_pairs={{0,8},{2,10},{4,12},{6,14},{8,0},{10,2},{12,4},{14,6},{1,9},{3,11}... | collective-permute-start | bytes 1179656 | tf_op jit(solution)/shard_map/ppermute | solution.py:56
  352.1 9.2 %shard_map.252 = (f32[1536,768]{1,0:T(8,128)}, f32[1536,768]{1,0:T(8,128)}) custom-call(bf16[128,1664]{1,0:T(8,128)(2,1)} %get-tuple-element.1257.refs_0_.refs_1_, bf16[128,1664]{1,0:T(8,128)(2,1)} %copy-done.37, bf16[128,1664]{1,0:T(8,128)(2,1)} %copy-done.35, bf16[128,1664]{1,0:T(8,128)(2,1)} %copy-done.33, bf16[128,1664]{1,0:T(8,128)(2,1)} %copy-done.39, ...), custom_call_target="tpu_custom_call" | custom-call | flops 77309411328 | bytes 1024 | tf_op jit(solution)/shard_map/pallas_call | solution.py:672
  371.0 11.9 %shard_map.253 = (f32[1536,768]{1,0:T(8,128)}, f32[1536,768]{1,0:T(8,128)}) custom-call(bf16[128,1664]{1,0:T(8,128)(2,1)} %get-tuple-element.1094.refs_0_.refs_1_, bf16[128,1664]{1,0:T(8,128)(2,1)} %copy-done.50, bf16[128,1664]{1,0:T(8,128)(2,1)} %copy-done.49, bf16[128,1664]{1,0:T(8,128)(2,1)} %copy-done.48, bf16[128,1664]{1,0:T(8,128)(2,1)} %copy-done.51, ...), custom_call_target="tpu_custom_call" | custom-call | flops 77309411328 | bytes 1024 | tf_op jit(solution)/shard_map/pallas_call | solution.py:672
  387.4 7.7 %shard_map.254 = (f32[128,1536]{1,0:T(8,128)}, bf16[128,1536]{1,0:T(8,128)(2,1)}, bf16[128,1536]{1,0:T(8,128)(2,1)}, bf16[128,1536]{1,0:T(8,128)(2,1)}, bf16[128...) custom-call(bf16[128,1536]{1,0:T(8,128)(2,1)} %copy-done.5, ...), custom_call_target="tpu_custom_call" | custom-call | flops 38654705664 | bytes 2961408 | tf_op jit(solution)/shard_map/pallas_call | solution.py:282
  398.2 11.8 %shard_map.255.refs_12_ = f32[768,1536]{1,0:T(8,128)} custom-call(bf16[128,1536]{1,0:T(8,128)(2,1)} %get-tuple-element.1152.refs_0_.grad, bf16[128,1536]{1,0:T(8,128)(2,1)} %copy-done.62, bf16[128,1536]{1,0:T(8,128)(2,1)} %copy-done.60, bf16[128,1536]{1,0:T(8,128)(2,1)} %get-tuple-element.1155.refs_2_.refs_3_, bf16[128,1536]{1,0:T(8,128)(2,1)} %copy-done.73, ...), custom_call_target="tpu_custom_call" | custom-call | flops 77309411328 | bytes 2048 | tf_op jit(solution)/shard_map/pallas_call | solution.py:672
  412.7 7.3 %collective-permute-start.93 = (bf16[128,1536]{1,0:T(8,128)(2,1)S(1)}, bf16[128,1536]{1,0:T(8,128)(2,1)S(1)}, u32[]{:S(2)}, u32[]{:S(2)}) collective-permute-start(bf16[128,1536]{1,0:T(8,128)(2,1)S(1)} %collective-permute-done.87.refs_0_.refs_8_.grad), channel_id=1, source_target_pairs={{0,1},{1,0},{2,3},{3,2},{4,5},{5,4},{6,7},{7,6},{8,9},{9,8},{10,11... | collective-permute-start | bytes 1179656 | tf_op jit(solution)/shard_map/ppermute | solution.py:56
  470.0 11.3 %shard_map.260 = (f32[1536,384]{1,0:T(8,128)}, f32[1536,384]{1,0:T(8,128)}, bf16[1536,768]{1,0:T(8,128)(2,1)}) custom-call(bf16[128,1664]{1,0:T(8,128)(2,1)} %get-tuple-element.1257.refs_0_.refs_1_, bf16[128,1664]{1,0:T(8,128)(2,1)} %copy-done.37, bf16[128,1664]{1,0:T(8,128)(2,1)} %copy-done.35, bf16[128,1664]{1,0:T(8,128)(2,1)} %copy-done.33, ...), custom_call_target="tpu_custom_call" | custom-call | flops 77309411328 | bytes 1024 | tf_op jit(solution)/shard_map/pallas_call | solution.py:672
  484.5 7.3 %shard_map.261 = (bf16[576,768]{1,0:T(8,128)(2,1)}, bf16[576,768]{1,0:T(8,128)(2,1)}, bf16[960,768]{1,0:T(8,128)(2,1)}, bf16[960,768]{1,0:T(8,128)(2,1)}) custom-call(bf16[128,1536]{1,0:T(8,128)(2,1)} %get-tuple-element.966.refs_0_, bf16[128,1536]{1,0:T(8,128)(2,1)} %get-tuple-element.1283.refs_1_, bf16[128,768]{1,0:T(8,128)(2,1)} %get-tuple-element.969.refs_2_.refs_4_, ...), custom_call_target="tpu_custom_call" | custom-call | tf_op jit(solution)/shard_map/pallas_call | solution.py:760
  500.4 7.5 %shard_map.262 = (f32[128,1536]{1,0:T(8,128)}, bf16[128,1536]{1,0:T(8,128)(2,1)}, bf16[128,1536]{1,0:T(8,128)(2,1)}, bf16[128,1536]{1,0:T(8,128)(2,1)}, bf16[128...) custom-call(bf16[128,1536]{1,0:T(8,128)(2,1)} %copy-done.4, ...), custom_call_target="tpu_custom_call" | custom-call | flops 38654705664 | bytes 2961408 | tf_op jit(solution)/shard_map/pallas_call | solution.py:282
  513.5 8.4 %shard_map.263 = (bf16[576,1152]{1,0:T(8,128)(2,1)}, bf16[576,1152]{1,0:T(8,128)(2,1)}, bf16[960,1152]{1,0:T(8,128)(2,1)}, bf16[960,1152]{1,0:T(8,128)(2,1)}) custom-call(bf16[128,1536]{1,0:T(8,128)(2,1)} %get-tuple-element.965.refs_0_, bf16[128,1536]{1,0:T(8,128)(2,1)} %get-tuple-element.1282.refs_1_, bf16[128,1536]{1,0:T(8,128)(2,1)} %get-tuple-element.1296.refs_2_, ...), custom_call_target="tpu_custom_call" | custom-call | tf_op jit(solution)/shard_map/pallas_call | solution.py:760
  536.4 8.0 %shard_map.264 = (f32[384,1536]{1,0:T(8,128)}, bf16[384,1536]{1,0:T(8,128)(2,1)}) custom-call(bf16[128,1536]{1,0:T(8,128)(2,1)} %copy-done.4, bf16[128,1536]{1,0:T(8,128)(2,1)} %copy-done.77, bf16[128,1536]{1,0:T(8,128)(2,1)} %copy-done.76, bf16[128,1536]{1,0:T(8,128)(2,1)} %copy-done.75, bf16[128,1536]{1,0:T(8,128)(2,1)} %copy-done.78, ...), custom_call_target="tpu_custom_call" | custom-call | flops 38654705664 | bytes 1024 | tf_op jit(solution)/shard_map/pallas_call | solution.py:672
  565.3 7.2 %collective-permute-done.129 = bf16[192,1152]{1,0:T(8,128)(2,1)S(1)} collective-permute-done((bf16[192,1152]{1,0:T(8,128)(2,1)S(1)}, bf16[192,1152]{1,0:T(8,128)(2,1)S(1)}, u32[]{:S(2)}, u32[]{:S(2)}) %collective-permute-start.129) | collective-permute-done | bytes 442400 | tf_op jit(solution)/shard_map/ppermute | solution.py:67
  (707 shorter events, 379.7 us)
Async XLA Ops:
  4.2 16.8 %collective-permute-start.2 = (bf16[128,1536]{1,0:T(8,128)(2,1)}, bf16[128,1536]{1,0:T(8,128)(2,1)S(1)}, u32[]{:S(2)}, u32[]{:S(2)}) collective-permute-start(bf16[128,1536]{1,0:T(8,128)(2,1)} %get-tuple-element.1152.refs_0_.grad), channel_id=1, source_target_pairs={{0,8},{2,10},{4,12},{6,14},{8,0},{10,2},{12,4},{14,6},{1,9},{3,11}... | collective-permute-start | bytes 1179656 | tf_op jit(solution)/shard_map/ppermute | solution.py:56
  65.9 16.2 %collective-permute-start.17 = (bf16[192,1024]{1,0:T(8,128)(2,1)S(1)}, bf16[192,1024]{1,0:T(8,128)(2,1)S(1)}, u32[]{:S(2)}, u32[]{:S(2)}) collective-permute-start(bf16[192,1024]{1,0:T(8,128)(2,1)S(1)} %collective-permute-done.refs_0_), channel_id=1, source_target_pairs={{0,8},{2,10},{4,12},{6,14},{8,0},{10,2},{12,4},{14,6},{1,9},{3,11}... | collective-permute-start | bytes 1179656 | tf_op jit(solution)/shard_map/ppermute | solution.py:56
  97.3 19.4 %collective-permute-start.28 = (bf16[128,1536]{1,0:T(8,128)(2,1)S(1)}, bf16[128,1536]{1,0:T(8,128)(2,1)S(1)}, u32[]{:S(2)}, u32[]{:S(2)}) collective-permute-start(bf16[128,1536]{1,0:T(8,128)(2,1)S(1)} %add_convert_fusion.26), channel_id=1, source_target_pairs={{0,8},{2,10},{4,12},{6,14},{8,0},{10,2},{12,4},{14,6},{1,9},{3,11}... | collective-permute-start | bytes 1179656 | tf_op jit(solution)/shard_map/ppermute | solution.py:56
  98.3 19.1 %collective-permute-start.27 = (bf16[128,1536]{1,0:T(8,128)(2,1)S(1)}, bf16[128,1536]{1,0:T(8,128)(2,1)S(1)}, u32[]{:S(2)}, u32[]{:S(2)}) collective-permute-start(bf16[128,1536]{1,0:T(8,128)(2,1)S(1)} %add_convert_fusion.27), channel_id=1, source_target_pairs={{0,4},{2,6},{4,0},{6,2},{8,12},{10,14},{12,8},{14,10},{1,5},{3,7},... | collective-permute-start | bytes 1179656 | tf_op jit(solution)/shard_map/ppermute | solution.py:56
  99.7 17.7 %collective-permute-start.30 = (bf16[128,1536]{1,0:T(8,128)(2,1)S(1)}, bf16[128,1536]{1,0:T(8,128)(2,1)S(1)}, u32[]{:S(2)}, u32[]{:S(2)}) collective-permute-start(bf16[128,1536]{1,0:T(8,128)(2,1)S(1)} %get-tuple-element.801), channel_id=1, source_target_pairs={{0,13},{1,12},{2,15},{3,14},{4,9},{5,8},{6,11},{7,10},{8,5},{9,4},... | collective-permute-start | bytes 1179656 | tf_op jit(solution)/shard_map/ppermute | solution.py:67
  118.4 19.9 %collective-permute-start.31 = (bf16[128,1536]{1,0:T(8,128)(2,1)}, bf16[128,1536]{1,0:T(8,128)(2,1)}, u32[]{:S(2)}, u32[]{:S(2)}) collective-permute-start(bf16[128,1536]{1,0:T(8,128)(2,1)} %add_convert_fusion.24), channel_id=1, source_target_pairs={{0,16},{1,17},{2,18},{3,19},{4,20},{5,21},{6,22},{7,23},{8,24},{9,... | collective-permute-start | bytes 1179656 | tf_op jit(solution)/shard_map/ppermute | solution.py:1032
  205.2 15.6 %collective-permute-start.51 = (bf16[128,1536]{1,0:T(8,128)(2,1)S(1)}, bf16[128,1536]{1,0:T(8,128)(2,1)S(1)}, u32[]{:S(2)}, u32[]{:S(2)}) collective-permute-start(bf16[128,1536]{1,0:T(8,128)(2,1)S(1)} %add_convert_fusion.23), channel_id=1, source_target_pairs={{0,4},{2,6},{4,0},{6,2},{8,12},{10,14},{12,8},{14,10},{1,5},{3,7},... | collective-permute-start | bytes 1179656 | tf_op jit(solution)/shard_map/ppermute | solution.py:56
  207.6 16.2 %collective-permute-start.54 = (bf16[128,1536]{1,0:T(8,128)(2,1)S(1)}, bf16[128,1536]{1,0:T(8,128)(2,1)S(1)}, u32[]{:S(2)}, u32[]{:S(2)}) collective-permute-start(bf16[128,1536]{1,0:T(8,128)(2,1)S(1)} %get-tuple-element.890), channel_id=1, source_target_pairs={{0,13},{1,12},{2,15},{3,14},{4,9},{5,8},{6,11},{7,10},{8,5},{9,4},... | collective-permute-start | bytes 1179656 | tf_op jit(solution)/shard_map/ppermute | solution.py:67
  224.1 16.0 %collective-permute-start.55 = (bf16[128,1536]{1,0:T(8,128)(2,1)}, bf16[128,1536]{1,0:T(8,128)(2,1)S(1)}, u32[]{:S(2)}, u32[]{:S(2)}) collective-permute-start(bf16[128,1536]{1,0:T(8,128)(2,1)} %get-tuple-element.920), channel_id=1, source_target_pairs={{0,8},{2,10},{4,12},{6,14},{8,0},{10,2},{12,4},{14,6},{1,9},{3,11}... | collective-permute-start | bytes 1179656 | tf_op jit(solution)/shard_map/ppermute | solution.py:56
  224.7 15.4 %collective-permute-start.56 = (bf16[128,1536]{1,0:T(8,128)(2,1)}, bf16[128,1536]{1,0:T(8,128)(2,1)S(1)}, u32[]{:S(2)}, u32[]{:S(2)}) collective-permute-start(bf16[128,1536]{1,0:T(8,128)(2,1)} %get-tuple-element.921), channel_id=1, source_target_pairs={{0,1},{1,0},{2,3},{3,2},{4,5},{5,4},{6,7},{7,6},{8,9},{9,8},{10,11... | collective-permute-start | bytes 1179656 | tf_op jit(solution)/shard_map/ppermute | solution.py:56
  226.7 16.6 %collective-permute-start.58 = (bf16[128,1536]{1,0:T(8,128)(2,1)S(1)}, bf16[128,1536]{1,0:T(8,128)(2,1)S(1)}, u32[]{:S(2)}, u32[]{:S(2)}) collective-permute-start(bf16[128,1536]{1,0:T(8,128)(2,1)S(1)} %add_convert_fusion.20), channel_id=1, source_target_pairs={{0,16},{1,17},{2,18},{3,19},{4,20},{5,21},{6,22},{7,23},{8,24},{9,... | collective-permute-start | bytes 1179656 | tf_op jit(solution)/shard_map/ppermute | solution.py:1091
  245.8 17.4 %collective-permute-start.62 = (bf16[128,1536]{1,0:T(8,128)(2,1)S(1)}, bf16[128,1536]{1,0:T(8,128)(2,1)S(1)}, u32[]{:S(2)}, u32[]{:S(2)}) collective-permute-start(bf16[128,1536]{1,0:T(8,128)(2,1)S(1)} %get-tuple-element.944), channel_id=1, source_target_pairs={{0,13},{1,12},{2,15},{3,14},{4,9},{5,8},{6,11},{7,10},{8,5},{9,4},... | collective-permute-start | bytes 1179656 | tf_op jit(solution)/shard_map/ppermute | solution.py:67
  340.0 25.6 %collective-permute-start.79 = (bf16[128,1536]{1,0:T(8,128)(2,1)S(1)}, bf16[128,1536]{1,0:T(8,128)(2,1)S(1)}, u32[]{:S(2)}, u32[]{:S(2)}) collective-permute-start(bf16[128,1536]{1,0:T(8,128)(2,1)S(1)} %get-tuple-element.1044), channel_id=1, source_target_pairs={{0,8},{2,10},{4,12},{6,14},{8,0},{10,2},{12,4},{14,6},{1,9},{3,11}... | collective-permute-start | bytes 1179656 | tf_op jit(solution)/shard_map/ppermute | solution.py:56
  348.6 17.1 %collective-permute-start.80 = (bf16[128,1536]{1,0:T(8,128)(2,1)S(1)}, bf16[128,1536]{1,0:T(8,128)(2,1)S(1)}, u32[]{:S(2)}, u32[]{:S(2)}) collective-permute-start(bf16[128,1536]{1,0:T(8,128)(2,1)S(1)} %get-tuple-element.1045), channel_id=1, source_target_pairs={{0,1},{1,0},{2,3},{3,2},{4,5},{5,4},{6,7},{7,6},{8,9},{9,8},{10,11... | collective-permute-start | bytes 1179656 | tf_op jit(solution)/shard_map/ppermute | solution.py:56
  366.0 17.0 %collective-permute-start.83 = (bf16[128,1536]{1,0:T(8,128)(2,1)S(1)}, bf16[128,1536]{1,0:T(8,128)(2,1)S(1)}, u32[]{:S(2)}, u32[]{:S(2)}) collective-permute-start(bf16[128,1536]{1,0:T(8,128)(2,1)S(1)} %add_convert_fusion.16), channel_id=1, source_target_pairs={{0,4},{2,6},{4,0},{6,2},{8,12},{10,14},{12,8},{14,10},{1,5},{3,7},... | collective-permute-start | bytes 1179656 | tf_op jit(solution)/shard_map/ppermute | solution.py:56
  367.0 15.9 %collective-permute-start.84 = (bf16[128,1536]{1,0:T(8,128)(2,1)S(1)}, bf16[128,1536]{1,0:T(8,128)(2,1)S(1)}, u32[]{:S(2)}, u32[]{:S(2)}) collective-permute-start(bf16[128,1536]{1,0:T(8,128)(2,1)S(1)} %add_convert_fusion.15), channel_id=1, source_target_pairs={{0,8},{2,10},{4,12},{6,14},{8,0},{10,2},{12,4},{14,6},{1,9},{3,11}... | collective-permute-start | bytes 1179656 | tf_op jit(solution)/shard_map/ppermute | solution.py:56
  370.0 16.3 %collective-permute-start.86 = (bf16[128,1536]{1,0:T(8,128)(2,1)S(1)}, bf16[128,1536]{1,0:T(8,128)(2,1)S(1)}, u32[]{:S(2)}, u32[]{:S(2)}) collective-permute-start(bf16[128,1536]{1,0:T(8,128)(2,1)S(1)} %get-tuple-element.1092), channel_id=1, source_target_pairs={{0,13},{1,12},{2,15},{3,14},{4,9},{5,8},{6,11},{7,10},{8,5},{9,4},... | collective-permute-start | bytes 1179656 | tf_op jit(solution)/shard_map/ppermute | solution.py:67
  396.5 16.2 %collective-permute-start.89 = (bf16[128,1536]{1,0:T(8,128)(2,1)S(1)}, bf16[128,1536]{1,0:T(8,128)(2,1)S(1)}, u32[]{:S(2)}, u32[]{:S(2)}) collective-permute-start(bf16[128,1536]{1,0:T(8,128)(2,1)S(1)} %copy-done.85), channel_id=1, source_target_pairs={{0,1},{1,0},{2,3},{3,2},{4,5},{5,4},{6,7},{7,6},{8,9},{9,8},{10,11... | collective-permute-start | bytes 1179656 | tf_op jit(solution)/shard_map/ppermute | solution.py:56
  396.6 16.0 %collective-permute-start.90 = (bf16[128,1536]{1,0:T(8,128)(2,1)S(1)}, bf16[128,1536]{1,0:T(8,128)(2,1)S(1)}, u32[]{:S(2)}, u32[]{:S(2)}) collective-permute-start(bf16[128,1536]{1,0:T(8,128)(2,1)S(1)} %copy-done.83), channel_id=1, source_target_pairs={{0,4},{2,6},{4,0},{6,2},{8,12},{10,14},{12,8},{14,10},{1,5},{3,7},... | collective-permute-start | bytes 1179656 | tf_op jit(solution)/shard_map/ppermute | solution.py:56
  396.9 15.8 %collective-permute-start.87 = (bf16[128,1536]{1,0:T(8,128)(2,1)}, bf16[128,1536]{1,0:T(8,128)(2,1)S(1)}, u32[]{:S(2)}, u32[]{:S(2)}) collective-permute-start(bf16[128,1536]{1,0:T(8,128)(2,1)} %get-tuple-element.1134), channel_id=1, source_target_pairs={{16,0},{17,1},{18,2},{19,3},{20,4},{21,5},{22,6},{23,7},{24,8},{25... | collective-permute-start | bytes 1179656 | tf_op jit(solution)/shard_map/ppermute | solution.py:1168
  412.7 15.6 %collective-permute-start.93 = (bf16[128,1536]{1,0:T(8,128)(2,1)S(1)}, bf16[128,1536]{1,0:T(8,128)(2,1)S(1)}, u32[]{:S(2)}, u32[]{:S(2)}) collective-permute-start(bf16[128,1536]{1,0:T(8,128)(2,1)S(1)} %collective-permute-done.87.refs_0_.refs_8_.grad), channel_id=1, source_target_pairs={{0,1},{1,0},{2,3},{3,2},{4,5},{5,4},{6,7},{7,6},{8,9},{9,8},{10,11... | collective-permute-start | bytes 1179656 | tf_op jit(solution)/shard_map/ppermute | solution.py:56
  465.0 16.3 %collective-permute-start.104 = (bf16[128,1536]{1,0:T(8,128)(2,1)S(1)}, bf16[128,1536]{1,0:T(8,128)(2,1)S(1)}, u32[]{:S(2)}, u32[]{:S(2)}) collective-permute-start(bf16[128,1536]{1,0:T(8,128)(2,1)S(1)} %add_convert_fusion.9), channel_id=1, source_target_pairs={{0,4},{2,6},{4,0},{6,2},{8,12},{10,14},{12,8},{14,10},{1,5},{3,7},... | collective-permute-start | bytes 1179656 | tf_op jit(solution)/shard_map/ppermute | solution.py:56
  465.4 15.9 %collective-permute-start.105 = (bf16[128,1536]{1,0:T(8,128)(2,1)S(1)}, bf16[128,1536]{1,0:T(8,128)(2,1)S(1)}, u32[]{:S(2)}, u32[]{:S(2)}) collective-permute-start(bf16[128,1536]{1,0:T(8,128)(2,1)S(1)} %add_convert_fusion.8), channel_id=1, source_target_pairs={{0,8},{2,10},{4,12},{6,14},{8,0},{10,2},{12,4},{14,6},{1,9},{3,11}... | collective-permute-start | bytes 1179656 | tf_op jit(solution)/shard_map/ppermute | solution.py:56
  553.1 19.4 %collective-permute-start.129 = (bf16[192,1152]{1,0:T(8,128)(2,1)S(1)}, bf16[192,1152]{1,0:T(8,128)(2,1)S(1)}, u32[]{:S(2)}, u32[]{:S(2)}) collective-permute-start(bf16[192,1152]{1,0:T(8,128)(2,1)S(1)} %get-tuple-element.1379), channel_id=1, source_target_pairs={{0,13},{1,12},{2,15},{3,14},{4,9},{5,8},{6,11},{7,10},{8,5},{9,4},... | collective-permute-start | bytes 1327112 | tf_op jit(solution)/shard_map/ppermute | solution.py:67
  (286 other events, 3440.4 us)
